TPU v7x, 128 devices: a whole 4x4x4 slice. The times are simulated.
128 devices in a mesh: seq: 32 (over z, x, core), mp: 4 (over y).
Axes of the slice: x: 4, y: 4, z: 4, core: 2. Of those that a mesh axis runs over, the one named last changes fastest.
Arguments:
- inputs: bfloat16 [4096, 1536], P('seq', 'mp'), may hold values from -6 to 6
- cotangent: bfloat16 [4096, 1536], P('seq', 'mp'), may hold values from -6 to 6
- conv_kernels: bfloat16 [4, 3, 768, 1536], P(None, None, 'mp'), may hold values from -0.09375 to 0.09375
- point_weights: bfloat16 [4, 768, 1536], P(None, 'mp'), may hold values from -0.21875 to 0.21875
Outputs:
- input_grad: float32 [4096, 1536], P('seq', 'mp')
- kernel_grad: float32 [4, 3, 768, 1536], P(None, None, ('mp', 'seq'))
- point_grad: float32 [4, 768, 1536], P(None, ('mp', 'seq'))
All inputs are finite; a program needn't handle non-finite values.
Results may differ from a plain program's by a relative error of at most 0.03.
Values may be sent and summed in bfloat16 or wider, within the bound.
No kernel may reach another device: no remote copies, remote signals or barrier semaphores. Data moves between devices by JAX's collectives and lax.ppermute only.
A program may use at most 192 MiB of HBM per device.

v0:
```python
import jax
import jax.numpy as jnp
from jax import lax
from jax.sharding import PartitionSpec as P

LAYERS = 4


def from_behind(x, axis, by):
    peers = lax.axis_size(axis)
    pairs = [(i, i + by) for i in range(peers) if 0 <= i + by < peers]
    return lax.ppermute(x, axis, pairs)


def gelu_slope(values):
    return jax.vjp(jax.nn.gelu, values)[1](jnp.ones_like(values))[0]


def neighbour(shard, steps):
    if steps == 0:
        return shard
    return from_behind(shard, "seq", -steps)


def fetch(shard, offset):
    length = shard.shape[0]
    whole_steps = offset // length
    remainder = offset % length
    if remainder == 0:
        return neighbour(shard, whole_steps)
    first = neighbour(shard[remainder:], whole_steps)
    second = neighbour(shard[:remainder], whole_steps + 1)
    return jnp.concatenate([first, second], axis=0)


def full_channels(values):
    return lax.all_gather(values, "mp", axis=1, tiled=True)


def channel_sum(terms):
    return lax.psum_scatter(terms, "mp", scatter_dimension=1, tiled=True)


def weight_sum(kernel_terms, point_terms):
    return (
        lax.psum_scatter(
            kernel_terms.astype(jnp.bfloat16), "seq", scatter_dimension=1, tiled=True
        ).astype(jnp.float32),
        lax.psum_scatter(
            point_terms.astype(jnp.bfloat16), "seq", scatter_dimension=1, tiled=True
        ).astype(jnp.float32),
    )


def shards(inputs, cotangent, conv_kernels, point_weights):
    length = inputs.shape[0]
    stream = inputs
    saved = []
    for layer_index in range(LAYERS):
        distance = length * 2**layer_index // 4
        active = jax.nn.gelu(stream.astype(jnp.float32)).astype(jnp.bfloat16)
        gathered = full_channels(active)
        taps = (fetch(gathered, -distance), gathered, fetch(gathered, distance))
        inner = jnp.dot(taps[0], conv_kernels[layer_index, 0].T, preferred_element_type=jnp.float32)
        for tap_index in (1, 2):
            inner = inner + jnp.dot(
                taps[tap_index],
                conv_kernels[layer_index, tap_index].T,
                preferred_element_type=jnp.float32,
            )
        hidden = jax.nn.gelu(inner).astype(jnp.bfloat16)
        projected = jnp.dot(hidden, point_weights[layer_index], preferred_element_type=jnp.float32)
        output = stream.astype(jnp.float32) + channel_sum(projected)
        saved.append((stream, taps, inner, hidden))
        stream = output.astype(jnp.bfloat16)
    gradient = cotangent.astype(jnp.float32)
    kernel_list = [None] * LAYERS
    point_list = [None] * LAYERS
    for layer_index in reversed(range(LAYERS)):
        before, taps, inner, hidden = saved[layer_index]
        distance = length * 2**layer_index // 4
        grad_b = full_channels(gradient.astype(jnp.bfloat16))
        hidden_grad = jnp.dot(
            grad_b, point_weights[layer_index].T, preferred_element_type=jnp.float32
        )
        inner_grad = (hidden_grad * gelu_slope(inner)).astype(jnp.bfloat16)
        point_term = jnp.dot(hidden.T, grad_b, preferred_element_type=jnp.float32)
        kernel_term = jnp.stack(
            [
                jnp.dot(inner_grad.T, taps[tap_index], preferred_element_type=jnp.float32)
                for tap_index in range(3)
            ]
        )
        back = jnp.dot(
            fetch(inner_grad, distance),
            conv_kernels[layer_index, 0],
            preferred_element_type=jnp.float32,
        )
        back = back + jnp.dot(
            inner_grad, conv_kernels[layer_index, 1], preferred_element_type=jnp.float32
        )
        back = back + jnp.dot(
            fetch(inner_grad, -distance),
            conv_kernels[layer_index, 2],
            preferred_element_type=jnp.float32,
        )
        gradient = gradient + gelu_slope(before.astype(jnp.float32)) * channel_sum(back)
        kernel_sum, point_total = weight_sum(kernel_term, point_term[None])
        kernel_list[layer_index] = kernel_sum
        point_list[layer_index] = point_total[0]
    kernel_out = jnp.stack(kernel_list)
    point_out = jnp.stack(point_list)
    return (gradient, kernel_out, point_out)


def solution(mesh):
    return jax.shard_map(
        shards,
        mesh=mesh,
        in_specs=(P("seq", "mp"), P("seq", "mp"), P(None, None, "mp", None), P(None, "mp", None)),
        out_specs=(
            P("seq", "mp"),
            P(None, None, ("mp", "seq"), None),
            P(None, ("mp", "seq"), None),
        ),
        check_vma=False,
    )
```

profile of v0, /device:TPU:0, one launch (start us, length us, event | category | flops | bytes accessed | tf_op | source)
XLA Modules:
  0.0 557.7 jit_solution(10216558827408069132)
XLA Ops:
  8.2 13.3 %all_gather.24 = bf16[128,1536]{1,0:T(8,128)(2,1)S(1)} all-gather(bf16[128,384]{1,0:T(8,128)(2,1)S(1)} %fusion.141), channel_id=1, replica_groups=mesh['seq'=32,'mp'=4] {'mp'}, dimensions={1}, use_global_device_ids=true | all-gather | bytes 491520 | tf_op jit(solution)/shard_map/all_gather | solution.py:37
  22.8 3.2 collective-permute-start
  26.1 1.6 fusion.78
  33.1 25.1 %reduce-scatter.24.cloned.1.call-done = f32[128,384]{1,0:T(8,128)} async-done(((f32[128,1536]{1,0:T(8,128)}), f32[128,384]{1,0:T(8,128)}) %reduce-scatter.24.cloned.1.call-update) | async-done | bytes 196624 | tf_op jit(solution)/shard_map/reduce_scatter | solution.py:41
  59.2 12.7 %all_gather.25 = bf16[128,1536]{1,0:T(8,128)(2,1)S(1)} all-gather(bf16[128,384]{1,0:T(8,128)(2,1)S(1)} %get-tuple-element.29), channel_id=1, replica_groups=mesh['seq'=32,'mp'=4] {'mp'}, dimensions={1}, use_global_device_ids=true | all-gather | bytes 491520 | tf_op jit(solution)/shard_map/all_gather | solution.py:37
  73.3 3.0 collective-permute-start.2
  77.7 1.4 fusion.61
  79.2 1.5 fusion.26
  82.6 23.9 %reduce-scatter.26.cloned.1.call-done = f32[128,384]{1,0:T(8,128)} async-done(((f32[128,1536]{1,0:T(8,128)}), f32[128,384]{1,0:T(8,128)}) %reduce-scatter.26.cloned.1.call-update) | async-done | bytes 196624 | tf_op jit(solution)/shard_map/reduce_scatter | solution.py:41
  107.6 12.7 %all_gather.26 = bf16[128,1536]{1,0:T(8,128)(2,1)S(1)} all-gather(bf16[128,384]{1,0:T(8,128)(2,1)S(1)} %get-tuple-element.27), channel_id=1, replica_groups=mesh['seq'=32,'mp'=4] {'mp'}, dimensions={1}, use_global_device_ids=true | all-gather | bytes 491520 | tf_op jit(solution)/shard_map/all_gather | solution.py:37
  121.6 3.1 collective-permute-start.4
  126.0 1.5 fusion.48
  129.0 2.3 fusion.44
  131.3 25.9 %reduce-scatter.28.cloned.1.call-done = f32[128,384]{1,0:T(8,128)} async-done(((f32[128,1536]{1,0:T(8,128)}), f32[128,384]{1,0:T(8,128)}) %reduce-scatter.28.cloned.1.call-update) | async-done | bytes 196624 | tf_op jit(solution)/shard_map/reduce_scatter | solution.py:41
  158.2 12.8 %all_gather.28 = bf16[128,1536]{1,0:T(8,128)(2,1)S(1)} all-gather(bf16[128,384]{1,0:T(8,128)(2,1)S(1)} %fusion.137), channel_id=1, replica_groups=mesh['seq'=32,'mp'=4] {'mp'}, dimensions={1}, use_global_device_ids=true | all-gather | bytes 491520 | tf_op jit(solution)/shard_map/all_gather | solution.py:37
  172.3 13.2 %all_gather.27 = bf16[128,1536]{1,0:T(8,128)(2,1)S(1)} all-gather(bf16[128,384]{1,0:T(8,128)(2,1)S(1)} %copy-done.31), channel_id=1, replica_groups=mesh['seq'=32,'mp'=4] {'mp'}, dimensions={1}, use_global_device_ids=true | all-gather | bytes 491520 | tf_op jit(solution)/shard_map/all_gather | solution.py:37
  185.5 4.3 collective-permute-start.6
  191.2 1.5 fusion.33
  192.7 2.9 collective-permute-done.6
  195.6 1.5 fusion.24
  198.5 4.4 collective-permute-start.9
  207.2 3.3 collective-permute-done.8
  210.4 2.2 fusion.4
  212.7 27.7 %reduce-scatter.30.cloned.1.call-done = f32[128,384]{1,0:T(8,128)} async-done(((f32[128,1536]{1,0:T(8,128)}), f32[128,384]{1,0:T(8,128)}) %reduce-scatter.30.cloned.1.call-update) | async-done | bytes 196624 | tf_op jit(solution)/shard_map/reduce_scatter | solution.py:41
  241.6 12.7 %all_gather.29 = bf16[128,1536]{1,0:T(8,128)(2,1)S(1)} all-gather(bf16[128,384]{1,0:T(8,128)(2,1)S(1)} %get-tuple-element.25), channel_id=1, replica_groups=mesh['seq'=32,'mp'=4] {'mp'}, dimensions={1}, use_global_device_ids=true | all-gather | bytes 491520 | tf_op jit(solution)/shard_map/all_gather | solution.py:37
  261.0 2.1 collective-permute-done.10
  263.2 2.2 fusion.5
  265.5 26.2 %reduce-scatter.32.cloned.1.call-done = f32[128,384]{1,0:T(8,128)} async-done(((f32[128,1536]{1,0:T(8,128)}), f32[128,384]{1,0:T(8,128)}) %reduce-scatter.32.cloned.1.call-update) | async-done | bytes 196624 | tf_op jit(solution)/shard_map/reduce_scatter | solution.py:41
  291.7 1.8 fusion.217
  293.5 12.8 %all_gather.30 = bf16[128,1536]{1,0:T(8,128)(2,1)S(1)} all-gather(bf16[128,384]{1,0:T(8,128)(2,1)S(1)} %get-tuple-element.23), channel_id=1, replica_groups=mesh['seq'=32,'mp'=4] {'mp'}, dimensions={1}, use_global_device_ids=true | all-gather | bytes 491520 | tf_op jit(solution)/shard_map/all_gather | solution.py:37
  306.2 1.5 fusion.29
  313.2 2.1 collective-permute-done.12
  315.3 2.3 fusion.6
  324.7 19.3 %reduce-scatter.34.cloned.1.call-done = f32[128,384]{1,0:T(8,128)} async-done(((f32[128,1536]{1,0:T(8,128)}), f32[128,384]{1,0:T(8,128)}) %reduce-scatter.34.cloned.1.call-update) | async-done | bytes 196624 | tf_op jit(solution)/shard_map/reduce_scatter | solution.py:41
  344.0 1.9 fusion.215
  345.9 12.7 %all_gather.31 = bf16[128,1536]{1,0:T(8,128)(2,1)S(1)} all-gather(bf16[128,384]{1,0:T(8,128)(2,1)S(1)} %get-tuple-element.21), channel_id=1, replica_groups=mesh['seq'=32,'mp'=4] {'mp'}, dimensions={1}, use_global_device_ids=true | all-gather | bytes 491520 | tf_op jit(solution)/shard_map/all_gather | solution.py:37
  358.6 1.5 fusion.30
  365.8 2.1 collective-permute-done.14
  367.8 2.3 fusion.7
  370.4 1.5 pad_maximum_fusion.2
  372.9 1.5 pad_maximum_fusion.1
  379.2 81.8 %fusion.214 = (bf16[8,1536]{1,0:T(8,128)(2,1)S(1)}, bf16[8,1536]{1,0:T(8,128)(2,1)S(1)}, bf16[8,1536]{1,0:T(8,128)(2,1)S(1)}, bf16[8,1536]{1,0:T(8,128)(2,1)S(1)}) fusion(bf16[1,192,1536]{2,1,0:T(8,128)(2,1)S(1)} %fusion.23, bf16[1,192,1536]{2,1,0:T(8,128)(2,1)S(1)} %fusion.22, bf16[1,192,1536]{2,1,0:T(8,128)(2,1)S(1)} %fusion.21, ...), kind=kCustom, calls=%all-reduce-scatter.4 | all-reduce-scatter fusion | flops 1572865 | bytes 2458112
  467.6 6.0 %collective-permute-start.39 = (bf16[6,1536]{1,0:T(8,128)(2,1)S(1)}, bf16[6,1536]{1,0:T(8,128)(2,1)S(1)}, u32[]{:S(2)}, u32[]{:S(2)}) collective-permute-start(bf16[6,1536]{1,0:T(8,128)(2,1)S(1)} %slice.145), channel_id=1, source_target_pairs={{0,32},{4,36},{8,40},{12,44},{16,48},{20,52},{24,56},{28,60},{32,6... | collective-permute-start | bytes 55304
  473.6 1.9 collective-permute-start.47
  475.5 5.7 %collective-permute-start.19 = (bf16[8,1536]{1,0:T(8,128)(2,1)S(1)}, bf16[8,1536]{1,0:T(8,128)(2,1)S(1)}, u32[]{:S(2)}, u32[]{:S(2)}) collective-permute-start(bf16[8,1536]{1,0:T(8,128)(2,1)S(1)} %get-tuple-element.20), channel_id=1, source_target_pairs={{0,16},{4,20},{8,24},{12,28},{16,32},{20,36},{24,40},{28,44},{32,4... | collective-permute-start | bytes 73736
  481.3 3.7 collective-permute-start.20
  485.0 3.9 collective-permute-start.21
  490.2 2.6 collective-permute-start.24
  492.8 3.0 collective-permute-start.25
  495.8 1.6 collective-permute-start.26
  497.5 4.9 collective-permute-start.27
  502.4 1.9 collective-permute-start.28
  504.3 2.4 collective-permute-start.29
  506.8 1.5 collective-permute-start.30
  509.7 2.3 collective-permute-start.33
  512.0 2.7 collective-permute-start.34
  514.8 3.8 collective-permute-start.35
  518.6 1.9 collective-permute-start.36
  520.5 1.9 collective-permute-start.37
  525.2 2.1 collective-permute-start.41
  527.4 3.0 collective-permute-start.42
  530.4 3.8 collective-permute-start.43
  534.2 1.6 collective-permute-start.44
  545.8 1.7 fusion.128
  (233 shorter events, 83.3 us)
Async XLA Ops:
  7.2 51.0 %reduce-scatter.24.cloned.1.call-start = ((), (), s32[]{:S(2)}) async-start(), calls=%async_computation.7 | async-start | bytes 983040 | tf_op jit(solution)/shard_map/reduce_scatter | solution.py:41
  21.5 6.1 %collective-permute-start.1 = (bf16[32,1536]{1,0:T(8,128)(2,1)S(1)}, bf16[32,1536]{1,0:T(8,128)(2,1)S(1)}, u32[]{:S(2)}, u32[]{:S(2)}) collective-permute-start(bf16[32,1536]{1,0:T(8,128)(2,1)S(1)} %get-tuple-element.34), channel_id=1, source_target_pairs={{4,0},{8,4},{12,8},{16,12},{20,16},{24,20},{28,24},{32,28},{36,32}... | collective-permute-start | bytes 294920 | tf_op jit(solution)/shard_map/ppermute | solution.py:12
  22.8 6.3 %collective-permute-start = (bf16[32,1536]{1,0:T(8,128)(2,1)S(1)}, bf16[32,1536]{1,0:T(8,128)(2,1)S(1)}, u32[]{:S(2)}, u32[]{:S(2)}) collective-permute-start(bf16[32,1536]{1,0:T(8,128)(2,1)S(1)} %get-tuple-element.33), channel_id=1, source_target_pairs={{0,4},{4,8},{8,12},{12,16},{16,20},{20,24},{24,28},{28,32},{32,36}... | collective-permute-start | bytes 294920 | tf_op jit(solution)/shard_map/ppermute | solution.py:12
  33.0 73.5 %reduce-scatter.26.cloned.1.call-start = ((), (), s32[]{:S(2)}) async-start(), calls=%async_computation.8 | async-start | bytes 983040 | tf_op jit(solution)/shard_map/reduce_scatter | solution.py:41
  59.2 47.4 %copy-start.11 = (bf16[128,384]{1,0:T(8,128)(2,1)}, bf16[128,384]{1,0:T(8,128)(2,1)S(1)}, u32[]{:S(2)}) copy-start(bf16[128,384]{1,0:T(8,128)(2,1)S(1)} %get-tuple-element.30) | copy-start | bytes 294916
  72.0 5.7 %collective-permute-start.3 = (bf16[64,1536]{1,0:T(8,128)(2,1)S(1)}, bf16[64,1536]{1,0:T(8,128)(2,1)S(1)}, u32[]{:S(2)}, u32[]{:S(2)}) collective-permute-start(bf16[64,1536]{1,0:T(8,128)(2,1)S(1)} %get-tuple-element.32), channel_id=1, source_target_pairs={{4,0},{8,4},{12,8},{16,12},{20,16},{24,20},{28,24},{32,28},{36,32}... | collective-permute-start | bytes 589832 | tf_op jit(solution)/shard_map/ppermute | solution.py:12
  73.3 5.9 %collective-permute-start.2 = (bf16[64,1536]{1,0:T(8,128)(2,1)S(1)}, bf16[64,1536]{1,0:T(8,128)(2,1)S(1)}, u32[]{:S(2)}, u32[]{:S(2)}) collective-permute-start(bf16[64,1536]{1,0:T(8,128)(2,1)S(1)} %get-tuple-element.31), channel_id=1, source_target_pairs={{0,4},{4,8},{8,12},{12,16},{16,20},{20,24},{24,28},{28,32},{32,36}... | collective-permute-start | bytes 589832 | tf_op jit(solution)/shard_map/ppermute | solution.py:12
  82.6 74.6 %reduce-scatter.28.cloned.1.call-start = ((), (), s32[]{:S(2)}) async-start(), calls=%async_computation.9 | async-start | bytes 983040 | tf_op jit(solution)/shard_map/reduce_scatter | solution.py:41
  120.3 5.7 %collective-permute-start.5 = (bf16[128,1536]{1,0:T(8,128)(2,1)S(1)}, bf16[128,1536]{1,0:T(8,128)(2,1)S(1)}, u32[]{:S(2)}, u32[]{:S(2)}) collective-permute-start(bf16[128,1536]{1,0:T(8,128)(2,1)S(1)} %all_gather.26), channel_id=1, source_target_pairs={{4,0},{8,4},{12,8},{16,12},{20,16},{24,20},{28,24},{32,28},{36,32}... | collective-permute-start | bytes 1179656 | tf_op jit(solution)/shard_map/ppermute | solution.py:12
  121.6 6.0 %collective-permute-start.4 = (bf16[128,1536]{1,0:T(8,128)(2,1)S(1)}, bf16[128,1536]{1,0:T(8,128)(2,1)S(1)}, u32[]{:S(2)}, u32[]{:S(2)}) collective-permute-start(bf16[128,1536]{1,0:T(8,128)(2,1)S(1)} %all_gather.26), channel_id=1, source_target_pairs={{0,4},{4,8},{8,12},{12,16},{16,20},{20,24},{24,28},{28,32},{32,36}... | collective-permute-start | bytes 1179656 | tf_op jit(solution)/shard_map/ppermute | solution.py:12
  127.5 44.7 %copy-start.31 = (bf16[128,384]{1,0:T(8,128)(2,1)S(1)}, bf16[128,384]{1,0:T(8,128)(2,1)}, u32[]{:S(2)}) copy-start(bf16[128,384]{1,0:T(8,128)(2,1)} %param.5) | copy-start | bytes 294916
  131.3 109.2 %reduce-scatter.30.cloned.1.call-start = ((), (), s32[]{:S(2)}) async-start(), calls=%async_computation.10 | async-start | bytes 983040 | tf_op jit(solution)/shard_map/reduce_scatter | solution.py:41
  171.0 84.7 %copy-start.4 = (bf16[128,1536]{1,0:T(8,128)(2,1)}, bf16[128,1536]{1,0:T(8,128)(2,1)S(1)}, u32[]{:S(2)}) copy-start(bf16[128,1536]{1,0:T(8,128)(2,1)S(1)} %all_gather.28) | copy-start | bytes 1179652
  171.0 20.2 %collective-permute-start.7 = (bf16[128,1536]{1,0:T(8,128)(2,1)S(1)}, bf16[128,1536]{1,0:T(8,128)(2,1)S(1)}, u32[]{:S(2)}, u32[]{:S(2)}) collective-permute-start(bf16[128,1536]{1,0:T(8,128)(2,1)S(1)} %all_gather.28), channel_id=1, source_target_pairs={{8,0},{12,4},{16,8},{20,12},{24,16},{28,20},{32,24},{36,28},{40,32... | collective-permute-start | bytes 1179656 | tf_op jit(solution)/shard_map/ppermute | solution.py:12
  185.5 10.1 %collective-permute-start.6 = (bf16[128,1536]{1,0:T(8,128)(2,1)S(1)}, bf16[128,1536]{1,0:T(8,128)(2,1)S(1)}, u32[]{:S(2)}, u32[]{:S(2)}) collective-permute-start(bf16[128,1536]{1,0:T(8,128)(2,1)S(1)} %all_gather.28), channel_id=1, source_target_pairs={{0,8},{4,12},{8,16},{12,20},{16,24},{20,28},{24,32},{28,36},{32,40... | collective-permute-start | bytes 1179656 | tf_op jit(solution)/shard_map/ppermute | solution.py:12
  198.5 7.2 %collective-permute-start.9 = (bf16[128,192]{0,1:T(8,128)(2,1)S(1)}, bf16[128,192]{0,1:T(8,128)(2,1)S(1)}, u32[]{:S(2)}, u32[]{:S(2)}) collective-permute-start(bf16[128,192]{0,1:T(8,128)(2,1)S(1)} %fusion.181), channel_id=1, source_target_pairs={{0,8},{4,12},{8,16},{12,20},{16,24},{20,28},{24,32},{28,36},{32,40... | collective-permute-start | bytes 147464 | tf_op jit(solution)/shard_map/ppermute | solution.py:12
  204.3 6.1 %collective-permute-start.8 = (bf16[128,192]{0,1:T(8,128)(2,1)S(1)}, bf16[128,192]{0,1:T(8,128)(2,1)S(1)}, u32[]{:S(2)}, u32[]{:S(2)}) collective-permute-start(bf16[128,192]{0,1:T(8,128)(2,1)S(1)} %fusion.181), channel_id=1, source_target_pairs={{8,0},{12,4},{16,8},{20,12},{24,16},{28,20},{32,24},{36,28},{40,32... | collective-permute-start | bytes 147464 | tf_op jit(solution)/shard_map/ppermute | solution.py:12
  212.7 79.0 %reduce-scatter.32.cloned.1.call-start = ((), (), s32[]{:S(2)}) async-start(), calls=%async_computation.11 | async-start | bytes 983040 | tf_op jit(solution)/shard_map/reduce_scatter | solution.py:41
  255.7 67.6 %copy-start.14 = (bf16[128,192]{0,1:T(8,128)(2,1)}, bf16[128,192]{0,1:T(8,128)(2,1)S(1)}, u32[]{:S(2)}) copy-start(bf16[128,192]{0,1:T(8,128)(2,1)S(1)} %fusion.28) | copy-start | bytes 147460
  255.7 4.0 collective-permute-start.11
  258.4 4.8 collective-permute-start.10
  261.0 45.2 %copy-start.24 = (f32[128,192]{0,1:T(8,128)S(1)}, f32[128,192]{0,1:T(8,128)}, u32[]{:S(2)}) copy-start(f32[128,192]{0,1:T(8,128)} %copy-done.23) | copy-start | bytes 294916
  265.5 78.6 %reduce-scatter.34.cloned.1.call-start = ((), (), s32[]{:S(2)}) async-start(), calls=%async_computation.12 | async-start | bytes 983040 | tf_op jit(solution)/shard_map/reduce_scatter | solution.py:41
  307.8 4.0 collective-permute-start.13
  310.5 4.8 collective-permute-start.12
  317.7 228.2 %reduce-scatter.36.cloned.1.call-start = ((), (), s32[]{:S(2)}) async-start(), calls=%async_computation.13 | async-start | bytes 983040 | tf_op jit(solution)/shard_map/reduce_scatter | solution.py:41
  361.6 2.7 collective-permute-start.15
  363.0 4.8 collective-permute-start.14
  370.2 177.4 %all-reduce.16.cloned.1.call-start = ((), (), s32[]{:S(2)}) async-start(), calls=%async_computation.14 | async-start | bytes 14155776
  378.6 160.0 %copy-start.41 = (u32[128]{0:T(128)S(1)}, u32[128]{0:T(128)}, u32[]{:S(2)}) copy-start(u32[128]{0:T(128)} %constant.26) | copy-start | bytes 1540
  379.2 166.7 %copy-start.13 = (bf16[128,384]{1,0:T(8,128)(2,1)S(1)}, bf16[128,384]{1,0:T(8,128)(2,1)}, u32[]{:S(2)}) copy-start(bf16[128,384]{1,0:T(8,128)(2,1)} %param.4) | copy-start | bytes 294916
  379.2 166.6 %copy-start.16 = (f32[128,384]{1,0:T(8,128)S(1)}, f32[128,384]{1,0:T(8,128)}, u32[]{:S(2)}) copy-start(f32[128,384]{1,0:T(8,128)} %get-tuple-element.22) | copy-start | bytes 589828
  461.1 6.6 %collective-permute-start.23 = (bf16[6,1536]{1,0:T(8,128)(2,1)S(1)}, bf16[6,1536]{1,0:T(8,128)(2,1)S(1)}, u32[]{:S(2)}, u32[]{:S(2)}) collective-permute-start(bf16[6,1536]{1,0:T(8,128)(2,1)S(1)} %slice.143), channel_id=1, source_target_pairs={{0,32},{4,36},{8,40},{12,44},{16,48},{20,52},{24,56},{28,60},{32,6... | collective-permute-start | bytes 55304
  462.4 11.2 %collective-permute-start.31 = (bf16[6,1536]{1,0:T(8,128)(2,1)S(1)}, bf16[6,1536]{1,0:T(8,128)(2,1)S(1)}, u32[]{:S(2)}, u32[]{:S(2)}) collective-permute-start(bf16[6,1536]{1,0:T(8,128)(2,1)S(1)} %slice.144), channel_id=1, source_target_pairs={{0,32},{4,36},{8,40},{12,44},{16,48},{20,52},{24,56},{28,60},{32,6... | collective-permute-start | bytes 55304
  463.7 21.3 %collective-permute-start.16 = (bf16[8,1536]{1,0:T(8,128)(2,1)S(1)}, bf16[8,1536]{1,0:T(8,128)(2,1)S(1)}, u32[]{:S(2)}, u32[]{:S(2)}) collective-permute-start(bf16[8,1536]{1,0:T(8,128)(2,1)S(1)} %get-tuple-element.20), channel_id=1, source_target_pairs={{0,4},{4,8},{8,12},{12,16},{16,20},{20,24},{24,28},{28,32},{32,36}... | collective-permute-start | bytes 73736
  465.0 23.9 %collective-permute-start.17 = (bf16[8,1536]{1,0:T(8,128)(2,1)S(1)}, bf16[8,1536]{1,0:T(8,128)(2,1)S(1)}, u32[]{:S(2)}, u32[]{:S(2)}) collective-permute-start(bf16[8,1536]{1,0:T(8,128)(2,1)S(1)} %get-tuple-element.20), channel_id=1, source_target_pairs={{0,8},{4,12},{8,16},{12,20},{16,24},{20,28},{24,32},{28,36},{32,40... | collective-permute-start | bytes 73736
  466.3 23.9 %collective-permute-start.18 = (bf16[8,1536]{1,0:T(8,128)(2,1)S(1)}, bf16[8,1536]{1,0:T(8,128)(2,1)S(1)}, u32[]{:S(2)}, u32[]{:S(2)}) collective-permute-start(bf16[8,1536]{1,0:T(8,128)(2,1)S(1)} %get-tuple-element.20), channel_id=1, source_target_pairs={{0,12},{4,16},{8,20},{12,24},{16,28},{20,32},{24,36},{28,40},{32,4... | collective-permute-start | bytes 73736
  467.6 7.9 %collective-permute-start.39 = (bf16[6,1536]{1,0:T(8,128)(2,1)S(1)}, bf16[6,1536]{1,0:T(8,128)(2,1)S(1)}, u32[]{:S(2)}, u32[]{:S(2)}) collective-permute-start(bf16[6,1536]{1,0:T(8,128)(2,1)S(1)} %slice.145), channel_id=1, source_target_pairs={{0,32},{4,36},{8,40},{12,44},{16,48},{20,52},{24,56},{28,60},{32,6... | collective-permute-start | bytes 55304
  473.6 7.7 %collective-permute-start.47 = (bf16[6,1536]{1,0:T(8,128)(2,1)S(1)}, bf16[6,1536]{1,0:T(8,128)(2,1)S(1)}, u32[]{:S(2)}, u32[]{:S(2)}) collective-permute-start(bf16[6,1536]{1,0:T(8,128)(2,1)S(1)} %slice.146), channel_id=1, source_target_pairs={{0,32},{4,36},{8,40},{12,44},{16,48},{20,52},{24,56},{28,60},{32,6... | collective-permute-start | bytes 55304
  475.5 17.3 %collective-permute-start.19 = (bf16[8,1536]{1,0:T(8,128)(2,1)S(1)}, bf16[8,1536]{1,0:T(8,128)(2,1)S(1)}, u32[]{:S(2)}, u32[]{:S(2)}) collective-permute-start(bf16[8,1536]{1,0:T(8,128)(2,1)S(1)} %get-tuple-element.20), channel_id=1, source_target_pairs={{0,16},{4,20},{8,24},{12,28},{16,32},{20,36},{24,40},{28,44},{32,4... | collective-permute-start | bytes 73736
  481.3 14.5 %collective-permute-start.20 = (bf16[8,1536]{1,0:T(8,128)(2,1)S(1)}, bf16[8,1536]{1,0:T(8,128)(2,1)S(1)}, u32[]{:S(2)}, u32[]{:S(2)}) collective-permute-start(bf16[8,1536]{1,0:T(8,128)(2,1)S(1)} %get-tuple-element.20), channel_id=1, source_target_pairs={{0,20},{4,24},{8,28},{12,32},{16,36},{20,40},{24,44},{28,48},{32,5... | collective-permute-start | bytes 73736
  485.0 12.4 %collective-permute-start.21 = (bf16[8,1536]{1,0:T(8,128)(2,1)S(1)}, bf16[8,1536]{1,0:T(8,128)(2,1)S(1)}, u32[]{:S(2)}, u32[]{:S(2)}) collective-permute-start(bf16[8,1536]{1,0:T(8,128)(2,1)S(1)} %get-tuple-element.20), channel_id=1, source_target_pairs={{0,24},{4,28},{8,32},{12,36},{16,40},{20,44},{24,48},{28,52},{32,5... | collective-permute-start | bytes 73736
  488.9 13.5 %collective-permute-start.22 = (bf16[8,1536]{1,0:T(8,128)(2,1)S(1)}, bf16[8,1536]{1,0:T(8,128)(2,1)S(1)}, u32[]{:S(2)}, u32[]{:S(2)}) collective-permute-start(bf16[8,1536]{1,0:T(8,128)(2,1)S(1)} %get-tuple-element.20), channel_id=1, source_target_pairs={{0,28},{4,32},{8,36},{12,40},{16,44},{20,48},{24,52},{28,56},{32,6... | collective-permute-start | bytes 73736
  490.2 14.1 %collective-permute-start.24 = (bf16[8,1536]{1,0:T(8,128)(2,1)S(1)}, bf16[8,1536]{1,0:T(8,128)(2,1)S(1)}, u32[]{:S(2)}, u32[]{:S(2)}) collective-permute-start(bf16[8,1536]{1,0:T(8,128)(2,1)S(1)} %get-tuple-element.19), channel_id=1, source_target_pairs={{0,4},{4,8},{8,12},{12,16},{16,20},{20,24},{24,28},{28,32},{32,36}... | collective-permute-start | bytes 73736
  492.8 14.0 %collective-permute-start.25 = (bf16[8,1536]{1,0:T(8,128)(2,1)S(1)}, bf16[8,1536]{1,0:T(8,128)(2,1)S(1)}, u32[]{:S(2)}, u32[]{:S(2)}) collective-permute-start(bf16[8,1536]{1,0:T(8,128)(2,1)S(1)} %get-tuple-element.19), channel_id=1, source_target_pairs={{0,8},{4,12},{8,16},{12,20},{16,24},{20,28},{24,32},{28,36},{32,40... | collective-permute-start | bytes 73736
  495.8 12.4 %collective-permute-start.26 = (bf16[8,1536]{1,0:T(8,128)(2,1)S(1)}, bf16[8,1536]{1,0:T(8,128)(2,1)S(1)}, u32[]{:S(2)}, u32[]{:S(2)}) collective-permute-start(bf16[8,1536]{1,0:T(8,128)(2,1)S(1)} %get-tuple-element.19), channel_id=1, source_target_pairs={{0,12},{4,16},{8,20},{12,24},{16,28},{20,32},{24,36},{28,40},{32,4... | collective-permute-start | bytes 73736
  497.5 12.2 %collective-permute-start.27 = (bf16[8,1536]{1,0:T(8,128)(2,1)S(1)}, bf16[8,1536]{1,0:T(8,128)(2,1)S(1)}, u32[]{:S(2)}, u32[]{:S(2)}) collective-permute-start(bf16[8,1536]{1,0:T(8,128)(2,1)S(1)} %get-tuple-element.19), channel_id=1, source_target_pairs={{0,16},{4,20},{8,24},{12,28},{16,32},{20,36},{24,40},{28,44},{32,4... | collective-permute-start | bytes 73736
  502.4 9.6 %collective-permute-start.28 = (bf16[8,1536]{1,0:T(8,128)(2,1)S(1)}, bf16[8,1536]{1,0:T(8,128)(2,1)S(1)}, u32[]{:S(2)}, u32[]{:S(2)}) collective-permute-start(bf16[8,1536]{1,0:T(8,128)(2,1)S(1)} %get-tuple-element.19), channel_id=1, source_target_pairs={{0,20},{4,24},{8,28},{12,32},{16,36},{20,40},{24,44},{28,48},{32,5... | collective-permute-start | bytes 73736
  504.3 10.4 %collective-permute-start.29 = (bf16[8,1536]{1,0:T(8,128)(2,1)S(1)}, bf16[8,1536]{1,0:T(8,128)(2,1)S(1)}, u32[]{:S(2)}, u32[]{:S(2)}) collective-permute-start(bf16[8,1536]{1,0:T(8,128)(2,1)S(1)} %get-tuple-element.19), channel_id=1, source_target_pairs={{0,24},{4,28},{8,32},{12,36},{16,40},{20,44},{24,48},{28,52},{32,5... | collective-permute-start | bytes 73736
  506.8 11.8 %collective-permute-start.30 = (bf16[8,1536]{1,0:T(8,128)(2,1)S(1)}, bf16[8,1536]{1,0:T(8,128)(2,1)S(1)}, u32[]{:S(2)}, u32[]{:S(2)}) collective-permute-start(bf16[8,1536]{1,0:T(8,128)(2,1)S(1)} %get-tuple-element.19), channel_id=1, source_target_pairs={{0,28},{4,32},{8,36},{12,40},{16,44},{20,48},{24,52},{28,56},{32,6... | collective-permute-start | bytes 73736
  508.3 12.2 %collective-permute-start.32 = (bf16[8,1536]{1,0:T(8,128)(2,1)S(1)}, bf16[8,1536]{1,0:T(8,128)(2,1)S(1)}, u32[]{:S(2)}, u32[]{:S(2)}) collective-permute-start(bf16[8,1536]{1,0:T(8,128)(2,1)S(1)} %get-tuple-element.18), channel_id=1, source_target_pairs={{0,4},{4,8},{8,12},{12,16},{16,20},{20,24},{24,28},{28,32},{32,36}... | collective-permute-start | bytes 73736
  509.7 12.7 %collective-permute-start.33 = (bf16[8,1536]{1,0:T(8,128)(2,1)S(1)}, bf16[8,1536]{1,0:T(8,128)(2,1)S(1)}, u32[]{:S(2)}, u32[]{:S(2)}) collective-permute-start(bf16[8,1536]{1,0:T(8,128)(2,1)S(1)} %get-tuple-element.18), channel_id=1, source_target_pairs={{0,8},{4,12},{8,16},{12,20},{16,24},{20,28},{24,32},{28,36},{32,40... | collective-permute-start | bytes 73736
  512.0 11.8 %collective-permute-start.34 = (bf16[8,1536]{1,0:T(8,128)(2,1)S(1)}, bf16[8,1536]{1,0:T(8,128)(2,1)S(1)}, u32[]{:S(2)}, u32[]{:S(2)}) collective-permute-start(bf16[8,1536]{1,0:T(8,128)(2,1)S(1)} %get-tuple-element.18), channel_id=1, source_target_pairs={{0,12},{4,16},{8,20},{12,24},{16,28},{20,32},{24,36},{28,40},{32,4... | collective-permute-start | bytes 73736
  514.8 10.5 %collective-permute-start.35 = (bf16[8,1536]{1,0:T(8,128)(2,1)S(1)}, bf16[8,1536]{1,0:T(8,128)(2,1)S(1)}, u32[]{:S(2)}, u32[]{:S(2)}) collective-permute-start(bf16[8,1536]{1,0:T(8,128)(2,1)S(1)} %get-tuple-element.18), channel_id=1, source_target_pairs={{0,16},{4,20},{8,24},{12,28},{16,32},{20,36},{24,40},{28,44},{32,4... | collective-permute-start | bytes 73736
  518.6 8.8 %collective-permute-start.36 = (bf16[8,1536]{1,0:T(8,128)(2,1)S(1)}, bf16[8,1536]{1,0:T(8,128)(2,1)S(1)}, u32[]{:S(2)}, u32[]{:S(2)}) collective-permute-start(bf16[8,1536]{1,0:T(8,128)(2,1)S(1)} %get-tuple-element.18), channel_id=1, source_target_pairs={{0,20},{4,24},{8,28},{12,32},{16,36},{20,40},{24,44},{28,48},{32,5... | collective-permute-start | bytes 73736
  520.5 9.9 %collective-permute-start.37 = (bf16[8,1536]{1,0:T(8,128)(2,1)S(1)}, bf16[8,1536]{1,0:T(8,128)(2,1)S(1)}, u32[]{:S(2)}, u32[]{:S(2)}) collective-permute-start(bf16[8,1536]{1,0:T(8,128)(2,1)S(1)} %get-tuple-element.18), channel_id=1, source_target_pairs={{0,24},{4,28},{8,32},{12,36},{16,40},{20,44},{24,48},{28,52},{32,5... | collective-permute-start | bytes 73736
  522.4 11.7 %collective-permute-start.38 = (bf16[8,1536]{1,0:T(8,128)(2,1)S(1)}, bf16[8,1536]{1,0:T(8,128)(2,1)S(1)}, u32[]{:S(2)}, u32[]{:S(2)}) collective-permute-start(bf16[8,1536]{1,0:T(8,128)(2,1)S(1)} %get-tuple-element.18), channel_id=1, source_target_pairs={{0,28},{4,32},{8,36},{12,40},{16,44},{20,48},{24,52},{28,56},{32,6... | collective-permute-start | bytes 73736
  523.8 12.0 %collective-permute-start.40 = (bf16[8,1536]{1,0:T(8,128)(2,1)S(1)}, bf16[8,1536]{1,0:T(8,128)(2,1)S(1)}, u32[]{:S(2)}, u32[]{:S(2)}) collective-permute-start(bf16[8,1536]{1,0:T(8,128)(2,1)S(1)} %get-tuple-element.17), channel_id=1, source_target_pairs={{0,4},{4,8},{8,12},{12,16},{16,20},{20,24},{24,28},{28,32},{32,36}... | collective-permute-start | bytes 73736
  525.2 11.9 %collective-permute-start.41 = (bf16[8,1536]{1,0:T(8,128)(2,1)S(1)}, bf16[8,1536]{1,0:T(8,128)(2,1)S(1)}, u32[]{:S(2)}, u32[]{:S(2)}) collective-permute-start(bf16[8,1536]{1,0:T(8,128)(2,1)S(1)} %get-tuple-element.17), channel_id=1, source_target_pairs={{0,8},{4,12},{8,16},{12,20},{16,24},{20,28},{24,32},{28,36},{32,40... | collective-permute-start | bytes 73736
  527.4 16.4 %collective-permute-start.42 = (bf16[8,1536]{1,0:T(8,128)(2,1)S(1)}, bf16[8,1536]{1,0:T(8,128)(2,1)S(1)}, u32[]{:S(2)}, u32[]{:S(2)}) collective-permute-start(bf16[8,1536]{1,0:T(8,128)(2,1)S(1)} %get-tuple-element.17), channel_id=1, source_target_pairs={{0,12},{4,16},{8,20},{12,24},{16,28},{20,32},{24,36},{28,40},{32,4... | collective-permute-start | bytes 73736
  530.4 13.4 %collective-permute-start.43 = (bf16[8,1536]{1,0:T(8,128)(2,1)S(1)}, bf16[8,1536]{1,0:T(8,128)(2,1)S(1)}, u32[]{:S(2)}, u32[]{:S(2)}) collective-permute-start(bf16[8,1536]{1,0:T(8,128)(2,1)S(1)} %get-tuple-element.17), channel_id=1, source_target_pairs={{0,16},{4,20},{8,24},{12,28},{16,32},{20,36},{24,40},{28,44},{32,4... | collective-permute-start | bytes 73736
  534.2 9.6 %collective-permute-start.44 = (bf16[8,1536]{1,0:T(8,128)(2,1)S(1)}, bf16[8,1536]{1,0:T(8,128)(2,1)S(1)}, u32[]{:S(2)}, u32[]{:S(2)}) collective-permute-start(bf16[8,1536]{1,0:T(8,128)(2,1)S(1)} %get-tuple-element.17), channel_id=1, source_target_pairs={{0,20},{4,24},{8,28},{12,32},{16,36},{20,40},{24,44},{28,48},{32,5... | collective-permute-start | bytes 73736
  535.9 7.9 %collective-permute-start.45 = (bf16[8,1536]{1,0:T(8,128)(2,1)S(1)}, bf16[8,1536]{1,0:T(8,128)(2,1)S(1)}, u32[]{:S(2)}, u32[]{:S(2)}) collective-permute-start(bf16[8,1536]{1,0:T(8,128)(2,1)S(1)} %get-tuple-element.17), channel_id=1, source_target_pairs={{0,24},{4,28},{8,32},{12,36},{16,40},{20,44},{24,48},{28,52},{32,5... | collective-permute-start | bytes 73736
  537.2 6.6 %collective-permute-start.46 = (bf16[8,1536]{1,0:T(8,128)(2,1)S(1)}, bf16[8,1536]{1,0:T(8,128)(2,1)S(1)}, u32[]{:S(2)}, u32[]{:S(2)}) collective-permute-start(bf16[8,1536]{1,0:T(8,128)(2,1)S(1)} %get-tuple-element.17), channel_id=1, source_target_pairs={{0,28},{4,32},{8,36},{12,40},{16,44},{20,48},{24,52},{28,56},{32,6... | collective-permute-start | bytes 73736
  (34 other events, 250.2 us)
Sparse Core Ops, SparseCore 0:
  33.2 24.9 reduce-scatter.23
  82.7 23.8 reduce-scatter.25
  131.4 25.7 reduce-scatter.27
  212.8 27.6 reduce-scatter.29
  265.6 26.0 reduce-scatter.31
  317.8 26.1 reduce-scatter.33
  370.3 26.0 reduce-scatter.35
  400.2 121.6 all-reduce.15
where the time goes:
time: 561 us; the launch traced here: 558 us
  blocking collectives  185 us (33%)
  waiting for transfers between devices  161 us (29%)
  starting transfers between devices  110 us (20%)
  matrix products  56.5 us (10%)
  between operations  17 us (3%)
  other arithmetic  16.4 us (3%)
  local copies, waits for them, and re-layouts  12.6 us (2%)
    reduce_scatter x7, waiting for transfers between devices, channel_sum(): return lax.psum_scatter(terms, 'mp', scatter_dimension=1, tiled=True)  148 us
    all_gather x8, blocking collectives, full_channels(): return lax.all_gather(values, 'mp', axis=1, tiled=True)  103 us
    unnamed x1, blocking collectives  81.8 us
    unnamed x33, starting transfers between devices  77.1 us
    ppermute x16, starting transfers between devices, from_behind(): return lax.ppermute(x, axis, pairs)  32.2 us
    ppermute x16, waiting for transfers between devices, from_behind(): return lax.ppermute(x, axis, pairs)  12.4 us
    dot_general x8, matrix products, shards(): jnp.dot(taps[tap_index], conv_kernels[layer_index, tap_index].T, preferre...  11.6 us
  transfers between devices with their start and end apart: 56, of which 11 were waited for; matrix products, arithmetic and copies ran while one was open for 22% of the time, Pallas kernels for 0%

commit v1 on v0

v1 whole, which is shorter than its diff:
```python
import functools

import jax
import jax.numpy as jnp
import numpy as np
from jax import lax
from jax.experimental import pallas as pl
from jax.experimental.pallas import tpu as pltpu
from jax.sharding import PartitionSpec as P

LAYERS = 4
ROWS = 128
C = 1536
H = 192
HALF = C // 2
SHARD = C // 4
PEERS = 32
BF16 = jnp.bfloat16
F32 = jnp.float32
ORDER = (0, 3, 1, 2)
ROOT = float(np.sqrt(2.0 / np.pi))
CUBE = 0.044715


def together(*values):
    return lax.optimization_barrier(values)


def dot(a, b, ca=1, cb=0):
    return lax.dot_general(a, b, (((ca,), (cb,)), ((), ())), preferred_element_type=F32)


def swap(values, axis, mask):
    peers = lax.axis_size(axis)
    return lax.ppermute(values, axis, [(i, i ^ mask) for i in range(peers)])


def add(a, b):
    return (a.astype(F32) + b.astype(F32)).astype(BF16)


def slope(x):
    square = x * x
    t = jnp.tanh(ROOT * x * (1.0 + CUBE * square))
    return 0.5 * (1.0 + t) + 0.5 * x * (1.0 - t * t) * (ROOT * (1.0 + 3.0 * CUBE * square))


def shifted(values, by):
    if by == 0:
        return values
    length = values.shape[0]
    zeros = jnp.zeros((abs(by),) + values.shape[1:], values.dtype)
    if by > 0:
        return jnp.concatenate([values[by:], zeros], axis=0)
    return jnp.concatenate([zeros, values[: length + by]], axis=0)


def struct(shape, kind):
    return jax.ShapeDtypeStruct(shape, kind)


def call(body, outs, scratch, args, spaces=None, flops=4e8):
    spaces = spaces or {}
    return pl.pallas_call(
        body,
        out_shape=outs,
        in_specs=[
            pl.BlockSpec(memory_space=spaces.get(i, pltpu.VMEM)) for i in range(len(args))
        ],
        out_specs=[pl.BlockSpec(memory_space=pltpu.VMEM)] * len(outs),
        scratch_shapes=scratch,
        compiler_params=pltpu.CompilerParams(vmem_limit_bytes=40 * 2**20),
        cost_estimate=pl.CostEstimate(flops=int(flops), bytes_accessed=4_000_000, transcendentals=0),
    )(*args)


WEIGHTS = [
    pltpu.VMEM((3, H, C), BF16),
    pltpu.VMEM((H, C), BF16),
    pltpu.SemaphoreType.DMA,
    pltpu.SemaphoreType.DMA,
]


def fetch(layer, kernels, points, k_mem, p_mem, k_sem, p_sem):
    k_copy = pltpu.make_async_copy(kernels.at[layer], k_mem, k_sem)
    p_copy = pltpu.make_async_copy(points.at[layer], p_mem, p_sem)
    return k_copy, p_copy


def chunks():
    return [slice(i, i + 16) for i in range(0, ROWS, 16)]


def total_of(rows, half, first, second):
    a, b = (first, second)[half]
    return a[rows].astype(F32) + b[rows].astype(F32)


def conv(active, k_mem, distance):
    taps = [dot(active, k_mem[k], 1, 1) for k in range(3)]
    return taps[1] + shifted(taps[0], -distance) + shifted(taps[2], distance)


def conv_back(inner_grad, k_mem, distance):
    out = None
    for k in range(3):
        moved = shifted(inner_grad, (1 - k) * distance).astype(BF16)
        part = dot(moved, k_mem[k])
        out = part if out is None else out + part
    return out


def put_halves(term, ta, tb):
    term = term.astype(BF16)
    ta[...] = term[:, :HALF]
    tb[...] = term[:, HALF:]


def backward_of(inner, grad_b, p_mem):
    hidden_grad = dot(grad_b, p_mem[...], 1, 1)
    return (hidden_grad * slope(inner)).astype(BF16)


def start_kernel(me, own, one, three, two, kernels, points, *rest):
    x, g, active, inner, hidden, ta, tb, k_mem, p_mem, k_sem, p_sem = rest
    k_copy, p_copy = fetch(0, kernels, points, k_mem, p_mem, k_sem, p_sem)
    k_copy.start()
    p_copy.start()
    for mask, block in ((0, own), (1, one), (3, three), (2, two)):
        at = pl.ds(pl.multiple_of((me[0] ^ mask) * SHARD, 128), SHARD)
        x[:, at] = block[:ROWS]
        g[:, at] = block[ROWS:]
    for rows in chunks():
        active[rows] = jax.nn.gelu(x[rows].astype(F32)).astype(BF16)
    k_copy.wait()
    values = conv(active[...], k_mem, 1)
    inner[...] = values
    values = jax.nn.gelu(values).astype(BF16)
    hidden[...] = values
    p_copy.wait()
    put_halves(dot(values, p_mem[...]), ta, tb)


def forward_kernel(layer, x, a, b, a2, b2, kernels, points, *rest):
    x1, active, inner, hidden, ta, tb, k_mem, p_mem, k_sem, p_sem = rest
    k_copy, p_copy = fetch(layer, kernels, points, k_mem, p_mem, k_sem, p_sem)
    k_copy.start()
    p_copy.start()
    advance(x, a, b, a2, b2, x1, active)
    k_copy.wait()
    values = conv(active[...], k_mem, 2**layer)
    inner[...] = values
    values = jax.nn.gelu(values).astype(BF16)
    hidden[...] = values
    p_copy.wait()
    put_halves(dot(values, p_mem[...]), ta, tb)


def advance(x, a, b, a2, b2, x1, active):
    for rows in chunks():
        for half in (0, 1):
            at = slice(half * HALF, half * HALF + HALF)
            total = total_of(rows, half, (a, a2), (b, b2))
            values = (x[rows, at].astype(F32) + total).astype(BF16)
            x1[rows, at] = values
            active[rows, at] = jax.nn.gelu(values.astype(F32)).astype(BF16)


def turn_kernel(layer, x, a, b, a2, b2, g, kernels, points, *rest):
    x1, active, hidden, inner_grad, ta, tb, k_mem, p_mem, k_sem, p_sem = rest
    k_copy, p_copy = fetch(layer, kernels, points, k_mem, p_mem, k_sem, p_sem)
    k_copy.start()
    p_copy.start()
    advance(x, a, b, a2, b2, x1, active)
    k_copy.wait()
    inner = conv(active[...], k_mem, 2**layer)
    hidden[...] = jax.nn.gelu(inner).astype(BF16)
    p_copy.wait()
    values = backward_of(inner, g[...], p_mem)
    inner_grad[...] = values
    put_halves(conv_back(values.astype(F32), k_mem, 2**layer), ta, tb)


def retreat(g, a, b, a2, b2, x, g1, grad_b):
    for rows in chunks():
        for half in (0, 1):
            at = slice(half * HALF, half * HALF + HALF)
            total = total_of(rows, half, (a, a2), (b, b2))
            values = g[rows, at].astype(F32) + slope(x[rows, at].astype(F32)) * total
            if g1 is not None:
                g1[rows, at] = values
            grad_b[rows, at] = values.astype(BF16)


def backward_kernel(layer, g, a, b, a2, b2, x, inner, kernels, points, *rest):
    g1, grad_b, inner_grad, ta, tb, k_mem, p_mem, k_sem, p_sem = rest
    k_copy, p_copy = fetch(layer, kernels, points, k_mem, p_mem, k_sem, p_sem)
    p_copy.start()
    k_copy.start()
    retreat(g, a, b, a2, b2, x, g1, grad_b)
    p_copy.wait()
    values = backward_of(inner[...], grad_b[...], p_mem)
    inner_grad[...] = values
    k_copy.wait()
    put_halves(conv_back(values.astype(F32), k_mem, 2**layer), ta, tb)


def final_kernel(me, g, a, b, a2, b2, x, inner, order, points, *rest):
    grad_b, inner_grad, sent, p_mem, p_sem = rest
    p_copy = pltpu.make_async_copy(points.at[0], p_mem, p_sem)
    p_copy.start()
    retreat(g, a, b, a2, b2, x, None, grad_b)
    p_copy.wait()
    values = backward_of(inner[...], grad_b[...], p_mem)
    inner_grad[...] = values
    own = grad_b[:, pl.ds(pl.multiple_of(me[0] * SHARD, 128), SHARD)]
    parts = jnp.concatenate([values, own[:, :H], own[:, H:]], axis=0)
    sent[...] = dot(order[...], parts).astype(BF16)


def last_kernel(me, got, order, kernels, *rest):
    own, one, three, two, g, k_mem, term, k_sem = rest
    k_copy = pltpu.make_async_copy(kernels.at[0], k_mem, k_sem)
    k_copy.start()
    values = dot(order[...], got[...])
    moved = values.astype(BF16)
    g[:, :H] = values[192:320]
    g[:, H:] = values[320:448]
    k_copy.wait()
    out = dot(moved[64:192], k_mem[0])
    out = out + dot(moved[32:160], k_mem[1])
    term[...] = out + dot(moved[:128], k_mem[2])
    for mask, ref in ((0, own), (1, one), (3, three), (2, two)):
        at = pl.ds(pl.multiple_of((me[0] ^ mask) * SHARD, 128), SHARD)
        ref[...] = term[:, at].astype(ref.dtype)


def weight_kernel(distance, count, inner_grad, hidden, active, grad_b, *rest):
    tables, outs = rest[:count], rest[count:]
    grad = inner_grad[...].astype(F32)
    moved = [shifted(grad, (1 - k) * distance).astype(BF16) for k in range(3)]
    width = C // count
    for index, table in enumerate(tables):
        top = sum(dot(moved[k], table[k * H : (k + 1) * H]) for k in range(3))
        bottom = dot(hidden[...], table[3 * H :])
        left = jnp.concatenate([top, bottom], axis=0).T.astype(BF16)
        at = slice(index * width, (index + 1) * width)
        right = jnp.concatenate([active[:, at], grad_b[:, at]], axis=0)
        for part in (0, 1):
            ref = outs[part * count + index]
            for row in range(0, 384, 128):
                rows = left[part * 384 + row : part * 384 + row + 128]
                ref[row : row + 128] = dot(rows, right).astype(BF16)


def weight_terms(layer, tables, inner_grad, hidden, active, grad_b):
    count = len(tables)
    outs = [struct((384, C // count), BF16)] * (2 * count)
    body = functools.partial(weight_kernel, 2**layer, count)
    return call(body, outs, [], (inner_grad, hidden, active, grad_b, *tables), flops=8e8)


def sums_kernel(first, k0, k1, c0, c1, late, kernel_out, point_out):
    total = first[0].astype(F32)
    for i in range(1, 16):
        total = total + first[i].astype(F32)
    second = [k0[...].astype(F32) + c0[...].astype(F32), k1[...].astype(F32) + c1[...].astype(F32)]
    second = jnp.concatenate(second, axis=1)
    for layer, values in enumerate((total, second, late[0].astype(F32), late[1].astype(F32))):
        for k in range(3):
            kernel_out[layer, k] = values[6 * k : 6 * k + 6]
        point_out[layer] = values[18:]


def table_of(source, columns):
    (source,) = together(jnp.asarray(source, jnp.int32))
    return (lax.broadcasted_iota(jnp.int32, (len(source), columns), 1) == source[:, None]).astype(
        BF16
    )


def by_source(blocks):
    column = np.arange(768)
    row = column % 24
    fixed = jnp.asarray(row // 6 * H + row % 6, jnp.int32)
    (source,) = together(fixed + 6 * jnp.repeat(blocks, 24))
    return (lax.broadcasted_iota(jnp.int32, (768, 768), 0) == source[None]).astype(BF16)


def absolute_order():
    core = lax.axis_index("seq") % 2
    block = np.arange(32)
    return by_source(2 * (block % 16) + (core ^ jnp.asarray(block // 16, jnp.int32)))


def relative_orders():
    me = lax.axis_index("seq")
    first = [c + 2 * x + 8 * z for c in (0, 1) for x in ORDER for z in ORDER]
    second = [c + 2 * x + 8 * z for c in (0, 1) for z in ORDER for x in ORDER]
    return [by_source(me ^ jnp.asarray(masks, jnp.int32)) for masks in (first, second)]


def block_to_residue():
    n = np.arange(256)
    r, t = n // 8, n % 8
    go = t // 4 * 128 + t % 4 * 32 + r
    come = n % 128 // 4 * 8 + n // 128 * 4 + n % 4
    return table_of(go, 256), table_of(come, 256)


def residue_to_block():
    n = np.arange(512)
    s, t = n // 16, n % 16
    a = 4 * s + t - 1
    grad = np.where((t < 6) & (a >= 0) & (a < 128), a, -1)
    half = 128 + (t - 6) // 4 * 128 + 4 * s + (t - 6) % 4
    go = np.where(t < 6, grad, np.where(t < 14, half, -1))
    n = np.arange(448)
    m = n - 192
    come = np.where(
        n < 192, n % 32 * 16 + n // 32, m % 32 * 16 + 6 + m // 128 * 4 + m % 128 // 32
    )
    return table_of(go, 384), table_of(come, 512)


def over_chips(values):
    groups = [[2 * i + core for i in range(PEERS // 2)] for core in (0, 1)]
    return lax.all_to_all(
        values.reshape(16, 24, values.shape[1]), "seq", 0, 0, axis_index_groups=groups
    )


def halving(kept, sent, step):
    masks = ((2, 8), (6, 24), (8, 2), (24, 6))[step]
    return kept, [swap(s, "seq", mask) for s, mask in zip(sent, masks)]


def add_split(kept, come):
    rows = kept[0].shape[0] // 2
    low = [add(k[:rows], c[:rows]) for k, c in zip(kept, come)]
    high = [add(k[rows:], c[rows:]) for k, c in zip(kept, come)]
    return low, high


def over_chips_first(values):
    both = jnp.concatenate([v.reshape(4, 1, 96, C) for v in values], axis=1)
    along_z = [[8 * i + j for i in range(4)] for j in range(8)]
    both = both.reshape(4, len(values) * 96, C)
    return lax.psum_scatter(both, "seq", scatter_dimension=0, axis_index_groups=along_z)


def over_chips_second(part, count):
    along_x = [[8 * z + 2 * i + c for i in range(4)] for z in range(4) for c in range(2)]
    part = part.reshape(count, 4, 24, C).transpose(1, 0, 2, 3).reshape(4, count * 24, C)
    part = lax.psum_scatter(part, "seq", scatter_dimension=0, axis_index_groups=along_x)
    return part.reshape(count, 24, C)


def sum_mp(a, b, first=()):
    a1, b1, *first = together(swap(a, "mp", 1), swap(b, "mp", 3), *first)
    a, b = add(a, a1), add(b, b1)
    a2, b2 = swap(a, "mp", 3), swap(b, "mp", 1)
    kept, sent = first[: len(first) // 2], first[len(first) // 2 :]
    a2, b2, *other = together(a2, b2, *[swap(s, "seq", 1) for s in sent])
    return (a, b, a2, b2), kept, other


def shards(inputs, cotangent, conv_kernels, point_weights):
    me = lax.axis_index("mp").astype(jnp.int32)[None]
    weights = (conv_kernels, point_weights)
    go, come = block_to_residue()
    sent = dot(go, jnp.concatenate([inputs, cotangent], axis=0)).astype(BF16)
    got = lax.all_to_all(sent.reshape(PEERS, 8, SHARD), "seq", 0, 0)
    own = dot(come, got.reshape(256, SHARD)).astype(BF16)
    one, three, two = (swap(own, "mp", mask) for mask in (1, 3, 2))
    full, inner_like, hid = struct((ROWS, C), BF16), struct((ROWS, H), F32), struct((ROWS, H), BF16)
    half = struct((ROWS, HALF), BF16)
    x, g, active, inner, hidden, ta, tb = call(
        start_kernel,
        [full, full, full, inner_like, hid, half, half],
        WEIGHTS,
        (me, own, one, three, two, *weights),
        {0: pltpu.SMEM, 5: pl.ANY, 6: pl.ANY},
    )
    saved = [(x, active, inner, hidden)]
    table = absolute_order()
    relative = relative_orders()
    block_go, block_come = residue_to_block()
    for layer in (1, 2):
        terms, _, _ = sum_mp(ta, tb)
        x, active, inner, hidden, ta, tb = call(
            functools.partial(forward_kernel, layer),
            [full, full, inner_like, hid, half, half],
            WEIGHTS,
            (x, *terms, *weights),
            {5: pl.ANY, 6: pl.ANY},
        )
        saved.append((x, active, inner, hidden))
    terms, _, _ = sum_mp(ta, tb)
    x, active, hidden, inner_grad, ta, tb = call(
        functools.partial(turn_kernel, 3),
        [full, full, hid, hid, half, half],
        WEIGHTS,
        (x, *terms, g, *weights),
        {6: pl.ANY, 7: pl.ANY},
    )
    grad_b = g
    halves = [None] * LAYERS
    for layer in (3, 2, 1):
        tables = [table] if layer > 1 else relative
        first = weight_terms(layer, tables, inner_grad, hidden, active, grad_b)
        terms, kept, other = sum_mp(ta, tb, first)
        halves[layer] = (kept, other)
        above, (x, active, inner, hidden) = x, saved[layer - 1]
        if layer > 1:
            g, grad_b, inner_grad, ta, tb = call(
                functools.partial(backward_kernel, layer - 1),
                [struct((ROWS, C), F32), full, hid, half, half],
                WEIGHTS,
                (g, *terms, above, inner, *weights),
                {7: pl.ANY, 8: pl.ANY},
            )
    late = over_chips_first([add(halves[n][0][0], halves[n][1][0]) for n in (2, 3)])
    kept, sent = add_split(*halves[1])
    grad_b, inner_grad, sent_blocks = call(
        final_kernel,
        [full, hid, struct((512, H), BF16)],
        [pltpu.VMEM((H, C), BF16), pltpu.SemaphoreType.DMA],
        (me, g, *terms, above, inner, block_go, point_weights),
        {0: pltpu.SMEM, 9: pl.ANY},
    )
    got = lax.all_to_all(sent_blocks.reshape(PEERS, 16, H), "seq", 0, 0)
    keep, send = weight_terms(0, [table], inner_grad, hidden, active, grad_b)
    other = swap(send, "seq", 1)
    kept, moved = halving(kept, sent, 0)
    got, other, late, *moved = together(got, other, late, *moved)
    kept, sent = add_split(kept, moved)
    late = over_chips_second(late, 2)
    first = over_chips(add(keep, other))
    piece = struct((ROWS, SHARD), BF16)
    total, one, three, two, gradient = call(
        last_kernel,
        [struct((ROWS, SHARD), F32), piece, piece, piece, struct((ROWS, SHARD), F32)],
        [pltpu.VMEM((3, H, C), BF16), pltpu.VMEM((ROWS, C), F32), pltpu.SemaphoreType.DMA],
        (me, got.reshape(512, H), block_come, conv_kernels),
        {0: pltpu.SMEM, 3: pl.ANY},
    )
    got = [swap(s, "mp", mask) for s, mask in ((one, 1), (three, 3), (two, 2))]
    kept, moved = halving(kept, sent, 1)
    *got, move0, move1 = together(*got, *moved)
    for g in got:
        total = total + g.astype(F32)
    gradient = gradient + slope(inputs.astype(F32)) * total
    kept, sent = add_split(kept, (move0, move1))
    kept, moved = halving(kept, sent, 2)
    kept, sent = add_split(kept, moved)
    kept, moved = halving(kept, sent, 3)
    kernel_grad, point_grad = call(
        sums_kernel,
        [struct((LAYERS, 3, 6, C), F32), struct((LAYERS, 6, C), F32)],
        [],
        (first, *kept, *moved, late),
    )
    return gradient, kernel_grad, point_grad


def solution(mesh):
    return jax.shard_map(
        shards,
        mesh=mesh,
        in_specs=(P("seq", "mp"), P("seq", "mp"), P(None, None, "mp", None), P(None, "mp", None)),
        out_specs=(
            P("seq", "mp"),
            P(None, None, ("mp", "seq"), None),
            P(None, ("mp", "seq"), None),
        ),
        check_vma=False,
    )
```

time: 561 us -> 265 us (0.47)
  blocking collectives: 185 us -> 0 us
  waiting for transfers between devices: 161 us -> 106 us
  matrix products: 56.5 us -> 2.87 us
  starting transfers between devices: 110 us -> 64.8 us
  local copies, waits for them, and re-layouts: 12.6 us -> 36.7 us
  Pallas kernels: 0 us -> 23.4 us
    reduce_scatter x7 -> x2, waiting for transfers between devices: 148 us -> 0.02 us  [the longest x1 0.02 us: over_chips_first(): lax.psum_scatter(both, 'seq', scatter_dimension=0, axis_index_groups=alon...]
    all_gather x8 -> x0, blocking collectives: 103 us -> none  [full_channels(): return lax.all_gather(values, 'mp', axis=1, tiled=True)]
    unnamed x1 -> x0, blocking collectives: 81.8 us -> none
    unnamed x33 -> x0, starting transfers between devices: 77.1 us -> none
    ppermute x16 -> x43, waiting for transfers between devices: 12.4 us -> 89.3 us  [swap(): return lax.ppermute(values, axis, [(i, i ^ mask) for i in range(peers)])]
    dot_general x47 -> x2, matrix products: 56.5 us -> 2.87 us  [dot(): lax.dot_general(a, b, (((ca,), (cb,)), ((), ())), preferred_element_type=...]
    pallas_call x0 -> x13, Pallas kernels: none -> 23.4 us  [call(): pl.pallas_call(body, out_shape=outs, in_specs=[pl.BlockSpec(memory_space=...]
    unnamed x99 -> x124, local copies, waits for them, and re-layouts: 10.2 us -> 32.3 us
  transfers between devices with their start and end apart: 56 -> 48, of which waited for: 11 -> 31; matrix products, arithmetic and copies ran while one was open for 22% -> 6% of each run, Pallas kernels for 0% -> 4%
where the time goes in v1:
time: 265 us; the launch traced here: 264 us
  waiting for transfers between devices  106 us (40%)
  starting transfers between devices  64.8 us (24%)
  local copies, waits for them, and re-layouts  36.7 us (14%)
  Pallas kernels  23.4 us (9%)
  other arithmetic  15.4 us (6%)
  between operations  14.8 us (6%)
  matrix products  2.87 us (1%)
    ppermute x43, waiting for transfers between devices, swap(): return lax.ppermute(values, axis, [(i, i ^ mask) for i in range(peers)])  89.3 us
    ppermute x43, starting transfers between devices, swap(): return lax.ppermute(values, axis, [(i, i ^ mask) for i in range(peers)])  47.2 us
    unnamed x124, local copies, waits for them, and re-layouts  32.3 us
    pallas_call x13, Pallas kernels, call(): pl.pallas_call(body, out_shape=outs, in_specs=[pl.BlockSpec(memory_space=...  23.4 us
    convert_element_type x23, other arithmetic, add(): return (a.astype(F32) + b.astype(F32)).astype(BF16)  9.02 us
    all_to_all x1, waiting for transfers between devices, shards(): got = lax.all_to_all(sent_blocks.reshape(PEERS, 16, H), 'seq', 0, 0)  8.69 us
    all_to_all x1, starting transfers between devices, shards(): got = lax.all_to_all(sent.reshape(PEERS, 8, SHARD), 'seq', 0, 0)  8.25 us
    all_to_all x1, waiting for transfers between devices, shards(): got = lax.all_to_all(sent.reshape(PEERS, 8, SHARD), 'seq', 0, 0)  8.15 us
  transfers between devices with their start and end apart: 48, of which 31 were waited for; matrix products, arithmetic and copies ran while one was open for 6% of the time, Pallas kernels for 4%

profile of v1, /device:TPU:0, one launch (start us, length us, event | category | flops | bytes accessed | tf_op | source)
XLA Modules:
  0.0 264.1 jit_solution(4206697869044815376)
XLA Ops:
  7.2 1.9 fusion.3
  9.1 8.2 %all-to-all-start = ((bf16[32,8,384]{2,1,0:T(8,128)(2,1)}), bf16[32,8,384]{2,1,0:T(8,128)(2,1)S(1)}, u32[]{:S(2)}, u32[]{:S(2)}) async-start(bf16[32,8,384]{2,1,0:T(8,128)(2,1)} %fusion.3), calls=%async_computation | async-start | bytes 393216 | tf_op jit(solution)/shard_map/all_to_all | solution.py:374
  17.4 8.1 %all-to-all-done = bf16[32,8,384]{2,1,0:T(8,128)(2,1)S(1)} async-done(((bf16[32,8,384]{2,1,0:T(8,128)(2,1)}), bf16[32,8,384]{2,1,0:T(8,128)(2,1)S(1)}, u32[]{:S(2)}, u32[]{:S(2)}) %all-to-all-start) | async-done | bytes 196640 | tf_op jit(solution)/shard_map/all_to_all | solution.py:374
  26.5 3.3 %collective-permute-start.2 = (bf16[256,384]{1,0:T(8,128)(2,1)S(1)}, bf16[256,384]{1,0:T(8,128)(2,1)S(1)}, u32[]{:S(2)}, u32[]{:S(2)}) collective-permute-start(bf16[256,384]{1,0:T(8,128)(2,1)S(1)} %convolution_convert_fusion.own), channel_id=1, source_target_pairs={{0,2},{1,3},{2,0},{3,1},{4,6},{5,7},{6,4},{7,5},{8,10},{9,11},{10,... | collective-permute-start | bytes 589832 | tf_op jit(solution)/shard_map/ppermute | solution.py:35
  30.8 4.7 %collective-permute-done.2.two = bf16[256,384]{1,0:T(8,128)(2,1)S(1)} collective-permute-done((bf16[256,384]{1,0:T(8,128)(2,1)S(1)}, bf16[256,384]{1,0:T(8,128)(2,1)S(1)}, u32[]{:S(2)}, u32[]{:S(2)}) %collective-permute-start.2) | collective-permute-done | bytes 196640 | tf_op jit(solution)/shard_map/ppermute | solution.py:35
  35.6 3.9 %collective-permute-done.1.three = bf16[256,384]{1,0:T(8,128)(2,1)S(1)} collective-permute-done((bf16[256,384]{1,0:T(8,128)(2,1)S(1)}, bf16[256,384]{1,0:T(8,128)(2,1)S(1)}, u32[]{:S(2)}, u32[]{:S(2)}) %collective-permute-start.1) | collective-permute-done | bytes 196640 | tf_op jit(solution)/shard_map/ppermute | solution.py:35
  39.8 3.0 %copy-done = bf16[4,3,192,1536]{3,2,1,0:T(8,128)(2,1)S(1)} copy-done((bf16[4,3,192,1536]{3,2,1,0:T(8,128)(2,1)S(1)}, bf16[4,3,192,1536]{3,2,1,0:T(8,128)(2,1)}, u32[]{:S(2)}) %copy-start) | copy-done | bytes 7077912
  42.8 1.7 copy-done.6
  44.5 2.0 shard_map.166
  49.3 3.7 %collective-permute-done.3 = bf16[128,768]{1,0:T(8,128)(2,1)S(1)} collective-permute-done((bf16[128,768]{1,0:T(8,128)(2,1)S(1)}, bf16[128,768]{1,0:T(8,128)(2,1)S(1)}, u32[]{:S(2)}, u32[]{:S(2)}) %collective-permute-start.3) | collective-permute-done | bytes 196640 | tf_op jit(solution)/shard_map/ppermute | solution.py:35
  53.1 2.5 collective-permute-done.4
  55.8 2.2 collective-permute-start.5
  58.0 3.4 %collective-permute-done.6.b2 = bf16[128,768]{1,0:T(8,128)(2,1)S(1)} collective-permute-done((bf16[128,768]{1,0:T(8,128)(2,1)S(1)}, bf16[128,768]{1,0:T(8,128)(2,1)S(1)}, u32[]{:S(2)}, u32[]{:S(2)}) %collective-permute-start.6) | collective-permute-done | bytes 196640 | tf_op jit(solution)/shard_map/ppermute | solution.py:35
  62.8 2.1 shard_map.167
  67.8 1.9 collective-permute-start.8
  69.6 3.1 %collective-permute-done.7 = bf16[128,768]{1,0:T(8,128)(2,1)S(1)} collective-permute-done((bf16[128,768]{1,0:T(8,128)(2,1)S(1)}, bf16[128,768]{1,0:T(8,128)(2,1)S(1)}, u32[]{:S(2)}, u32[]{:S(2)}) %collective-permute-start.7) | collective-permute-done | bytes 196640 | tf_op jit(solution)/shard_map/ppermute | solution.py:35
  72.7 1.9 collective-permute-done.8
  74.9 2.2 collective-permute-start.9
  77.1 3.4 %collective-permute-done.10.b2 = bf16[128,768]{1,0:T(8,128)(2,1)S(1)} collective-permute-done((bf16[128,768]{1,0:T(8,128)(2,1)S(1)}, bf16[128,768]{1,0:T(8,128)(2,1)S(1)}, u32[]{:S(2)}, u32[]{:S(2)}) %collective-permute-start.10) | collective-permute-done | bytes 196640 | tf_op jit(solution)/shard_map/ppermute | solution.py:35
  81.8 3.0 %copy-done.2 = bf16[4,3,192,1536]{3,2,1,0:T(8,128)(2,1)S(1)} copy-done((bf16[4,3,192,1536]{3,2,1,0:T(8,128)(2,1)S(1)}, bf16[4,3,192,1536]{3,2,1,0:T(8,128)(2,1)}, u32[]{:S(2)}) %copy-start.2) | copy-done | bytes 7077912
  84.8 1.7 copy-done.8
  86.5 2.1 shard_map.168
  90.1 1.9 collective-permute-start.12
  91.9 4.3 %collective-permute-done.11 = bf16[128,768]{1,0:T(8,128)(2,1)S(1)} collective-permute-done((bf16[128,768]{1,0:T(8,128)(2,1)S(1)}, bf16[128,768]{1,0:T(8,128)(2,1)S(1)}, u32[]{:S(2)}, u32[]{:S(2)}) %collective-permute-start.11) | collective-permute-done | bytes 196640 | tf_op jit(solution)/shard_map/ppermute | solution.py:35
  96.3 2.7 %collective-permute-done.12 = bf16[128,768]{1,0:T(8,128)(2,1)S(1)} collective-permute-done((bf16[128,768]{1,0:T(8,128)(2,1)S(1)}, bf16[128,768]{1,0:T(8,128)(2,1)S(1)}, u32[]{:S(2)}, u32[]{:S(2)}) %collective-permute-start.12) | collective-permute-done | bytes 196640 | tf_op jit(solution)/shard_map/ppermute | solution.py:35
  99.8 1.8 collective-permute-start.13
  103.7 2.1 collective-permute-done.14.b2
  106.8 3.0 %copy-done.3 = bf16[4,3,192,1536]{3,2,1,0:T(8,128)(2,1)S(1)} copy-done((bf16[4,3,192,1536]{3,2,1,0:T(8,128)(2,1)S(1)}, bf16[4,3,192,1536]{3,2,1,0:T(8,128)(2,1)}, u32[]{:S(2)}) %copy-start.3) | copy-done | bytes 7077912
  109.9 1.7 copy-done.9
  112.5 3.9 %shard_map.169 = (bf16[128,1536]{1,0:T(8,128)(2,1)S(1)}, bf16[128,1536]{1,0:T(8,128)(2,1)S(1)}, bf16[128,192]{1,0:T(8,128)(2,1)S(1)}, bf16[128,192]{1,0:T(8,128)...) custom-call(bf16[128,1536]{1,0:T(8,128)(2,1)S(1)} %copy-done.12, ...), custom_call_target="tpu_custom_call" | custom-call | flops 400000000 | bytes 4000000 | tf_op jit(solution)/shard_map/pallas_call | solution.py:64
  117.3 1.4 collective-permute-start.16
  120.3 1.9 collective-permute-done.15
  122.2 2.0 collective-permute-done.16
  124.4 1.7 collective-permute-start.17
  126.2 5.5 %collective-permute-done.18.b2 = bf16[128,768]{1,0:T(8,128)(2,1)S(1)} collective-permute-done((bf16[128,768]{1,0:T(8,128)(2,1)S(1)}, bf16[128,768]{1,0:T(8,128)(2,1)S(1)}, u32[]{:S(2)}, u32[]{:S(2)}) %collective-permute-start.18) | collective-permute-done | bytes 196640 | tf_op jit(solution)/shard_map/ppermute | solution.py:35
  133.0 2.2 shard_map.171
  135.8 1.4 collective-permute-start.21
  138.4 3.5 %collective-permute-done.20 = bf16[128,768]{1,0:T(8,128)(2,1)S(1)} collective-permute-done((bf16[128,768]{1,0:T(8,128)(2,1)S(1)}, bf16[128,768]{1,0:T(8,128)(2,1)S(1)}, u32[]{:S(2)}, u32[]{:S(2)}) %collective-permute-start.20) | collective-permute-done | bytes 196640 | tf_op jit(solution)/shard_map/ppermute | solution.py:35
  145.4 5.3 %collective-permute-done.23.b2 = bf16[128,768]{1,0:T(8,128)(2,1)S(1)} collective-permute-done((bf16[128,768]{1,0:T(8,128)(2,1)S(1)}, bf16[128,768]{1,0:T(8,128)(2,1)S(1)}, u32[]{:S(2)}, u32[]{:S(2)}) %collective-permute-start.23) | collective-permute-done | bytes 196640 | tf_op jit(solution)/shard_map/ppermute | solution.py:35
  150.6 1.5 collective-permute-done.22.a2
  152.8 1.6 pad_maximum_fusion
  154.5 1.5 reshape.67
  157.8 3.4 %copy-done.4 = bf16[4,3,192,1536]{3,2,1,0:T(8,128)(2,1)S(1)} copy-done((bf16[4,3,192,1536]{3,2,1,0:T(8,128)(2,1)S(1)}, bf16[4,3,192,1536]{3,2,1,0:T(8,128)(2,1)}, u32[]{:S(2)}) %copy-start.4) | copy-done | bytes 7077912
  165.9 2.2 shard_map.173
  169.8 1.5 shard_map.174
  171.4 3.0 %collective-permute-done.25 = bf16[128,768]{1,0:T(8,128)(2,1)S(1)} collective-permute-done((bf16[128,768]{1,0:T(8,128)(2,1)S(1)}, bf16[128,768]{1,0:T(8,128)(2,1)S(1)}, u32[]{:S(2)}, u32[]{:S(2)}) %collective-permute-start.25) | collective-permute-done | bytes 196640 | tf_op jit(solution)/shard_map/ppermute | solution.py:35
  177.9 5.2 %collective-permute-done.28.b2 = bf16[128,768]{1,0:T(8,128)(2,1)S(1)} collective-permute-done((bf16[128,768]{1,0:T(8,128)(2,1)S(1)}, bf16[128,768]{1,0:T(8,128)(2,1)S(1)}, u32[]{:S(2)}, u32[]{:S(2)}) %collective-permute-start.28) | collective-permute-done | bytes 196640 | tf_op jit(solution)/shard_map/ppermute | solution.py:35
  183.1 1.5 collective-permute-done.27.a2
  184.7 2.3 shard_map.175
  191.0 5.2 %all-to-all-start.1 = ((bf16[32,16,192]{2,1,0:T(8,128)(2,1)}), bf16[32,16,192]{2,1,0:T(8,128)(2,1)S(1)}, u32[]{:S(2)}, u32[]{:S(2)}) async-start(bf16[32,16,192]{2,1,0:T(8,128)(2,1)} %bitcast.3), calls=%async_computation.1 | async-start | bytes 524288 | tf_op jit(solution)/shard_map/all_to_all | solution.py:433
  196.5 8.7 %all-to-all-done.1 = bf16[32,16,192]{2,1,0:T(8,128)(2,1)S(1)} async-done(((bf16[32,16,192]{2,1,0:T(8,128)(2,1)}), bf16[32,16,192]{2,1,0:T(8,128)(2,1)S(1)}, u32[]{:S(2)}, u32[]{:S(2)}) %all-to-all-start.1) | async-done | bytes 196640 | tf_op jit(solution)/shard_map/all_to_all | solution.py:433
  205.2 3.0 %copy-done.5 = bf16[4,3,192,1536]{3,2,1,0:T(8,128)(2,1)S(1)} copy-done((bf16[4,3,192,1536]{3,2,1,0:T(8,128)(2,1)S(1)}, bf16[4,3,192,1536]{3,2,1,0:T(8,128)(2,1)}, u32[]{:S(2)}) %copy-start.5) | copy-done | bytes 7077912
  208.2 1.4 shard_map.177
  211.3 2.6 collective-permute-start.36
  216.0 1.7 add_convert_fusion.20
  217.7 2.3 collective-permute-start.37
  220.9 2.6 add_convert_fusion
  223.4 4.0 %all-to-all-start.2 = ((bf16[16,24,1536]{2,1,0:T(8,128)(2,1)}), bf16[16,24,1536]{2,1,0:T(8,128)(2,1)S(1)}, u32[]{:S(2)}, u32[]{:S(2)}) async-start(bf16[16,24,1536]{2,1,0:T(8,128)(2,1)} %bitcast.27), calls=%async_computation.3 | async-start | bytes 2359296 | tf_op jit(solution)/shard_map/all_to_all | solution.py:329
  227.6 2.0 collective-permute-start.40
  229.6 1.5 collective-permute-start.39
  231.2 15.7 %collective-permute-done.40 = bf16[48,768]{1,0:T(8,128)(2,1)S(1)} collective-permute-done((bf16[48,768]{1,0:T(8,128)(2,1)S(1)}, bf16[48,768]{1,0:T(8,128)(2,1)S(1)}, u32[]{:S(2)}, u32[]{:S(2)}) %collective-permute-start.40) | collective-permute-done | bytes 73760 | tf_op jit(solution)/shard_map/ppermute | solution.py:35
  246.9 2.1 collective-permute-start.42
  249.1 3.0 %collective-permute-start.41 = (bf16[24,768]{1,0:T(8,128)(2,1)S(1)}, bf16[24,768]{1,0:T(8,128)(2,1)S(1)}, u32[]{:S(2)}, u32[]{:S(2)}) collective-permute-start(bf16[24,768]{1,0:T(8,128)(2,1)S(1)} %get-tuple-element.228), channel_id=1, source_target_pairs={{0,96},{4,100},{8,104},{12,108},{16,112},{20,116},{24,120},{28,124... | collective-permute-start | bytes 110600 | tf_op jit(solution)/shard_map/ppermute | solution.py:35
  252.1 1.8 fusion.16
  (211 shorter events, 51.3 us)
Async XLA Ops:
  9.1 16.5 %all-to-all-start = ((bf16[32,8,384]{2,1,0:T(8,128)(2,1)}), bf16[32,8,384]{2,1,0:T(8,128)(2,1)S(1)}, u32[]{:S(2)}, u32[]{:S(2)}) async-start(bf16[32,8,384]{2,1,0:T(8,128)(2,1)} %fusion.3), calls=%async_computation | async-start | bytes 393216 | tf_op jit(solution)/shard_map/all_to_all | solution.py:374
  17.3 187.9 %reduce-scatter.3.cloned.1.call-start = ((), (), s32[]{:S(2)}) async-start(), calls=%async_computation.5 | async-start | bytes 2949120 | tf_op jit(solution)/shard_map/reduce_scatter | solution.py:350
  26.5 9.1 %collective-permute-start.2 = (bf16[256,384]{1,0:T(8,128)(2,1)S(1)}, bf16[256,384]{1,0:T(8,128)(2,1)S(1)}, u32[]{:S(2)}, u32[]{:S(2)}) collective-permute-start(bf16[256,384]{1,0:T(8,128)(2,1)S(1)} %convolution_convert_fusion.own), channel_id=1, source_target_pairs={{0,2},{1,3},{2,0},{3,1},{4,6},{5,7},{6,4},{7,5},{8,10},{9,11},{10,... | collective-permute-start | bytes 589832 | tf_op jit(solution)/shard_map/ppermute | solution.py:35
  29.8 9.7 %collective-permute-start.1 = (bf16[256,384]{1,0:T(8,128)(2,1)S(1)}, bf16[256,384]{1,0:T(8,128)(2,1)S(1)}, u32[]{:S(2)}, u32[]{:S(2)}) collective-permute-start(bf16[256,384]{1,0:T(8,128)(2,1)S(1)} %convolution_convert_fusion.own), channel_id=1, source_target_pairs={{0,3},{1,2},{2,1},{3,0},{4,7},{5,6},{6,5},{7,4},{8,11},{9,10},{10,... | collective-permute-start | bytes 589832 | tf_op jit(solution)/shard_map/ppermute | solution.py:35
  30.8 9.0 %collective-permute-start = (bf16[256,384]{1,0:T(8,128)(2,1)S(1)}, bf16[256,384]{1,0:T(8,128)(2,1)S(1)}, u32[]{:S(2)}, u32[]{:S(2)}) collective-permute-start(bf16[256,384]{1,0:T(8,128)(2,1)S(1)} %convolution_convert_fusion.own), channel_id=1, source_target_pairs={{0,1},{1,0},{2,3},{3,2},{4,5},{5,4},{6,7},{7,6},{8,9},{9,8},{10,11... | collective-permute-start | bytes 589832 | tf_op jit(solution)/shard_map/ppermute | solution.py:35
  44.5 18.3 %copy-start.1 = (bf16[4,3,192,1536]{3,2,1,0:T(8,128)(2,1)S(1)}, bf16[4,3,192,1536]{3,2,1,0:T(8,128)(2,1)}, u32[]{:S(2)}) copy-start(bf16[4,3,192,1536]{3,2,1,0:T(8,128)(2,1)} %kernels.13) | copy-start | bytes 21233668
  44.5 18.3 %copy-start.7 = (bf16[4,192,1536]{2,1,0:T(8,128)(2,1)S(1)}, bf16[4,192,1536]{2,1,0:T(8,128)(2,1)}, u32[]{:S(2)}) copy-start(bf16[4,192,1536]{2,1,0:T(8,128)(2,1)} %points.13) | copy-start | bytes 7077892
  46.5 16.2 %copy-start.35 = (f32[128,192]{1,0:T(8,128)}, f32[128,192]{1,0:T(8,128)S(1)}, u32[]{:S(2)}) copy-start(f32[128,192]{1,0:T(8,128)S(1)} %get-tuple-element.172.inner) | copy-start | bytes 294916
  46.5 18.4 %copy-start.39 = (bf16[128,1536]{1,0:T(8,128)(2,1)}, bf16[128,1536]{1,0:T(8,128)(2,1)S(1)}, u32[]{:S(2)}) copy-start(bf16[128,1536]{1,0:T(8,128)(2,1)S(1)} %get-tuple-element.176.active) | copy-start | bytes 1179652
  46.5 18.4 %copy-start.44 = (bf16[128,192]{1,0:T(8,128)(2,1)}, bf16[128,192]{1,0:T(8,128)(2,1)S(1)}, u32[]{:S(2)}) copy-start(bf16[128,192]{1,0:T(8,128)(2,1)S(1)} %get-tuple-element.175.hidden) | copy-start | bytes 147460
  46.5 6.5 %collective-permute-start.3 = (bf16[128,768]{1,0:T(8,128)(2,1)S(1)}, bf16[128,768]{1,0:T(8,128)(2,1)S(1)}, u32[]{:S(2)}, u32[]{:S(2)}) collective-permute-start(bf16[128,768]{1,0:T(8,128)(2,1)S(1)} %get-tuple-element.106), channel_id=1, source_target_pairs={{0,1},{1,0},{2,3},{3,2},{4,5},{5,4},{6,7},{7,6},{8,9},{9,8},{10,11... | collective-permute-start | bytes 589832 | tf_op jit(solution)/shard_map/ppermute | solution.py:35
  48.0 7.6 %collective-permute-start.4 = (bf16[128,768]{1,0:T(8,128)(2,1)S(1)}, bf16[128,768]{1,0:T(8,128)(2,1)S(1)}, u32[]{:S(2)}, u32[]{:S(2)}) collective-permute-start(bf16[128,768]{1,0:T(8,128)(2,1)S(1)} %get-tuple-element.107), channel_id=1, source_target_pairs={{0,3},{1,2},{2,1},{3,0},{4,7},{5,6},{6,5},{7,4},{8,11},{9,10},{10,... | collective-permute-start | bytes 589832 | tf_op jit(solution)/shard_map/ppermute | solution.py:35
  55.7 5.7 %collective-permute-start.6 = (bf16[128,768]{1,0:T(8,128)(2,1)S(1)}, bf16[128,768]{1,0:T(8,128)(2,1)S(1)}, u32[]{:S(2)}, u32[]{:S(2)}) collective-permute-start(bf16[128,768]{1,0:T(8,128)(2,1)S(1)} %add_convert_fusion.17.b), channel_id=1, source_target_pairs={{0,1},{1,0},{2,3},{3,2},{4,5},{5,4},{6,7},{7,6},{8,9},{9,8},{10,11... | collective-permute-start | bytes 589832 | tf_op jit(solution)/shard_map/ppermute | solution.py:35
  55.8 7.0 %collective-permute-start.5 = (bf16[128,768]{1,0:T(8,128)(2,1)S(1)}, bf16[128,768]{1,0:T(8,128)(2,1)S(1)}, u32[]{:S(2)}, u32[]{:S(2)}) collective-permute-start(bf16[128,768]{1,0:T(8,128)(2,1)S(1)} %add_convert_fusion.18.a), channel_id=1, source_target_pairs={{0,3},{1,2},{2,1},{3,0},{4,7},{5,6},{6,5},{7,4},{8,11},{9,10},{10,... | collective-permute-start | bytes 589832 | tf_op jit(solution)/shard_map/ppermute | solution.py:35
  67.0 14.8 %copy-start.37 = (bf16[128,192]{1,0:T(8,128)(2,1)}, bf16[128,192]{1,0:T(8,128)(2,1)S(1)}, u32[]{:S(2)}) copy-start(bf16[128,192]{1,0:T(8,128)(2,1)S(1)} %get-tuple-element.159.hidden) | copy-start | bytes 147460
  67.0 5.7 %collective-permute-start.7 = (bf16[128,768]{1,0:T(8,128)(2,1)S(1)}, bf16[128,768]{1,0:T(8,128)(2,1)S(1)}, u32[]{:S(2)}, u32[]{:S(2)}) collective-permute-start(bf16[128,768]{1,0:T(8,128)(2,1)S(1)} %get-tuple-element.113), channel_id=1, source_target_pairs={{0,1},{1,0},{2,3},{3,2},{4,5},{5,4},{6,7},{7,6},{8,9},{9,8},{10,11... | collective-permute-start | bytes 589832 | tf_op jit(solution)/shard_map/ppermute | solution.py:35
  67.8 6.9 %collective-permute-start.8 = (bf16[128,768]{1,0:T(8,128)(2,1)S(1)}, bf16[128,768]{1,0:T(8,128)(2,1)S(1)}, u32[]{:S(2)}, u32[]{:S(2)}) collective-permute-start(bf16[128,768]{1,0:T(8,128)(2,1)S(1)} %get-tuple-element.114), channel_id=1, source_target_pairs={{0,3},{1,2},{2,1},{3,0},{4,7},{5,6},{6,5},{7,4},{8,11},{9,10},{10,... | collective-permute-start | bytes 589832 | tf_op jit(solution)/shard_map/ppermute | solution.py:35
  69.6 12.2 %copy-start.15 = (bf16[128,1536]{1,0:T(8,128)(2,1)S(1)}, bf16[128,1536]{1,0:T(8,128)(2,1)}, u32[]{:S(2)}) copy-start(bf16[128,1536]{1,0:T(8,128)(2,1)} %copy-done.14) | copy-start | bytes 1179652
  74.7 5.7 %collective-permute-start.10 = (bf16[128,768]{1,0:T(8,128)(2,1)S(1)}, bf16[128,768]{1,0:T(8,128)(2,1)S(1)}, u32[]{:S(2)}, u32[]{:S(2)}) collective-permute-start(bf16[128,768]{1,0:T(8,128)(2,1)S(1)} %add_convert_fusion.15.b), channel_id=1, source_target_pairs={{0,1},{1,0},{2,3},{3,2},{4,5},{5,4},{6,7},{7,6},{8,9},{9,8},{10,11... | collective-permute-start | bytes 589832 | tf_op jit(solution)/shard_map/ppermute | solution.py:35
  74.9 6.9 %collective-permute-start.9 = (bf16[128,768]{1,0:T(8,128)(2,1)S(1)}, bf16[128,768]{1,0:T(8,128)(2,1)S(1)}, u32[]{:S(2)}, u32[]{:S(2)}) collective-permute-start(bf16[128,768]{1,0:T(8,128)(2,1)S(1)} %add_convert_fusion.16.a), channel_id=1, source_target_pairs={{0,3},{1,2},{2,1},{3,0},{4,7},{5,6},{6,5},{7,4},{8,11},{9,10},{10,... | collective-permute-start | bytes 589832 | tf_op jit(solution)/shard_map/ppermute | solution.py:35
  86.5 46.5 %slice-start = ((s8[7077888]{0:T(1024)(128)(4,1)}), s8[2883584]{0:T(1024)(128)(4,1)S(1)}, s32[]{:S(2)}) async-start(s8[7077888]{0:T(1024)(128)(4,1)} %bitcast.22), calls=%async_computation.7 | async-start | bytes 5767168
  89.3 10.4 %copy-start.41 = (bf16[128,1536]{1,0:T(8,128)(2,1)}, bf16[128,1536]{1,0:T(8,128)(2,1)S(1)}, u32[]{:S(2)}) copy-start(bf16[128,1536]{1,0:T(8,128)(2,1)S(1)} %get-tuple-element.145.active) | copy-start | bytes 1179652
  89.3 12.2 %copy-start.52 = (s32[32,24]{1,0:T(8,128)S(1)}, s32[32,24]{1,0:T(8,128)}, u32[]{:S(2)}) copy-start(s32[32,24]{1,0:T(8,128)} %constant.61) | copy-start | bytes 9220
  89.3 6.9 %collective-permute-start.11 = (bf16[128,768]{1,0:T(8,128)(2,1)S(1)}, bf16[128,768]{1,0:T(8,128)(2,1)S(1)}, u32[]{:S(2)}, u32[]{:S(2)}) collective-permute-start(bf16[128,768]{1,0:T(8,128)(2,1)S(1)} %get-tuple-element.120), channel_id=1, source_target_pairs={{0,1},{1,0},{2,3},{3,2},{4,5},{5,4},{6,7},{7,6},{8,9},{9,8},{10,11... | collective-permute-start | bytes 589832 | tf_op jit(solution)/shard_map/ppermute | solution.py:35
  90.1 8.9 %collective-permute-start.12 = (bf16[128,768]{1,0:T(8,128)(2,1)S(1)}, bf16[128,768]{1,0:T(8,128)(2,1)S(1)}, u32[]{:S(2)}, u32[]{:S(2)}) collective-permute-start(bf16[128,768]{1,0:T(8,128)(2,1)S(1)} %get-tuple-element.121), channel_id=1, source_target_pairs={{0,3},{1,2},{2,1},{3,0},{4,7},{5,6},{6,5},{7,4},{8,11},{9,10},{10,... | collective-permute-start | bytes 589832 | tf_op jit(solution)/shard_map/ppermute | solution.py:35
  99.8 6.0 %collective-permute-start.14 = (bf16[128,768]{1,0:T(8,128)(2,1)}, bf16[128,768]{1,0:T(8,128)(2,1)}, u32[]{:S(2)}, u32[]{:S(2)}) collective-permute-start(bf16[128,768]{1,0:T(8,128)(2,1)} %add_convert_fusion.13.b), channel_id=1, source_target_pairs={{0,1},{1,0},{2,3},{3,2},{4,5},{5,4},{6,7},{7,6},{8,9},{9,8},{10,11... | collective-permute-start | bytes 589832 | tf_op jit(solution)/shard_map/ppermute | solution.py:35
  99.8 7.1 %collective-permute-start.13 = (bf16[128,768]{1,0:T(8,128)(2,1)S(1)}, bf16[128,768]{1,0:T(8,128)(2,1)}, u32[]{:S(2)}, u32[]{:S(2)}) collective-permute-start(bf16[128,768]{1,0:T(8,128)(2,1)S(1)} %add_convert_fusion.14.a), channel_id=1, source_target_pairs={{0,3},{1,2},{2,1},{3,0},{4,7},{5,6},{6,5},{7,4},{8,11},{9,10},{10,... | collective-permute-start | bytes 589832 | tf_op jit(solution)/shard_map/ppermute | solution.py:35
  112.5 20.5 %slice-start.1 = ((s8[7077888]{0:T(1024)(128)(4,1)}), s8[4194304]{0:T(1024)(128)(4,1)S(1)}, s32[]{:S(2)}) async-start(s8[7077888]{0:T(1024)(128)(4,1)} %bitcast.22), calls=%async_computation.8 | async-start | bytes 8388608
  116.5 5.7 %collective-permute-start.15 = (bf16[128,768]{1,0:T(8,128)(2,1)S(1)}, bf16[128,768]{1,0:T(8,128)(2,1)S(1)}, u32[]{:S(2)}, u32[]{:S(2)}) collective-permute-start(bf16[128,768]{1,0:T(8,128)(2,1)S(1)} %get-tuple-element.126), channel_id=1, source_target_pairs={{0,1},{1,0},{2,3},{3,2},{4,5},{5,4},{6,7},{7,6},{8,9},{9,8},{10,11... | collective-permute-start | bytes 589832 | tf_op jit(solution)/shard_map/ppermute | solution.py:35
  117.3 6.9 %collective-permute-start.16 = (bf16[128,768]{1,0:T(8,128)(2,1)S(1)}, bf16[128,768]{1,0:T(8,128)(2,1)S(1)}, u32[]{:S(2)}, u32[]{:S(2)}) collective-permute-start(bf16[128,768]{1,0:T(8,128)(2,1)S(1)} %get-tuple-element.127), channel_id=1, source_target_pairs={{0,3},{1,2},{2,1},{3,0},{4,7},{5,6},{6,5},{7,4},{8,11},{9,10},{10,... | collective-permute-start | bytes 589832 | tf_op jit(solution)/shard_map/ppermute | solution.py:35
  119.2 18.1 %copy-start.17 = (bf16[768,768]{1,0:T(8,128)(2,1)}, bf16[768,768]{1,0:T(8,128)(2,1)S(1)}, u32[]{:S(2)}) copy-start(bf16[768,768]{1,0:T(8,128)(2,1)S(1)} %fusion.rest_0_) | copy-start | bytes 3538948
  120.3 12.7 %copy-start.34 = (f32[128,192]{1,0:T(8,128)S(1)}, f32[128,192]{1,0:T(8,128)}, u32[]{:S(2)}) copy-start(f32[128,192]{1,0:T(8,128)} %copy-done.33) | copy-start | bytes 294916
  124.2 8.8 %collective-permute-start.19 = (bf16[384,1536]{1,0:T(8,128)(2,1)S(1)}, bf16[384,1536]{1,0:T(8,128)(2,1)S(1)}, u32[]{:S(2)}, u32[]{:S(2)}) collective-permute-start(bf16[384,1536]{1,0:T(8,128)(2,1)S(1)} %get-tuple-element.135), channel_id=1, source_target_pairs={{0,4},{4,0},{8,12},{12,8},{16,20},{20,16},{24,28},{28,24},{32,36},... | collective-permute-start | bytes 3538952 | tf_op jit(solution)/shard_map/ppermute | solution.py:35
  124.3 7.4 %collective-permute-start.18 = (bf16[128,768]{1,0:T(8,128)(2,1)S(1)}, bf16[128,768]{1,0:T(8,128)(2,1)S(1)}, u32[]{:S(2)}, u32[]{:S(2)}) collective-permute-start(bf16[128,768]{1,0:T(8,128)(2,1)S(1)} %add_convert_fusion.11.b), channel_id=1, source_target_pairs={{0,1},{1,0},{2,3},{3,2},{4,5},{5,4},{6,7},{7,6},{8,9},{9,8},{10,11... | collective-permute-start | bytes 589832 | tf_op jit(solution)/shard_map/ppermute | solution.py:35
  124.4 8.5 %collective-permute-start.17 = (bf16[128,768]{1,0:T(8,128)(2,1)S(1)}, bf16[128,768]{1,0:T(8,128)(2,1)S(1)}, u32[]{:S(2)}, u32[]{:S(2)}) collective-permute-start(bf16[128,768]{1,0:T(8,128)(2,1)S(1)} %add_convert_fusion.12.a), channel_id=1, source_target_pairs={{0,3},{1,2},{2,1},{3,0},{4,7},{5,6},{6,5},{7,4},{8,11},{9,10},{10,... | collective-permute-start | bytes 589832 | tf_op jit(solution)/shard_map/ppermute | solution.py:35
  135.2 6.6 %collective-permute-start.20 = (bf16[128,768]{1,0:T(8,128)(2,1)S(1)}, bf16[128,768]{1,0:T(8,128)(2,1)S(1)}, u32[]{:S(2)}, u32[]{:S(2)}) collective-permute-start(bf16[128,768]{1,0:T(8,128)(2,1)S(1)} %get-tuple-element.141), channel_id=1, source_target_pairs={{0,1},{1,0},{2,3},{3,2},{4,5},{5,4},{6,7},{7,6},{8,9},{9,8},{10,11... | collective-permute-start | bytes 589832 | tf_op jit(solution)/shard_map/ppermute | solution.py:35
  135.8 7.4 %collective-permute-start.21 = (bf16[128,768]{1,0:T(8,128)(2,1)S(1)}, bf16[128,768]{1,0:T(8,128)(2,1)S(1)}, u32[]{:S(2)}, u32[]{:S(2)}) collective-permute-start(bf16[128,768]{1,0:T(8,128)(2,1)S(1)} %get-tuple-element.142), channel_id=1, source_target_pairs={{0,3},{1,2},{2,1},{3,0},{4,7},{5,6},{6,5},{7,4},{8,11},{9,10},{10,... | collective-permute-start | bytes 589832 | tf_op jit(solution)/shard_map/ppermute | solution.py:35
  143.2 9.0 %collective-permute-start.24 = (bf16[384,1536]{1,0:T(8,128)(2,1)S(1)}, bf16[384,1536]{1,0:T(8,128)(2,1)S(1)}, u32[]{:S(2)}, u32[]{:S(2)}) collective-permute-start(bf16[384,1536]{1,0:T(8,128)(2,1)S(1)} %get-tuple-element.151), channel_id=1, source_target_pairs={{0,4},{4,0},{8,12},{12,8},{16,20},{20,16},{24,28},{28,24},{32,36},... | collective-permute-start | bytes 3538952 | tf_op jit(solution)/shard_map/ppermute | solution.py:35
  143.2 7.4 %collective-permute-start.23 = (bf16[128,768]{1,0:T(8,128)(2,1)S(1)}, bf16[128,768]{1,0:T(8,128)(2,1)S(1)}, u32[]{:S(2)}, u32[]{:S(2)}) collective-permute-start(bf16[128,768]{1,0:T(8,128)(2,1)S(1)} %add_convert_fusion.9.b), channel_id=1, source_target_pairs={{0,1},{1,0},{2,3},{3,2},{4,5},{5,4},{6,7},{7,6},{8,9},{9,8},{10,11... | collective-permute-start | bytes 589832 | tf_op jit(solution)/shard_map/ppermute | solution.py:35
  143.8 8.3 %collective-permute-start.22 = (bf16[128,768]{1,0:T(8,128)(2,1)S(1)}, bf16[128,768]{1,0:T(8,128)(2,1)S(1)}, u32[]{:S(2)}, u32[]{:S(2)}) collective-permute-start(bf16[128,768]{1,0:T(8,128)(2,1)S(1)} %add_convert_fusion.10.a), channel_id=1, source_target_pairs={{0,3},{1,2},{2,1},{3,0},{4,7},{5,6},{6,5},{7,4},{8,11},{9,10},{10,... | collective-permute-start | bytes 589832 | tf_op jit(solution)/shard_map/ppermute | solution.py:35
  168.1 6.3 %collective-permute-start.25 = (bf16[128,768]{1,0:T(8,128)(2,1)S(1)}, bf16[128,768]{1,0:T(8,128)(2,1)S(1)}, u32[]{:S(2)}, u32[]{:S(2)}) collective-permute-start(bf16[128,768]{1,0:T(8,128)(2,1)S(1)} %get-tuple-element.156), channel_id=1, source_target_pairs={{0,1},{1,0},{2,3},{3,2},{4,5},{5,4},{6,7},{7,6},{8,9},{9,8},{10,11... | collective-permute-start | bytes 589832 | tf_op jit(solution)/shard_map/ppermute | solution.py:35
  168.5 7.2 %collective-permute-start.26 = (bf16[128,768]{1,0:T(8,128)(2,1)S(1)}, bf16[128,768]{1,0:T(8,128)(2,1)S(1)}, u32[]{:S(2)}, u32[]{:S(2)}) collective-permute-start(bf16[128,768]{1,0:T(8,128)(2,1)S(1)} %get-tuple-element.157), channel_id=1, source_target_pairs={{0,3},{1,2},{2,1},{3,0},{4,7},{5,6},{6,5},{7,4},{8,11},{9,10},{10,... | collective-permute-start | bytes 589832 | tf_op jit(solution)/shard_map/ppermute | solution.py:35
  171.3 13.3 %copy-start.16 = (bf16[128,1536]{1,0:T(8,128)(2,1)S(1)}, bf16[128,1536]{1,0:T(8,128)(2,1)}, u32[]{:S(2)}) copy-start(bf16[128,1536]{1,0:T(8,128)(2,1)} %copy-done.14) | copy-start | bytes 1179652
  171.3 13.3 %copy-start.36 = (f32[128,192]{1,0:T(8,128)S(1)}, f32[128,192]{1,0:T(8,128)}, u32[]{:S(2)}) copy-start(f32[128,192]{1,0:T(8,128)} %copy-done.35) | copy-start | bytes 294916
  175.7 9.0 %collective-permute-start.29 = (bf16[384,768]{1,0:T(8,128)(2,1)S(1)}, bf16[384,768]{1,0:T(8,128)(2,1)S(1)}, u32[]{:S(2)}, u32[]{:S(2)}) collective-permute-start(bf16[384,768]{1,0:T(8,128)(2,1)S(1)} %get-tuple-element.168), channel_id=1, source_target_pairs={{0,4},{4,0},{8,12},{12,8},{16,20},{20,16},{24,28},{28,24},{32,36},... | collective-permute-start | bytes 1769480 | tf_op jit(solution)/shard_map/ppermute | solution.py:35
  175.7 9.0 %collective-permute-start.30 = (bf16[384,768]{1,0:T(8,128)(2,1)S(1)}, bf16[384,768]{1,0:T(8,128)(2,1)S(1)}, u32[]{:S(2)}, u32[]{:S(2)}) collective-permute-start(bf16[384,768]{1,0:T(8,128)(2,1)S(1)} %get-tuple-element.169), channel_id=1, source_target_pairs={{0,4},{4,0},{8,12},{12,8},{16,20},{20,16},{24,28},{28,24},{32,36},... | collective-permute-start | bytes 1769480 | tf_op jit(solution)/shard_map/ppermute | solution.py:35
  176.3 6.9 %collective-permute-start.28 = (bf16[128,768]{1,0:T(8,128)(2,1)S(1)}, bf16[128,768]{1,0:T(8,128)(2,1)S(1)}, u32[]{:S(2)}, u32[]{:S(2)}) collective-permute-start(bf16[128,768]{1,0:T(8,128)(2,1)S(1)} %add_convert_fusion.7.b), channel_id=1, source_target_pairs={{0,1},{1,0},{2,3},{3,2},{4,5},{5,4},{6,7},{7,6},{8,9},{9,8},{10,11... | collective-permute-start | bytes 589832 | tf_op jit(solution)/shard_map/ppermute | solution.py:35
  176.8 7.8 %collective-permute-start.27 = (bf16[128,768]{1,0:T(8,128)(2,1)S(1)}, bf16[128,768]{1,0:T(8,128)(2,1)S(1)}, u32[]{:S(2)}, u32[]{:S(2)}) collective-permute-start(bf16[128,768]{1,0:T(8,128)(2,1)S(1)} %add_convert_fusion.8.a), channel_id=1, source_target_pairs={{0,3},{1,2},{2,1},{3,0},{4,7},{5,6},{6,5},{7,4},{8,11},{9,10},{10,... | collective-permute-start | bytes 589832 | tf_op jit(solution)/shard_map/ppermute | solution.py:35
  188.2 17.0 %collective-permute-start.31 = (bf16[384,1536]{1,0:T(8,128)(2,1)S(1)}, bf16[384,1536]{1,0:T(8,128)(2,1)}, u32[]{:S(2)}, u32[]{:S(2)}) collective-permute-start(bf16[384,1536]{1,0:T(8,128)(2,1)S(1)} %get-tuple-element.178), channel_id=1, source_target_pairs={{0,4},{4,0},{8,12},{12,8},{16,20},{20,16},{24,28},{28,24},{32,36},... | collective-permute-start | bytes 3538952 | tf_op jit(solution)/shard_map/ppermute | solution.py:35
  189.2 15.9 %collective-permute-start.33 = (bf16[192,768]{1,0:T(8,128)(2,1)}, bf16[192,768]{1,0:T(8,128)(2,1)}, u32[]{:S(2)}, u32[]{:S(2)}) collective-permute-start(bf16[192,768]{1,0:T(8,128)(2,1)} %get-tuple-element.215), channel_id=1, source_target_pairs={{0,32},{4,36},{8,40},{12,44},{16,48},{20,52},{24,56},{28,60},{32,0... | collective-permute-start | bytes 884744 | tf_op jit(solution)/shard_map/ppermute | solution.py:35
  190.4 14.8 %collective-permute-start.32 = (bf16[192,768]{1,0:T(8,128)(2,1)}, bf16[192,768]{1,0:T(8,128)(2,1)}, u32[]{:S(2)}, u32[]{:S(2)}) collective-permute-start(bf16[192,768]{1,0:T(8,128)(2,1)} %get-tuple-element.217), channel_id=1, source_target_pairs={{0,8},{4,12},{8,0},{12,4},{16,24},{20,28},{24,16},{28,20},{32,40},... | collective-permute-start | bytes 884744 | tf_op jit(solution)/shard_map/ppermute | solution.py:35
  191.0 14.1 %all-to-all-start.1 = ((bf16[32,16,192]{2,1,0:T(8,128)(2,1)}), bf16[32,16,192]{2,1,0:T(8,128)(2,1)S(1)}, u32[]{:S(2)}, u32[]{:S(2)}) async-start(bf16[32,16,192]{2,1,0:T(8,128)(2,1)} %bitcast.3), calls=%async_computation.1 | async-start | bytes 524288 | tf_op jit(solution)/shard_map/all_to_all | solution.py:433
  196.3 58.1 %reduce-scatter.5.cloned.1.call-start = ((), (), s32[]{:S(2)}) async-start(), calls=%async_computation.6 | async-start | bytes 737280 | tf_op jit(solution)/shard_map/reduce_scatter | solution.py:356
  209.7 17.8 %collective-permute-start.34 = (bf16[128,384]{1,0:T(8,128)(2,1)S(1)}, bf16[128,384]{1,0:T(8,128)(2,1)S(1)}, u32[]{:S(2)}, u32[]{:S(2)}) collective-permute-start(bf16[128,384]{1,0:T(8,128)(2,1)S(1)} %get-tuple-element.190), channel_id=1, source_target_pairs={{0,1},{1,0},{2,3},{3,2},{4,5},{5,4},{6,7},{7,6},{8,9},{9,8},{10,11... | collective-permute-start | bytes 294920 | tf_op jit(solution)/shard_map/ppermute | solution.py:35
  210.1 17.4 %collective-permute-start.35 = (bf16[128,384]{1,0:T(8,128)(2,1)S(1)}, bf16[128,384]{1,0:T(8,128)(2,1)}, u32[]{:S(2)}, u32[]{:S(2)}) collective-permute-start(bf16[128,384]{1,0:T(8,128)(2,1)S(1)} %get-tuple-element.191), channel_id=1, source_target_pairs={{0,3},{1,2},{2,1},{3,0},{4,7},{5,6},{6,5},{7,4},{8,11},{9,10},{10,... | collective-permute-start | bytes 294920 | tf_op jit(solution)/shard_map/ppermute | solution.py:35
  211.3 16.2 %collective-permute-start.36 = (bf16[128,384]{1,0:T(8,128)(2,1)S(1)}, bf16[128,384]{1,0:T(8,128)(2,1)}, u32[]{:S(2)}, u32[]{:S(2)}) collective-permute-start(bf16[128,384]{1,0:T(8,128)(2,1)S(1)} %get-tuple-element.192), channel_id=1, source_target_pairs={{0,2},{1,3},{2,0},{3,1},{4,6},{5,7},{6,4},{7,5},{8,10},{9,11},{10,... | collective-permute-start | bytes 294920 | tf_op jit(solution)/shard_map/ppermute | solution.py:35
  214.9 12.6 %collective-permute-start.38 = (bf16[96,768]{1,0:T(8,128)(2,1)S(1)}, bf16[96,768]{1,0:T(8,128)(2,1)S(1)}, u32[]{:S(2)}, u32[]{:S(2)}) collective-permute-start(bf16[96,768]{1,0:T(8,128)(2,1)S(1)} %get-tuple-element.219), channel_id=1, source_target_pairs={{0,96},{4,100},{8,104},{12,108},{16,112},{20,116},{24,120},{28,124... | collective-permute-start | bytes 442376 | tf_op jit(solution)/shard_map/ppermute | solution.py:35
  217.7 9.9 %collective-permute-start.37 = (bf16[96,768]{1,0:T(8,128)(2,1)}, bf16[96,768]{1,0:T(8,128)(2,1)S(1)}, u32[]{:S(2)}, u32[]{:S(2)}) collective-permute-start(bf16[96,768]{1,0:T(8,128)(2,1)} %get-tuple-element.221), channel_id=1, source_target_pairs={{0,24},{4,28},{8,16},{12,20},{16,8},{20,12},{24,0},{28,4},{32,56},... | collective-permute-start | bytes 442376 | tf_op jit(solution)/shard_map/ppermute | solution.py:35
  223.4 30.9 %all-to-all-start.2 = ((bf16[16,24,1536]{2,1,0:T(8,128)(2,1)}), bf16[16,24,1536]{2,1,0:T(8,128)(2,1)S(1)}, u32[]{:S(2)}, u32[]{:S(2)}) async-start(bf16[16,24,1536]{2,1,0:T(8,128)(2,1)} %bitcast.27), calls=%async_computation.3 | async-start | bytes 2359296 | tf_op jit(solution)/shard_map/all_to_all | solution.py:329
  227.5 24.7 %copy-start.48 = (bf16[128,384]{1,0:T(8,128)(2,1)S(1)}, bf16[128,384]{1,0:T(8,128)(2,1)}, u32[]{:S(2)}) copy-start(bf16[128,384]{1,0:T(8,128)(2,1)} %param.15) | copy-start | bytes 294916
  227.6 19.3 %collective-permute-start.40 = (bf16[48,768]{1,0:T(8,128)(2,1)S(1)}, bf16[48,768]{1,0:T(8,128)(2,1)S(1)}, u32[]{:S(2)}, u32[]{:S(2)}) collective-permute-start(bf16[48,768]{1,0:T(8,128)(2,1)S(1)} %get-tuple-element.223), channel_id=1, source_target_pairs={{0,8},{4,12},{8,0},{12,4},{16,24},{20,28},{24,16},{28,20},{32,40},... | collective-permute-start | bytes 221192 | tf_op jit(solution)/shard_map/ppermute | solution.py:35
  229.6 19.4 %collective-permute-start.39 = (bf16[48,768]{1,0:T(8,128)(2,1)S(1)}, bf16[48,768]{1,0:T(8,128)(2,1)S(1)}, u32[]{:S(2)}, u32[]{:S(2)}) collective-permute-start(bf16[48,768]{1,0:T(8,128)(2,1)S(1)} %get-tuple-element.225), channel_id=1, source_target_pairs={{0,32},{4,36},{8,40},{12,44},{16,48},{20,52},{24,56},{28,60},{32,0... | collective-permute-start | bytes 221192 | tf_op jit(solution)/shard_map/ppermute | solution.py:35
  246.9 7.1 %collective-permute-start.42 = (bf16[24,768]{1,0:T(8,128)(2,1)S(1)}, bf16[24,768]{1,0:T(8,128)(2,1)S(1)}, u32[]{:S(2)}, u32[]{:S(2)}) collective-permute-start(bf16[24,768]{1,0:T(8,128)(2,1)S(1)} %get-tuple-element.226), channel_id=1, source_target_pairs={{0,24},{4,28},{8,16},{12,20},{16,8},{20,12},{24,0},{28,4},{32,56},... | collective-permute-start | bytes 110600 | tf_op jit(solution)/shard_map/ppermute | solution.py:35
  249.1 5.2 %collective-permute-start.41 = (bf16[24,768]{1,0:T(8,128)(2,1)S(1)}, bf16[24,768]{1,0:T(8,128)(2,1)S(1)}, u32[]{:S(2)}, u32[]{:S(2)}) collective-permute-start(bf16[24,768]{1,0:T(8,128)(2,1)S(1)} %get-tuple-element.228), channel_id=1, source_target_pairs={{0,96},{4,100},{8,104},{12,108},{16,112},{20,116},{24,120},{28,124... | collective-permute-start | bytes 110600 | tf_op jit(solution)/shard_map/ppermute | solution.py:35
  (45 other events, 146.7 us)
Sparse Core Ops, SparseCore 0:
  154.6 27.7 reduce-scatter.2
  221.0 22.8 reduce-scatter.4

commit v2 on v1

v2 whole, which is shorter than its diff:
```python
import functools

import jax
import jax.numpy as jnp
import numpy as np
from jax import lax
from jax.experimental import pallas as pl
from jax.experimental.pallas import tpu as pltpu
from jax.sharding import PartitionSpec as P

LAYERS = 4
ROWS = 128
C = 1536
H = 192
HALF = C // 2
SHARD = C // 4
PEERS = 32
BF16 = jnp.bfloat16
F32 = jnp.float32
ROOT = float(np.sqrt(2.0 / np.pi))
CUBE = 0.044715


def together(*values):
    return lax.optimization_barrier(values)


def dot(a, b, ca=1, cb=0):
    return lax.dot_general(a, b, (((ca,), (cb,)), ((), ())), preferred_element_type=F32)


def swap(values, axis, mask):
    peers = lax.axis_size(axis)
    return lax.ppermute(values, axis, [(i, i ^ mask) for i in range(peers)])


def add(a, b):
    return (a.astype(F32) + b.astype(F32)).astype(BF16)


def slope(x):
    square = x * x
    t = jnp.tanh(ROOT * x * (1.0 + CUBE * square))
    return 0.5 * (1.0 + t) + 0.5 * x * (1.0 - t * t) * (ROOT * (1.0 + 3.0 * CUBE * square))


def shifted(values, by):
    if by == 0:
        return values
    length = values.shape[0]
    zeros = jnp.zeros((abs(by),) + values.shape[1:], values.dtype)
    if by > 0:
        return jnp.concatenate([values[by:], zeros], axis=0)
    return jnp.concatenate([zeros, values[: length + by]], axis=0)


def struct(shape, kind):
    return jax.ShapeDtypeStruct(shape, kind)


def call(body, outs, scratch, args, spaces=None, flops=4e8):
    spaces = spaces or {}
    return pl.pallas_call(
        body,
        out_shape=outs,
        in_specs=[
            pl.BlockSpec(memory_space=spaces.get(i, pltpu.VMEM)) for i in range(len(args))
        ],
        out_specs=[pl.BlockSpec(memory_space=pltpu.VMEM)] * len(outs),
        scratch_shapes=scratch,
        compiler_params=pltpu.CompilerParams(vmem_limit_bytes=16 * 2**20),
        cost_estimate=pl.CostEstimate(flops=int(flops), bytes_accessed=4_000_000, transcendentals=0),
    )(*args)


def chunks():
    return [slice(i, i + 16) for i in range(0, ROWS, 16)]


def total_of(rows, half, first, second):
    a, b = (first, second)[half]
    return a[rows].astype(F32) + b[rows].astype(F32)


def conv(active, k_mem, distance):
    taps = [dot(active, k_mem[k], 1, 1) for k in range(3)]
    return taps[1] + shifted(taps[0], -distance) + shifted(taps[2], distance)


def conv_back(inner_grad, k_mem, distance):
    out = None
    for k in range(3):
        moved = shifted(inner_grad, (1 - k) * distance).astype(BF16)
        part = dot(moved, k_mem[k])
        out = part if out is None else out + part
    return out


def put_halves(term, ta, tb):
    term = term.astype(BF16)
    ta[...] = term[:, :HALF]
    tb[...] = term[:, HALF:]


def backward_of(inner, grad_b, p_mem):
    hidden_grad = dot(grad_b, p_mem[...], 1, 1)
    return (hidden_grad * slope(inner)).astype(BF16)


def start_kernel(me, own, one, three, two, k_mem, p_mem, *rest):
    x, g, inner, ta, tb, active = rest
    for mask, block in ((0, own), (1, one), (3, three), (2, two)):
        at = pl.ds(pl.multiple_of((me[0] ^ mask) * SHARD, 128), SHARD)
        x[:, at] = block[:ROWS]
        g[:, at] = block[ROWS:]
    for rows in chunks():
        active[rows] = jax.nn.gelu(x[rows].astype(F32)).astype(BF16)
    values = conv(active[...], k_mem, 1)
    inner[...] = values
    put_halves(dot(jax.nn.gelu(values).astype(BF16), p_mem[...]), ta, tb)


def forward_kernel(layer, x, a, b, a2, b2, k_mem, p_mem, *rest):
    x1, inner, ta, tb, active = rest
    advance(x, a, b, a2, b2, x1, active)
    values = conv(active[...], k_mem, 2**layer)
    inner[...] = values
    put_halves(dot(jax.nn.gelu(values).astype(BF16), p_mem[...]), ta, tb)


def advance(x, a, b, a2, b2, x1, active):
    for rows in chunks():
        for half in (0, 1):
            at = slice(half * HALF, half * HALF + HALF)
            total = total_of(rows, half, (a, a2), (b, b2))
            values = (x[rows, at].astype(F32) + total).astype(BF16)
            x1[rows, at] = values
            active[rows, at] = jax.nn.gelu(values.astype(F32)).astype(BF16)


def turn_kernel(layer, x, a, b, a2, b2, g, k_mem, p_mem, *rest):
    x1, inner, inner_grad, ta, tb, active = rest
    advance(x, a, b, a2, b2, x1, active)
    before = conv(active[...], k_mem, 2**layer)
    inner[...] = before
    values = backward_of(before, g[...], p_mem)
    inner_grad[...] = values
    put_halves(conv_back(values.astype(F32), k_mem, 2**layer), ta, tb)


def retreat(g, a, b, a2, b2, x, g1, grad_b):
    for rows in chunks():
        for half in (0, 1):
            at = slice(half * HALF, half * HALF + HALF)
            total = total_of(rows, half, (a, a2), (b, b2))
            values = g[rows, at].astype(F32) + slope(x[rows, at].astype(F32)) * total
            if g1 is not None:
                g1[rows, at] = values
            grad_b[rows, at] = values.astype(BF16)


def backward_kernel(layer, g, a, b, a2, b2, x, inner, k_mem, p_mem, *rest):
    g1, grad_b, inner_grad, ta, tb = rest
    retreat(g, a, b, a2, b2, x, g1, grad_b)
    values = backward_of(inner[...], grad_b[...], p_mem)
    inner_grad[...] = values
    put_halves(conv_back(values.astype(F32), k_mem, 2**layer), ta, tb)


def final_kernel(me, g, a, b, a2, b2, x, inner, order, p_mem, *rest):
    grad_b, inner_grad, sent = rest
    retreat(g, a, b, a2, b2, x, None, grad_b)
    values = backward_of(inner[...], grad_b[...], p_mem)
    inner_grad[...] = values
    own = grad_b[:, pl.ds(pl.multiple_of(me[0] * SHARD, 128), SHARD)]
    parts = jnp.concatenate([values, own[:, :H], own[:, H:]], axis=0)
    sent[...] = dot(order[...], parts).astype(BF16)


def last_kernel(me, got, order, k_mem, *rest):
    own, one, three, two, g, term = rest
    values = dot(order[...], got[...])
    moved = values.astype(BF16)
    g[:, :H] = values[192:320]
    g[:, H:] = values[320:448]
    out = dot(moved[64:192], k_mem[0])
    out = out + dot(moved[32:160], k_mem[1])
    term[...] = out + dot(moved[:128], k_mem[2])
    for mask, ref in ((0, own), (1, one), (3, three), (2, two)):
        at = pl.ds(pl.multiple_of((me[0] ^ mask) * SHARD, 128), SHARD)
        ref[...] = term[:, at].astype(ref.dtype)


def weight_kernel(distance, inner_grad, inner, x, grad_b, table, keep, send):
    grad = inner_grad[...].astype(F32)
    top = None
    for k in range(3):
        moved = shifted(grad, (1 - k) * distance).astype(BF16)
        part = dot(moved, table[k * H : (k + 1) * H])
        top = part if top is None else top + part
    bottom = dot(jax.nn.gelu(inner[...]).astype(BF16), table[3 * H :])
    left = jnp.concatenate([top, bottom], axis=0).T.astype(BF16)
    for column in range(0, C, 384):
        at = slice(column, column + 384)
        active = jax.nn.gelu(x[:, at].astype(F32)).astype(BF16)
        right = jnp.concatenate([active, grad_b[:, at]], axis=0)
        for ref, row in ((keep, 0), (send, 384)):
            ref[:, at] = dot(left[row : row + 384], right).astype(BF16)


def weight_terms(layer, table, inner_grad, inner, x, grad_b):
    body = functools.partial(weight_kernel, 2**layer)
    outs = [struct((384, C), BF16)] * 2
    return call(body, outs, [], (inner_grad, inner, x, grad_b, table), flops=8e8)


def merge_kernel(*refs):
    out = refs[-1]
    for layer in range(len(refs) // 2):
        a, b = refs[2 * layer], refs[2 * layer + 1]
        for z in range(4):
            rows = slice(96 * z, 96 * z + 96)
            out[z, 96 * layer : 96 * layer + 96] = add(a[rows], b[rows])


def split_kernel(me, *refs):
    parts, outs = refs[:-4], refs[-4:]
    for mask, out in enumerate(outs):
        at = me[0] ^ mask
        row = 0
        for part in parts:
            for layer in range(part.shape[0] // 96):
                rows = pl.ds(pl.multiple_of(96 * layer + 24 * at, 8), 24)
                out[row : row + 24] = part[rows]
                row += 24


def sums_kernel(first, own, one, two, three, kernel_out, point_out):
    total = first[0].astype(F32)
    for i in range(1, 16):
        total = total + first[i].astype(F32)
    late = own[...].astype(F32)
    for ref in (one, two, three):
        late = late + ref[...].astype(F32)
    for layer, values in enumerate((total, late[24:48], late[48:], late[:24])):
        for k in range(3):
            kernel_out[layer, k] = values[6 * k : 6 * k + 6]
        point_out[layer] = values[18:]


def table_of(source, columns):
    (source,) = together(jnp.asarray(source, jnp.int32))
    return (lax.broadcasted_iota(jnp.int32, (len(source), columns), 1) == source[:, None]).astype(
        BF16
    )


def by_source(blocks):
    column = np.arange(768)
    row = column % 24
    fixed = jnp.asarray(row // 6 * H + row % 6, jnp.int32)
    (source,) = together(fixed + 6 * jnp.repeat(blocks, 24))
    return (lax.broadcasted_iota(jnp.int32, (768, 768), 0) == source[None]).astype(BF16)


def absolute_order():
    core = lax.axis_index("seq") % 2
    block = np.arange(32)
    return by_source(2 * (block % 16) + (core ^ jnp.asarray(block // 16, jnp.int32)))


def block_to_residue():
    n = np.arange(256)
    r, t = n // 8, n % 8
    go = t // 4 * 128 + t % 4 * 32 + r
    come = n % 128 // 4 * 8 + n // 128 * 4 + n % 4
    return table_of(go, 256), table_of(come, 256)


def residue_to_block():
    n = np.arange(512)
    s, t = n // 16, n % 16
    a = 4 * s + t - 1
    grad = np.where((t < 6) & (a >= 0) & (a < 128), a, -1)
    half = 128 + (t - 6) // 4 * 128 + 4 * s + (t - 6) % 4
    go = np.where(t < 6, grad, np.where(t < 14, half, -1))
    n = np.arange(448)
    m = n - 192
    come = np.where(
        n < 192, n % 32 * 16 + n // 32, m % 32 * 16 + 6 + m // 128 * 4 + m % 128 // 32
    )
    return table_of(go, 384), table_of(come, 512)


def over_chips(values):
    groups = [[2 * i + core for i in range(PEERS // 2)] for core in (0, 1)]
    return lax.all_to_all(
        values.reshape(16, 24, values.shape[1]), "seq", 0, 0, axis_index_groups=groups
    )


def over_z(values):
    along_z = [[8 * i + j for i in range(4)] for j in range(8)]
    got = lax.psum_scatter(values, "seq", scatter_dimension=0, axis_index_groups=along_z)
    return got


def sum_mp(a, b, load, first=()):
    a1, b1, *first = together(swap(a, "mp", 1), swap(b, "mp", 3), *first)
    a, b = add(a, a1), add(b, b1)
    a2, b2 = swap(a, "mp", 3), swap(b, "mp", 1)
    sent = [swap(s, "seq", 1) for s in first[1:]]
    loaded = load(a)
    a2, b2, *rest = together(a2, b2, *sent, *loaded)
    kept = [*first[:1], *rest[: len(sent)]]
    return (a, b, a2, b2), kept, rest[len(sent) :]


def shards(inputs, cotangent, conv_kernels, point_weights):
    me = lax.axis_index("mp").astype(jnp.int32)[None]
    along_x = (lax.axis_index("seq") // 2 % 4).astype(jnp.int32)[None]

    def weights(layer):
        def load(after):
            _, kernels, points = together(after, conv_kernels, point_weights)
            return kernels[layer], points[layer]

        return load

    go, come = block_to_residue()
    sent = dot(go, jnp.concatenate([inputs, cotangent], axis=0)).astype(BF16)
    got = lax.all_to_all(sent.reshape(PEERS, 8, SHARD), "seq", 0, 0)
    own = dot(come, got.reshape(256, SHARD)).astype(BF16)
    loaded = weights(0)(own)
    one, three, two, *loaded = together(*[swap(own, "mp", mask) for mask in (1, 3, 2)], *loaded)
    full, narrow, hid = struct((ROWS, C), BF16), struct((ROWS, H), F32), struct((ROWS, H), BF16)
    half = struct((ROWS, HALF), BF16)
    scratch = [pltpu.VMEM((ROWS, C), BF16)]
    x, g, inner, ta, tb = call(
        start_kernel,
        [full, full, narrow, half, half],
        scratch,
        (me, own, one, three, two, *loaded),
        {0: pltpu.SMEM},
    )
    saved = [(x, inner)]
    table = absolute_order()
    block_go, block_come = residue_to_block()
    for layer in (1, 2):
        terms, _, loaded = sum_mp(ta, tb, weights(layer))
        x, inner, ta, tb = call(
            functools.partial(forward_kernel, layer),
            [full, narrow, half, half],
            scratch,
            (x, *terms, *loaded),
        )
        saved.append((x, inner))
    terms, _, loaded = sum_mp(ta, tb, weights(3))
    x, inner, inner_grad, ta, tb = call(
        functools.partial(turn_kernel, 3),
        [full, narrow, hid, half, half],
        scratch,
        (x, *terms, g, *loaded),
    )
    grad_b = g
    halves = [None] * LAYERS
    for layer in (3, 2, 1):
        first = weight_terms(layer, table, inner_grad, inner, x, grad_b)
        terms, halves[layer], loaded = sum_mp(ta, tb, weights(layer - 1), first)
        above, (x, inner) = x, saved[layer - 1]
        if layer == 3:
            (merged,) = call(merge_kernel, [struct((4, 96, C), BF16)], [], halves[3])
            late = over_z(merged)
        if layer > 1:
            g, grad_b, inner_grad, ta, tb = call(
                functools.partial(backward_kernel, layer - 1),
                [struct((ROWS, C), F32), full, hid, half, half],
                [],
                (g, *terms, above, inner, *loaded),
            )
    (merged,) = call(merge_kernel, [struct((4, 192, C), BF16)], [], halves[1] + halves[2])
    later = over_z(merged)
    grad_b, inner_grad, sent_blocks = call(
        final_kernel,
        [full, hid, struct((512, H), BF16)],
        [],
        (me, g, *terms, above, inner, block_go, loaded[1]),
        {0: pltpu.SMEM},
    )
    got = lax.all_to_all(sent_blocks.reshape(PEERS, 16, H), "seq", 0, 0)
    keep, send = weight_terms(0, table, inner_grad, inner, x, grad_b)
    other = swap(send, "seq", 1)
    got, other = together(got, other)
    first = over_chips(add(keep, other))
    piece = struct((ROWS, SHARD), BF16)
    total, one, three, two, gradient = call(
        last_kernel,
        [struct((ROWS, SHARD), F32), piece, piece, piece, struct((ROWS, SHARD), F32)],
        [pltpu.VMEM((ROWS, C), F32)],
        (me, got.reshape(512, H), block_come, loaded[0]),
        {0: pltpu.SMEM},
    )
    for s, mask in ((one, 1), (three, 3), (two, 2)):
        total = total + swap(s, "mp", mask).astype(F32)
    gradient = gradient + slope(inputs.astype(F32)) * total
    own, *sent = call(
        split_kernel,
        [struct((72, C), BF16)] * 4,
        [],
        (along_x, late.reshape(96, C), later.reshape(192, C)),
        {0: pltpu.SMEM},
    )
    parts = [swap(s, "seq", 2 * mask) for mask, s in zip((1, 2, 3), sent)]
    kernel_grad, point_grad = call(
        sums_kernel,
        [struct((LAYERS, 3, 6, C), F32), struct((LAYERS, 6, C), F32)],
        [],
        (first, own, *parts),
    )
    return gradient, kernel_grad, point_grad


def solution(mesh):
    return jax.shard_map(
        shards,
        mesh=mesh,
        in_specs=(P("seq", "mp"), P("seq", "mp"), P(None, None, "mp", None), P(None, "mp", None)),
        out_specs=(
            P("seq", "mp"),
            P(None, None, ("mp", "seq"), None),
            P(None, ("mp", "seq"), None),
        ),
        check_vma=False,
    )
```

time: 265 us -> 228 us (0.86)
  waiting for transfers between devices: 106 us -> 84.9 us
  blocking collectives: 0 us -> 12.2 us
  starting transfers between devices: 64.8 us -> 55.9 us
  other arithmetic: 15.4 us -> 6.53 us
  local copies, waits for them, and re-layouts: 36.7 us -> 28.9 us
  Pallas kernels: 23.4 us -> 20.1 us
    ppermute x43 -> x37, waiting for transfers between devices: 89.3 us -> 71.8 us  [swap(): return lax.ppermute(values, axis, [(i, i ^ mask) for i in range(peers)])]
    unnamed x124 -> x68, local copies, waits for them, and re-layouts: 32.3 us -> 15.9 us
    squeeze x0 -> x14, local copies, waits for them, and re-layouts: none -> 12.9 us  [load(): return (kernels[layer], points[layer])]
    all_to_all x0 -> x1, blocking collectives: none -> 12.2 us  [shards(): got = lax.all_to_all(sent_blocks.reshape(PEERS, 16, H), 'seq', 0, 0)]
    all_to_all x1 -> x0, waiting for transfers between devices: 8.69 us -> none  [shards(): got = lax.all_to_all(sent_blocks.reshape(PEERS, 16, H), 'seq', 0, 0)]
    all_to_all x1 -> x0, starting transfers between devices: 5.24 us -> none  [shards(): got = lax.all_to_all(sent_blocks.reshape(PEERS, 16, H), 'seq', 0, 0)]
    convert_element_type x23 -> x13, other arithmetic: 9.02 us -> 3.93 us  [add(): return (a.astype(F32) + b.astype(F32)).astype(BF16)]
    reduce_scatter x2, waiting for transfers between devices: 0.02 us -> 4.94 us  [over_z(): lax.psum_scatter(values, 'seq', scatter_dimension=0, axis_index_groups=al...]
  transfers between devices with their start and end apart: 48 -> 41, of which waited for: 31 -> 29; matrix products, arithmetic and copies ran while one was open for 6% -> 9% of each run, Pallas kernels for 4% -> 6%
where the time goes in v2:
time: 228 us; the launch traced here: 226 us
  waiting for transfers between devices  84.9 us (37%)
  starting transfers between devices  55.9 us (25%)
  local copies, waits for them, and re-layouts  28.9 us (13%)
  Pallas kernels  20.1 us (9%)
  between operations  14.6 us (6%)
  blocking collectives  12.2 us (5%)
  other arithmetic  6.53 us (3%)
  matrix products  2.87 us (1%)
    ppermute x37, waiting for transfers between devices, swap(): return lax.ppermute(values, axis, [(i, i ^ mask) for i in range(peers)])  71.8 us
    ppermute x37, starting transfers between devices, swap(): return lax.ppermute(values, axis, [(i, i ^ mask) for i in range(peers)])  43.3 us
    pallas_call x16, Pallas kernels, call(): pl.pallas_call(body, out_shape=outs, in_specs=[pl.BlockSpec(memory_space=...  20.1 us
    unnamed x68, local copies, waits for them, and re-layouts  15.9 us
    squeeze x14, local copies, waits for them, and re-layouts, load(): return (kernels[layer], points[layer])  12.9 us
    all_to_all x1, blocking collectives, shards(): got = lax.all_to_all(sent_blocks.reshape(PEERS, 16, H), 'seq', 0, 0)  12.2 us
    all_to_all x1, starting transfers between devices, shards(): got = lax.all_to_all(sent.reshape(PEERS, 8, SHARD), 'seq', 0, 0)  8.25 us
    all_to_all x1, waiting for transfers between devices, shards(): got = lax.all_to_all(sent.reshape(PEERS, 8, SHARD), 'seq', 0, 0)  8.14 us
  transfers between devices with their start and end apart: 41, of which 29 were waited for; matrix products, arithmetic and copies ran while one was open for 9% of the time, Pallas kernels for 6%

profile of v2, /device:TPU:0, one launch (start us, length us, event | category | flops | bytes accessed | tf_op | source)
XLA Modules:
  0.0 226.0 jit_solution(10417784379692494164)
XLA Ops:
  7.2 1.9 fusion.1
  9.1 8.2 %all-to-all-start = ((bf16[32,8,384]{2,1,0:T(8,128)(2,1)}), bf16[32,8,384]{2,1,0:T(8,128)(2,1)S(1)}, u32[]{:S(2)}, u32[]{:S(2)}) async-start(bf16[32,8,384]{2,1,0:T(8,128)(2,1)} %fusion.1), calls=%async_computation | async-start | bytes 393216 | tf_op jit(solution)/shard_map/all_to_all | solution.py:332
  17.4 8.1 %all-to-all-done = bf16[32,8,384]{2,1,0:T(8,128)(2,1)S(1)} async-done(((bf16[32,8,384]{2,1,0:T(8,128)(2,1)}), bf16[32,8,384]{2,1,0:T(8,128)(2,1)S(1)}, u32[]{:S(2)}, u32[]{:S(2)}) %all-to-all-start) | async-done | bytes 196640 | tf_op jit(solution)/shard_map/all_to_all | solution.py:332
  26.5 1.7 collective-permute-start
  28.1 2.2 collective-permute-start.1
  31.0 1.6 slice_bitcast_fusion.6.k_mem
  34.3 4.6 %collective-permute-done.1.three = bf16[256,384]{1,0:T(8,128)(2,1)S(1)} collective-permute-done((bf16[256,384]{1,0:T(8,128)(2,1)S(1)}, bf16[256,384]{1,0:T(8,128)(2,1)S(1)}, u32[]{:S(2)}, u32[]{:S(2)}) %collective-permute-start.1) | collective-permute-done | bytes 196640 | tf_op jit(solution)/shard_map/ppermute | solution.py:34
  38.9 1.5 collective-permute-done.2.two
  42.4 2.2 collective-permute-start.4
  44.5 4.0 %collective-permute-done.3 = bf16[128,768]{1,0:T(8,128)(2,1)S(1)} collective-permute-done((bf16[128,768]{1,0:T(8,128)(2,1)S(1)}, bf16[128,768]{1,0:T(8,128)(2,1)S(1)}, u32[]{:S(2)}, u32[]{:S(2)}) %collective-permute-start.3) | collective-permute-done | bytes 196640 | tf_op jit(solution)/shard_map/ppermute | solution.py:34
  49.8 2.0 collective-permute-start.5
  52.0 1.7 slice_bitcast_fusion.5.k_mem
  54.1 2.7 %collective-permute-done.5.a2 = bf16[128,768]{1,0:T(8,128)(2,1)S(1)} collective-permute-done((bf16[128,768]{1,0:T(8,128)(2,1)S(1)}, bf16[128,768]{1,0:T(8,128)(2,1)S(1)}, u32[]{:S(2)}, u32[]{:S(2)}) %collective-permute-start.5) | collective-permute-done | bytes 196640 | tf_op jit(solution)/shard_map/ppermute | solution.py:34
  59.0 1.4 collective-permute-start.8
  60.4 4.2 %collective-permute-done.7 = bf16[128,768]{1,0:T(8,128)(2,1)S(1)} collective-permute-done((bf16[128,768]{1,0:T(8,128)(2,1)S(1)}, bf16[128,768]{1,0:T(8,128)(2,1)S(1)}, u32[]{:S(2)}, u32[]{:S(2)}) %collective-permute-start.7) | collective-permute-done | bytes 196640 | tf_op jit(solution)/shard_map/ppermute | solution.py:34
  64.6 1.4 collective-permute-done.8
  66.1 1.3 collective-permute-start.9
  67.4 1.9 collective-permute-start.10
  69.4 1.6 slice_bitcast_fusion.4.k_mem
  71.0 2.1 collective-permute-done.9.a2
  73.1 1.6 collective-permute-done.10.b2
  75.9 2.2 collective-permute-start.11
  78.1 1.2 collective-permute-start.12
  79.5 4.3 %collective-permute-done.11 = bf16[128,768]{1,0:T(8,128)(2,1)S(1)} collective-permute-done((bf16[128,768]{1,0:T(8,128)(2,1)S(1)}, bf16[128,768]{1,0:T(8,128)(2,1)S(1)}, u32[]{:S(2)}, u32[]{:S(2)}) %collective-permute-start.11) | collective-permute-done | bytes 196640 | tf_op jit(solution)/shard_map/ppermute | solution.py:34
  83.8 1.2 collective-permute-done.12
  85.0 1.3 collective-permute-start.13
  86.5 1.7 slice_bitcast_fusion.3.k_mem
  88.6 5.3 %collective-permute-done.13.a2 = bf16[128,768]{1,0:T(8,128)(2,1)S(1)} collective-permute-done((bf16[128,768]{1,0:T(8,128)(2,1)S(1)}, bf16[128,768]{1,0:T(8,128)(2,1)S(1)}, u32[]{:S(2)}, u32[]{:S(2)}) %collective-permute-start.13) | collective-permute-done | bytes 196640 | tf_op jit(solution)/shard_map/ppermute | solution.py:34
  93.9 1.6 shard_map.133
  95.6 1.3 collective-permute-start.16
  97.3 1.3 shard_map.134
  98.6 2.6 %collective-permute-done.15 = bf16[128,768]{1,0:T(8,128)(2,1)S(1)} collective-permute-done((bf16[128,768]{1,0:T(8,128)(2,1)S(1)}, bf16[128,768]{1,0:T(8,128)(2,1)S(1)}, u32[]{:S(2)}, u32[]{:S(2)}) %collective-permute-start.15) | collective-permute-done | bytes 196640 | tf_op jit(solution)/shard_map/ppermute | solution.py:34
  101.2 1.5 collective-permute-done.16
  104.0 1.6 slice_bitcast_fusion.2.k_mem
  105.7 4.1 %collective-permute-done.17.a2 = bf16[128,768]{1,0:T(8,128)(2,1)S(1)} collective-permute-done((bf16[128,768]{1,0:T(8,128)(2,1)S(1)}, bf16[128,768]{1,0:T(8,128)(2,1)S(1)}, u32[]{:S(2)}, u32[]{:S(2)}) %collective-permute-start.17) | collective-permute-done | bytes 196640 | tf_op jit(solution)/shard_map/ppermute | solution.py:34
  109.7 1.6 collective-permute-done.18.b2
  111.3 2.0 shard_map.135
  115.0 2.2 collective-permute-start.21
  117.2 1.3 shard_map.142
  118.7 1.3 copy-done.1
  120.9 1.3 shard_map.136
  124.1 2.2 collective-permute-start.22
  127.4 1.7 slice_bitcast_fusion.1.k_mem
  129.5 1.5 collective-permute-done.22.a2
  131.0 3.7 %collective-permute-done.23.b2 = bf16[128,768]{1,0:T(8,128)(2,1)S(1)} collective-permute-done((bf16[128,768]{1,0:T(8,128)(2,1)S(1)}, bf16[128,768]{1,0:T(8,128)(2,1)S(1)}, u32[]{:S(2)}, u32[]{:S(2)}) %collective-permute-start.23) | collective-permute-done | bytes 196640 | tf_op jit(solution)/shard_map/ppermute | solution.py:34
  134.7 1.3 shard_map.137
  137.5 1.3 shard_map.138
  138.8 3.9 %collective-permute-done.25 = bf16[128,768]{1,0:T(8,128)(2,1)S(1)} collective-permute-done((bf16[128,768]{1,0:T(8,128)(2,1)S(1)}, bf16[128,768]{1,0:T(8,128)(2,1)S(1)}, u32[]{:S(2)}, u32[]{:S(2)}) %collective-permute-start.25) | collective-permute-done | bytes 196640 | tf_op jit(solution)/shard_map/ppermute | solution.py:34
  142.7 1.4 collective-permute-done.26
  145.7 1.6 slice_bitcast_fusion.k_mem
  147.4 3.8 %collective-permute-done.27.a2 = bf16[128,768]{1,0:T(8,128)(2,1)S(1)} collective-permute-done((bf16[128,768]{1,0:T(8,128)(2,1)S(1)}, bf16[128,768]{1,0:T(8,128)(2,1)S(1)}, u32[]{:S(2)}, u32[]{:S(2)}) %collective-permute-start.27) | collective-permute-done | bytes 196640 | tf_op jit(solution)/shard_map/ppermute | solution.py:34
  153.7 1.9 shard_map.143
  161.6 1.3 shard_map.140
  163.0 12.2 %all_to_all.15 = bf16[32,16,192]{2,1,0:T(8,128)(2,1)S(1)} all-to-all(bf16[32,16,192]{2,1,0:T(8,128)(2,1)S(1)} %bitcast.41), channel_id=1, replica_groups=mesh['seq'=32,'mp'=4] {'seq'}, dimensions={0} | all-to-all | bytes 393216 | tf_op jit(solution)/shard_map/all_to_all | solution.py:390
  175.2 1.3 add_convert_fusion
  176.5 4.3 %all-to-all-start.2 = ((bf16[16,24,1536]{2,1,0:T(8,128)(2,1)}), bf16[16,24,1536]{2,1,0:T(8,128)(2,1)S(1)}, u32[]{:S(2)}, u32[]{:S(2)}) async-start(bf16[16,24,1536]{2,1,0:T(8,128)(2,1)} %bitcast.44), calls=%async_computation.2 | async-start | bytes 2359296 | tf_op jit(solution)/shard_map/all_to_all | solution.py:297
  181.0 1.6 shard_map.141
  183.2 2.1 collective-permute-start.33
  186.7 4.9 %reduce-scatter.5.cloned.1.call-done = bf16[1,192,1536]{2,1,0:T(8,128)(2,1)} async-done(((bf16[4,192,1536]{2,1,0:T(8,128)(2,1)}), bf16[1,192,1536]{2,1,0:T(8,128)(2,1)}) %reduce-scatter.5.cloned.1.call-update) | async-done | bytes 589840 | tf_op jit(solution)/shard_map/reduce_scatter | solution.py:304
  193.7 5.8 %collective-permute-start.34 = (bf16[72,1536]{1,0:T(8,128)(2,1)S(1)}, bf16[72,1536]{1,0:T(8,128)(2,1)S(1)}, u32[]{:S(2)}, u32[]{:S(2)}) collective-permute-start(bf16[72,1536]{1,0:T(8,128)(2,1)S(1)} %get-tuple-element.230), channel_id=1, source_target_pairs={{0,8},{4,12},{8,0},{12,4},{16,24},{20,28},{24,16},{28,20},{32,40},... | collective-permute-start | bytes 663560 | tf_op jit(solution)/shard_map/ppermute | solution.py:34
  199.6 5.2 %collective-permute-start.35 = (bf16[72,1536]{1,0:T(8,128)(2,1)S(1)}, bf16[72,1536]{1,0:T(8,128)(2,1)S(1)}, u32[]{:S(2)}, u32[]{:S(2)}) collective-permute-start(bf16[72,1536]{1,0:T(8,128)(2,1)S(1)} %get-tuple-element.231), channel_id=1, source_target_pairs={{0,16},{4,20},{8,24},{12,28},{16,0},{20,4},{24,8},{28,12},{32,48},... | collective-permute-start | bytes 663560 | tf_op jit(solution)/shard_map/ppermute | solution.py:34
  204.8 1.8 fusion.14
  206.6 7.8 %collective-permute-done.35.two = bf16[72,1536]{1,0:T(8,128)(2,1)S(1)} collective-permute-done((bf16[72,1536]{1,0:T(8,128)(2,1)S(1)}, bf16[72,1536]{1,0:T(8,128)(2,1)S(1)}, u32[]{:S(2)}, u32[]{:S(2)}) %collective-permute-start.35) | collective-permute-done | bytes 221216 | tf_op jit(solution)/shard_map/ppermute | solution.py:34
  214.5 2.6 %collective-permute-done.36.three = bf16[72,1536]{1,0:T(8,128)(2,1)S(1)} collective-permute-done((bf16[72,1536]{1,0:T(8,128)(2,1)S(1)}, bf16[72,1536]{1,0:T(8,128)(2,1)S(1)}, u32[]{:S(2)}, u32[]{:S(2)}) %collective-permute-start.36) | collective-permute-done | bytes 221216 | tf_op jit(solution)/shard_map/ppermute | solution.py:34
  (141 shorter events, 37.1 us)
Async XLA Ops:
  9.1 16.5 %all-to-all-start = ((bf16[32,8,384]{2,1,0:T(8,128)(2,1)}), bf16[32,8,384]{2,1,0:T(8,128)(2,1)S(1)}, u32[]{:S(2)}, u32[]{:S(2)}) async-start(bf16[32,8,384]{2,1,0:T(8,128)(2,1)} %fusion.1), calls=%async_computation | async-start | bytes 393216 | tf_op jit(solution)/shard_map/all_to_all | solution.py:332
  17.3 169.4 %reduce-scatter.3.cloned.1.call-start = ((), (), s32[]{:S(2)}) async-start(), calls=%async_computation.5 | async-start | bytes 1474560 | tf_op jit(solution)/shard_map/reduce_scatter | solution.py:304
  26.5 7.8 %collective-permute-start = (bf16[256,384]{1,0:T(8,128)(2,1)S(1)}, bf16[256,384]{1,0:T(8,128)(2,1)S(1)}, u32[]{:S(2)}, u32[]{:S(2)}) collective-permute-start(bf16[256,384]{1,0:T(8,128)(2,1)S(1)} %convolution_convert_fusion.own), channel_id=1, source_target_pairs={{0,1},{1,0},{2,3},{3,2},{4,5},{5,4},{6,7},{7,6},{8,9},{9,8},{10,11... | collective-permute-start | bytes 589832 | tf_op jit(solution)/shard_map/ppermute | solution.py:34
  28.1 10.8 %collective-permute-start.1 = (bf16[256,384]{1,0:T(8,128)(2,1)S(1)}, bf16[256,384]{1,0:T(8,128)(2,1)S(1)}, u32[]{:S(2)}, u32[]{:S(2)}) collective-permute-start(bf16[256,384]{1,0:T(8,128)(2,1)S(1)} %convolution_convert_fusion.own), channel_id=1, source_target_pairs={{0,3},{1,2},{2,1},{3,0},{4,7},{5,6},{6,5},{7,4},{8,11},{9,10},{10,... | collective-permute-start | bytes 589832 | tf_op jit(solution)/shard_map/ppermute | solution.py:34
  30.3 10.1 %collective-permute-start.2 = (bf16[256,384]{1,0:T(8,128)(2,1)S(1)}, bf16[256,384]{1,0:T(8,128)(2,1)S(1)}, u32[]{:S(2)}, u32[]{:S(2)}) collective-permute-start(bf16[256,384]{1,0:T(8,128)(2,1)S(1)} %convolution_convert_fusion.own), channel_id=1, source_target_pairs={{0,2},{1,3},{2,0},{3,1},{4,6},{5,7},{6,4},{7,5},{8,10},{9,11},{10,... | collective-permute-start | bytes 589832 | tf_op jit(solution)/shard_map/ppermute | solution.py:34
  42.3 15.4 %copy-start.5 = (bf16[128,1536]{1,0:T(8,128)(2,1)}, bf16[128,1536]{1,0:T(8,128)(2,1)S(1)}, u32[]{:S(2)}) copy-start(bf16[128,1536]{1,0:T(8,128)(2,1)S(1)} %get-tuple-element.127.x) | copy-start | bytes 1179652
  42.3 6.3 %collective-permute-start.3 = (bf16[128,768]{1,0:T(8,128)(2,1)S(1)}, bf16[128,768]{1,0:T(8,128)(2,1)S(1)}, u32[]{:S(2)}, u32[]{:S(2)}) collective-permute-start(bf16[128,768]{1,0:T(8,128)(2,1)S(1)} %get-tuple-element.128), channel_id=1, source_target_pairs={{0,1},{1,0},{2,3},{3,2},{4,5},{5,4},{6,7},{7,6},{8,9},{9,8},{10,11... | collective-permute-start | bytes 589832 | tf_op jit(solution)/shard_map/ppermute | solution.py:34
  42.4 7.4 %collective-permute-start.4 = (bf16[128,768]{1,0:T(8,128)(2,1)S(1)}, bf16[128,768]{1,0:T(8,128)(2,1)S(1)}, u32[]{:S(2)}, u32[]{:S(2)}) collective-permute-start(bf16[128,768]{1,0:T(8,128)(2,1)S(1)} %get-tuple-element.129), channel_id=1, source_target_pairs={{0,3},{1,2},{2,1},{3,0},{4,7},{5,6},{6,5},{7,4},{8,11},{9,10},{10,... | collective-permute-start | bytes 589832 | tf_op jit(solution)/shard_map/ppermute | solution.py:34
  49.8 7.0 %collective-permute-start.5 = (bf16[128,768]{1,0:T(8,128)(2,1)S(1)}, bf16[128,768]{1,0:T(8,128)(2,1)S(1)}, u32[]{:S(2)}, u32[]{:S(2)}) collective-permute-start(bf16[128,768]{1,0:T(8,128)(2,1)S(1)} %add_convert_fusion.12.a), channel_id=1, source_target_pairs={{0,3},{1,2},{2,1},{3,0},{4,7},{5,6},{6,5},{7,4},{8,11},{9,10},{10,... | collective-permute-start | bytes 589832 | tf_op jit(solution)/shard_map/ppermute | solution.py:34
  51.9 2.2 copy-start.25
  51.9 5.7 %collective-permute-start.6 = (bf16[128,768]{1,0:T(8,128)(2,1)S(1)}, bf16[128,768]{1,0:T(8,128)(2,1)S(1)}, u32[]{:S(2)}, u32[]{:S(2)}) collective-permute-start(bf16[128,768]{1,0:T(8,128)(2,1)S(1)} %add_convert_fusion.11.b), channel_id=1, source_target_pairs={{0,1},{1,0},{2,3},{3,2},{4,5},{5,4},{6,7},{7,6},{8,9},{9,8},{10,11... | collective-permute-start | bytes 589832 | tf_op jit(solution)/shard_map/ppermute | solution.py:34
  57.6 2.7 %copy-start.31 = (s32[32]{0:T(128)S(1)}, s32[32]{0:T(128)}, u32[]{:S(2)}) copy-start(s32[32]{0:T(128)} %constant.72.clone) | copy-start | bytes 388
  57.6 2.7 %copy-start.32 = (s32[32]{0:T(128)S(1)}, s32[32]{0:T(128)}, u32[]{:S(2)}) copy-start(s32[32]{0:T(128)} %constant.71.clone) | copy-start | bytes 388
  58.9 12.1 %copy-start.14 = (f32[128,192]{1,0:T(8,128)}, f32[128,192]{1,0:T(8,128)S(1)}, u32[]{:S(2)}) copy-start(f32[128,192]{1,0:T(8,128)S(1)} %get-tuple-element.191.inner) | copy-start | bytes 294916
  58.9 5.7 %collective-permute-start.7 = (bf16[128,768]{1,0:T(8,128)(2,1)S(1)}, bf16[128,768]{1,0:T(8,128)(2,1)S(1)}, u32[]{:S(2)}, u32[]{:S(2)}) collective-permute-start(bf16[128,768]{1,0:T(8,128)(2,1)S(1)} %get-tuple-element.139), channel_id=1, source_target_pairs={{0,1},{1,0},{2,3},{3,2},{4,5},{5,4},{6,7},{7,6},{8,9},{9,8},{10,11... | collective-permute-start | bytes 589832 | tf_op jit(solution)/shard_map/ppermute | solution.py:34
  59.0 7.1 %collective-permute-start.8 = (bf16[128,768]{1,0:T(8,128)(2,1)S(1)}, bf16[128,768]{1,0:T(8,128)(2,1)S(1)}, u32[]{:S(2)}, u32[]{:S(2)}) collective-permute-start(bf16[128,768]{1,0:T(8,128)(2,1)S(1)} %get-tuple-element.140), channel_id=1, source_target_pairs={{0,3},{1,2},{2,1},{3,0},{4,7},{5,6},{6,5},{7,4},{8,11},{9,10},{10,... | collective-permute-start | bytes 589832 | tf_op jit(solution)/shard_map/ppermute | solution.py:34
  66.1 7.0 %collective-permute-start.9 = (bf16[128,768]{1,0:T(8,128)(2,1)S(1)}, bf16[128,768]{1,0:T(8,128)(2,1)S(1)}, u32[]{:S(2)}, u32[]{:S(2)}) collective-permute-start(bf16[128,768]{1,0:T(8,128)(2,1)S(1)} %add_convert_fusion.10.a), channel_id=1, source_target_pairs={{0,3},{1,2},{2,1},{3,0},{4,7},{5,6},{6,5},{7,4},{8,11},{9,10},{10,... | collective-permute-start | bytes 589832 | tf_op jit(solution)/shard_map/ppermute | solution.py:34
  67.4 7.2 %collective-permute-start.10 = (bf16[128,768]{1,0:T(8,128)(2,1)S(1)}, bf16[128,768]{1,0:T(8,128)(2,1)S(1)}, u32[]{:S(2)}, u32[]{:S(2)}) collective-permute-start(bf16[128,768]{1,0:T(8,128)(2,1)S(1)} %add_convert_fusion.9.b), channel_id=1, source_target_pairs={{0,1},{1,0},{2,3},{3,2},{4,5},{5,4},{6,7},{7,6},{8,9},{9,8},{10,11... | collective-permute-start | bytes 589832 | tf_op jit(solution)/shard_map/ppermute | solution.py:34
  74.6 4.7 %copy-start.28 = (s32[32,24]{1,0:T(8,128)S(1)}, s32[32,24]{1,0:T(8,128)}, u32[]{:S(2)}) copy-start(s32[32,24]{1,0:T(8,128)} %constant.76) | copy-start | bytes 9220
  75.9 12.4 %copy-start.16 = (f32[128,192]{1,0:T(8,128)}, f32[128,192]{1,0:T(8,128)S(1)}, u32[]{:S(2)}) copy-start(f32[128,192]{1,0:T(8,128)S(1)} %get-tuple-element.174.inner) | copy-start | bytes 294916
  75.9 7.9 %collective-permute-start.11 = (bf16[128,768]{1,0:T(8,128)(2,1)S(1)}, bf16[128,768]{1,0:T(8,128)(2,1)S(1)}, u32[]{:S(2)}, u32[]{:S(2)}) collective-permute-start(bf16[128,768]{1,0:T(8,128)(2,1)S(1)} %get-tuple-element.150), channel_id=1, source_target_pairs={{0,1},{1,0},{2,3},{3,2},{4,5},{5,4},{6,7},{7,6},{8,9},{9,8},{10,11... | collective-permute-start | bytes 589832 | tf_op jit(solution)/shard_map/ppermute | solution.py:34
  78.1 6.9 %collective-permute-start.12 = (bf16[128,768]{1,0:T(8,128)(2,1)S(1)}, bf16[128,768]{1,0:T(8,128)(2,1)S(1)}, u32[]{:S(2)}, u32[]{:S(2)}) collective-permute-start(bf16[128,768]{1,0:T(8,128)(2,1)S(1)} %get-tuple-element.151), channel_id=1, source_target_pairs={{0,3},{1,2},{2,1},{3,0},{4,7},{5,6},{6,5},{7,4},{8,11},{9,10},{10,... | collective-permute-start | bytes 589832 | tf_op jit(solution)/shard_map/ppermute | solution.py:34
  85.0 8.9 %collective-permute-start.13 = (bf16[128,768]{1,0:T(8,128)(2,1)S(1)}, bf16[128,768]{1,0:T(8,128)(2,1)S(1)}, u32[]{:S(2)}, u32[]{:S(2)}) collective-permute-start(bf16[128,768]{1,0:T(8,128)(2,1)S(1)} %add_convert_fusion.8.a), channel_id=1, source_target_pairs={{0,3},{1,2},{2,1},{3,0},{4,7},{5,6},{6,5},{7,4},{8,11},{9,10},{10,... | collective-permute-start | bytes 589832 | tf_op jit(solution)/shard_map/ppermute | solution.py:34
  86.4 2.2 copy-start.26
  86.4 7.5 %collective-permute-start.14 = (bf16[128,768]{1,0:T(8,128)(2,1)S(1)}, bf16[128,768]{1,0:T(8,128)(2,1)S(1)}, u32[]{:S(2)}, u32[]{:S(2)}) collective-permute-start(bf16[128,768]{1,0:T(8,128)(2,1)S(1)} %add_convert_fusion.7.b), channel_id=1, source_target_pairs={{0,1},{1,0},{2,3},{3,2},{4,5},{5,4},{6,7},{7,6},{8,9},{9,8},{10,11... | collective-permute-start | bytes 589832 | tf_op jit(solution)/shard_map/ppermute | solution.py:34
  95.5 5.7 %collective-permute-start.15 = (bf16[128,768]{1,0:T(8,128)(2,1)S(1)}, bf16[128,768]{1,0:T(8,128)(2,1)S(1)}, u32[]{:S(2)}, u32[]{:S(2)}) collective-permute-start(bf16[128,768]{1,0:T(8,128)(2,1)S(1)} %get-tuple-element.160), channel_id=1, source_target_pairs={{0,1},{1,0},{2,3},{3,2},{4,5},{5,4},{6,7},{7,6},{8,9},{9,8},{10,11... | collective-permute-start | bytes 589832 | tf_op jit(solution)/shard_map/ppermute | solution.py:34
  95.6 7.1 %collective-permute-start.16 = (bf16[128,768]{1,0:T(8,128)(2,1)S(1)}, bf16[128,768]{1,0:T(8,128)(2,1)S(1)}, u32[]{:S(2)}, u32[]{:S(2)}) collective-permute-start(bf16[128,768]{1,0:T(8,128)(2,1)S(1)} %get-tuple-element.161), channel_id=1, source_target_pairs={{0,3},{1,2},{2,1},{3,0},{4,7},{5,6},{6,5},{7,4},{8,11},{9,10},{10,... | collective-permute-start | bytes 589832 | tf_op jit(solution)/shard_map/ppermute | solution.py:34
  97.3 5.5 %copy-start = (bf16[768,768]{1,0:T(8,128)(2,1)}, bf16[768,768]{1,0:T(8,128)(2,1)S(1)}, u32[]{:S(2)}) copy-start(bf16[768,768]{1,0:T(8,128)(2,1)S(1)} %fusion.table) | copy-start | bytes 3538948
  102.8 7.0 %collective-permute-start.17 = (bf16[128,768]{1,0:T(8,128)(2,1)S(1)}, bf16[128,768]{1,0:T(8,128)(2,1)S(1)}, u32[]{:S(2)}, u32[]{:S(2)}) collective-permute-start(bf16[128,768]{1,0:T(8,128)(2,1)S(1)} %add_convert_fusion.6.a), channel_id=1, source_target_pairs={{0,3},{1,2},{2,1},{3,0},{4,7},{5,6},{6,5},{7,4},{8,11},{9,10},{10,... | collective-permute-start | bytes 589832 | tf_op jit(solution)/shard_map/ppermute | solution.py:34
  103.9 7.5 %collective-permute-start.19 = (bf16[384,1536]{1,0:T(8,128)(2,1)S(1)}, bf16[384,1536]{1,0:T(8,128)(2,1)S(1)}, u32[]{:S(2)}, u32[]{:S(2)}) collective-permute-start(bf16[384,1536]{1,0:T(8,128)(2,1)S(1)} %get-tuple-element.169), channel_id=1, source_target_pairs={{0,4},{4,0},{8,12},{12,8},{16,20},{20,16},{24,28},{28,24},{32,36},... | collective-permute-start | bytes 3538952 | tf_op jit(solution)/shard_map/ppermute | solution.py:34
  103.9 7.4 %copy-start.17 = (f32[128,192]{1,0:T(8,128)S(1)}, f32[128,192]{1,0:T(8,128)}, u32[]{:S(2)}) copy-start(f32[128,192]{1,0:T(8,128)} %copy-done.16) | copy-start | bytes 294916
  103.9 7.4 %collective-permute-start.18 = (bf16[128,768]{1,0:T(8,128)(2,1)S(1)}, bf16[128,768]{1,0:T(8,128)(2,1)S(1)}, u32[]{:S(2)}, u32[]{:S(2)}) collective-permute-start(bf16[128,768]{1,0:T(8,128)(2,1)S(1)} %add_convert_fusion.5.b), channel_id=1, source_target_pairs={{0,1},{1,0},{2,3},{3,2},{4,5},{5,4},{6,7},{7,6},{8,9},{9,8},{10,11... | collective-permute-start | bytes 589832 | tf_op jit(solution)/shard_map/ppermute | solution.py:34
  114.7 7.5 %collective-permute-start.20 = (bf16[128,768]{1,0:T(8,128)(2,1)}, bf16[128,768]{1,0:T(8,128)(2,1)}, u32[]{:S(2)}, u32[]{:S(2)}) collective-permute-start(bf16[128,768]{1,0:T(8,128)(2,1)} %get-tuple-element.178), channel_id=1, source_target_pairs={{0,1},{1,0},{2,3},{3,2},{4,5},{5,4},{6,7},{7,6},{8,9},{9,8},{10,11... | collective-permute-start | bytes 589832 | tf_op jit(solution)/shard_map/ppermute | solution.py:34
  115.0 3.6 %copy-start.18 = (f32[128,192]{1,0:T(8,128)S(1)}, f32[128,192]{1,0:T(8,128)}, u32[]{:S(2)}) copy-start(f32[128,192]{1,0:T(8,128)} %copy-done.16) | copy-start | bytes 294916
  115.0 3.6 %copy-start.24 = (bf16[128,192]{1,0:T(8,128)(2,1)S(1)}, bf16[128,192]{1,0:T(8,128)(2,1)}, u32[]{:S(2)}) copy-start(bf16[128,192]{1,0:T(8,128)(2,1)} %copy-done.23) | copy-start | bytes 147460
  115.0 7.9 %collective-permute-start.21 = (bf16[128,768]{1,0:T(8,128)(2,1)}, bf16[128,768]{1,0:T(8,128)(2,1)S(1)}, u32[]{:S(2)}, u32[]{:S(2)}) collective-permute-start(bf16[128,768]{1,0:T(8,128)(2,1)} %get-tuple-element.179), channel_id=1, source_target_pairs={{0,3},{1,2},{2,1},{3,0},{4,7},{5,6},{6,5},{7,4},{8,11},{9,10},{10,... | collective-permute-start | bytes 589832 | tf_op jit(solution)/shard_map/ppermute | solution.py:34
  118.6 73.1 %reduce-scatter.5.cloned.1.call-start = ((), (), s32[]{:S(2)}) async-start(), calls=%async_computation.6 | async-start | bytes 2949120 | tf_op jit(solution)/shard_map/reduce_scatter | solution.py:304
  118.6 1.3 copy-start.1
  119.9 1.0 copy-start.21
  124.1 7.0 %collective-permute-start.22 = (bf16[128,768]{1,0:T(8,128)(2,1)S(1)}, bf16[128,768]{1,0:T(8,128)(2,1)S(1)}, u32[]{:S(2)}, u32[]{:S(2)}) collective-permute-start(bf16[128,768]{1,0:T(8,128)(2,1)S(1)} %add_convert_fusion.4.a), channel_id=1, source_target_pairs={{0,3},{1,2},{2,1},{3,0},{4,7},{5,6},{6,5},{7,4},{8,11},{9,10},{10,... | collective-permute-start | bytes 589832 | tf_op jit(solution)/shard_map/ppermute | solution.py:34
  126.3 8.4 %collective-permute-start.24 = (bf16[384,1536]{1,0:T(8,128)(2,1)S(1)}, bf16[384,1536]{1,0:T(8,128)(2,1)S(1)}, u32[]{:S(2)}, u32[]{:S(2)}) collective-permute-start(bf16[384,1536]{1,0:T(8,128)(2,1)S(1)} %get-tuple-element.186), channel_id=1, source_target_pairs={{0,4},{4,0},{8,12},{12,8},{16,20},{20,16},{24,28},{28,24},{32,36},... | collective-permute-start | bytes 3538952 | tf_op jit(solution)/shard_map/ppermute | solution.py:34
  127.3 2.2 copy-start.27
  127.3 7.4 %copy-start.15 = (f32[128,192]{1,0:T(8,128)S(1)}, f32[128,192]{1,0:T(8,128)}, u32[]{:S(2)}) copy-start(f32[128,192]{1,0:T(8,128)} %copy-done.14) | copy-start | bytes 294916
  127.3 7.4 %collective-permute-start.23 = (bf16[128,768]{1,0:T(8,128)(2,1)S(1)}, bf16[128,768]{1,0:T(8,128)(2,1)S(1)}, u32[]{:S(2)}, u32[]{:S(2)}) collective-permute-start(bf16[128,768]{1,0:T(8,128)(2,1)S(1)} %add_convert_fusion.3.b), channel_id=1, source_target_pairs={{0,1},{1,0},{2,3},{3,2},{4,5},{5,4},{6,7},{7,6},{8,9},{9,8},{10,11... | collective-permute-start | bytes 589832 | tf_op jit(solution)/shard_map/ppermute | solution.py:34
  136.0 8.2 %copy-start.3 = (f32[128,1536]{1,0:T(8,128)}, f32[128,1536]{1,0:T(8,128)S(1)}, u32[]{:S(2)}) copy-start(f32[128,1536]{1,0:T(8,128)S(1)} %get-tuple-element.194.g) | copy-start | bytes 2359300
  136.0 6.7 %collective-permute-start.25 = (bf16[128,768]{1,0:T(8,128)(2,1)S(1)}, bf16[128,768]{1,0:T(8,128)(2,1)S(1)}, u32[]{:S(2)}, u32[]{:S(2)}) collective-permute-start(bf16[128,768]{1,0:T(8,128)(2,1)S(1)} %get-tuple-element.195), channel_id=1, source_target_pairs={{0,1},{1,0},{2,3},{3,2},{4,5},{5,4},{6,7},{7,6},{8,9},{9,8},{10,11... | collective-permute-start | bytes 589832 | tf_op jit(solution)/shard_map/ppermute | solution.py:34
  136.4 7.8 %collective-permute-start.26 = (bf16[128,768]{1,0:T(8,128)(2,1)S(1)}, bf16[128,768]{1,0:T(8,128)(2,1)S(1)}, u32[]{:S(2)}, u32[]{:S(2)}) collective-permute-start(bf16[128,768]{1,0:T(8,128)(2,1)S(1)} %get-tuple-element.196), channel_id=1, source_target_pairs={{0,3},{1,2},{2,1},{3,0},{4,7},{5,6},{6,5},{7,4},{8,11},{9,10},{10,... | collective-permute-start | bytes 589832 | tf_op jit(solution)/shard_map/ppermute | solution.py:34
  144.2 7.0 %collective-permute-start.27 = (bf16[128,768]{1,0:T(8,128)(2,1)S(1)}, bf16[128,768]{1,0:T(8,128)(2,1)S(1)}, u32[]{:S(2)}, u32[]{:S(2)}) collective-permute-start(bf16[128,768]{1,0:T(8,128)(2,1)S(1)} %add_convert_fusion.2.a), channel_id=1, source_target_pairs={{0,3},{1,2},{2,1},{3,0},{4,7},{5,6},{6,5},{7,4},{8,11},{9,10},{10,... | collective-permute-start | bytes 589832 | tf_op jit(solution)/shard_map/ppermute | solution.py:34
  145.4 8.4 %collective-permute-start.29 = (bf16[384,1536]{1,0:T(8,128)(2,1)S(1)}, bf16[384,1536]{1,0:T(8,128)(2,1)S(1)}, u32[]{:S(2)}, u32[]{:S(2)}) collective-permute-start(bf16[384,1536]{1,0:T(8,128)(2,1)S(1)} %get-tuple-element.203), channel_id=1, source_target_pairs={{0,4},{4,0},{8,12},{12,8},{16,20},{20,16},{24,28},{28,24},{32,36},... | collective-permute-start | bytes 3538952 | tf_op jit(solution)/shard_map/ppermute | solution.py:34
  145.4 7.6 %collective-permute-start.28 = (bf16[128,768]{1,0:T(8,128)(2,1)S(1)}, bf16[128,768]{1,0:T(8,128)(2,1)S(1)}, u32[]{:S(2)}, u32[]{:S(2)}) collective-permute-start(bf16[128,768]{1,0:T(8,128)(2,1)S(1)} %add_convert_fusion.1.b), channel_id=1, source_target_pairs={{0,1},{1,0},{2,3},{3,2},{4,5},{5,4},{6,7},{7,6},{8,9},{9,8},{10,11... | collective-permute-start | bytes 589832 | tf_op jit(solution)/shard_map/ppermute | solution.py:34
  155.6 5.9 %copy-start.6 = (bf16[128,1536]{1,0:T(8,128)(2,1)S(1)}, bf16[128,1536]{1,0:T(8,128)(2,1)}, u32[]{:S(2)}) copy-start(bf16[128,1536]{1,0:T(8,128)(2,1)} %copy-done.5) | copy-start | bytes 1179652
  156.3 5.3 %copy-start.2 = (bf16[768,768]{1,0:T(8,128)(2,1)S(1)}, bf16[768,768]{1,0:T(8,128)(2,1)}, u32[]{:S(2)}) copy-start(bf16[768,768]{1,0:T(8,128)(2,1)} %copy-done) | copy-start | bytes 3538948
  156.5 1.2 copy-start.4
  163.0 12.3 %collective-permute-start.30 = (bf16[384,1536]{1,0:T(8,128)(2,1)S(1)}, bf16[384,1536]{1,0:T(8,128)(2,1)S(1)}, u32[]{:S(2)}, u32[]{:S(2)}) collective-permute-start(bf16[384,1536]{1,0:T(8,128)(2,1)S(1)} %get-tuple-element.213), channel_id=1, source_target_pairs={{0,4},{4,0},{8,12},{12,8},{16,20},{20,16},{24,28},{28,24},{32,36},... | collective-permute-start | bytes 3538952 | tf_op jit(solution)/shard_map/ppermute | solution.py:34
  176.5 4.3 %copy-start.29 = (s32[448]{0:T(512)S(1)}, s32[448]{0:T(512)}, u32[]{:S(2)}) copy-start(s32[448]{0:T(512)} %constant.75.clone) | copy-start | bytes 5380
  176.5 30.1 %all-to-all-start.2 = ((bf16[16,24,1536]{2,1,0:T(8,128)(2,1)}), bf16[16,24,1536]{2,1,0:T(8,128)(2,1)S(1)}, u32[]{:S(2)}, u32[]{:S(2)}) async-start(bf16[16,24,1536]{2,1,0:T(8,128)(2,1)} %bitcast.44), calls=%async_computation.2 | async-start | bytes 2359296 | tf_op jit(solution)/shard_map/all_to_all | solution.py:297
  183.2 21.6 %collective-permute-start.33 = (bf16[128,384]{1,0:T(8,128)(2,1)}, bf16[128,384]{1,0:T(8,128)(2,1)S(1)}, u32[]{:S(2)}, u32[]{:S(2)}) collective-permute-start(bf16[128,384]{1,0:T(8,128)(2,1)} %get-tuple-element.220), channel_id=1, source_target_pairs={{0,2},{1,3},{2,0},{3,1},{4,6},{5,7},{6,4},{7,5},{8,10},{9,11},{10,... | collective-permute-start | bytes 294920 | tf_op jit(solution)/shard_map/ppermute | solution.py:34
  185.3 19.4 %collective-permute-start.32 = (bf16[128,384]{1,0:T(8,128)(2,1)}, bf16[128,384]{1,0:T(8,128)(2,1)S(1)}, u32[]{:S(2)}, u32[]{:S(2)}) collective-permute-start(bf16[128,384]{1,0:T(8,128)(2,1)} %get-tuple-element.219), channel_id=1, source_target_pairs={{0,3},{1,2},{2,1},{3,0},{4,7},{5,6},{6,5},{7,4},{8,11},{9,10},{10,... | collective-permute-start | bytes 294920 | tf_op jit(solution)/shard_map/ppermute | solution.py:34
  186.2 18.6 %collective-permute-start.31 = (bf16[128,384]{1,0:T(8,128)(2,1)S(1)}, bf16[128,384]{1,0:T(8,128)(2,1)S(1)}, u32[]{:S(2)}, u32[]{:S(2)}) collective-permute-start(bf16[128,384]{1,0:T(8,128)(2,1)S(1)} %get-tuple-element.218), channel_id=1, source_target_pairs={{0,1},{1,0},{2,3},{3,2},{4,5},{5,4},{6,7},{7,6},{8,9},{9,8},{10,11... | collective-permute-start | bytes 294920 | tf_op jit(solution)/shard_map/ppermute | solution.py:34
  191.6 1.1 copy-start.19
  192.7 1.0 copy-start.22
  193.7 12.9 %collective-permute-start.34 = (bf16[72,1536]{1,0:T(8,128)(2,1)S(1)}, bf16[72,1536]{1,0:T(8,128)(2,1)S(1)}, u32[]{:S(2)}, u32[]{:S(2)}) collective-permute-start(bf16[72,1536]{1,0:T(8,128)(2,1)S(1)} %get-tuple-element.230), channel_id=1, source_target_pairs={{0,8},{4,12},{8,0},{12,4},{16,24},{20,28},{24,16},{28,20},{32,40},... | collective-permute-start | bytes 663560 | tf_op jit(solution)/shard_map/ppermute | solution.py:34
  199.6 14.9 %collective-permute-start.35 = (bf16[72,1536]{1,0:T(8,128)(2,1)S(1)}, bf16[72,1536]{1,0:T(8,128)(2,1)S(1)}, u32[]{:S(2)}, u32[]{:S(2)}) collective-permute-start(bf16[72,1536]{1,0:T(8,128)(2,1)S(1)} %get-tuple-element.231), channel_id=1, source_target_pairs={{0,16},{4,20},{8,24},{12,28},{16,0},{20,4},{24,8},{28,12},{32,48},... | collective-permute-start | bytes 663560 | tf_op jit(solution)/shard_map/ppermute | solution.py:34
  204.8 12.3 %collective-permute-start.36 = (bf16[72,1536]{1,0:T(8,128)(2,1)S(1)}, bf16[72,1536]{1,0:T(8,128)(2,1)S(1)}, u32[]{:S(2)}, u32[]{:S(2)}) collective-permute-start(bf16[72,1536]{1,0:T(8,128)(2,1)S(1)} %get-tuple-element.232), channel_id=1, source_target_pairs={{0,24},{4,28},{8,16},{12,20},{16,8},{20,12},{24,0},{28,4},{32,56},... | collective-permute-start | bytes 663560 | tf_op jit(solution)/shard_map/ppermute | solution.py:34
  (10 other events, 7.5 us)
Sparse Core Ops, SparseCore 0:
  118.7 20.3 reduce-scatter.2
  155.8 35.7 reduce-scatter.4

commit v3 on v2

--- a/solution.py
+++ b/solution.py
@@ -17,6 +17,8 @@
 PEERS = 32
 BF16 = jnp.bfloat16
 F32 = jnp.float32
+ORDER = (0, 3, 1, 2)
+X, Z = 2, 8
 ROOT = float(np.sqrt(2.0 / np.pi))
 CUBE = 0.044715
 
@@ -214,38 +216,32 @@
     return call(body, outs, [], (inner_grad, inner, x, grad_b, table), flops=8e8)
 
 
-def merge_kernel(*refs):
-    out = refs[-1]
-    for layer in range(len(refs) // 2):
-        a, b = refs[2 * layer], refs[2 * layer + 1]
-        for z in range(4):
-            rows = slice(96 * z, 96 * z + 96)
-            out[z, 96 * layer : 96 * layer + 96] = add(a[rows], b[rows])
-
-
-def split_kernel(me, *refs):
-    parts, outs = refs[:-4], refs[-4:]
-    for mask, out in enumerate(outs):
-        at = me[0] ^ mask
-        row = 0
-        for part in parts:
-            for layer in range(part.shape[0] // 96):
-                rows = pl.ds(pl.multiple_of(96 * layer + 24 * at, 8), 24)
-                out[row : row + 24] = part[rows]
-                row += 24
-
-
-def sums_kernel(first, own, one, two, three, kernel_out, point_out):
+def merge_kernel(kept, other, *outs):
+    size = outs[0].shape[0]
+    for number, out in enumerate(outs):
+        rows = slice(size * number, size * number + size)
+        out[...] = add(kept[rows], other[rows])
+
+
+def merge(kept, other, count):
+    return call(
+        merge_kernel, [struct((384 // count, C), BF16)] * count, [], (kept, other), flops=1e7
+    )
+
+
+def sums_kernel(first, kept, come, late_kept, late_come, kernel_out, point_out):
     total = first[0].astype(F32)
     for i in range(1, 16):
         total = total + first[i].astype(F32)
-    late = own[...].astype(F32)
-    for ref in (one, two, three):
-        late = late + ref[...].astype(F32)
-    for layer, values in enumerate((total, late[24:48], late[48:], late[:24])):
-        for k in range(3):
-            kernel_out[layer, k] = values[6 * k : 6 * k + 6]
-        point_out[layer] = values[18:]
+    second = kept[...].astype(F32) + come[...].astype(F32)
+    late = late_kept[...].astype(F32) + late_come[...].astype(F32)
+    layers = (total, second, late[:24], late[24:])
+    for row in range(24):
+        values = jnp.concatenate([v[row : row + 1] for v in layers], axis=0)
+        if row < 18:
+            kernel_out[row // 6, row % 6] = values
+        else:
+            point_out[row - 18] = values
 
 
 def table_of(source, columns):
@@ -258,15 +254,22 @@
 def by_source(blocks):
     column = np.arange(768)
     row = column % 24
-    fixed = jnp.asarray(row // 6 * H + row % 6, jnp.int32)
-    (source,) = together(fixed + 6 * jnp.repeat(blocks, 24))
+    (source,) = together(jnp.asarray(row // 6 * H + row % 6, jnp.int32) + 6 * blocks)
     return (lax.broadcasted_iota(jnp.int32, (768, 768), 0) == source[None]).astype(BF16)
 
 
 def absolute_order():
     core = lax.axis_index("seq") % 2
-    block = np.arange(32)
-    return by_source(2 * (block % 16) + (core ^ jnp.asarray(block // 16, jnp.int32)))
+    block = np.arange(768) // 24
+    return by_source(
+        jnp.asarray(2 * (block % 16), jnp.int32) + (core ^ jnp.asarray(block // 16, jnp.int32))
+    )
+
+
+def relative_order(outer, inner):
+    me = lax.axis_index("seq")
+    masks = [c + outer * i + inner * j for c in (0, 1) for i in ORDER for j in ORDER]
+    return by_source(me ^ jnp.asarray(np.repeat(masks, 24), jnp.int32))
 
 
 def block_to_residue():
@@ -292,6 +295,11 @@
     return table_of(go, 384), table_of(come, 512)
 
 
+def halved(kept, come):
+    rows = kept.shape[0] // 2
+    return add(kept[:rows], come[:rows]), add(kept[rows:], come[rows:])
+
+
 def over_chips(values):
     groups = [[2 * i + core for i in range(PEERS // 2)] for core in (0, 1)]
     return lax.all_to_all(
@@ -299,26 +307,16 @@
     )
 
 
-def over_z(values):
-    along_z = [[8 * i + j for i in range(4)] for j in range(8)]
-    got = lax.psum_scatter(values, "seq", scatter_dimension=0, axis_index_groups=along_z)
-    return got
-
-
-def sum_mp(a, b, load, first=()):
+def sum_mp(a, b, load, first=(), second=()):
     a1, b1, *first = together(swap(a, "mp", 1), swap(b, "mp", 3), *first)
     a, b = add(a, a1), add(b, b1)
-    a2, b2 = swap(a, "mp", 3), swap(b, "mp", 1)
-    sent = [swap(s, "seq", 1) for s in first[1:]]
     loaded = load(a)
-    a2, b2, *rest = together(a2, b2, *sent, *loaded)
-    kept = [*first[:1], *rest[: len(sent)]]
-    return (a, b, a2, b2), kept, rest[len(sent) :]
+    a2, b2, *rest = together(swap(a, "mp", 3), swap(b, "mp", 1), *second, *loaded)
+    return (a, b, a2, b2), rest[len(second) :], first, rest[: len(second)]
 
 
 def shards(inputs, cotangent, conv_kernels, point_weights):
     me = lax.axis_index("mp").astype(jnp.int32)[None]
-    along_x = (lax.axis_index("seq") // 2 % 4).astype(jnp.int32)[None]
 
     def weights(layer):
         def load(after):
@@ -344,10 +342,11 @@
         {0: pltpu.SMEM},
     )
     saved = [(x, inner)]
-    table = absolute_order()
+    tables = {2: relative_order(Z, X), 1: relative_order(X, Z), 0: absolute_order()}
+    tables[3] = tables[2]
     block_go, block_come = residue_to_block()
     for layer in (1, 2):
-        terms, _, loaded = sum_mp(ta, tb, weights(layer))
+        terms, loaded, _, _ = sum_mp(ta, tb, weights(layer))
         x, inner, ta, tb = call(
             functools.partial(forward_kernel, layer),
             [full, narrow, half, half],
@@ -355,7 +354,7 @@
             (x, *terms, *loaded),
         )
         saved.append((x, inner))
-    terms, _, loaded = sum_mp(ta, tb, weights(3))
+    terms, loaded, _, _ = sum_mp(ta, tb, weights(3))
     x, inner, inner_grad, ta, tb = call(
         functools.partial(turn_kernel, 3),
         [full, narrow, hid, half, half],
@@ -363,14 +362,24 @@
         (x, *terms, g, *loaded),
     )
     grad_b = g
-    halves = [None] * LAYERS
     for layer in (3, 2, 1):
-        first = weight_terms(layer, table, inner_grad, inner, x, grad_b)
-        terms, halves[layer], loaded = sum_mp(ta, tb, weights(layer - 1), first)
+        keep, send = weight_terms(layer, tables[layer], inner_grad, inner, x, grad_b)
+        first, second = [keep], [swap(send, "seq", 1)]
+        if layer == 1:
+            three_kept, three_sent = halved(three_kept, three_got)
+            second += [swap(three_sent, "seq", 24), swap(two_sent, "seq", 8)]
+        if layer == 2:
+            second += [swap(three_sent, "seq", 8)]
+        terms, loaded, (keep,), (other, *rest) = sum_mp(ta, tb, weights(layer - 1), first, second)
+        kept, sent = merge(keep, other, 2)
+        if layer == 3:
+            three_kept, three_sent = kept, sent
+        if layer == 2:
+            (three_got,) = rest
+            two_kept, two_sent = kept, sent
+        if layer == 1:
+            three_got, two_got = rest
         above, (x, inner) = x, saved[layer - 1]
-        if layer == 3:
-            (merged,) = call(merge_kernel, [struct((4, 96, C), BF16)], [], halves[3])
-            late = over_z(merged)
         if layer > 1:
             g, grad_b, inner_grad, ta, tb = call(
                 functools.partial(backward_kernel, layer - 1),
@@ -378,8 +387,9 @@
                 [],
                 (g, *terms, above, inner, *loaded),
             )
-    (merged,) = call(merge_kernel, [struct((4, 192, C), BF16)], [], halves[1] + halves[2])
-    later = over_z(merged)
+    two_kept, two_sent = halved(two_kept, two_got)
+    a, kept, sent, two_kept, two_sent = together(terms[0], kept, sent, two_kept, two_sent)
+    terms = (a, *terms[1:])
     grad_b, inner_grad, sent_blocks = call(
         final_kernel,
         [full, hid, struct((512, H), BF16)],
@@ -388,10 +398,24 @@
         {0: pltpu.SMEM},
     )
     got = lax.all_to_all(sent_blocks.reshape(PEERS, 16, H), "seq", 0, 0)
-    keep, send = weight_terms(0, table, inner_grad, inner, x, grad_b)
-    other = swap(send, "seq", 1)
-    got, other = together(got, other)
-    first = over_chips(add(keep, other))
+    keep, send = weight_terms(0, tables[0], inner_grad, inner, x, grad_b)
+    (first,) = merge(keep, swap(send, "seq", 1), 1)
+    got, first, come, two_got = together(
+        got, first, swap(sent, "seq", X), swap(two_sent, "seq", 3 * Z)
+    )
+    first = over_chips(first)
+    kept, sent = halved(kept, come)
+    come = swap(sent, "seq", 3 * X)
+    late = [halved(two_kept, two_got), halved(three_kept, three_got)]
+    late_kept, late_sent = (jnp.concatenate(parts, axis=0) for parts in zip(*late))
+    got, late_come = together(got, swap(late_sent, "seq", X))
+    late_kept, late_sent = (
+        jnp.concatenate(
+            [add(late_kept[n : n + 24], late_come[n : n + 24]) for n in (at, at + 48)], axis=0
+        )
+        for at in (0, 24)
+    )
+    late_come = swap(late_sent, "seq", 3 * X)
     piece = struct((ROWS, SHARD), BF16)
     total, one, three, two, gradient = call(
         last_kernel,
@@ -400,24 +424,22 @@
         (me, got.reshape(512, H), block_come, loaded[0]),
         {0: pltpu.SMEM},
     )
-    for s, mask in ((one, 1), (three, 3), (two, 2)):
-        total = total + swap(s, "mp", mask).astype(F32)
+    got = [swap(s, "mp", mask) for s, mask in ((one, 1), (three, 3), (two, 2))]
+    for s in got:
+        total = total + s.astype(F32)
     gradient = gradient + slope(inputs.astype(F32)) * total
-    own, *sent = call(
-        split_kernel,
-        [struct((72, C), BF16)] * 4,
-        [],
-        (along_x, late.reshape(96, C), later.reshape(192, C)),
-        {0: pltpu.SMEM},
-    )
-    parts = [swap(s, "seq", 2 * mask) for mask, s in zip((1, 2, 3), sent)]
+    kept, sent = halved(kept, come)
+    come = swap(sent, "seq", Z)
+    kept, sent = halved(kept, come)
+    come = swap(sent, "seq", 3 * Z)
     kernel_grad, point_grad = call(
         sums_kernel,
-        [struct((LAYERS, 3, 6, C), F32), struct((LAYERS, 6, C), F32)],
+        [struct((3, 6, LAYERS, C), F32), struct((6, LAYERS, C), F32)],
         [],
-        (first, own, *parts),
-    )
-    return gradient, kernel_grad, point_grad
+        (first, kept, come, late_kept, late_come),
+        flops=1e7,
+    )
+    return gradient, kernel_grad.transpose(2, 0, 1, 3), point_grad.transpose(1, 0, 2)
 
 
 def solution(mesh):

time: 228 us -> 202 us (0.89)
  local copies, waits for them, and re-layouts: 28.9 us -> 4.52 us
  between operations: 14.6 us -> 1.16 us
  blocking collectives: 12.2 us -> 0 us
  starting transfers between devices: 55.9 us -> 66.1 us
  other arithmetic: 6.53 us -> 14.5 us
  waiting for transfers between devices: 84.9 us -> 88.8 us
  Pallas kernels: 20.1 us -> 22.4 us
    unnamed x68 -> x28, local copies, waits for them, and re-layouts: 15.9 us -> 0.75 us
    all_to_all x1 -> x0, blocking collectives: 12.2 us -> none  [shards(): got = lax.all_to_all(sent_blocks.reshape(PEERS, 16, H), 'seq', 0, 0)]
    squeeze x14, local copies, waits for them, and re-layouts: 12.9 us -> 3.77 us  [load(): return (kernels[layer], points[layer])]
    all_to_all x0 -> x1, waiting for transfers between devices: none -> 6.77 us  [shards(): got = lax.all_to_all(sent_blocks.reshape(PEERS, 16, H), 'seq', 0, 0)]
    convert_element_type x13 -> x20, other arithmetic: 3.93 us -> 10.5 us  [add(): return (a.astype(F32) + b.astype(F32)).astype(BF16)]
    all_to_all x0 -> x1, starting transfers between devices: none -> 5.56 us  [shards(): got = lax.all_to_all(sent_blocks.reshape(PEERS, 16, H), 'seq', 0, 0)]
    ppermute x37 -> x44, starting transfers between devices: 43.3 us -> 48.5 us  [swap(): return lax.ppermute(values, axis, [(i, i ^ mask) for i in range(peers)])]
    reduce_scatter x2 -> x0, waiting for transfers between devices: 4.94 us -> none  [over_z(): lax.psum_scatter(values, 'seq', scatter_dimension=0, axis_index_groups=al...]
  transfers between devices with their start and end apart: 41 -> 47, of which waited for: 29 -> 30; matrix products, arithmetic and copies ran while one was open for 9% -> 7% of each run, Pallas kernels for 6% -> 5%
where the time goes in v3:
time: 202 us; the launch traced here: 201 us
  waiting for transfers between devices  88.8 us (44%)
  starting transfers between devices  66.1 us (33%)
  Pallas kernels  22.4 us (11%)
  other arithmetic  14.5 us (7%)
  local copies, waits for them, and re-layouts  4.52 us (2%)
  matrix products  3.02 us (1%)
    ppermute x44, waiting for transfers between devices, swap(): return lax.ppermute(values, axis, [(i, i ^ mask) for i in range(peers)])  73.9 us
    ppermute x44, starting transfers between devices, swap(): return lax.ppermute(values, axis, [(i, i ^ mask) for i in range(peers)])  48.5 us
    pallas_call x17, Pallas kernels, call(): pl.pallas_call(body, out_shape=outs, in_specs=[pl.BlockSpec(memory_space=...  22.4 us
    convert_element_type x20, other arithmetic, add(): return (a.astype(F32) + b.astype(F32)).astype(BF16)  10.5 us
    all_to_all x1, starting transfers between devices, shards(): got = lax.all_to_all(sent.reshape(PEERS, 8, SHARD), 'seq', 0, 0)  8.25 us
    all_to_all x1, waiting for transfers between devices, shards(): got = lax.all_to_all(sent.reshape(PEERS, 8, SHARD), 'seq', 0, 0)  8.18 us
    all_to_all x1, waiting for transfers between devices, shards(): got = lax.all_to_all(sent_blocks.reshape(PEERS, 16, H), 'seq', 0, 0)  6.77 us
    all_to_all x1, starting transfers between devices, shards(): got = lax.all_to_all(sent_blocks.reshape(PEERS, 16, H), 'seq', 0, 0)  5.56 us
  transfers between devices with their start and end apart: 47, of which 30 were waited for; matrix products, arithmetic and copies ran while one was open for 7% of the time, Pallas kernels for 5%

profile of v3, /device:TPU:0, one launch (start us, length us, event | category | flops | bytes accessed | tf_op | source)
XLA Modules:
  0.0 200.6 jit_solution(5163095947489769018)
XLA Ops:
  0.6 2.1 %fusion.3 = bf16[32,8,384]{2,1,0:T(8,128)(2,1)} fusion(bf16[128,384]{1,0:T(8,128)(2,1)} %param.16, bf16[128,384]{1,0:T(8,128)(2,1)} %param.15, s32[256]{0:T(256)} %constant.52.clone), kind=kOutput, calls=%fused_computation.15 | convolution fusion | flops 50888704 | bytes 394240 | tf_op jit(solution)/shard_map/dot_general | solution.py:31
  2.7 8.2 %all-to-all-start = ((bf16[32,8,384]{2,1,0:T(8,128)(2,1)}), bf16[32,8,384]{2,1,0:T(8,128)(2,1)S(1)}, u32[]{:S(2)}, u32[]{:S(2)}) async-start(bf16[32,8,384]{2,1,0:T(8,128)(2,1)} %fusion.3), calls=%async_computation | async-start | bytes 393216 | tf_op jit(solution)/shard_map/all_to_all | solution.py:330
  11.0 8.2 %all-to-all-done = bf16[32,8,384]{2,1,0:T(8,128)(2,1)S(1)} async-done(((bf16[32,8,384]{2,1,0:T(8,128)(2,1)}), bf16[32,8,384]{2,1,0:T(8,128)(2,1)S(1)}, u32[]{:S(2)}, u32[]{:S(2)}) %all-to-all-start) | async-done | bytes 196640 | tf_op jit(solution)/shard_map/all_to_all | solution.py:330
  20.1 1.7 collective-permute-start
  21.8 2.2 %collective-permute-start.1 = (bf16[256,384]{1,0:T(8,128)(2,1)S(1)}, bf16[256,384]{1,0:T(8,128)(2,1)S(1)}, u32[]{:S(2)}, u32[]{:S(2)}) collective-permute-start(bf16[256,384]{1,0:T(8,128)(2,1)S(1)} %convolution_convert_fusion.own), channel_id=1, source_target_pairs={{0,3},{1,2},{2,1},{3,0},{4,7},{5,6},{6,5},{7,4},{8,11},{9,10},{10,... | collective-permute-start | bytes 589832 | tf_op jit(solution)/shard_map/ppermute | solution.py:36
  24.8 1.7 slice_bitcast_fusion.6.k_mem
  26.6 1.3 collective-permute-done.one
  27.9 4.6 %collective-permute-done.1.three = bf16[256,384]{1,0:T(8,128)(2,1)S(1)} collective-permute-done((bf16[256,384]{1,0:T(8,128)(2,1)S(1)}, bf16[256,384]{1,0:T(8,128)(2,1)S(1)}, u32[]{:S(2)}, u32[]{:S(2)}) %collective-permute-start.1) | collective-permute-done | bytes 196640 | tf_op jit(solution)/shard_map/ppermute | solution.py:36
  32.6 1.5 collective-permute-done.2.two
  35.4 2.2 %collective-permute-start.4 = (bf16[128,768]{1,0:T(8,128)(2,1)S(1)}, bf16[128,768]{1,0:T(8,128)(2,1)S(1)}, u32[]{:S(2)}, u32[]{:S(2)}) collective-permute-start(bf16[128,768]{1,0:T(8,128)(2,1)S(1)} %get-tuple-element.140), channel_id=1, source_target_pairs={{0,3},{1,2},{2,1},{3,0},{4,7},{5,6},{6,5},{7,4},{8,11},{9,10},{10,... | collective-permute-start | bytes 589832 | tf_op jit(solution)/shard_map/ppermute | solution.py:36
  37.6 4.0 %collective-permute-done.3 = bf16[128,768]{1,0:T(8,128)(2,1)S(1)} collective-permute-done((bf16[128,768]{1,0:T(8,128)(2,1)S(1)}, bf16[128,768]{1,0:T(8,128)(2,1)S(1)}, u32[]{:S(2)}, u32[]{:S(2)}) %collective-permute-start.3) | collective-permute-done | bytes 196640 | tf_op jit(solution)/shard_map/ppermute | solution.py:36
  41.6 1.3 collective-permute-done.4
  43.0 2.0 collective-permute-start.5
  45.3 5.6 %collective-permute-done.6.b2 = bf16[128,768]{1,0:T(8,128)(2,1)S(1)} collective-permute-done((bf16[128,768]{1,0:T(8,128)(2,1)S(1)}, bf16[128,768]{1,0:T(8,128)(2,1)S(1)}, u32[]{:S(2)}, u32[]{:S(2)}) %collective-permute-start.6) | collective-permute-done | bytes 196640 | tf_op jit(solution)/shard_map/ppermute | solution.py:36
  50.9 1.2 shard_map.167
  52.2 1.4 collective-permute-start.8
  54.0 3.8 %collective-permute-done.7 = bf16[128,768]{1,0:T(8,128)(2,1)S(1)} collective-permute-done((bf16[128,768]{1,0:T(8,128)(2,1)S(1)}, bf16[128,768]{1,0:T(8,128)(2,1)S(1)}, u32[]{:S(2)}, u32[]{:S(2)}) %collective-permute-start.7) | collective-permute-done | bytes 196640 | tf_op jit(solution)/shard_map/ppermute | solution.py:36
  57.9 1.3 collective-permute-done.8
  59.2 1.4 collective-permute-start.9
  60.8 1.5 collective-permute-start.10
  62.4 5.6 %collective-permute-done.10.b2 = bf16[128,768]{1,0:T(8,128)(2,1)S(1)} collective-permute-done((bf16[128,768]{1,0:T(8,128)(2,1)S(1)}, bf16[128,768]{1,0:T(8,128)(2,1)S(1)}, u32[]{:S(2)}, u32[]{:S(2)}) %collective-permute-start.10) | collective-permute-done | bytes 196640 | tf_op jit(solution)/shard_map/ppermute | solution.py:36
  69.2 2.1 %collective-permute-start.11 = (bf16[128,768]{1,0:T(8,128)(2,1)S(1)}, bf16[128,768]{1,0:T(8,128)(2,1)S(1)}, u32[]{:S(2)}, u32[]{:S(2)}) collective-permute-start(bf16[128,768]{1,0:T(8,128)(2,1)S(1)} %get-tuple-element.161), channel_id=1, source_target_pairs={{0,1},{1,0},{2,3},{3,2},{4,5},{5,4},{6,7},{7,6},{8,9},{9,8},{10,11... | collective-permute-start | bytes 589832 | tf_op jit(solution)/shard_map/ppermute | solution.py:36
  71.2 1.5 collective-permute-start.12
  73.2 3.5 %collective-permute-done.11 = bf16[128,768]{1,0:T(8,128)(2,1)S(1)} collective-permute-done((bf16[128,768]{1,0:T(8,128)(2,1)S(1)}, bf16[128,768]{1,0:T(8,128)(2,1)S(1)}, u32[]{:S(2)}, u32[]{:S(2)}) %collective-permute-start.11) | collective-permute-done | bytes 196640 | tf_op jit(solution)/shard_map/ppermute | solution.py:36
  76.7 1.4 collective-permute-done.12
  78.2 1.6 collective-permute-start.13
  80.1 5.6 %collective-permute-done.14.b2 = bf16[128,768]{1,0:T(8,128)(2,1)S(1)} collective-permute-done((bf16[128,768]{1,0:T(8,128)(2,1)S(1)}, bf16[128,768]{1,0:T(8,128)(2,1)S(1)}, u32[]{:S(2)}, u32[]{:S(2)}) %collective-permute-start.14) | collective-permute-done | bytes 196640 | tf_op jit(solution)/shard_map/ppermute | solution.py:36
  85.7 1.4 collective-permute-done.13.a2
  87.1 1.6 shard_map.169
  88.7 1.7 collective-permute-start.16
  90.8 1.3 shard_map.170
  92.2 2.2 %collective-permute-done.15 = bf16[128,768]{1,0:T(8,128)(2,1)S(1)} collective-permute-done((bf16[128,768]{1,0:T(8,128)(2,1)S(1)}, bf16[128,768]{1,0:T(8,128)(2,1)S(1)}, u32[]{:S(2)}, u32[]{:S(2)}) %collective-permute-start.15) | collective-permute-done | bytes 196640 | tf_op jit(solution)/shard_map/ppermute | solution.py:36
  94.4 1.5 collective-permute-done.16
  95.9 1.5 collective-permute-start.17
  97.7 5.5 %collective-permute-done.18.b2 = bf16[128,768]{1,0:T(8,128)(2,1)S(1)} collective-permute-done((bf16[128,768]{1,0:T(8,128)(2,1)S(1)}, bf16[128,768]{1,0:T(8,128)(2,1)S(1)}, u32[]{:S(2)}, u32[]{:S(2)}) %collective-permute-start.18) | collective-permute-done | bytes 196640 | tf_op jit(solution)/shard_map/ppermute | solution.py:36
  103.2 1.3 shard_map.171
  104.7 2.4 %collective-permute-start.21 = (bf16[128,768]{1,0:T(8,128)(2,1)S(1)}, bf16[128,768]{1,0:T(8,128)(2,1)S(1)}, u32[]{:S(2)}, u32[]{:S(2)}) collective-permute-start(bf16[128,768]{1,0:T(8,128)(2,1)S(1)} %get-tuple-element.189), channel_id=1, source_target_pairs={{0,3},{1,2},{2,1},{3,0},{4,7},{5,6},{6,5},{7,4},{8,11},{9,10},{10,... | collective-permute-start | bytes 589832 | tf_op jit(solution)/shard_map/ppermute | solution.py:36
  108.0 1.3 shard_map.172
  110.3 1.3 collective-permute-done.21
  111.7 2.4 %collective-permute-start.22 = (bf16[128,768]{1,0:T(8,128)(2,1)S(1)}, bf16[128,768]{1,0:T(8,128)(2,1)S(1)}, u32[]{:S(2)}, u32[]{:S(2)}) collective-permute-start(bf16[128,768]{1,0:T(8,128)(2,1)S(1)} %add_convert_fusion.9.a), channel_id=1, source_target_pairs={{0,3},{1,2},{2,1},{3,0},{4,7},{5,6},{6,5},{7,4},{8,11},{9,10},{10,... | collective-permute-start | bytes 589832 | tf_op jit(solution)/shard_map/ppermute | solution.py:36
  114.5 5.5 %collective-permute-done.23.b2 = bf16[128,768]{1,0:T(8,128)(2,1)S(1)} collective-permute-done((bf16[128,768]{1,0:T(8,128)(2,1)S(1)}, bf16[128,768]{1,0:T(8,128)(2,1)S(1)}, u32[]{:S(2)}, u32[]{:S(2)}) %collective-permute-start.23) | collective-permute-done | bytes 196640 | tf_op jit(solution)/shard_map/ppermute | solution.py:36
  120.8 1.3 shard_map.174
  122.3 1.8 collective-permute-start.27
  126.1 1.3 shard_map.175
  127.8 1.3 collective-permute-done.27
  129.2 1.9 collective-permute-start.28
  132.9 4.2 %collective-permute-done.29.b2 = bf16[128,768]{1,0:T(8,128)(2,1)S(1)} collective-permute-done((bf16[128,768]{1,0:T(8,128)(2,1)S(1)}, bf16[128,768]{1,0:T(8,128)(2,1)S(1)}, u32[]{:S(2)}, u32[]{:S(2)}) %collective-permute-start.29) | collective-permute-done | bytes 196640 | tf_op jit(solution)/shard_map/ppermute | solution.py:36
  140.9 2.4 %shard_map.179 = (bf16[384,1536]{1,0:T(8,128)(2,1)S(1)}, bf16[384,1536]{1,0:T(8,128)(2,1)}) custom-call(bf16[128,192]{1,0:T(8,128)(2,1)S(1)} %get-tuple-element.234.inner_grad, f32[128,192]{1,0:T(8,128)S(1)} %get-tuple-element.231.inner, bf16[128,1536]{1,0:T(8,128)(2,1)S(1)} %get-tuple-element.138.x, bf16[128,1536]{1,0:T(8,128)(2,1)S(1)} %get-tuple-element.235.grad_b, ...), custom_call_target="tpu_custom_call" | custom-call | flops 800000000 | bytes 4000000 | tf_op jit(solution)/shard_map/pallas_call | solution.py:65
  144.0 5.6 %all-to-all-start.1 = ((bf16[32,16,192]{2,1,0:T(8,128)(2,1)}), bf16[32,16,192]{2,1,0:T(8,128)(2,1)}, u32[]{:S(2)}, u32[]{:S(2)}) async-start(bf16[32,16,192]{2,1,0:T(8,128)(2,1)} %bitcast.39), calls=%async_computation.1 | async-start | bytes 524288 | tf_op jit(solution)/shard_map/all_to_all | solution.py:400
  149.6 3.1 %collective-permute-start.35 = (bf16[96,1536]{1,0:T(8,128)(2,1)}, bf16[96,1536]{1,0:T(8,128)(2,1)}, u32[]{:S(2)}, u32[]{:S(2)}) collective-permute-start(bf16[96,1536]{1,0:T(8,128)(2,1)} %get-tuple-element.239), channel_id=1, source_target_pairs={{0,96},{4,100},{8,104},{12,108},{16,112},{20,116},{24,120},{28,124... | collective-permute-start | bytes 884744 | tf_op jit(solution)/shard_map/ppermute | solution.py:36
  152.6 1.9 add_convert_fusion.18
  154.5 2.6 %shard_map.180 = bf16[384,1536]{1,0:T(8,128)(2,1)} custom-call(bf16[384,1536]{1,0:T(8,128)(2,1)S(1)} %get-tuple-element.236.kept, bf16[384,1536]{1,0:T(8,128)(2,1)} %collective-permute-done.33.other), custom_call_target="tpu_custom_call" | custom-call | flops 10000000 | bytes 4000000 | tf_op jit(solution)/shard_map/pallas_call | solution.py:65
  157.0 6.8 %all-to-all-done.1 = bf16[32,16,192]{2,1,0:T(8,128)(2,1)} async-done(((bf16[32,16,192]{2,1,0:T(8,128)(2,1)}), bf16[32,16,192]{2,1,0:T(8,128)(2,1)}, u32[]{:S(2)}, u32[]{:S(2)}) %all-to-all-start.1) | async-done | bytes 196640 | tf_op jit(solution)/shard_map/all_to_all | solution.py:400
  163.8 1.9 add_convert_fusion.19
  165.7 1.6 pad_maximum_fusion
  168.0 2.0 add_convert_fusion.1
  170.0 2.0 collective-permute-start.40
  171.9 3.8 %all-to-all-start.2 = ((bf16[16,24,1536]{2,1,0:T(8,128)(2,1)}), bf16[16,24,1536]{2,1,0:T(8,128)(2,1)S(1)}, u32[]{:S(2)}, u32[]{:S(2)}) async-start(bf16[16,24,1536]{2,1,0:T(8,128)(2,1)} %bitcast.19), calls=%async_computation.2 | async-start | bytes 2359296 | tf_op jit(solution)/shard_map/all_to_all | solution.py:305
  177.9 2.2 %collective-permute-start.43 = (bf16[48,1536]{1,0:T(8,128)(2,1)S(1)}, bf16[48,1536]{1,0:T(8,128)(2,1)S(1)}, u32[]{:S(2)}, u32[]{:S(2)}) collective-permute-start(bf16[48,1536]{1,0:T(8,128)(2,1)S(1)} %pad_maximum_fusion.2), channel_id=1, source_target_pairs={{0,24},{4,28},{8,16},{12,20},{16,8},{20,12},{24,0},{28,4},{32,56},... | collective-permute-start | bytes 442376 | tf_op jit(solution)/shard_map/ppermute | solution.py:36
  180.1 5.1 %collective-permute-done.40 = bf16[96,1536]{1,0:T(8,128)(2,1)} collective-permute-done((bf16[96,1536]{1,0:T(8,128)(2,1)}, bf16[96,1536]{1,0:T(8,128)(2,1)}, u32[]{:S(2)}, u32[]{:S(2)}) %collective-permute-start.40) | collective-permute-done | bytes 294944 | tf_op jit(solution)/shard_map/ppermute | solution.py:36
  186.5 1.8 shard_map.181
  189.4 3.1 %collective-permute-start.39 = (bf16[128,384]{1,0:T(8,128)(2,1)S(1)}, bf16[128,384]{1,0:T(8,128)(2,1)S(1)}, u32[]{:S(2)}, u32[]{:S(2)}) collective-permute-start(bf16[128,384]{1,0:T(8,128)(2,1)S(1)} %get-tuple-element.250), channel_id=1, source_target_pairs={{0,2},{1,3},{2,0},{3,1},{4,6},{5,7},{6,4},{7,5},{8,10},{9,11},{10,... | collective-permute-start | bytes 294920 | tf_op jit(solution)/shard_map/ppermute | solution.py:36
  193.7 2.1 %collective-permute-start.42 = (bf16[24,1536]{1,0:T(8,128)(2,1)S(1)}, bf16[24,1536]{1,0:T(8,128)(2,1)S(1)}, u32[]{:S(2)}, u32[]{:S(2)}) collective-permute-start(bf16[24,1536]{1,0:T(8,128)(2,1)S(1)} %get-tuple-element.275), channel_id=1, source_target_pairs={{0,96},{4,100},{8,104},{12,108},{16,112},{20,116},{24,120},{28,124... | collective-permute-start | bytes 221192 | tf_op jit(solution)/shard_map/ppermute | solution.py:36
  197.1 2.3 %collective-permute-done.42.come = bf16[24,1536]{1,0:T(8,128)(2,1)S(1)} collective-permute-done((bf16[24,1536]{1,0:T(8,128)(2,1)S(1)}, bf16[24,1536]{1,0:T(8,128)(2,1)S(1)}, u32[]{:S(2)}, u32[]{:S(2)}) %collective-permute-start.42) | collective-permute-done | bytes 73760 | tf_op jit(solution)/shard_map/ppermute | solution.py:36
  (121 shorter events, 28.2 us)
Async XLA Ops:
  0.6 25.9 %copy-start.4 = (bf16[4,192,1536]{2,1,0:T(8,128)(2,1)S(1)}, bf16[4,192,1536]{2,1,0:T(8,128)(2,1)}, u32[]{:S(2)}) copy-start(bf16[4,192,1536]{2,1,0:T(8,128)(2,1)} %param.18) | copy-start | bytes 7077892
  2.7 16.5 %all-to-all-start = ((bf16[32,8,384]{2,1,0:T(8,128)(2,1)}), bf16[32,8,384]{2,1,0:T(8,128)(2,1)S(1)}, u32[]{:S(2)}, u32[]{:S(2)}) async-start(bf16[32,8,384]{2,1,0:T(8,128)(2,1)} %fusion.3), calls=%async_computation | async-start | bytes 393216 | tf_op jit(solution)/shard_map/all_to_all | solution.py:330
  20.1 7.8 %collective-permute-start = (bf16[256,384]{1,0:T(8,128)(2,1)S(1)}, bf16[256,384]{1,0:T(8,128)(2,1)S(1)}, u32[]{:S(2)}, u32[]{:S(2)}) collective-permute-start(bf16[256,384]{1,0:T(8,128)(2,1)S(1)} %convolution_convert_fusion.own), channel_id=1, source_target_pairs={{0,1},{1,0},{2,3},{3,2},{4,5},{5,4},{6,7},{7,6},{8,9},{9,8},{10,11... | collective-permute-start | bytes 589832 | tf_op jit(solution)/shard_map/ppermute | solution.py:36
  21.8 10.8 %collective-permute-start.1 = (bf16[256,384]{1,0:T(8,128)(2,1)S(1)}, bf16[256,384]{1,0:T(8,128)(2,1)S(1)}, u32[]{:S(2)}, u32[]{:S(2)}) collective-permute-start(bf16[256,384]{1,0:T(8,128)(2,1)S(1)} %convolution_convert_fusion.own), channel_id=1, source_target_pairs={{0,3},{1,2},{2,1},{3,0},{4,7},{5,6},{6,5},{7,4},{8,11},{9,10},{10,... | collective-permute-start | bytes 589832 | tf_op jit(solution)/shard_map/ppermute | solution.py:36
  24.0 13.6 %copy-start.7 = (s32[768]{0:T(1024)S(1)}, s32[768]{0:T(1024)}, u32[]{:S(2)}) copy-start(s32[768]{0:T(1024)} %constant.54.clone) | copy-start | bytes 9220
  24.0 13.6 %copy-start.8 = (s32[768]{0:T(1024)S(1)}, s32[768]{0:T(1024)}, u32[]{:S(2)}) copy-start(s32[768]{0:T(1024)} %constant.55.clone) | copy-start | bytes 9220
  24.0 13.6 %copy-start.9 = (s32[768]{0:T(1024)S(1)}, s32[768]{0:T(1024)}, u32[]{:S(2)}) copy-start(s32[768]{0:T(1024)} %constant.56.clone) | copy-start | bytes 9220
  24.0 13.6 %copy-start.10 = (s32[768]{0:T(1024)S(1)}, s32[768]{0:T(1024)}, u32[]{:S(2)}) copy-start(s32[768]{0:T(1024)} %constant.57.clone) | copy-start | bytes 9220
  24.0 13.6 %copy-start.11 = (s32[768]{0:T(1024)S(1)}, s32[768]{0:T(1024)}, u32[]{:S(2)}) copy-start(s32[768]{0:T(1024)} %constant.58.clone) | copy-start | bytes 9220
  24.0 10.1 %collective-permute-start.2 = (bf16[256,384]{1,0:T(8,128)(2,1)S(1)}, bf16[256,384]{1,0:T(8,128)(2,1)S(1)}, u32[]{:S(2)}, u32[]{:S(2)}) collective-permute-start(bf16[256,384]{1,0:T(8,128)(2,1)S(1)} %convolution_convert_fusion.own), channel_id=1, source_target_pairs={{0,2},{1,3},{2,0},{3,1},{4,6},{5,7},{6,4},{7,5},{8,10},{9,11},{10,... | collective-permute-start | bytes 589832 | tf_op jit(solution)/shard_map/ppermute | solution.py:36
  24.8 20.2 %copy-start.3 = (bf16[4,3,192,1536]{3,2,1,0:T(8,128)(2,1)S(1)}, bf16[4,3,192,1536]{3,2,1,0:T(8,128)(2,1)}, u32[]{:S(2)}) copy-start(bf16[4,3,192,1536]{3,2,1,0:T(8,128)(2,1)} %param.17) | copy-start | bytes 21233668
  35.2 6.4 %collective-permute-start.3 = (bf16[128,768]{1,0:T(8,128)(2,1)S(1)}, bf16[128,768]{1,0:T(8,128)(2,1)S(1)}, u32[]{:S(2)}, u32[]{:S(2)}) collective-permute-start(bf16[128,768]{1,0:T(8,128)(2,1)S(1)} %get-tuple-element.139), channel_id=1, source_target_pairs={{0,1},{1,0},{2,3},{3,2},{4,5},{5,4},{6,7},{7,6},{8,9},{9,8},{10,11... | collective-permute-start | bytes 589832 | tf_op jit(solution)/shard_map/ppermute | solution.py:36
  35.4 7.5 %collective-permute-start.4 = (bf16[128,768]{1,0:T(8,128)(2,1)S(1)}, bf16[128,768]{1,0:T(8,128)(2,1)S(1)}, u32[]{:S(2)}, u32[]{:S(2)}) collective-permute-start(bf16[128,768]{1,0:T(8,128)(2,1)S(1)} %get-tuple-element.140), channel_id=1, source_target_pairs={{0,3},{1,2},{2,1},{3,0},{4,7},{5,6},{6,5},{7,4},{8,11},{9,10},{10,... | collective-permute-start | bytes 589832 | tf_op jit(solution)/shard_map/ppermute | solution.py:36
  43.0 7.9 %collective-permute-start.5 = (bf16[128,768]{1,0:T(8,128)(2,1)S(1)}, bf16[128,768]{1,0:T(8,128)(2,1)S(1)}, u32[]{:S(2)}, u32[]{:S(2)}) collective-permute-start(bf16[128,768]{1,0:T(8,128)(2,1)S(1)} %add_convert_fusion.17.a), channel_id=1, source_target_pairs={{0,3},{1,2},{2,1},{3,0},{4,7},{5,6},{6,5},{7,4},{8,11},{9,10},{10,... | collective-permute-start | bytes 589832 | tf_op jit(solution)/shard_map/ppermute | solution.py:36
  45.2 5.7 %collective-permute-start.6 = (bf16[128,768]{1,0:T(8,128)(2,1)S(1)}, bf16[128,768]{1,0:T(8,128)(2,1)S(1)}, u32[]{:S(2)}, u32[]{:S(2)}) collective-permute-start(bf16[128,768]{1,0:T(8,128)(2,1)S(1)} %add_convert_fusion.16.b), channel_id=1, source_target_pairs={{0,1},{1,0},{2,3},{3,2},{4,5},{5,4},{6,7},{7,6},{8,9},{9,8},{10,11... | collective-permute-start | bytes 589832 | tf_op jit(solution)/shard_map/ppermute | solution.py:36
  52.1 5.7 %collective-permute-start.7 = (bf16[128,768]{1,0:T(8,128)(2,1)S(1)}, bf16[128,768]{1,0:T(8,128)(2,1)S(1)}, u32[]{:S(2)}, u32[]{:S(2)}) collective-permute-start(bf16[128,768]{1,0:T(8,128)(2,1)S(1)} %get-tuple-element.150), channel_id=1, source_target_pairs={{0,1},{1,0},{2,3},{3,2},{4,5},{5,4},{6,7},{7,6},{8,9},{9,8},{10,11... | collective-permute-start | bytes 589832 | tf_op jit(solution)/shard_map/ppermute | solution.py:36
  52.2 7.0 %collective-permute-start.8 = (bf16[128,768]{1,0:T(8,128)(2,1)S(1)}, bf16[128,768]{1,0:T(8,128)(2,1)S(1)}, u32[]{:S(2)}, u32[]{:S(2)}) collective-permute-start(bf16[128,768]{1,0:T(8,128)(2,1)S(1)} %get-tuple-element.151), channel_id=1, source_target_pairs={{0,3},{1,2},{2,1},{3,0},{4,7},{5,6},{6,5},{7,4},{8,11},{9,10},{10,... | collective-permute-start | bytes 589832 | tf_op jit(solution)/shard_map/ppermute | solution.py:36
  59.2 8.7 %collective-permute-start.9 = (bf16[128,768]{1,0:T(8,128)(2,1)S(1)}, bf16[128,768]{1,0:T(8,128)(2,1)S(1)}, u32[]{:S(2)}, u32[]{:S(2)}) collective-permute-start(bf16[128,768]{1,0:T(8,128)(2,1)S(1)} %add_convert_fusion.15.a), channel_id=1, source_target_pairs={{0,3},{1,2},{2,1},{3,0},{4,7},{5,6},{6,5},{7,4},{8,11},{9,10},{10,... | collective-permute-start | bytes 589832 | tf_op jit(solution)/shard_map/ppermute | solution.py:36
  60.8 7.1 %collective-permute-start.10 = (bf16[128,768]{1,0:T(8,128)(2,1)S(1)}, bf16[128,768]{1,0:T(8,128)(2,1)S(1)}, u32[]{:S(2)}, u32[]{:S(2)}) collective-permute-start(bf16[128,768]{1,0:T(8,128)(2,1)S(1)} %add_convert_fusion.14.b), channel_id=1, source_target_pairs={{0,1},{1,0},{2,3},{3,2},{4,5},{5,4},{6,7},{7,6},{8,9},{9,8},{10,11... | collective-permute-start | bytes 589832 | tf_op jit(solution)/shard_map/ppermute | solution.py:36
  69.2 7.5 %collective-permute-start.11 = (bf16[128,768]{1,0:T(8,128)(2,1)S(1)}, bf16[128,768]{1,0:T(8,128)(2,1)S(1)}, u32[]{:S(2)}, u32[]{:S(2)}) collective-permute-start(bf16[128,768]{1,0:T(8,128)(2,1)S(1)} %get-tuple-element.161), channel_id=1, source_target_pairs={{0,1},{1,0},{2,3},{3,2},{4,5},{5,4},{6,7},{7,6},{8,9},{9,8},{10,11... | collective-permute-start | bytes 589832 | tf_op jit(solution)/shard_map/ppermute | solution.py:36
  71.2 6.9 %collective-permute-start.12 = (bf16[128,768]{1,0:T(8,128)(2,1)S(1)}, bf16[128,768]{1,0:T(8,128)(2,1)S(1)}, u32[]{:S(2)}, u32[]{:S(2)}) collective-permute-start(bf16[128,768]{1,0:T(8,128)(2,1)S(1)} %get-tuple-element.162), channel_id=1, source_target_pairs={{0,3},{1,2},{2,1},{3,0},{4,7},{5,6},{6,5},{7,4},{8,11},{9,10},{10,... | collective-permute-start | bytes 589832 | tf_op jit(solution)/shard_map/ppermute | solution.py:36
  78.2 8.9 %collective-permute-start.13 = (bf16[128,768]{1,0:T(8,128)(2,1)S(1)}, bf16[128,768]{1,0:T(8,128)(2,1)S(1)}, u32[]{:S(2)}, u32[]{:S(2)}) collective-permute-start(bf16[128,768]{1,0:T(8,128)(2,1)S(1)} %add_convert_fusion.13.a), channel_id=1, source_target_pairs={{0,3},{1,2},{2,1},{3,0},{4,7},{5,6},{6,5},{7,4},{8,11},{9,10},{10,... | collective-permute-start | bytes 589832 | tf_op jit(solution)/shard_map/ppermute | solution.py:36
  79.9 5.7 %collective-permute-start.14 = (bf16[128,768]{1,0:T(8,128)(2,1)S(1)}, bf16[128,768]{1,0:T(8,128)(2,1)S(1)}, u32[]{:S(2)}, u32[]{:S(2)}) collective-permute-start(bf16[128,768]{1,0:T(8,128)(2,1)S(1)} %add_convert_fusion.12.b), channel_id=1, source_target_pairs={{0,1},{1,0},{2,3},{3,2},{4,5},{5,4},{6,7},{7,6},{8,9},{9,8},{10,11... | collective-permute-start | bytes 589832 | tf_op jit(solution)/shard_map/ppermute | solution.py:36
  88.6 5.7 %collective-permute-start.15 = (bf16[128,768]{1,0:T(8,128)(2,1)S(1)}, bf16[128,768]{1,0:T(8,128)(2,1)S(1)}, u32[]{:S(2)}, u32[]{:S(2)}) collective-permute-start(bf16[128,768]{1,0:T(8,128)(2,1)S(1)} %get-tuple-element.171), channel_id=1, source_target_pairs={{0,1},{1,0},{2,3},{3,2},{4,5},{5,4},{6,7},{7,6},{8,9},{9,8},{10,11... | collective-permute-start | bytes 589832 | tf_op jit(solution)/shard_map/ppermute | solution.py:36
  88.7 7.1 %collective-permute-start.16 = (bf16[128,768]{1,0:T(8,128)(2,1)S(1)}, bf16[128,768]{1,0:T(8,128)(2,1)S(1)}, u32[]{:S(2)}, u32[]{:S(2)}) collective-permute-start(bf16[128,768]{1,0:T(8,128)(2,1)S(1)} %get-tuple-element.172), channel_id=1, source_target_pairs={{0,3},{1,2},{2,1},{3,0},{4,7},{5,6},{6,5},{7,4},{8,11},{9,10},{10,... | collective-permute-start | bytes 589832 | tf_op jit(solution)/shard_map/ppermute | solution.py:36
  92.1 11.1 %collective-permute-start.19 = (bf16[384,1536]{1,0:T(8,128)(2,1)S(1)}, bf16[384,1536]{1,0:T(8,128)(2,1)S(1)}, u32[]{:S(2)}, u32[]{:S(2)}) collective-permute-start(bf16[384,1536]{1,0:T(8,128)(2,1)S(1)} %get-tuple-element.179), channel_id=1, source_target_pairs={{0,4},{4,0},{8,12},{12,8},{16,20},{20,16},{24,28},{28,24},{32,36},... | collective-permute-start | bytes 3538952 | tf_op jit(solution)/shard_map/ppermute | solution.py:36
  95.9 7.3 %collective-permute-start.17 = (bf16[128,768]{1,0:T(8,128)(2,1)S(1)}, bf16[128,768]{1,0:T(8,128)(2,1)S(1)}, u32[]{:S(2)}, u32[]{:S(2)}) collective-permute-start(bf16[128,768]{1,0:T(8,128)(2,1)S(1)} %add_convert_fusion.11.a), channel_id=1, source_target_pairs={{0,3},{1,2},{2,1},{3,0},{4,7},{5,6},{6,5},{7,4},{8,11},{9,10},{10,... | collective-permute-start | bytes 589832 | tf_op jit(solution)/shard_map/ppermute | solution.py:36
  97.4 5.8 %collective-permute-start.18 = (bf16[128,768]{1,0:T(8,128)(2,1)S(1)}, bf16[128,768]{1,0:T(8,128)(2,1)S(1)}, u32[]{:S(2)}, u32[]{:S(2)}) collective-permute-start(bf16[128,768]{1,0:T(8,128)(2,1)S(1)} %add_convert_fusion.10.b), channel_id=1, source_target_pairs={{0,1},{1,0},{2,3},{3,2},{4,5},{5,4},{6,7},{7,6},{8,9},{9,8},{10,11... | collective-permute-start | bytes 589832 | tf_op jit(solution)/shard_map/ppermute | solution.py:36
  103.2 3.8 %copy-start.13 = (s32[512]{0:T(512)S(1)}, s32[512]{0:T(512)}, u32[]{:S(2)}) copy-start(s32[512]{0:T(512)} %constant.59.clone) | copy-start | bytes 6148
  104.6 5.7 %collective-permute-start.20 = (bf16[128,768]{1,0:T(8,128)(2,1)S(1)}, bf16[128,768]{1,0:T(8,128)(2,1)S(1)}, u32[]{:S(2)}, u32[]{:S(2)}) collective-permute-start(bf16[128,768]{1,0:T(8,128)(2,1)S(1)} %get-tuple-element.188), channel_id=1, source_target_pairs={{0,1},{1,0},{2,3},{3,2},{4,5},{5,4},{6,7},{7,6},{8,9},{9,8},{10,11... | collective-permute-start | bytes 589832 | tf_op jit(solution)/shard_map/ppermute | solution.py:36
  104.7 7.0 %collective-permute-start.21 = (bf16[128,768]{1,0:T(8,128)(2,1)S(1)}, bf16[128,768]{1,0:T(8,128)(2,1)S(1)}, u32[]{:S(2)}, u32[]{:S(2)}) collective-permute-start(bf16[128,768]{1,0:T(8,128)(2,1)S(1)} %get-tuple-element.189), channel_id=1, source_target_pairs={{0,3},{1,2},{2,1},{3,0},{4,7},{5,6},{6,5},{7,4},{8,11},{9,10},{10,... | collective-permute-start | bytes 589832 | tf_op jit(solution)/shard_map/ppermute | solution.py:36
  107.5 12.5 %collective-permute-start.25 = (bf16[192,1536]{1,0:T(8,128)(2,1)S(1)}, bf16[192,1536]{1,0:T(8,128)(2,1)S(1)}, u32[]{:S(2)}, u32[]{:S(2)}) collective-permute-start(bf16[192,1536]{1,0:T(8,128)(2,1)S(1)} %get-tuple-element.198), channel_id=1, source_target_pairs={{0,32},{4,36},{8,40},{12,44},{16,48},{20,52},{24,56},{28,60},{32,0... | collective-permute-start | bytes 1769480 | tf_op jit(solution)/shard_map/ppermute | solution.py:36
  109.3 10.7 %collective-permute-start.24 = (bf16[384,1536]{1,0:T(8,128)(2,1)S(1)}, bf16[384,1536]{1,0:T(8,128)(2,1)S(1)}, u32[]{:S(2)}, u32[]{:S(2)}) collective-permute-start(bf16[384,1536]{1,0:T(8,128)(2,1)S(1)} %get-tuple-element.195), channel_id=1, source_target_pairs={{0,4},{4,0},{8,12},{12,8},{16,20},{20,16},{24,28},{28,24},{32,36},... | collective-permute-start | bytes 3538952 | tf_op jit(solution)/shard_map/ppermute | solution.py:36
  111.7 8.3 %collective-permute-start.22 = (bf16[128,768]{1,0:T(8,128)(2,1)S(1)}, bf16[128,768]{1,0:T(8,128)(2,1)S(1)}, u32[]{:S(2)}, u32[]{:S(2)}) collective-permute-start(bf16[128,768]{1,0:T(8,128)(2,1)S(1)} %add_convert_fusion.9.a), channel_id=1, source_target_pairs={{0,3},{1,2},{2,1},{3,0},{4,7},{5,6},{6,5},{7,4},{8,11},{9,10},{10,... | collective-permute-start | bytes 589832 | tf_op jit(solution)/shard_map/ppermute | solution.py:36
  114.2 5.7 %collective-permute-start.23 = (bf16[128,768]{1,0:T(8,128)(2,1)S(1)}, bf16[128,768]{1,0:T(8,128)(2,1)S(1)}, u32[]{:S(2)}, u32[]{:S(2)}) collective-permute-start(bf16[128,768]{1,0:T(8,128)(2,1)S(1)} %add_convert_fusion.8.b), channel_id=1, source_target_pairs={{0,1},{1,0},{2,3},{3,2},{4,5},{5,4},{6,7},{7,6},{8,9},{9,8},{10,11... | collective-permute-start | bytes 589832 | tf_op jit(solution)/shard_map/ppermute | solution.py:36
  120.3 16.8 %collective-permute-start.32 = (bf16[192,1536]{1,0:T(8,128)(2,1)S(1)}, bf16[192,1536]{1,0:T(8,128)(2,1)S(1)}, u32[]{:S(2)}, u32[]{:S(2)}) collective-permute-start(bf16[192,1536]{1,0:T(8,128)(2,1)S(1)} %get-tuple-element.220), channel_id=1, source_target_pairs={{0,32},{4,36},{8,40},{12,44},{16,48},{20,52},{24,56},{28,60},{32,0... | collective-permute-start | bytes 1769480 | tf_op jit(solution)/shard_map/ppermute | solution.py:36
  122.1 5.7 %collective-permute-start.26 = (bf16[128,768]{1,0:T(8,128)(2,1)S(1)}, bf16[128,768]{1,0:T(8,128)(2,1)S(1)}, u32[]{:S(2)}, u32[]{:S(2)}) collective-permute-start(bf16[128,768]{1,0:T(8,128)(2,1)S(1)} %get-tuple-element.207), channel_id=1, source_target_pairs={{0,1},{1,0},{2,3},{3,2},{4,5},{5,4},{6,7},{7,6},{8,9},{9,8},{10,11... | collective-permute-start | bytes 589832 | tf_op jit(solution)/shard_map/ppermute | solution.py:36
  122.3 6.9 %collective-permute-start.27 = (bf16[128,768]{1,0:T(8,128)(2,1)S(1)}, bf16[128,768]{1,0:T(8,128)(2,1)S(1)}, u32[]{:S(2)}, u32[]{:S(2)}) collective-permute-start(bf16[128,768]{1,0:T(8,128)(2,1)S(1)} %get-tuple-element.208), channel_id=1, source_target_pairs={{0,3},{1,2},{2,1},{3,0},{4,7},{5,6},{6,5},{7,4},{8,11},{9,10},{10,... | collective-permute-start | bytes 589832 | tf_op jit(solution)/shard_map/ppermute | solution.py:36
  125.0 7.9 %collective-permute-start.31 = (bf16[96,1536]{1,0:T(8,128)(2,1)S(1)}, bf16[96,1536]{1,0:T(8,128)(2,1)S(1)}, u32[]{:S(2)}, u32[]{:S(2)}) collective-permute-start(bf16[96,1536]{1,0:T(8,128)(2,1)S(1)} %get-tuple-element.260), channel_id=1, source_target_pairs={{0,96},{4,100},{8,104},{12,108},{16,112},{20,116},{24,120},{28,124... | collective-permute-start | bytes 884744 | tf_op jit(solution)/shard_map/ppermute | solution.py:36
  127.4 9.7 %collective-permute-start.30 = (bf16[384,1536]{1,0:T(8,128)(2,1)S(1)}, bf16[384,1536]{1,0:T(8,128)(2,1)S(1)}, u32[]{:S(2)}, u32[]{:S(2)}) collective-permute-start(bf16[384,1536]{1,0:T(8,128)(2,1)S(1)} %get-tuple-element.215), channel_id=1, source_target_pairs={{0,4},{4,0},{8,12},{12,8},{16,20},{20,16},{24,28},{28,24},{32,36},... | collective-permute-start | bytes 3538952 | tf_op jit(solution)/shard_map/ppermute | solution.py:36
  129.2 7.9 %collective-permute-start.28 = (bf16[128,768]{1,0:T(8,128)(2,1)S(1)}, bf16[128,768]{1,0:T(8,128)(2,1)S(1)}, u32[]{:S(2)}, u32[]{:S(2)}) collective-permute-start(bf16[128,768]{1,0:T(8,128)(2,1)S(1)} %add_convert_fusion.7.a), channel_id=1, source_target_pairs={{0,3},{1,2},{2,1},{3,0},{4,7},{5,6},{6,5},{7,4},{8,11},{9,10},{10,... | collective-permute-start | bytes 589832 | tf_op jit(solution)/shard_map/ppermute | solution.py:36
  131.3 5.7 %collective-permute-start.29 = (bf16[128,768]{1,0:T(8,128)(2,1)S(1)}, bf16[128,768]{1,0:T(8,128)(2,1)S(1)}, u32[]{:S(2)}, u32[]{:S(2)}) collective-permute-start(bf16[128,768]{1,0:T(8,128)(2,1)S(1)} %add_convert_fusion.6.b), channel_id=1, source_target_pairs={{0,1},{1,0},{2,3},{3,2},{4,5},{5,4},{6,7},{7,6},{8,9},{9,8},{10,11... | collective-permute-start | bytes 589832 | tf_op jit(solution)/shard_map/ppermute | solution.py:36
  132.9 4.2 %copy-start.5 = (bf16[96,1536]{1,0:T(8,128)(2,1)}, bf16[96,1536]{1,0:T(8,128)(2,1)S(1)}, u32[]{:S(2)}) copy-start(bf16[96,1536]{1,0:T(8,128)(2,1)S(1)} %collective-permute-done.31) | copy-start | bytes 884740
  139.1 4.2 %copy-start = (bf16[192,1536]{1,0:T(8,128)(2,1)}, bf16[192,1536]{1,0:T(8,128)(2,1)S(1)}, u32[]{:S(2)}) copy-start(bf16[192,1536]{1,0:T(8,128)(2,1)S(1)} %get-tuple-element.252) | copy-start | bytes 1769476
  140.2 0.7 copy-start.2
  140.2 3.6 %copy-start.12 = (s32[448]{0:T(512)S(1)}, s32[448]{0:T(512)}, u32[]{:S(2)}) copy-start(s32[448]{0:T(512)} %constant.60.clone) | copy-start | bytes 5380
  143.3 11.2 %collective-permute-start.33 = (bf16[384,1536]{1,0:T(8,128)(2,1)}, bf16[384,1536]{1,0:T(8,128)(2,1)}, u32[]{:S(2)}, u32[]{:S(2)}) collective-permute-start(bf16[384,1536]{1,0:T(8,128)(2,1)} %get-tuple-element.237), channel_id=1, source_target_pairs={{0,4},{4,0},{8,12},{12,8},{16,20},{20,16},{24,28},{28,24},{32,36},... | collective-permute-start | bytes 3538952 | tf_op jit(solution)/shard_map/ppermute | solution.py:36
  143.3 20.5 %collective-permute-start.34 = (bf16[192,1536]{1,0:T(8,128)(2,1)}, bf16[192,1536]{1,0:T(8,128)(2,1)}, u32[]{:S(2)}, u32[]{:S(2)}) collective-permute-start(bf16[192,1536]{1,0:T(8,128)(2,1)} %get-tuple-element.238), channel_id=1, source_target_pairs={{0,8},{4,12},{8,0},{12,4},{16,24},{20,28},{24,16},{28,20},{32,40},... | collective-permute-start | bytes 1769480 | tf_op jit(solution)/shard_map/ppermute | solution.py:36
  144.0 19.8 %all-to-all-start.1 = ((bf16[32,16,192]{2,1,0:T(8,128)(2,1)}), bf16[32,16,192]{2,1,0:T(8,128)(2,1)}, u32[]{:S(2)}, u32[]{:S(2)}) async-start(bf16[32,16,192]{2,1,0:T(8,128)(2,1)} %bitcast.39), calls=%async_computation.1 | async-start | bytes 524288 | tf_op jit(solution)/shard_map/all_to_all | solution.py:400
  149.6 14.2 %collective-permute-start.35 = (bf16[96,1536]{1,0:T(8,128)(2,1)}, bf16[96,1536]{1,0:T(8,128)(2,1)}, u32[]{:S(2)}, u32[]{:S(2)}) collective-permute-start(bf16[96,1536]{1,0:T(8,128)(2,1)} %get-tuple-element.239), channel_id=1, source_target_pairs={{0,96},{4,100},{8,104},{12,108},{16,112},{20,116},{24,120},{28,124... | collective-permute-start | bytes 884744 | tf_op jit(solution)/shard_map/ppermute | solution.py:36
  157.0 11.0 %copy-start.1 = (bf16[192,1536]{1,0:T(8,128)(2,1)S(1)}, bf16[192,1536]{1,0:T(8,128)(2,1)}, u32[]{:S(2)}) copy-start(bf16[192,1536]{1,0:T(8,128)(2,1)} %copy-done) | copy-start | bytes 1769476
  167.3 9.4 %collective-permute-start.36 = (bf16[96,1536]{1,0:T(8,128)(2,1)}, bf16[96,1536]{1,0:T(8,128)(2,1)}, u32[]{:S(2)}, u32[]{:S(2)}) collective-permute-start(bf16[96,1536]{1,0:T(8,128)(2,1)} %pad_maximum_fusion), channel_id=1, source_target_pairs={{0,8},{4,12},{8,0},{12,4},{16,24},{20,28},{24,16},{28,20},{32,40},... | collective-permute-start | bytes 884744 | tf_op jit(solution)/shard_map/ppermute | solution.py:36
  170.0 15.2 %collective-permute-start.40 = (bf16[96,1536]{1,0:T(8,128)(2,1)}, bf16[96,1536]{1,0:T(8,128)(2,1)}, u32[]{:S(2)}, u32[]{:S(2)}) collective-permute-start(bf16[96,1536]{1,0:T(8,128)(2,1)} %get-tuple-element.258), channel_id=1, source_target_pairs={{0,24},{4,28},{8,16},{12,20},{16,8},{20,12},{24,0},{28,4},{32,56},... | collective-permute-start | bytes 884744 | tf_op jit(solution)/shard_map/ppermute | solution.py:36
  171.9 27.5 %all-to-all-start.2 = ((bf16[16,24,1536]{2,1,0:T(8,128)(2,1)}), bf16[16,24,1536]{2,1,0:T(8,128)(2,1)S(1)}, u32[]{:S(2)}, u32[]{:S(2)}) async-start(bf16[16,24,1536]{2,1,0:T(8,128)(2,1)} %bitcast.19), calls=%async_computation.2 | async-start | bytes 2359296 | tf_op jit(solution)/shard_map/all_to_all | solution.py:305
  177.9 19.2 %collective-permute-start.43 = (bf16[48,1536]{1,0:T(8,128)(2,1)S(1)}, bf16[48,1536]{1,0:T(8,128)(2,1)S(1)}, u32[]{:S(2)}, u32[]{:S(2)}) collective-permute-start(bf16[48,1536]{1,0:T(8,128)(2,1)S(1)} %pad_maximum_fusion.2), channel_id=1, source_target_pairs={{0,24},{4,28},{8,16},{12,20},{16,8},{20,12},{24,0},{28,4},{32,56},... | collective-permute-start | bytes 442376 | tf_op jit(solution)/shard_map/ppermute | solution.py:36
  186.4 9.8 %copy-start.6 = (bf16[128,384]{1,0:T(8,128)(2,1)S(1)}, bf16[128,384]{1,0:T(8,128)(2,1)}, u32[]{:S(2)}) copy-start(bf16[128,384]{1,0:T(8,128)(2,1)} %param.15) | copy-start | bytes 294916
  186.4 7.3 %collective-permute-start.41 = (bf16[48,1536]{1,0:T(8,128)(2,1)S(1)}, bf16[48,1536]{1,0:T(8,128)(2,1)S(1)}, u32[]{:S(2)}, u32[]{:S(2)}) collective-permute-start(bf16[48,1536]{1,0:T(8,128)(2,1)S(1)} %get-tuple-element.268), channel_id=1, source_target_pairs={{0,32},{4,36},{8,40},{12,44},{16,48},{20,52},{24,56},{28,60},{32,0... | collective-permute-start | bytes 442376 | tf_op jit(solution)/shard_map/ppermute | solution.py:36
  188.4 7.5 %collective-permute-start.37 = (bf16[128,384]{1,0:T(8,128)(2,1)S(1)}, bf16[128,384]{1,0:T(8,128)(2,1)S(1)}, u32[]{:S(2)}, u32[]{:S(2)}) collective-permute-start(bf16[128,384]{1,0:T(8,128)(2,1)S(1)} %get-tuple-element.248), channel_id=1, source_target_pairs={{0,1},{1,0},{2,3},{3,2},{4,5},{5,4},{6,7},{7,6},{8,9},{9,8},{10,11... | collective-permute-start | bytes 294920 | tf_op jit(solution)/shard_map/ppermute | solution.py:36
  189.3 6.9 %collective-permute-start.38 = (bf16[128,384]{1,0:T(8,128)(2,1)S(1)}, bf16[128,384]{1,0:T(8,128)(2,1)S(1)}, u32[]{:S(2)}, u32[]{:S(2)}) collective-permute-start(bf16[128,384]{1,0:T(8,128)(2,1)S(1)} %get-tuple-element.249), channel_id=1, source_target_pairs={{0,3},{1,2},{2,1},{3,0},{4,7},{5,6},{6,5},{7,4},{8,11},{9,10},{10,... | collective-permute-start | bytes 294920 | tf_op jit(solution)/shard_map/ppermute | solution.py:36
  189.4 6.8 %collective-permute-start.39 = (bf16[128,384]{1,0:T(8,128)(2,1)S(1)}, bf16[128,384]{1,0:T(8,128)(2,1)S(1)}, u32[]{:S(2)}, u32[]{:S(2)}) collective-permute-start(bf16[128,384]{1,0:T(8,128)(2,1)S(1)} %get-tuple-element.250), channel_id=1, source_target_pairs={{0,2},{1,3},{2,0},{3,1},{4,6},{5,7},{6,4},{7,5},{8,10},{9,11},{10,... | collective-permute-start | bytes 294920 | tf_op jit(solution)/shard_map/ppermute | solution.py:36
  193.7 5.6 %collective-permute-start.42 = (bf16[24,1536]{1,0:T(8,128)(2,1)S(1)}, bf16[24,1536]{1,0:T(8,128)(2,1)S(1)}, u32[]{:S(2)}, u32[]{:S(2)}) collective-permute-start(bf16[24,1536]{1,0:T(8,128)(2,1)S(1)} %get-tuple-element.275), channel_id=1, source_target_pairs={{0,96},{4,100},{8,104},{12,108},{16,112},{20,116},{24,120},{28,124... | collective-permute-start | bytes 221192 | tf_op jit(solution)/shard_map/ppermute | solution.py:36

commit v4 on v3

--- a/solution.py
+++ b/solution.py
@@ -71,7 +71,7 @@
         out_specs=[pl.BlockSpec(memory_space=pltpu.VMEM)] * len(outs),
         scratch_shapes=scratch,
         compiler_params=pltpu.CompilerParams(vmem_limit_bytes=16 * 2**20),
-        cost_estimate=pl.CostEstimate(flops=int(flops), bytes_accessed=4_000_000, transcendentals=0),
+        cost_estimate=pl.CostEstimate(flops=1000, bytes_accessed=1000, transcendentals=0),
     )(*args)
 
 
@@ -366,19 +366,23 @@
         keep, send = weight_terms(layer, tables[layer], inner_grad, inner, x, grad_b)
         first, second = [keep], [swap(send, "seq", 1)]
         if layer == 1:
+            second = [*merge(keep, second[0], 2)]
+        if layer == 1:
             three_kept, three_sent = halved(three_kept, three_got)
             second += [swap(three_sent, "seq", 24), swap(two_sent, "seq", 8)]
         if layer == 2:
             second += [swap(three_sent, "seq", 8)]
         terms, loaded, (keep,), (other, *rest) = sum_mp(ta, tb, weights(layer - 1), first, second)
-        kept, sent = merge(keep, other, 2)
+        if layer > 1:
+            kept, sent = merge(keep, other, 2)
         if layer == 3:
             three_kept, three_sent = kept, sent
         if layer == 2:
             (three_got,) = rest
             two_kept, two_sent = kept, sent
         if layer == 1:
-            three_got, two_got = rest
+            kept = other
+            sent, three_got, two_got = rest
         above, (x, inner) = x, saved[layer - 1]
         if layer > 1:
             g, grad_b, inner_grad, ta, tb = call(
@@ -388,8 +392,6 @@
                 (g, *terms, above, inner, *loaded),
             )
     two_kept, two_sent = halved(two_kept, two_got)
-    a, kept, sent, two_kept, two_sent = together(terms[0], kept, sent, two_kept, two_sent)
-    terms = (a, *terms[1:])
     grad_b, inner_grad, sent_blocks = call(
         final_kernel,
         [full, hid, struct((512, H), BF16)],
@@ -398,16 +400,15 @@
         {0: pltpu.SMEM},
     )
     got = lax.all_to_all(sent_blocks.reshape(PEERS, 16, H), "seq", 0, 0)
+    come = swap(sent, "seq", X)
+    inner_grad, two_got = together(inner_grad, swap(two_sent, "seq", 3 * Z))
     keep, send = weight_terms(0, tables[0], inner_grad, inner, x, grad_b)
     (first,) = merge(keep, swap(send, "seq", 1), 1)
-    got, first, come, two_got = together(
-        got, first, swap(sent, "seq", X), swap(two_sent, "seq", 3 * Z)
-    )
+    late = [halved(two_kept, two_got), halved(three_kept, three_got)]
+    late = [jnp.concatenate(parts, axis=0) for parts in zip(*late)]
+    got, first, kept, sent, late_kept, late_sent = together(got, first, *halved(kept, come), *late)
     first = over_chips(first)
-    kept, sent = halved(kept, come)
     come = swap(sent, "seq", 3 * X)
-    late = [halved(two_kept, two_got), halved(three_kept, three_got)]
-    late_kept, late_sent = (jnp.concatenate(parts, axis=0) for parts in zip(*late))
     got, late_come = together(got, swap(late_sent, "seq", X))
     late_kept, late_sent = (
         jnp.concatenate(

time: 202 us -> 192 us (0.950)
  waiting for transfers between devices: 88.8 us -> 79 us
  local copies, waits for them, and re-layouts: 4.52 us -> 8.22 us
  Pallas kernels: 22.4 us -> 20.1 us
  other arithmetic: 14.5 us -> 12.4 us
    all_to_all x1, waiting for transfers between devices: 6.77 us -> 0.01 us  [shards(): got = lax.all_to_all(sent_blocks.reshape(PEERS, 16, H), 'seq', 0, 0)]
    unnamed x28 -> x40, local copies, waits for them, and re-layouts: 0.75 us -> 5.52 us
    ppermute x44, waiting for transfers between devices: 73.9 us -> 70.8 us  [swap(): return lax.ppermute(values, axis, [(i, i ^ mask) for i in range(peers)])]
    pallas_call x17, Pallas kernels: 22.4 us -> 20.1 us  [call(): pl.pallas_call(body, out_shape=outs, in_specs=[pl.BlockSpec(memory_space=...]
  transfers between devices with their start and end apart: 47 -> 47, of which waited for: 30 -> 29; matrix products, arithmetic and copies ran while one was open for 7% -> 7% of each run, Pallas kernels for 5% -> 6%
where the time goes in v4:
time: 192 us
  waiting for transfers between devices  79 us (41%)
  starting transfers between devices  67.9 us (35%)
  Pallas kernels  20.1 us (10%)
  other arithmetic  12.4 us (6%)
  local copies, waits for them, and re-layouts  8.22 us (4%)
  matrix products  3.02 us (2%)
    ppermute x44, waiting for transfers between devices, swap(): return lax.ppermute(values, axis, [(i, i ^ mask) for i in range(peers)])  70.8 us
    ppermute x44, starting transfers between devices, swap(): return lax.ppermute(values, axis, [(i, i ^ mask) for i in range(peers)])  49.8 us
    pallas_call x17, Pallas kernels, call(): pl.pallas_call(body, out_shape=outs, in_specs=[pl.BlockSpec(memory_space=...  20.1 us
    convert_element_type x20, other arithmetic, add(): return (a.astype(F32) + b.astype(F32)).astype(BF16)  9.1 us
    all_to_all x1, starting transfers between devices, shards(): got = lax.all_to_all(sent.reshape(PEERS, 8, SHARD), 'seq', 0, 0)  8.25 us
    all_to_all x1, waiting for transfers between devices, shards(): got = lax.all_to_all(sent.reshape(PEERS, 8, SHARD), 'seq', 0, 0)  8.18 us
    unnamed x40, local copies, waits for them, and re-layouts  5.52 us
    all_to_all x1, starting transfers between devices, shards(): got = lax.all_to_all(sent_blocks.reshape(PEERS, 16, H), 'seq', 0, 0)  4.95 us
  transfers between devices with their start and end apart: 47, of which 29 were waited for; matrix products, arithmetic and copies ran while one was open for 7% of the time, Pallas kernels for 6%

profile of v4, /device:TPU:0, one launch (start us, length us, event | category | flops | bytes accessed | tf_op | source)
XLA Modules:
  0.0 191.8 jit_solution(5011040436731891693)
XLA Ops:
  0.6 2.1 %fusion.3 = bf16[32,8,384]{2,1,0:T(8,128)(2,1)} fusion(bf16[128,384]{1,0:T(8,128)(2,1)} %param.16, bf16[128,384]{1,0:T(8,128)(2,1)} %param.15, s32[256]{0:T(256)} %constant.52.clone), kind=kOutput, calls=%fused_computation.15 | convolution fusion | flops 50888704 | bytes 394240 | tf_op jit(solution)/shard_map/dot_general | solution.py:31
  2.7 8.2 %all-to-all-start = ((bf16[32,8,384]{2,1,0:T(8,128)(2,1)}), bf16[32,8,384]{2,1,0:T(8,128)(2,1)S(1)}, u32[]{:S(2)}, u32[]{:S(2)}) async-start(bf16[32,8,384]{2,1,0:T(8,128)(2,1)} %fusion.3), calls=%async_computation | async-start | bytes 393216 | tf_op jit(solution)/shard_map/all_to_all | solution.py:330
  11.0 8.2 %all-to-all-done = bf16[32,8,384]{2,1,0:T(8,128)(2,1)S(1)} async-done(((bf16[32,8,384]{2,1,0:T(8,128)(2,1)}), bf16[32,8,384]{2,1,0:T(8,128)(2,1)S(1)}, u32[]{:S(2)}, u32[]{:S(2)}) %all-to-all-start) | async-done | bytes 196640 | tf_op jit(solution)/shard_map/all_to_all | solution.py:330
  20.1 1.7 collective-permute-start
  21.8 2.2 %collective-permute-start.1 = (bf16[256,384]{1,0:T(8,128)(2,1)S(1)}, bf16[256,384]{1,0:T(8,128)(2,1)S(1)}, u32[]{:S(2)}, u32[]{:S(2)}) collective-permute-start(bf16[256,384]{1,0:T(8,128)(2,1)S(1)} %convolution_convert_fusion.own), channel_id=1, source_target_pairs={{0,3},{1,2},{2,1},{3,0},{4,7},{5,6},{6,5},{7,4},{8,11},{9,10},{10,... | collective-permute-start | bytes 589832 | tf_op jit(solution)/shard_map/ppermute | solution.py:36
  24.8 1.7 slice_bitcast_fusion.6.k_mem
  26.6 1.3 collective-permute-done.one
  27.9 4.6 %collective-permute-done.1.three = bf16[256,384]{1,0:T(8,128)(2,1)S(1)} collective-permute-done((bf16[256,384]{1,0:T(8,128)(2,1)S(1)}, bf16[256,384]{1,0:T(8,128)(2,1)S(1)}, u32[]{:S(2)}, u32[]{:S(2)}) %collective-permute-start.1) | collective-permute-done | bytes 196640 | tf_op jit(solution)/shard_map/ppermute | solution.py:36
  32.6 1.5 collective-permute-done.2.two
  35.4 2.2 %collective-permute-start.4 = (bf16[128,768]{1,0:T(8,128)(2,1)S(1)}, bf16[128,768]{1,0:T(8,128)(2,1)S(1)}, u32[]{:S(2)}, u32[]{:S(2)}) collective-permute-start(bf16[128,768]{1,0:T(8,128)(2,1)S(1)} %get-tuple-element.139), channel_id=1, source_target_pairs={{0,3},{1,2},{2,1},{3,0},{4,7},{5,6},{6,5},{7,4},{8,11},{9,10},{10,... | collective-permute-start | bytes 589832 | tf_op jit(solution)/shard_map/ppermute | solution.py:36
  37.6 4.0 %collective-permute-done.3 = bf16[128,768]{1,0:T(8,128)(2,1)S(1)} collective-permute-done((bf16[128,768]{1,0:T(8,128)(2,1)S(1)}, bf16[128,768]{1,0:T(8,128)(2,1)S(1)}, u32[]{:S(2)}, u32[]{:S(2)}) %collective-permute-start.3) | collective-permute-done | bytes 196640 | tf_op jit(solution)/shard_map/ppermute | solution.py:36
  41.6 1.3 collective-permute-done.4
  43.0 2.0 %collective-permute-start.5 = (bf16[128,768]{1,0:T(8,128)(2,1)S(1)}, bf16[128,768]{1,0:T(8,128)(2,1)S(1)}, u32[]{:S(2)}, u32[]{:S(2)}) collective-permute-start(bf16[128,768]{1,0:T(8,128)(2,1)S(1)} %add_convert_fusion.17.a), channel_id=1, source_target_pairs={{0,3},{1,2},{2,1},{3,0},{4,7},{5,6},{6,5},{7,4},{8,11},{9,10},{10,... | collective-permute-start | bytes 589832 | tf_op jit(solution)/shard_map/ppermute | solution.py:36
  45.3 5.6 %collective-permute-done.6.b2 = bf16[128,768]{1,0:T(8,128)(2,1)S(1)} collective-permute-done((bf16[128,768]{1,0:T(8,128)(2,1)S(1)}, bf16[128,768]{1,0:T(8,128)(2,1)S(1)}, u32[]{:S(2)}, u32[]{:S(2)}) %collective-permute-start.6) | collective-permute-done | bytes 196640 | tf_op jit(solution)/shard_map/ppermute | solution.py:36
  52.2 1.4 collective-permute-start.8
  54.0 3.8 %collective-permute-done.7 = bf16[128,768]{1,0:T(8,128)(2,1)S(1)} collective-permute-done((bf16[128,768]{1,0:T(8,128)(2,1)S(1)}, bf16[128,768]{1,0:T(8,128)(2,1)S(1)}, u32[]{:S(2)}, u32[]{:S(2)}) %collective-permute-start.7) | collective-permute-done | bytes 196640 | tf_op jit(solution)/shard_map/ppermute | solution.py:36
  57.9 1.3 collective-permute-done.8
  59.2 1.4 collective-permute-start.9
  60.8 1.5 collective-permute-start.10
  62.3 5.6 %collective-permute-done.10.b2 = bf16[128,768]{1,0:T(8,128)(2,1)S(1)} collective-permute-done((bf16[128,768]{1,0:T(8,128)(2,1)S(1)}, bf16[128,768]{1,0:T(8,128)(2,1)S(1)}, u32[]{:S(2)}, u32[]{:S(2)}) %collective-permute-start.10) | collective-permute-done | bytes 196640 | tf_op jit(solution)/shard_map/ppermute | solution.py:36
  69.1 2.1 %collective-permute-start.11 = (bf16[128,768]{1,0:T(8,128)(2,1)S(1)}, bf16[128,768]{1,0:T(8,128)(2,1)S(1)}, u32[]{:S(2)}, u32[]{:S(2)}) collective-permute-start(bf16[128,768]{1,0:T(8,128)(2,1)S(1)} %get-tuple-element.160), channel_id=1, source_target_pairs={{0,1},{1,0},{2,3},{3,2},{4,5},{5,4},{6,7},{7,6},{8,9},{9,8},{10,11... | collective-permute-start | bytes 589832 | tf_op jit(solution)/shard_map/ppermute | solution.py:36
  71.2 1.5 collective-permute-start.12
  73.1 3.5 %collective-permute-done.11 = bf16[128,768]{1,0:T(8,128)(2,1)S(1)} collective-permute-done((bf16[128,768]{1,0:T(8,128)(2,1)S(1)}, bf16[128,768]{1,0:T(8,128)(2,1)S(1)}, u32[]{:S(2)}, u32[]{:S(2)}) %collective-permute-start.11) | collective-permute-done | bytes 196640 | tf_op jit(solution)/shard_map/ppermute | solution.py:36
  76.7 1.4 collective-permute-done.12
  78.1 1.6 collective-permute-start.13
  80.1 5.6 %collective-permute-done.14.b2 = bf16[128,768]{1,0:T(8,128)(2,1)S(1)} collective-permute-done((bf16[128,768]{1,0:T(8,128)(2,1)S(1)}, bf16[128,768]{1,0:T(8,128)(2,1)S(1)}, u32[]{:S(2)}, u32[]{:S(2)}) %collective-permute-start.14) | collective-permute-done | bytes 196640 | tf_op jit(solution)/shard_map/ppermute | solution.py:36
  85.7 1.4 collective-permute-done.13.a2
  87.0 1.6 shard_map.169
  88.7 1.7 collective-permute-start.16
  90.8 1.3 shard_map.170
  92.2 2.1 %collective-permute-done.15 = bf16[128,768]{1,0:T(8,128)(2,1)S(1)} collective-permute-done((bf16[128,768]{1,0:T(8,128)(2,1)S(1)}, bf16[128,768]{1,0:T(8,128)(2,1)S(1)}, u32[]{:S(2)}, u32[]{:S(2)}) %collective-permute-start.15) | collective-permute-done | bytes 196640 | tf_op jit(solution)/shard_map/ppermute | solution.py:36
  94.3 1.5 collective-permute-done.16
  95.9 1.5 collective-permute-start.17
  97.7 1.4 copy-done.9
  99.1 4.1 %collective-permute-done.18.b2 = bf16[128,768]{1,0:T(8,128)(2,1)S(1)} collective-permute-done((bf16[128,768]{1,0:T(8,128)(2,1)S(1)}, bf16[128,768]{1,0:T(8,128)(2,1)S(1)}, u32[]{:S(2)}, u32[]{:S(2)}) %collective-permute-start.18) | collective-permute-done | bytes 196640 | tf_op jit(solution)/shard_map/ppermute | solution.py:36
  103.2 1.3 shard_map.171
  104.7 2.3 %collective-permute-start.21 = (bf16[128,768]{1,0:T(8,128)(2,1)S(1)}, bf16[128,768]{1,0:T(8,128)(2,1)S(1)}, u32[]{:S(2)}, u32[]{:S(2)}) collective-permute-start(bf16[128,768]{1,0:T(8,128)(2,1)S(1)} %get-tuple-element.188), channel_id=1, source_target_pairs={{0,3},{1,2},{2,1},{3,0},{4,7},{5,6},{6,5},{7,4},{8,11},{9,10},{10,... | collective-permute-start | bytes 589832 | tf_op jit(solution)/shard_map/ppermute | solution.py:36
  107.9 1.3 shard_map.172
  110.3 1.3 collective-permute-done.21
  111.7 2.3 %collective-permute-start.22 = (bf16[128,768]{1,0:T(8,128)(2,1)S(1)}, bf16[128,768]{1,0:T(8,128)(2,1)S(1)}, u32[]{:S(2)}, u32[]{:S(2)}) collective-permute-start(bf16[128,768]{1,0:T(8,128)(2,1)S(1)} %add_convert_fusion.9.a), channel_id=1, source_target_pairs={{0,3},{1,2},{2,1},{3,0},{4,7},{5,6},{6,5},{7,4},{8,11},{9,10},{10,... | collective-permute-start | bytes 589832 | tf_op jit(solution)/shard_map/ppermute | solution.py:36
  114.4 5.5 %collective-permute-done.23.b2 = bf16[128,768]{1,0:T(8,128)(2,1)S(1)} collective-permute-done((bf16[128,768]{1,0:T(8,128)(2,1)S(1)}, bf16[128,768]{1,0:T(8,128)(2,1)S(1)}, u32[]{:S(2)}, u32[]{:S(2)}) %collective-permute-start.23) | collective-permute-done | bytes 196640 | tf_op jit(solution)/shard_map/ppermute | solution.py:36
  120.7 1.3 shard_map.174
  122.3 1.8 collective-permute-start.27
  126.1 1.3 shard_map.175
  127.8 1.3 collective-permute-done.27
  129.2 1.9 %collective-permute-start.28 = (bf16[128,768]{1,0:T(8,128)(2,1)S(1)}, bf16[128,768]{1,0:T(8,128)(2,1)S(1)}, u32[]{:S(2)}, u32[]{:S(2)}) collective-permute-start(bf16[128,768]{1,0:T(8,128)(2,1)S(1)} %add_convert_fusion.7.a), channel_id=1, source_target_pairs={{0,3},{1,2},{2,1},{3,0},{4,7},{5,6},{6,5},{7,4},{8,11},{9,10},{10,... | collective-permute-start | bytes 589832 | tf_op jit(solution)/shard_map/ppermute | solution.py:36
  132.9 4.1 %collective-permute-done.29.b2 = bf16[128,768]{1,0:T(8,128)(2,1)S(1)} collective-permute-done((bf16[128,768]{1,0:T(8,128)(2,1)S(1)}, bf16[128,768]{1,0:T(8,128)(2,1)S(1)}, u32[]{:S(2)}, u32[]{:S(2)}) %collective-permute-start.29) | collective-permute-done | bytes 196640 | tf_op jit(solution)/shard_map/ppermute | solution.py:36
  138.0 1.6 collective-permute-start.33
  143.0 4.9 %all-to-all-start.1 = ((bf16[32,16,192]{2,1,0:T(8,128)(2,1)}), bf16[32,16,192]{2,1,0:T(8,128)(2,1)}, u32[]{:S(2)}, u32[]{:S(2)}) async-start(bf16[32,16,192]{2,1,0:T(8,128)(2,1)} %bitcast.39), calls=%async_computation.1 | async-start | bytes 524288 | tf_op jit(solution)/shard_map/all_to_all | solution.py:402
  150.3 1.3 shard_map.179
  153.8 1.3 collective-permute-done.35
  155.1 2.0 %add_convert_fusion.2 = (bf16[96,1536]{1,0:T(8,128)(2,1)}, bf16[96,1536]{1,0:T(8,128)(2,1)}) fusion(bf16[192,1536]{1,0:T(8,128)(2,1)} %collective-permute-done.35, bf16[192,1536]{1,0:T(8,128)(2,1)S(1)} %copy-done.1), kind=kLoop, calls=%fused_computation.22 | loop fusion | flops 1179648 | bytes 1769472 | tf_op jit(solution)/shard_map/convert_element_type | solution.py:40
  157.1 1.3 shard_map.180
  159.2 1.8 collective-permute-start.40
  161.1 4.9 %all-to-all-start.2 = ((bf16[16,24,1536]{2,1,0:T(8,128)(2,1)}), bf16[16,24,1536]{2,1,0:T(8,128)(2,1)S(1)}, u32[]{:S(2)}, u32[]{:S(2)}) async-start(bf16[16,24,1536]{2,1,0:T(8,128)(2,1)} %bitcast.19), calls=%async_computation.2 | async-start | bytes 2359296 | tf_op jit(solution)/shard_map/all_to_all | solution.py:305
  167.9 3.0 %collective-permute-start.43 = (bf16[48,1536]{1,0:T(8,128)(2,1)S(1)}, bf16[48,1536]{1,0:T(8,128)(2,1)S(1)}, u32[]{:S(2)}, u32[]{:S(2)}) collective-permute-start(bf16[48,1536]{1,0:T(8,128)(2,1)S(1)} %pad_maximum_fusion.3), channel_id=1, source_target_pairs={{0,24},{4,28},{8,16},{12,20},{16,8},{20,12},{24,0},{28,4},{32,56},... | collective-permute-start | bytes 442376 | tf_op jit(solution)/shard_map/ppermute | solution.py:36
  170.9 2.1 %collective-permute-done.40 = bf16[96,1536]{1,0:T(8,128)(2,1)} collective-permute-done((bf16[96,1536]{1,0:T(8,128)(2,1)}, bf16[96,1536]{1,0:T(8,128)(2,1)}, u32[]{:S(2)}, u32[]{:S(2)}) %collective-permute-start.40) | collective-permute-done | bytes 294944 | tf_op jit(solution)/shard_map/ppermute | solution.py:36
  174.1 1.6 collective-permute-start.41
  175.7 1.8 shard_map.181
  177.8 1.7 collective-permute-start.38
  179.5 2.2 %collective-permute-start.39 = (bf16[128,384]{1,0:T(8,128)(2,1)S(1)}, bf16[128,384]{1,0:T(8,128)(2,1)S(1)}, u32[]{:S(2)}, u32[]{:S(2)}) collective-permute-start(bf16[128,384]{1,0:T(8,128)(2,1)S(1)} %get-tuple-element.247), channel_id=1, source_target_pairs={{0,2},{1,3},{2,0},{3,1},{4,6},{5,7},{6,4},{7,5},{8,10},{9,11},{10,... | collective-permute-start | bytes 294920 | tf_op jit(solution)/shard_map/ppermute | solution.py:36
  181.7 2.3 %collective-permute-done.41 = bf16[48,1536]{1,0:T(8,128)(2,1)S(1)} collective-permute-done((bf16[48,1536]{1,0:T(8,128)(2,1)S(1)}, bf16[48,1536]{1,0:T(8,128)(2,1)S(1)}, u32[]{:S(2)}, u32[]{:S(2)}) %collective-permute-start.41) | collective-permute-done | bytes 147488 | tf_op jit(solution)/shard_map/ppermute | solution.py:36
  184.1 2.1 %collective-permute-start.42 = (bf16[24,1536]{1,0:T(8,128)(2,1)S(1)}, bf16[24,1536]{1,0:T(8,128)(2,1)S(1)}, u32[]{:S(2)}, u32[]{:S(2)}) collective-permute-start(bf16[24,1536]{1,0:T(8,128)(2,1)S(1)} %get-tuple-element.271), channel_id=1, source_target_pairs={{0,96},{4,100},{8,104},{12,108},{16,112},{20,116},{24,120},{28,124... | collective-permute-start | bytes 221192 | tf_op jit(solution)/shard_map/ppermute | solution.py:36
  187.8 2.0 %collective-permute-done.42.come = bf16[24,1536]{1,0:T(8,128)(2,1)S(1)} collective-permute-done((bf16[24,1536]{1,0:T(8,128)(2,1)S(1)}, bf16[24,1536]{1,0:T(8,128)(2,1)S(1)}, u32[]{:S(2)}, u32[]{:S(2)}) %collective-permute-start.42) | collective-permute-done | bytes 73760 | tf_op jit(solution)/shard_map/ppermute | solution.py:36
  (133 shorter events, 32.6 us)
Async XLA Ops:
  0.6 25.9 %copy-start.8 = (bf16[4,192,1536]{2,1,0:T(8,128)(2,1)S(1)}, bf16[4,192,1536]{2,1,0:T(8,128)(2,1)}, u32[]{:S(2)}) copy-start(bf16[4,192,1536]{2,1,0:T(8,128)(2,1)} %param.18) | copy-start | bytes 7077892
  2.7 16.5 %all-to-all-start = ((bf16[32,8,384]{2,1,0:T(8,128)(2,1)}), bf16[32,8,384]{2,1,0:T(8,128)(2,1)S(1)}, u32[]{:S(2)}, u32[]{:S(2)}) async-start(bf16[32,8,384]{2,1,0:T(8,128)(2,1)} %fusion.3), calls=%async_computation | async-start | bytes 393216 | tf_op jit(solution)/shard_map/all_to_all | solution.py:330
  20.1 7.8 %collective-permute-start = (bf16[256,384]{1,0:T(8,128)(2,1)S(1)}, bf16[256,384]{1,0:T(8,128)(2,1)S(1)}, u32[]{:S(2)}, u32[]{:S(2)}) collective-permute-start(bf16[256,384]{1,0:T(8,128)(2,1)S(1)} %convolution_convert_fusion.own), channel_id=1, source_target_pairs={{0,1},{1,0},{2,3},{3,2},{4,5},{5,4},{6,7},{7,6},{8,9},{9,8},{10,11... | collective-permute-start | bytes 589832 | tf_op jit(solution)/shard_map/ppermute | solution.py:36
  21.8 10.8 %collective-permute-start.1 = (bf16[256,384]{1,0:T(8,128)(2,1)S(1)}, bf16[256,384]{1,0:T(8,128)(2,1)S(1)}, u32[]{:S(2)}, u32[]{:S(2)}) collective-permute-start(bf16[256,384]{1,0:T(8,128)(2,1)S(1)} %convolution_convert_fusion.own), channel_id=1, source_target_pairs={{0,3},{1,2},{2,1},{3,0},{4,7},{5,6},{6,5},{7,4},{8,11},{9,10},{10,... | collective-permute-start | bytes 589832 | tf_op jit(solution)/shard_map/ppermute | solution.py:36
  24.0 13.6 %copy-start.13 = (s32[768]{0:T(1024)S(1)}, s32[768]{0:T(1024)}, u32[]{:S(2)}) copy-start(s32[768]{0:T(1024)} %constant.54.clone) | copy-start | bytes 9220
  24.0 13.6 %copy-start.14 = (s32[768]{0:T(1024)S(1)}, s32[768]{0:T(1024)}, u32[]{:S(2)}) copy-start(s32[768]{0:T(1024)} %constant.55.clone) | copy-start | bytes 9220
  24.0 13.6 %copy-start.15 = (s32[768]{0:T(1024)S(1)}, s32[768]{0:T(1024)}, u32[]{:S(2)}) copy-start(s32[768]{0:T(1024)} %constant.56.clone) | copy-start | bytes 9220
  24.0 13.6 %copy-start.16 = (s32[768]{0:T(1024)S(1)}, s32[768]{0:T(1024)}, u32[]{:S(2)}) copy-start(s32[768]{0:T(1024)} %constant.57.clone) | copy-start | bytes 9220
  24.0 13.6 %copy-start.17 = (s32[768]{0:T(1024)S(1)}, s32[768]{0:T(1024)}, u32[]{:S(2)}) copy-start(s32[768]{0:T(1024)} %constant.58.clone) | copy-start | bytes 9220
  24.0 10.1 %collective-permute-start.2 = (bf16[256,384]{1,0:T(8,128)(2,1)S(1)}, bf16[256,384]{1,0:T(8,128)(2,1)S(1)}, u32[]{:S(2)}, u32[]{:S(2)}) collective-permute-start(bf16[256,384]{1,0:T(8,128)(2,1)S(1)} %convolution_convert_fusion.own), channel_id=1, source_target_pairs={{0,2},{1,3},{2,0},{3,1},{4,6},{5,7},{6,4},{7,5},{8,10},{9,11},{10,... | collective-permute-start | bytes 589832 | tf_op jit(solution)/shard_map/ppermute | solution.py:36
  24.8 20.2 %copy-start.7 = (bf16[4,3,192,1536]{3,2,1,0:T(8,128)(2,1)S(1)}, bf16[4,3,192,1536]{3,2,1,0:T(8,128)(2,1)}, u32[]{:S(2)}) copy-start(bf16[4,3,192,1536]{3,2,1,0:T(8,128)(2,1)} %param.17) | copy-start | bytes 21233668
  35.2 6.4 %collective-permute-start.3 = (bf16[128,768]{1,0:T(8,128)(2,1)S(1)}, bf16[128,768]{1,0:T(8,128)(2,1)S(1)}, u32[]{:S(2)}, u32[]{:S(2)}) collective-permute-start(bf16[128,768]{1,0:T(8,128)(2,1)S(1)} %get-tuple-element.138), channel_id=1, source_target_pairs={{0,1},{1,0},{2,3},{3,2},{4,5},{5,4},{6,7},{7,6},{8,9},{9,8},{10,11... | collective-permute-start | bytes 589832 | tf_op jit(solution)/shard_map/ppermute | solution.py:36
  35.4 7.5 %collective-permute-start.4 = (bf16[128,768]{1,0:T(8,128)(2,1)S(1)}, bf16[128,768]{1,0:T(8,128)(2,1)S(1)}, u32[]{:S(2)}, u32[]{:S(2)}) collective-permute-start(bf16[128,768]{1,0:T(8,128)(2,1)S(1)} %get-tuple-element.139), channel_id=1, source_target_pairs={{0,3},{1,2},{2,1},{3,0},{4,7},{5,6},{6,5},{7,4},{8,11},{9,10},{10,... | collective-permute-start | bytes 589832 | tf_op jit(solution)/shard_map/ppermute | solution.py:36
  43.0 7.9 %collective-permute-start.5 = (bf16[128,768]{1,0:T(8,128)(2,1)S(1)}, bf16[128,768]{1,0:T(8,128)(2,1)S(1)}, u32[]{:S(2)}, u32[]{:S(2)}) collective-permute-start(bf16[128,768]{1,0:T(8,128)(2,1)S(1)} %add_convert_fusion.17.a), channel_id=1, source_target_pairs={{0,3},{1,2},{2,1},{3,0},{4,7},{5,6},{6,5},{7,4},{8,11},{9,10},{10,... | collective-permute-start | bytes 589832 | tf_op jit(solution)/shard_map/ppermute | solution.py:36
  45.1 5.7 %collective-permute-start.6 = (bf16[128,768]{1,0:T(8,128)(2,1)S(1)}, bf16[128,768]{1,0:T(8,128)(2,1)S(1)}, u32[]{:S(2)}, u32[]{:S(2)}) collective-permute-start(bf16[128,768]{1,0:T(8,128)(2,1)S(1)} %add_convert_fusion.16.b), channel_id=1, source_target_pairs={{0,1},{1,0},{2,3},{3,2},{4,5},{5,4},{6,7},{7,6},{8,9},{9,8},{10,11... | collective-permute-start | bytes 589832 | tf_op jit(solution)/shard_map/ppermute | solution.py:36
  52.1 5.7 %collective-permute-start.7 = (bf16[128,768]{1,0:T(8,128)(2,1)S(1)}, bf16[128,768]{1,0:T(8,128)(2,1)S(1)}, u32[]{:S(2)}, u32[]{:S(2)}) collective-permute-start(bf16[128,768]{1,0:T(8,128)(2,1)S(1)} %get-tuple-element.149), channel_id=1, source_target_pairs={{0,1},{1,0},{2,3},{3,2},{4,5},{5,4},{6,7},{7,6},{8,9},{9,8},{10,11... | collective-permute-start | bytes 589832 | tf_op jit(solution)/shard_map/ppermute | solution.py:36
  52.2 7.0 %collective-permute-start.8 = (bf16[128,768]{1,0:T(8,128)(2,1)S(1)}, bf16[128,768]{1,0:T(8,128)(2,1)S(1)}, u32[]{:S(2)}, u32[]{:S(2)}) collective-permute-start(bf16[128,768]{1,0:T(8,128)(2,1)S(1)} %get-tuple-element.150), channel_id=1, source_target_pairs={{0,3},{1,2},{2,1},{3,0},{4,7},{5,6},{6,5},{7,4},{8,11},{9,10},{10,... | collective-permute-start | bytes 589832 | tf_op jit(solution)/shard_map/ppermute | solution.py:36
  59.2 8.7 %collective-permute-start.9 = (bf16[128,768]{1,0:T(8,128)(2,1)S(1)}, bf16[128,768]{1,0:T(8,128)(2,1)S(1)}, u32[]{:S(2)}, u32[]{:S(2)}) collective-permute-start(bf16[128,768]{1,0:T(8,128)(2,1)S(1)} %add_convert_fusion.15.a), channel_id=1, source_target_pairs={{0,3},{1,2},{2,1},{3,0},{4,7},{5,6},{6,5},{7,4},{8,11},{9,10},{10,... | collective-permute-start | bytes 589832 | tf_op jit(solution)/shard_map/ppermute | solution.py:36
  60.8 7.1 %collective-permute-start.10 = (bf16[128,768]{1,0:T(8,128)(2,1)S(1)}, bf16[128,768]{1,0:T(8,128)(2,1)S(1)}, u32[]{:S(2)}, u32[]{:S(2)}) collective-permute-start(bf16[128,768]{1,0:T(8,128)(2,1)S(1)} %add_convert_fusion.14.b), channel_id=1, source_target_pairs={{0,1},{1,0},{2,3},{3,2},{4,5},{5,4},{6,7},{7,6},{8,9},{9,8},{10,11... | collective-permute-start | bytes 589832 | tf_op jit(solution)/shard_map/ppermute | solution.py:36
  69.1 7.5 %collective-permute-start.11 = (bf16[128,768]{1,0:T(8,128)(2,1)S(1)}, bf16[128,768]{1,0:T(8,128)(2,1)S(1)}, u32[]{:S(2)}, u32[]{:S(2)}) collective-permute-start(bf16[128,768]{1,0:T(8,128)(2,1)S(1)} %get-tuple-element.160), channel_id=1, source_target_pairs={{0,1},{1,0},{2,3},{3,2},{4,5},{5,4},{6,7},{7,6},{8,9},{9,8},{10,11... | collective-permute-start | bytes 589832 | tf_op jit(solution)/shard_map/ppermute | solution.py:36
  71.2 6.9 %collective-permute-start.12 = (bf16[128,768]{1,0:T(8,128)(2,1)S(1)}, bf16[128,768]{1,0:T(8,128)(2,1)S(1)}, u32[]{:S(2)}, u32[]{:S(2)}) collective-permute-start(bf16[128,768]{1,0:T(8,128)(2,1)S(1)} %get-tuple-element.161), channel_id=1, source_target_pairs={{0,3},{1,2},{2,1},{3,0},{4,7},{5,6},{6,5},{7,4},{8,11},{9,10},{10,... | collective-permute-start | bytes 589832 | tf_op jit(solution)/shard_map/ppermute | solution.py:36
  78.1 8.9 %collective-permute-start.13 = (bf16[128,768]{1,0:T(8,128)(2,1)S(1)}, bf16[128,768]{1,0:T(8,128)(2,1)S(1)}, u32[]{:S(2)}, u32[]{:S(2)}) collective-permute-start(bf16[128,768]{1,0:T(8,128)(2,1)S(1)} %add_convert_fusion.13.a), channel_id=1, source_target_pairs={{0,3},{1,2},{2,1},{3,0},{4,7},{5,6},{6,5},{7,4},{8,11},{9,10},{10,... | collective-permute-start | bytes 589832 | tf_op jit(solution)/shard_map/ppermute | solution.py:36
  79.9 5.7 %collective-permute-start.14 = (bf16[128,768]{1,0:T(8,128)(2,1)S(1)}, bf16[128,768]{1,0:T(8,128)(2,1)S(1)}, u32[]{:S(2)}, u32[]{:S(2)}) collective-permute-start(bf16[128,768]{1,0:T(8,128)(2,1)S(1)} %add_convert_fusion.12.b), channel_id=1, source_target_pairs={{0,1},{1,0},{2,3},{3,2},{4,5},{5,4},{6,7},{7,6},{8,9},{9,8},{10,11... | collective-permute-start | bytes 589832 | tf_op jit(solution)/shard_map/ppermute | solution.py:36
  88.6 5.7 %collective-permute-start.15 = (bf16[128,768]{1,0:T(8,128)(2,1)S(1)}, bf16[128,768]{1,0:T(8,128)(2,1)S(1)}, u32[]{:S(2)}, u32[]{:S(2)}) collective-permute-start(bf16[128,768]{1,0:T(8,128)(2,1)S(1)} %get-tuple-element.170), channel_id=1, source_target_pairs={{0,1},{1,0},{2,3},{3,2},{4,5},{5,4},{6,7},{7,6},{8,9},{9,8},{10,11... | collective-permute-start | bytes 589832 | tf_op jit(solution)/shard_map/ppermute | solution.py:36
  88.7 7.1 %collective-permute-start.16 = (bf16[128,768]{1,0:T(8,128)(2,1)S(1)}, bf16[128,768]{1,0:T(8,128)(2,1)S(1)}, u32[]{:S(2)}, u32[]{:S(2)}) collective-permute-start(bf16[128,768]{1,0:T(8,128)(2,1)S(1)} %get-tuple-element.171), channel_id=1, source_target_pairs={{0,3},{1,2},{2,1},{3,0},{4,7},{5,6},{6,5},{7,4},{8,11},{9,10},{10,... | collective-permute-start | bytes 589832 | tf_op jit(solution)/shard_map/ppermute | solution.py:36
  92.1 11.1 %collective-permute-start.19 = (bf16[384,1536]{1,0:T(8,128)(2,1)S(1)}, bf16[384,1536]{1,0:T(8,128)(2,1)S(1)}, u32[]{:S(2)}, u32[]{:S(2)}) collective-permute-start(bf16[384,1536]{1,0:T(8,128)(2,1)S(1)} %get-tuple-element.178), channel_id=1, source_target_pairs={{0,4},{4,0},{8,12},{12,8},{16,20},{20,16},{24,28},{28,24},{32,36},... | collective-permute-start | bytes 3538952 | tf_op jit(solution)/shard_map/ppermute | solution.py:36
  95.9 7.3 %collective-permute-start.17 = (bf16[128,768]{1,0:T(8,128)(2,1)S(1)}, bf16[128,768]{1,0:T(8,128)(2,1)S(1)}, u32[]{:S(2)}, u32[]{:S(2)}) collective-permute-start(bf16[128,768]{1,0:T(8,128)(2,1)S(1)} %add_convert_fusion.11.a), channel_id=1, source_target_pairs={{0,3},{1,2},{2,1},{3,0},{4,7},{5,6},{6,5},{7,4},{8,11},{9,10},{10,... | collective-permute-start | bytes 589832 | tf_op jit(solution)/shard_map/ppermute | solution.py:36
  97.4 1.7 copy-start.9
  97.4 5.8 %collective-permute-start.18 = (bf16[128,768]{1,0:T(8,128)(2,1)S(1)}, bf16[128,768]{1,0:T(8,128)(2,1)S(1)}, u32[]{:S(2)}, u32[]{:S(2)}) collective-permute-start(bf16[128,768]{1,0:T(8,128)(2,1)S(1)} %add_convert_fusion.10.b), channel_id=1, source_target_pairs={{0,1},{1,0},{2,3},{3,2},{4,5},{5,4},{6,7},{7,6},{8,9},{9,8},{10,11... | collective-permute-start | bytes 589832 | tf_op jit(solution)/shard_map/ppermute | solution.py:36
  103.2 3.8 %copy-start.19 = (s32[512]{0:T(512)S(1)}, s32[512]{0:T(512)}, u32[]{:S(2)}) copy-start(s32[512]{0:T(512)} %constant.59.clone) | copy-start | bytes 6148
  104.6 5.7 %collective-permute-start.20 = (bf16[128,768]{1,0:T(8,128)(2,1)S(1)}, bf16[128,768]{1,0:T(8,128)(2,1)S(1)}, u32[]{:S(2)}, u32[]{:S(2)}) collective-permute-start(bf16[128,768]{1,0:T(8,128)(2,1)S(1)} %get-tuple-element.187), channel_id=1, source_target_pairs={{0,1},{1,0},{2,3},{3,2},{4,5},{5,4},{6,7},{7,6},{8,9},{9,8},{10,11... | collective-permute-start | bytes 589832 | tf_op jit(solution)/shard_map/ppermute | solution.py:36
  104.7 7.0 %collective-permute-start.21 = (bf16[128,768]{1,0:T(8,128)(2,1)S(1)}, bf16[128,768]{1,0:T(8,128)(2,1)S(1)}, u32[]{:S(2)}, u32[]{:S(2)}) collective-permute-start(bf16[128,768]{1,0:T(8,128)(2,1)S(1)} %get-tuple-element.188), channel_id=1, source_target_pairs={{0,3},{1,2},{2,1},{3,0},{4,7},{5,6},{6,5},{7,4},{8,11},{9,10},{10,... | collective-permute-start | bytes 589832 | tf_op jit(solution)/shard_map/ppermute | solution.py:36
  107.4 12.5 %collective-permute-start.25 = (bf16[192,1536]{1,0:T(8,128)(2,1)S(1)}, bf16[192,1536]{1,0:T(8,128)(2,1)S(1)}, u32[]{:S(2)}, u32[]{:S(2)}) collective-permute-start(bf16[192,1536]{1,0:T(8,128)(2,1)S(1)} %get-tuple-element.197), channel_id=1, source_target_pairs={{0,32},{4,36},{8,40},{12,44},{16,48},{20,52},{24,56},{28,60},{32,0... | collective-permute-start | bytes 1769480 | tf_op jit(solution)/shard_map/ppermute | solution.py:36
  109.3 10.6 %collective-permute-start.24 = (bf16[384,1536]{1,0:T(8,128)(2,1)S(1)}, bf16[384,1536]{1,0:T(8,128)(2,1)S(1)}, u32[]{:S(2)}, u32[]{:S(2)}) collective-permute-start(bf16[384,1536]{1,0:T(8,128)(2,1)S(1)} %get-tuple-element.194), channel_id=1, source_target_pairs={{0,4},{4,0},{8,12},{12,8},{16,20},{20,16},{24,28},{28,24},{32,36},... | collective-permute-start | bytes 3538952 | tf_op jit(solution)/shard_map/ppermute | solution.py:36
  111.7 8.3 %collective-permute-start.22 = (bf16[128,768]{1,0:T(8,128)(2,1)S(1)}, bf16[128,768]{1,0:T(8,128)(2,1)S(1)}, u32[]{:S(2)}, u32[]{:S(2)}) collective-permute-start(bf16[128,768]{1,0:T(8,128)(2,1)S(1)} %add_convert_fusion.9.a), channel_id=1, source_target_pairs={{0,3},{1,2},{2,1},{3,0},{4,7},{5,6},{6,5},{7,4},{8,11},{9,10},{10,... | collective-permute-start | bytes 589832 | tf_op jit(solution)/shard_map/ppermute | solution.py:36
  114.2 5.7 %collective-permute-start.23 = (bf16[128,768]{1,0:T(8,128)(2,1)S(1)}, bf16[128,768]{1,0:T(8,128)(2,1)S(1)}, u32[]{:S(2)}, u32[]{:S(2)}) collective-permute-start(bf16[128,768]{1,0:T(8,128)(2,1)S(1)} %add_convert_fusion.8.b), channel_id=1, source_target_pairs={{0,1},{1,0},{2,3},{3,2},{4,5},{5,4},{6,7},{7,6},{8,9},{9,8},{10,11... | collective-permute-start | bytes 589832 | tf_op jit(solution)/shard_map/ppermute | solution.py:36
  120.2 16.8 %collective-permute-start.32 = (bf16[192,1536]{1,0:T(8,128)(2,1)S(1)}, bf16[192,1536]{1,0:T(8,128)(2,1)S(1)}, u32[]{:S(2)}, u32[]{:S(2)}) collective-permute-start(bf16[192,1536]{1,0:T(8,128)(2,1)S(1)} %get-tuple-element.220), channel_id=1, source_target_pairs={{0,32},{4,36},{8,40},{12,44},{16,48},{20,52},{24,56},{28,60},{32,0... | collective-permute-start | bytes 1769480 | tf_op jit(solution)/shard_map/ppermute | solution.py:36
  122.1 5.7 %collective-permute-start.26 = (bf16[128,768]{1,0:T(8,128)(2,1)S(1)}, bf16[128,768]{1,0:T(8,128)(2,1)S(1)}, u32[]{:S(2)}, u32[]{:S(2)}) collective-permute-start(bf16[128,768]{1,0:T(8,128)(2,1)S(1)} %get-tuple-element.206), channel_id=1, source_target_pairs={{0,1},{1,0},{2,3},{3,2},{4,5},{5,4},{6,7},{7,6},{8,9},{9,8},{10,11... | collective-permute-start | bytes 589832 | tf_op jit(solution)/shard_map/ppermute | solution.py:36
  122.3 6.9 %collective-permute-start.27 = (bf16[128,768]{1,0:T(8,128)(2,1)S(1)}, bf16[128,768]{1,0:T(8,128)(2,1)S(1)}, u32[]{:S(2)}, u32[]{:S(2)}) collective-permute-start(bf16[128,768]{1,0:T(8,128)(2,1)S(1)} %get-tuple-element.207), channel_id=1, source_target_pairs={{0,3},{1,2},{2,1},{3,0},{4,7},{5,6},{6,5},{7,4},{8,11},{9,10},{10,... | collective-permute-start | bytes 589832 | tf_op jit(solution)/shard_map/ppermute | solution.py:36
  124.9 7.9 %collective-permute-start.31 = (bf16[96,1536]{1,0:T(8,128)(2,1)S(1)}, bf16[96,1536]{1,0:T(8,128)(2,1)S(1)}, u32[]{:S(2)}, u32[]{:S(2)}) collective-permute-start(bf16[96,1536]{1,0:T(8,128)(2,1)S(1)} %get-tuple-element.258), channel_id=1, source_target_pairs={{0,96},{4,100},{8,104},{12,108},{16,112},{20,116},{24,120},{28,124... | collective-permute-start | bytes 884744 | tf_op jit(solution)/shard_map/ppermute | solution.py:36
  127.4 4.0 %collective-permute-start.30 = (bf16[384,1536]{1,0:T(8,128)(2,1)S(1)}, bf16[384,1536]{1,0:T(8,128)(2,1)S(1)}, u32[]{:S(2)}, u32[]{:S(2)}) collective-permute-start(bf16[384,1536]{1,0:T(8,128)(2,1)S(1)} %get-tuple-element.213), channel_id=1, source_target_pairs={{0,4},{4,0},{8,12},{12,8},{16,20},{20,16},{24,28},{28,24},{32,36},... | collective-permute-start | bytes 3538952 | tf_op jit(solution)/shard_map/ppermute | solution.py:36
  129.2 7.8 %collective-permute-start.28 = (bf16[128,768]{1,0:T(8,128)(2,1)S(1)}, bf16[128,768]{1,0:T(8,128)(2,1)S(1)}, u32[]{:S(2)}, u32[]{:S(2)}) collective-permute-start(bf16[128,768]{1,0:T(8,128)(2,1)S(1)} %add_convert_fusion.7.a), channel_id=1, source_target_pairs={{0,3},{1,2},{2,1},{3,0},{4,7},{5,6},{6,5},{7,4},{8,11},{9,10},{10,... | collective-permute-start | bytes 589832 | tf_op jit(solution)/shard_map/ppermute | solution.py:36
  131.3 5.7 %collective-permute-start.29 = (bf16[128,768]{1,0:T(8,128)(2,1)S(1)}, bf16[128,768]{1,0:T(8,128)(2,1)S(1)}, u32[]{:S(2)}, u32[]{:S(2)}) collective-permute-start(bf16[128,768]{1,0:T(8,128)(2,1)S(1)} %add_convert_fusion.6.b), channel_id=1, source_target_pairs={{0,1},{1,0},{2,3},{3,2},{4,5},{5,4},{6,7},{7,6},{8,9},{9,8},{10,11... | collective-permute-start | bytes 589832 | tf_op jit(solution)/shard_map/ppermute | solution.py:36
  132.4 5.6 %copy-start = (bf16[192,1536]{1,0:T(8,128)(2,1)}, bf16[192,1536]{1,0:T(8,128)(2,1)S(1)}, u32[]{:S(2)}) copy-start(bf16[192,1536]{1,0:T(8,128)(2,1)S(1)} %get-tuple-element.235) | copy-start | bytes 1769476
  132.9 8.7 %copy-start.11 = (bf16[96,1536]{1,0:T(8,128)(2,1)}, bf16[96,1536]{1,0:T(8,128)(2,1)S(1)}, u32[]{:S(2)}) copy-start(bf16[96,1536]{1,0:T(8,128)(2,1)S(1)} %collective-permute-done.31) | copy-start | bytes 884740
  138.0 11.2 %collective-permute-start.33 = (bf16[96,1536]{1,0:T(8,128)(2,1)}, bf16[96,1536]{1,0:T(8,128)(2,1)}, u32[]{:S(2)}, u32[]{:S(2)}) collective-permute-start(bf16[96,1536]{1,0:T(8,128)(2,1)} %get-tuple-element.256), channel_id=1, source_target_pairs={{0,96},{4,100},{8,104},{12,108},{16,112},{20,116},{24,120},{28,124... | collective-permute-start | bytes 884744 | tf_op jit(solution)/shard_map/ppermute | solution.py:36
  139.6 15.5 %collective-permute-start.35 = (bf16[192,1536]{1,0:T(8,128)(2,1)}, bf16[192,1536]{1,0:T(8,128)(2,1)}, u32[]{:S(2)}, u32[]{:S(2)}) collective-permute-start(bf16[192,1536]{1,0:T(8,128)(2,1)} %get-tuple-element.236), channel_id=1, source_target_pairs={{0,8},{4,12},{8,0},{12,4},{16,24},{20,28},{24,16},{28,20},{32,40},... | collective-permute-start | bytes 1769480 | tf_op jit(solution)/shard_map/ppermute | solution.py:36
  143.0 15.4 %all-to-all-start.1 = ((bf16[32,16,192]{2,1,0:T(8,128)(2,1)}), bf16[32,16,192]{2,1,0:T(8,128)(2,1)}, u32[]{:S(2)}, u32[]{:S(2)}) async-start(bf16[32,16,192]{2,1,0:T(8,128)(2,1)} %bitcast.39), calls=%async_computation.1 | async-start | bytes 524288 | tf_op jit(solution)/shard_map/all_to_all | solution.py:402
  148.0 3.9 %copy-start.10 = (bf16[96,1536]{1,0:T(8,128)(2,1)S(1)}, bf16[96,1536]{1,0:T(8,128)(2,1)}, u32[]{:S(2)}) copy-start(bf16[96,1536]{1,0:T(8,128)(2,1)} %get-tuple-element.255) | copy-start | bytes 884740
  149.3 1.0 copy-start.3
  150.3 4.9 %copy-start.1 = (bf16[192,1536]{1,0:T(8,128)(2,1)S(1)}, bf16[192,1536]{1,0:T(8,128)(2,1)}, u32[]{:S(2)}) copy-start(bf16[192,1536]{1,0:T(8,128)(2,1)} %copy-done) | copy-start | bytes 1769476
  151.6 5.5 %collective-permute-start.34 = (bf16[384,1536]{1,0:T(8,128)(2,1)S(1)}, bf16[384,1536]{1,0:T(8,128)(2,1)S(1)}, u32[]{:S(2)}, u32[]{:S(2)}) collective-permute-start(bf16[384,1536]{1,0:T(8,128)(2,1)S(1)} %get-tuple-element.234), channel_id=1, source_target_pairs={{0,4},{4,0},{8,12},{12,8},{16,20},{20,16},{24,28},{28,24},{32,36},... | collective-permute-start | bytes 3538952 | tf_op jit(solution)/shard_map/ppermute | solution.py:36
  157.1 1.9 %copy-start.18 = (s32[448]{0:T(512)S(1)}, s32[448]{0:T(512)}, u32[]{:S(2)}) copy-start(s32[448]{0:T(512)} %constant.60.clone) | copy-start | bytes 5380
  158.4 8.2 %collective-permute-start.36 = (bf16[96,1536]{1,0:T(8,128)(2,1)}, bf16[96,1536]{1,0:T(8,128)(2,1)}, u32[]{:S(2)}, u32[]{:S(2)}) collective-permute-start(bf16[96,1536]{1,0:T(8,128)(2,1)} %get-tuple-element.240), channel_id=1, source_target_pairs={{0,8},{4,12},{8,0},{12,4},{16,24},{20,28},{24,16},{28,20},{32,40},... | collective-permute-start | bytes 884744 | tf_op jit(solution)/shard_map/ppermute | solution.py:36
  159.2 13.7 %collective-permute-start.40 = (bf16[96,1536]{1,0:T(8,128)(2,1)}, bf16[96,1536]{1,0:T(8,128)(2,1)}, u32[]{:S(2)}, u32[]{:S(2)}) collective-permute-start(bf16[96,1536]{1,0:T(8,128)(2,1)} %get-tuple-element.250), channel_id=1, source_target_pairs={{0,24},{4,28},{8,16},{12,20},{16,8},{20,12},{24,0},{28,4},{32,56},... | collective-permute-start | bytes 884744 | tf_op jit(solution)/shard_map/ppermute | solution.py:36
  161.1 28.7 %all-to-all-start.2 = ((bf16[16,24,1536]{2,1,0:T(8,128)(2,1)}), bf16[16,24,1536]{2,1,0:T(8,128)(2,1)S(1)}, u32[]{:S(2)}, u32[]{:S(2)}) async-start(bf16[16,24,1536]{2,1,0:T(8,128)(2,1)} %bitcast.19), calls=%async_computation.2 | async-start | bytes 2359296 | tf_op jit(solution)/shard_map/all_to_all | solution.py:305
  167.9 19.2 %collective-permute-start.43 = (bf16[48,1536]{1,0:T(8,128)(2,1)S(1)}, bf16[48,1536]{1,0:T(8,128)(2,1)S(1)}, u32[]{:S(2)}, u32[]{:S(2)}) collective-permute-start(bf16[48,1536]{1,0:T(8,128)(2,1)S(1)} %pad_maximum_fusion.3), channel_id=1, source_target_pairs={{0,24},{4,28},{8,16},{12,20},{16,8},{20,12},{24,0},{28,4},{32,56},... | collective-permute-start | bytes 442376 | tf_op jit(solution)/shard_map/ppermute | solution.py:36
  174.1 12.1 %copy-start.12 = (bf16[128,384]{1,0:T(8,128)(2,1)S(1)}, bf16[128,384]{1,0:T(8,128)(2,1)}, u32[]{:S(2)}) copy-start(bf16[128,384]{1,0:T(8,128)(2,1)} %param.15) | copy-start | bytes 294916
  174.1 9.9 %collective-permute-start.41 = (bf16[48,1536]{1,0:T(8,128)(2,1)S(1)}, bf16[48,1536]{1,0:T(8,128)(2,1)S(1)}, u32[]{:S(2)}, u32[]{:S(2)}) collective-permute-start(bf16[48,1536]{1,0:T(8,128)(2,1)S(1)} %get-tuple-element.266), channel_id=1, source_target_pairs={{0,32},{4,36},{8,40},{12,44},{16,48},{20,52},{24,56},{28,60},{32,0... | collective-permute-start | bytes 442376 | tf_op jit(solution)/shard_map/ppermute | solution.py:36
  177.5 8.7 %collective-permute-start.37 = (bf16[128,384]{1,0:T(8,128)(2,1)S(1)}, bf16[128,384]{1,0:T(8,128)(2,1)S(1)}, u32[]{:S(2)}, u32[]{:S(2)}) collective-permute-start(bf16[128,384]{1,0:T(8,128)(2,1)S(1)} %get-tuple-element.245), channel_id=1, source_target_pairs={{0,1},{1,0},{2,3},{3,2},{4,5},{5,4},{6,7},{7,6},{8,9},{9,8},{10,11... | collective-permute-start | bytes 294920 | tf_op jit(solution)/shard_map/ppermute | solution.py:36
  177.8 8.4 %collective-permute-start.38 = (bf16[128,384]{1,0:T(8,128)(2,1)S(1)}, bf16[128,384]{1,0:T(8,128)(2,1)S(1)}, u32[]{:S(2)}, u32[]{:S(2)}) collective-permute-start(bf16[128,384]{1,0:T(8,128)(2,1)S(1)} %get-tuple-element.246), channel_id=1, source_target_pairs={{0,3},{1,2},{2,1},{3,0},{4,7},{5,6},{6,5},{7,4},{8,11},{9,10},{10,... | collective-permute-start | bytes 294920 | tf_op jit(solution)/shard_map/ppermute | solution.py:36
  179.5 6.7 %collective-permute-start.39 = (bf16[128,384]{1,0:T(8,128)(2,1)S(1)}, bf16[128,384]{1,0:T(8,128)(2,1)S(1)}, u32[]{:S(2)}, u32[]{:S(2)}) collective-permute-start(bf16[128,384]{1,0:T(8,128)(2,1)S(1)} %get-tuple-element.247), channel_id=1, source_target_pairs={{0,2},{1,3},{2,0},{3,1},{4,6},{5,7},{6,4},{7,5},{8,10},{9,11},{10,... | collective-permute-start | bytes 294920 | tf_op jit(solution)/shard_map/ppermute | solution.py:36
  184.1 5.6 %collective-permute-start.42 = (bf16[24,1536]{1,0:T(8,128)(2,1)S(1)}, bf16[24,1536]{1,0:T(8,128)(2,1)S(1)}, u32[]{:S(2)}, u32[]{:S(2)}) collective-permute-start(bf16[24,1536]{1,0:T(8,128)(2,1)S(1)} %get-tuple-element.271), channel_id=1, source_target_pairs={{0,96},{4,100},{8,104},{12,108},{16,112},{20,116},{24,120},{28,124... | collective-permute-start | bytes 221192 | tf_op jit(solution)/shard_map/ppermute | solution.py:36
  189.7 0.9 copy-start.6
  (3 other events, 2.1 us)

commit v5 on v4

--- a/solution.py
+++ b/solution.py
@@ -156,8 +156,7 @@
             at = slice(half * HALF, half * HALF + HALF)
             total = total_of(rows, half, (a, a2), (b, b2))
             values = g[rows, at].astype(F32) + slope(x[rows, at].astype(F32)) * total
-            if g1 is not None:
-                g1[rows, at] = values
+            g1[rows, at] = values
             grad_b[rows, at] = values.astype(BF16)
 
 
@@ -169,28 +168,30 @@
     put_halves(conv_back(values.astype(F32), k_mem, 2**layer), ta, tb)
 
 
-def final_kernel(me, g, a, b, a2, b2, x, inner, order, p_mem, *rest):
-    grad_b, inner_grad, sent = rest
-    retreat(g, a, b, a2, b2, x, None, grad_b)
+def final_kernel(me, g, a, b, a2, b2, x, first, inner, k_mem, p_mem, *rest):
+    grad_b, inner_grad, own, one, three, two, base, rate, term, g1 = rest
+    retreat(g, a, b, a2, b2, x, g1, grad_b)
+    at = pl.ds(pl.multiple_of(me[0] * SHARD, 128), SHARD)
+    rate[...] = slope(first[:, at].astype(F32))
     values = backward_of(inner[...], grad_b[...], p_mem)
     inner_grad[...] = values
-    own = grad_b[:, pl.ds(pl.multiple_of(me[0] * SHARD, 128), SHARD)]
-    parts = jnp.concatenate([values, own[:, :H], own[:, H:]], axis=0)
-    sent[...] = dot(order[...], parts).astype(BF16)
-
-
-def last_kernel(me, got, order, k_mem, *rest):
-    own, one, three, two, g, term = rest
-    values = dot(order[...], got[...])
-    moved = values.astype(BF16)
-    g[:, :H] = values[192:320]
-    g[:, H:] = values[320:448]
-    out = dot(moved[64:192], k_mem[0])
-    out = out + dot(moved[32:160], k_mem[1])
-    term[...] = out + dot(moved[:128], k_mem[2])
+    term[...] = conv_back(values.astype(F32), k_mem, 1)
     for mask, ref in ((0, own), (1, one), (3, three), (2, two)):
         at = pl.ds(pl.multiple_of((me[0] ^ mask) * SHARD, 128), SHARD)
         ref[...] = term[:, at].astype(ref.dtype)
+    base[...] = g1[:, pl.ds(pl.multiple_of(me[0] * SHARD, 128), SHARD)]
+
+
+def pack_kernel(own, one, three, two, base, rate, order, keep, send):
+    total = own[...]
+    for ref in (one, three, two):
+        total = total + ref[...].astype(F32)
+    values = (base[...] + rate[...] * total).astype(BF16)
+    values = dot(order[...], values).astype(BF16)
+    for part, ref in enumerate((keep, send)):
+        for t in range(4):
+            rows = slice(32 * t + 16 * part, 32 * t + 16 * part + 16)
+            ref[:, t * SHARD : (t + 1) * SHARD] = values[rows]
 
 
 def weight_kernel(distance, inner_grad, inner, x, grad_b, table, keep, send):
@@ -229,13 +230,29 @@
     )
 
 
-def sums_kernel(first, kept, come, late_kept, late_come, kernel_out, point_out):
+def exchange_kernel(kept, other, mine, sibling, out):
+    total = kept[...].astype(F32) + other[...].astype(F32)
+    mine, sibling = mine[...].astype(F32), sibling[...].astype(F32)
+    for chip in range(16):
+        parts = [total[24 * chip : 24 * chip + 24], mine[chip : chip + 1], sibling[chip : chip + 1]]
+        out[chip] = jnp.concatenate([*parts, jnp.zeros((6, C), F32)], axis=0).astype(BF16)
+
+
+def sums_kernel(first, kept, come, late_kept, late_come, order, gradient, kernel_out, point_out):
     total = first[0].astype(F32)
+    ends = [total[24:]]
     for i in range(1, 16):
-        total = total + first[i].astype(F32)
+        part = first[i].astype(F32)
+        ends.append(part[24:])
+        total = total + part
+    ends = [jnp.concatenate([e[n : n + 1] for e in ends], axis=0) for n in (0, 1)]
+    ends = jnp.concatenate(ends, axis=0).astype(BF16)
+    for t in range(4):
+        rows = slice(32 * t, 32 * t + 32)
+        gradient[rows] = dot(order[...], ends[:, t * SHARD : (t + 1) * SHARD])
     second = kept[...].astype(F32) + come[...].astype(F32)
     late = late_kept[...].astype(F32) + late_come[...].astype(F32)
-    layers = (total, second, late[:24], late[24:])
+    layers = (total[:24], second, late[:24], late[24:])
     for row in range(24):
         values = jnp.concatenate([v[row : row + 1] for v in layers], axis=0)
         if row < 18:
@@ -281,18 +298,14 @@
 
 
 def residue_to_block():
-    n = np.arange(512)
-    s, t = n // 16, n % 16
-    a = 4 * s + t - 1
-    grad = np.where((t < 6) & (a >= 0) & (a < 128), a, -1)
-    half = 128 + (t - 6) // 4 * 128 + 4 * s + (t - 6) % 4
-    go = np.where(t < 6, grad, np.where(t < 14, half, -1))
-    n = np.arange(448)
-    m = n - 192
-    come = np.where(
-        n < 192, n % 32 * 16 + n // 32, m % 32 * 16 + 6 + m // 128 * 4 + m % 128 // 32
-    )
-    return table_of(go, 384), table_of(come, 512)
+    core = lax.axis_index("seq") % 2
+    n = np.arange(32)
+    device = jnp.asarray(2 * (n % 16), jnp.int32) + (core ^ jnp.asarray(n // 16, jnp.int32))
+    go = (4 * device[None] + jnp.arange(4, dtype=jnp.int32)[:, None]).reshape(128)
+    (go, device) = together(go, device)
+    go = lax.broadcasted_iota(jnp.int32, (128, 128), 1) == go[:, None]
+    come = lax.broadcasted_iota(jnp.int32, (32, 32), 0) == device[None]
+    return go.astype(BF16), come.astype(BF16)
 
 
 def halved(kept, come):
@@ -302,15 +315,17 @@
 
 def over_chips(values):
     groups = [[2 * i + core for i in range(PEERS // 2)] for core in (0, 1)]
-    return lax.all_to_all(
-        values.reshape(16, 24, values.shape[1]), "seq", 0, 0, axis_index_groups=groups
-    )
+    return lax.all_to_all(values, "seq", 0, 0, axis_index_groups=groups)
 
 
 def sum_mp(a, b, load, first=(), second=()):
-    a1, b1, *first = together(swap(a, "mp", 1), swap(b, "mp", 3), *first)
+    a1, b1 = swap(a, "mp", 1), swap(b, "mp", 3)
+    if first:
+        a1, b1, *first = together(a1, b1, *first)
+    else:
+        _, b1 = together(a1, b1)
     a, b = add(a, a1), add(b, b1)
-    loaded = load(a)
+    loaded = load(a) if first else load(a, b)
     a2, b2, *rest = together(swap(a, "mp", 3), swap(b, "mp", 1), *second, *loaded)
     return (a, b, a2, b2), rest[len(second) :], first, rest[: len(second)]
 
@@ -319,8 +334,8 @@
     me = lax.axis_index("mp").astype(jnp.int32)[None]
 
     def weights(layer):
-        def load(after):
-            _, kernels, points = together(after, conv_kernels, point_weights)
+        def load(*after):
+            *_, kernels, points = together(*after, conv_kernels, point_weights)
             return kernels[layer], points[layer]
 
         return load
@@ -392,24 +407,37 @@
                 (g, *terms, above, inner, *loaded),
             )
     two_kept, two_sent = halved(two_kept, two_got)
-    grad_b, inner_grad, sent_blocks = call(
+    piece, wide = struct((ROWS, SHARD), BF16), struct((ROWS, SHARD), F32)
+    grad_b, inner_grad, own, *pieces, base, rate = call(
         final_kernel,
-        [full, hid, struct((512, H), BF16)],
+        [full, hid, wide, piece, piece, piece, wide, wide],
+        [pltpu.VMEM((ROWS, C), F32), pltpu.VMEM((ROWS, C), F32)],
+        (me, g, *terms, above, x, inner, *loaded),
+        {0: pltpu.SMEM},
+    )
+    come = swap(sent, "seq", X)
+    pieces = [swap(s, "mp", mask) for s, mask in zip(pieces, (1, 3, 2))]
+    two_got = swap(two_sent, "seq", 3 * Z)
+    keep, send = weight_terms(0, tables[0], inner_grad, inner, x, grad_b)
+    other = swap(send, "seq", 1)
+    mine, send = call(
+        pack_kernel,
+        [struct((16, C), BF16)] * 2,
         [],
-        (me, g, *terms, above, inner, block_go, loaded[1]),
-        {0: pltpu.SMEM},
-    )
-    got = lax.all_to_all(sent_blocks.reshape(PEERS, 16, H), "seq", 0, 0)
-    come = swap(sent, "seq", X)
-    inner_grad, two_got = together(inner_grad, swap(two_sent, "seq", 3 * Z))
-    keep, send = weight_terms(0, tables[0], inner_grad, inner, x, grad_b)
-    (first,) = merge(keep, swap(send, "seq", 1), 1)
+        (own, *pieces, base, rate, block_go),
+        flops=1e7,
+    )
     late = [halved(two_kept, two_got), halved(three_kept, three_got)]
     late = [jnp.concatenate(parts, axis=0) for parts in zip(*late)]
-    got, first, kept, sent, late_kept, late_sent = together(got, first, *halved(kept, come), *late)
+    sibling = swap(send, "seq", 1)
+    kept, sent = halved(kept, come)
+    late_kept, late_sent = late
+    first = call(
+        exchange_kernel, [struct((16, 32, C), BF16)], [], (keep, other, mine, sibling), flops=1e7
+    )[0]
     first = over_chips(first)
     come = swap(sent, "seq", 3 * X)
-    got, late_come = together(got, swap(late_sent, "seq", X))
+    late_come = swap(late_sent, "seq", X)
     late_kept, late_sent = (
         jnp.concatenate(
             [add(late_kept[n : n + 24], late_come[n : n + 24]) for n in (at, at + 48)], axis=0
@@ -417,27 +445,15 @@
         for at in (0, 24)
     )
     late_come = swap(late_sent, "seq", 3 * X)
-    piece = struct((ROWS, SHARD), BF16)
-    total, one, three, two, gradient = call(
-        last_kernel,
-        [struct((ROWS, SHARD), F32), piece, piece, piece, struct((ROWS, SHARD), F32)],
-        [pltpu.VMEM((ROWS, C), F32)],
-        (me, got.reshape(512, H), block_come, loaded[0]),
-        {0: pltpu.SMEM},
-    )
-    got = [swap(s, "mp", mask) for s, mask in ((one, 1), (three, 3), (two, 2))]
-    for s in got:
-        total = total + s.astype(F32)
-    gradient = gradient + slope(inputs.astype(F32)) * total
     kept, sent = halved(kept, come)
     come = swap(sent, "seq", Z)
     kept, sent = halved(kept, come)
     come = swap(sent, "seq", 3 * Z)
-    kernel_grad, point_grad = call(
+    gradient, kernel_grad, point_grad = call(
         sums_kernel,
-        [struct((3, 6, LAYERS, C), F32), struct((6, LAYERS, C), F32)],
+        [wide, struct((3, 6, LAYERS, C), F32), struct((6, LAYERS, C), F32)],
         [],
-        (first, kept, come, late_kept, late_come),
+        (first, kept, come, late_kept, late_come, block_come),
         flops=1e7,
     )
     return gradient, kernel_grad.transpose(2, 0, 1, 3), point_grad.transpose(1, 0, 2)

time: 192 us -> 188 us (0.979)
  waiting for transfers between devices: 79 us -> 99.4 us
  starting transfers between devices: 67.9 us -> 58.8 us
  other arithmetic: 12.4 us -> 4.15 us
  local copies, waits for them, and re-layouts: 8.22 us -> 2.8 us
    ppermute x44 -> x45, waiting for transfers between devices: 70.8 us -> 92.7 us  [swap(): return lax.ppermute(values, axis, [(i, i ^ mask) for i in range(peers)])]
    convert_element_type x20, other arithmetic: 9.1 us -> 1.33 us  [add(): return (a.astype(F32) + b.astype(F32)).astype(BF16)]
    all_to_all x2 -> x1, starting transfers between devices: 9.9 us -> 3.92 us  [over_chips(): return lax.all_to_all(values, 'seq', 0, 0, axis_index_groups=groups)]
    unnamed x40 -> x4, local copies, waits for them, and re-layouts: 5.52 us -> 0.01 us
    ppermute x44 -> x45, starting transfers between devices: 49.8 us -> 46.6 us  [swap(): return lax.ppermute(values, axis, [(i, i ^ mask) for i in range(peers)])]
  transfers between devices with their start and end apart: 47 -> 47, of which waited for: 29 -> 34; matrix products, arithmetic and copies ran while one was open for 7% -> 4% of each run, Pallas kernels for 6% -> 6%
where the time goes in v5:
time: 188 us
  waiting for transfers between devices  99.4 us (53%)
  starting transfers between devices  58.8 us (31%)
  Pallas kernels  18.6 us (10%)
  other arithmetic  4.15 us (2%)
  matrix products  2.87 us (2%)
  local copies, waits for them, and re-layouts  2.8 us (1%)
    ppermute x45, waiting for transfers between devices, swap(): return lax.ppermute(values, axis, [(i, i ^ mask) for i in range(peers)])  92.7 us
    ppermute x45, starting transfers between devices, swap(): return lax.ppermute(values, axis, [(i, i ^ mask) for i in range(peers)])  46.6 us
    pallas_call x17, Pallas kernels, call(): pl.pallas_call(body, out_shape=outs, in_specs=[pl.BlockSpec(memory_space=...  18.6 us
    all_to_all x1, starting transfers between devices, shards(): got = lax.all_to_all(sent.reshape(PEERS, 8, SHARD), 'seq', 0, 0)  8.25 us
    all_to_all x1, waiting for transfers between devices, shards(): got = lax.all_to_all(sent.reshape(PEERS, 8, SHARD), 'seq', 0, 0)  6.65 us
    all_to_all x1, starting transfers between devices, over_chips(): return lax.all_to_all(values, 'seq', 0, 0, axis_index_groups=groups)  3.92 us
  transfers between devices with their start and end apart: 47, of which 34 were waited for; matrix products, arithmetic and copies ran while one was open for 4% of the time, Pallas kernels for 6%

profile of v5, /device:TPU:0, one launch (start us, length us, event | category | flops | bytes accessed | tf_op | source)
XLA Modules:
  0.0 187.7 jit_solution(785600295386544548)
XLA Ops:
  0.6 1.9 %fusion.3 = bf16[32,8,384]{2,1,0:T(8,128)(2,1)} fusion(bf16[128,384]{1,0:T(8,128)(2,1)} %param.16, bf16[128,384]{1,0:T(8,128)(2,1)} %param.15, s32[256]{0:T(256)} %constant.46.clone), kind=kOutput, calls=%fused_computation.15 | convolution fusion | flops 50888704 | bytes 394240 | tf_op jit(solution)/shard_map/dot_general | solution.py:31
  2.5 8.2 %all-to-all-start = ((bf16[32,8,384]{2,1,0:T(8,128)(2,1)}), bf16[32,8,384]{2,1,0:T(8,128)(2,1)S(1)}, u32[]{:S(2)}, u32[]{:S(2)}) async-start(bf16[32,8,384]{2,1,0:T(8,128)(2,1)} %fusion.3), calls=%async_computation | async-start | bytes 393216 | tf_op jit(solution)/shard_map/all_to_all | solution.py:345
  12.3 6.7 %all-to-all-done = bf16[32,8,384]{2,1,0:T(8,128)(2,1)S(1)} async-done(((bf16[32,8,384]{2,1,0:T(8,128)(2,1)}), bf16[32,8,384]{2,1,0:T(8,128)(2,1)S(1)}, u32[]{:S(2)}, u32[]{:S(2)}) %all-to-all-start) | async-done | bytes 196640 | tf_op jit(solution)/shard_map/all_to_all | solution.py:345
  20.0 1.7 collective-permute-start
  21.6 2.2 %collective-permute-start.1 = (bf16[256,384]{1,0:T(8,128)(2,1)S(1)}, bf16[256,384]{1,0:T(8,128)(2,1)S(1)}, u32[]{:S(2)}, u32[]{:S(2)}) collective-permute-start(bf16[256,384]{1,0:T(8,128)(2,1)S(1)} %convolution_convert_fusion.own), channel_id=1, source_target_pairs={{0,3},{1,2},{2,1},{3,0},{4,7},{5,6},{6,5},{7,4},{8,11},{9,10},{10,... | collective-permute-start | bytes 589832 | tf_op jit(solution)/shard_map/ppermute | solution.py:36
  24.5 1.7 slice_bitcast_fusion.6.k_mem
  26.3 1.4 collective-permute-done.one
  27.8 4.6 %collective-permute-done.1.three = bf16[256,384]{1,0:T(8,128)(2,1)S(1)} collective-permute-done((bf16[256,384]{1,0:T(8,128)(2,1)S(1)}, bf16[256,384]{1,0:T(8,128)(2,1)S(1)}, u32[]{:S(2)}, u32[]{:S(2)}) %collective-permute-start.1) | collective-permute-done | bytes 196640 | tf_op jit(solution)/shard_map/ppermute | solution.py:36
  32.4 1.5 collective-permute-done.2.two
  35.2 2.2 %collective-permute-start.4 = (bf16[128,768]{1,0:T(8,128)(2,1)S(1)}, bf16[128,768]{1,0:T(8,128)(2,1)S(1)}, u32[]{:S(2)}, u32[]{:S(2)}) collective-permute-start(bf16[128,768]{1,0:T(8,128)(2,1)S(1)} %get-tuple-element.131), channel_id=1, source_target_pairs={{0,3},{1,2},{2,1},{3,0},{4,7},{5,6},{6,5},{7,4},{8,11},{9,10},{10,... | collective-permute-start | bytes 589832 | tf_op jit(solution)/shard_map/ppermute | solution.py:36
  37.9 3.6 %collective-permute-done.3 = bf16[128,768]{1,0:T(8,128)(2,1)S(1)} collective-permute-done((bf16[128,768]{1,0:T(8,128)(2,1)S(1)}, bf16[128,768]{1,0:T(8,128)(2,1)S(1)}, u32[]{:S(2)}, u32[]{:S(2)}) %collective-permute-start.3) | collective-permute-done | bytes 196640 | tf_op jit(solution)/shard_map/ppermute | solution.py:36
  41.4 1.3 collective-permute-done.4
  43.4 2.0 %collective-permute-start.5 = (bf16[128,768]{1,0:T(8,128)(2,1)S(1)}, bf16[128,768]{1,0:T(8,128)(2,1)S(1)}, u32[]{:S(2)}, u32[]{:S(2)}) collective-permute-start(bf16[128,768]{1,0:T(8,128)(2,1)S(1)} %add_convert_fusion.17.a), channel_id=1, source_target_pairs={{0,3},{1,2},{2,1},{3,0},{4,7},{5,6},{6,5},{7,4},{8,11},{9,10},{10,... | collective-permute-start | bytes 589832 | tf_op jit(solution)/shard_map/ppermute | solution.py:36
  45.5 3.0 %collective-permute-done.6.b2 = bf16[128,768]{1,0:T(8,128)(2,1)S(1)} collective-permute-done((bf16[128,768]{1,0:T(8,128)(2,1)S(1)}, bf16[128,768]{1,0:T(8,128)(2,1)S(1)}, u32[]{:S(2)}, u32[]{:S(2)}) %collective-permute-start.6) | collective-permute-done | bytes 196640 | tf_op jit(solution)/shard_map/ppermute | solution.py:36
  48.5 1.8 collective-permute-done.5.a2
  50.3 1.2 shard_map.167
  52.0 1.9 %collective-permute-start.8 = (bf16[128,768]{1,0:T(8,128)(2,1)S(1)}, bf16[128,768]{1,0:T(8,128)(2,1)S(1)}, u32[]{:S(2)}, u32[]{:S(2)}) collective-permute-start(bf16[128,768]{1,0:T(8,128)(2,1)S(1)} %get-tuple-element.141), channel_id=1, source_target_pairs={{0,3},{1,2},{2,1},{3,0},{4,7},{5,6},{6,5},{7,4},{8,11},{9,10},{10,... | collective-permute-start | bytes 589832 | tf_op jit(solution)/shard_map/ppermute | solution.py:36
  54.3 3.0 %collective-permute-done.7 = bf16[128,768]{1,0:T(8,128)(2,1)S(1)} collective-permute-done((bf16[128,768]{1,0:T(8,128)(2,1)S(1)}, bf16[128,768]{1,0:T(8,128)(2,1)S(1)}, u32[]{:S(2)}, u32[]{:S(2)}) %collective-permute-start.7) | collective-permute-done | bytes 196640 | tf_op jit(solution)/shard_map/ppermute | solution.py:36
  57.3 1.6 collective-permute-done.8
  59.5 2.1 %collective-permute-start.9 = (bf16[128,768]{1,0:T(8,128)(2,1)S(1)}, bf16[128,768]{1,0:T(8,128)(2,1)S(1)}, u32[]{:S(2)}, u32[]{:S(2)}) collective-permute-start(bf16[128,768]{1,0:T(8,128)(2,1)S(1)} %add_convert_fusion.15.a), channel_id=1, source_target_pairs={{0,3},{1,2},{2,1},{3,0},{4,7},{5,6},{6,5},{7,4},{8,11},{9,10},{10,... | collective-permute-start | bytes 589832 | tf_op jit(solution)/shard_map/ppermute | solution.py:36
  61.7 3.0 %collective-permute-done.10.b2 = bf16[128,768]{1,0:T(8,128)(2,1)S(1)} collective-permute-done((bf16[128,768]{1,0:T(8,128)(2,1)S(1)}, bf16[128,768]{1,0:T(8,128)(2,1)S(1)}, u32[]{:S(2)}, u32[]{:S(2)}) %collective-permute-start.10) | collective-permute-done | bytes 196640 | tf_op jit(solution)/shard_map/ppermute | solution.py:36
  64.7 2.0 %collective-permute-done.9.a2 = bf16[128,768]{1,0:T(8,128)(2,1)S(1)} collective-permute-done((bf16[128,768]{1,0:T(8,128)(2,1)S(1)}, bf16[128,768]{1,0:T(8,128)(2,1)S(1)}, u32[]{:S(2)}, u32[]{:S(2)}) %collective-permute-start.9) | collective-permute-done | bytes 196640 | tf_op jit(solution)/shard_map/ppermute | solution.py:36
  66.6 1.2 shard_map.168
  68.4 2.2 %collective-permute-start.12 = (bf16[128,768]{1,0:T(8,128)(2,1)S(1)}, bf16[128,768]{1,0:T(8,128)(2,1)S(1)}, u32[]{:S(2)}, u32[]{:S(2)}) collective-permute-start(bf16[128,768]{1,0:T(8,128)(2,1)S(1)} %get-tuple-element.151), channel_id=1, source_target_pairs={{0,3},{1,2},{2,1},{3,0},{4,7},{5,6},{6,5},{7,4},{8,11},{9,10},{10,... | collective-permute-start | bytes 589832 | tf_op jit(solution)/shard_map/ppermute | solution.py:36
  71.0 4.3 %collective-permute-done.11 = bf16[128,768]{1,0:T(8,128)(2,1)S(1)} collective-permute-done((bf16[128,768]{1,0:T(8,128)(2,1)S(1)}, bf16[128,768]{1,0:T(8,128)(2,1)S(1)}, u32[]{:S(2)}, u32[]{:S(2)}) %collective-permute-start.11) | collective-permute-done | bytes 196640 | tf_op jit(solution)/shard_map/ppermute | solution.py:36
  75.3 1.4 collective-permute-done.12
  77.4 2.0 %collective-permute-start.13 = (bf16[128,768]{1,0:T(8,128)(2,1)S(1)}, bf16[128,768]{1,0:T(8,128)(2,1)S(1)}, u32[]{:S(2)}, u32[]{:S(2)}) collective-permute-start(bf16[128,768]{1,0:T(8,128)(2,1)S(1)} %add_convert_fusion.13.a), channel_id=1, source_target_pairs={{0,3},{1,2},{2,1},{3,0},{4,7},{5,6},{6,5},{7,4},{8,11},{9,10},{10,... | collective-permute-start | bytes 589832 | tf_op jit(solution)/shard_map/ppermute | solution.py:36
  79.6 5.0 %collective-permute-done.14.b2 = bf16[128,768]{1,0:T(8,128)(2,1)S(1)} collective-permute-done((bf16[128,768]{1,0:T(8,128)(2,1)S(1)}, bf16[128,768]{1,0:T(8,128)(2,1)S(1)}, u32[]{:S(2)}, u32[]{:S(2)}) %collective-permute-start.14) | collective-permute-done | bytes 196640 | tf_op jit(solution)/shard_map/ppermute | solution.py:36
  84.6 1.7 collective-permute-done.13.a2
  86.3 1.6 shard_map.169
  88.2 1.8 collective-permute-start.16
  90.1 1.3 shard_map.170
  91.5 2.1 %collective-permute-done.15 = bf16[128,768]{1,0:T(8,128)(2,1)S(1)} collective-permute-done((bf16[128,768]{1,0:T(8,128)(2,1)S(1)}, bf16[128,768]{1,0:T(8,128)(2,1)S(1)}, u32[]{:S(2)}, u32[]{:S(2)}) %collective-permute-start.15) | collective-permute-done | bytes 196640 | tf_op jit(solution)/shard_map/ppermute | solution.py:36
  93.6 1.5 collective-permute-done.16
  95.1 1.9 %collective-permute-start.17 = (bf16[128,768]{1,0:T(8,128)(2,1)S(1)}, bf16[128,768]{1,0:T(8,128)(2,1)S(1)}, u32[]{:S(2)}, u32[]{:S(2)}) collective-permute-start(bf16[128,768]{1,0:T(8,128)(2,1)S(1)} %add_convert_fusion.11.a), channel_id=1, source_target_pairs={{0,3},{1,2},{2,1},{3,0},{4,7},{5,6},{6,5},{7,4},{8,11},{9,10},{10,... | collective-permute-start | bytes 589832 | tf_op jit(solution)/shard_map/ppermute | solution.py:36
  97.3 6.3 %collective-permute-done.18.b2 = bf16[128,768]{1,0:T(8,128)(2,1)S(1)} collective-permute-done((bf16[128,768]{1,0:T(8,128)(2,1)S(1)}, bf16[128,768]{1,0:T(8,128)(2,1)S(1)}, u32[]{:S(2)}, u32[]{:S(2)}) %collective-permute-start.18) | collective-permute-done | bytes 196640 | tf_op jit(solution)/shard_map/ppermute | solution.py:36
  103.6 1.3 shard_map.171
  106.4 1.2 collective-permute-start.25
  107.6 1.3 shard_map.172
  109.0 1.7 collective-permute-done.20
  110.7 1.3 collective-permute-done.21
  113.6 5.5 %collective-permute-done.23.b2 = bf16[128,768]{1,0:T(8,128)(2,1)S(1)} collective-permute-done((bf16[128,768]{1,0:T(8,128)(2,1)S(1)}, bf16[128,768]{1,0:T(8,128)(2,1)S(1)}, u32[]{:S(2)}, u32[]{:S(2)}) %collective-permute-start.23) | collective-permute-done | bytes 196640 | tf_op jit(solution)/shard_map/ppermute | solution.py:36
  120.5 1.3 shard_map.174
  122.1 1.7 collective-permute-start.27
  123.9 1.5 collective-permute-start.31
  125.4 1.3 shard_map.175
  127.6 1.4 collective-permute-done.27
  129.0 2.0 %collective-permute-start.28 = (bf16[128,768]{1,0:T(8,128)(2,1)S(1)}, bf16[128,768]{1,0:T(8,128)(2,1)S(1)}, u32[]{:S(2)}, u32[]{:S(2)}) collective-permute-start(bf16[128,768]{1,0:T(8,128)(2,1)S(1)} %add_convert_fusion.7.a), channel_id=1, source_target_pairs={{0,3},{1,2},{2,1},{3,0},{4,7},{5,6},{6,5},{7,4},{8,11},{9,10},{10,... | collective-permute-start | bytes 589832 | tf_op jit(solution)/shard_map/ppermute | solution.py:36
  131.9 5.0 %collective-permute-done.29.b2 = bf16[128,768]{1,0:T(8,128)(2,1)S(1)} collective-permute-done((bf16[128,768]{1,0:T(8,128)(2,1)S(1)}, bf16[128,768]{1,0:T(8,128)(2,1)S(1)}, u32[]{:S(2)}, u32[]{:S(2)}) %collective-permute-start.29) | collective-permute-done | bytes 196640 | tf_op jit(solution)/shard_map/ppermute | solution.py:36
  137.1 1.5 collective-permute-start.42
  139.1 1.5 shard_map.178
  141.0 1.7 collective-permute-start.35
  142.8 2.0 %collective-permute-start.36 = (bf16[128,384]{1,0:T(8,128)(2,1)S(1)}, bf16[128,384]{1,0:T(8,128)(2,1)S(1)}, u32[]{:S(2)}, u32[]{:S(2)}) collective-permute-start(bf16[128,384]{1,0:T(8,128)(2,1)S(1)} %get-tuple-element.224), channel_id=1, source_target_pairs={{0,2},{1,3},{2,0},{3,1},{4,6},{5,7},{6,4},{7,5},{8,10},{9,11},{10,... | collective-permute-start | bytes 294920 | tf_op jit(solution)/shard_map/ppermute | solution.py:36
  144.9 1.3 shard_map.179
  146.9 2.0 %collective-permute-done.36.two = bf16[128,384]{1,0:T(8,128)(2,1)S(1)} collective-permute-done((bf16[128,384]{1,0:T(8,128)(2,1)S(1)}, bf16[128,384]{1,0:T(8,128)(2,1)S(1)}, u32[]{:S(2)}, u32[]{:S(2)}) %collective-permute-start.36) | collective-permute-done | bytes 98336 | tf_op jit(solution)/shard_map/ppermute | solution.py:36
  149.3 1.4 collective-permute-start.43
  151.2 1.4 collective-permute-start.39
  152.7 1.6 shard_map.181
  154.2 3.9 %all-to-all-start.1 = ((bf16[16,32,1536]{2,1,0:T(8,128)(2,1)}), bf16[16,32,1536]{2,1,0:T(8,128)(2,1)S(1)}, u32[]{:S(2)}, u32[]{:S(2)}) async-start(bf16[16,32,1536]{2,1,0:T(8,128)(2,1)} %shard_map.181), calls=%async_computation.1 | async-start | bytes 3145728 | tf_op jit(solution)/shard_map/all_to_all | solution.py:318
  158.9 2.4 %collective-permute-done.39 = bf16[96,1536]{1,0:T(8,128)(2,1)S(1)} collective-permute-done((bf16[96,1536]{1,0:T(8,128)(2,1)S(1)}, bf16[96,1536]{1,0:T(8,128)(2,1)S(1)}, u32[]{:S(2)}, u32[]{:S(2)}) %collective-permute-start.39) | collective-permute-done | bytes 294944 | tf_op jit(solution)/shard_map/ppermute | solution.py:36
  161.7 1.8 collective-permute-start.44
  163.5 17.1 %collective-permute-done.40 = bf16[48,1536]{1,0:T(8,128)(2,1)S(1)} collective-permute-done((bf16[48,1536]{1,0:T(8,128)(2,1)S(1)}, bf16[48,1536]{1,0:T(8,128)(2,1)S(1)}, u32[]{:S(2)}, u32[]{:S(2)}) %collective-permute-start.40) | collective-permute-done | bytes 147488 | tf_op jit(solution)/shard_map/ppermute | solution.py:36
  182.2 4.0 %collective-permute-done.41.come = bf16[24,1536]{1,0:T(8,128)(2,1)S(1)} collective-permute-done((bf16[24,1536]{1,0:T(8,128)(2,1)S(1)}, bf16[24,1536]{1,0:T(8,128)(2,1)S(1)}, u32[]{:S(2)}, u32[]{:S(2)}) %collective-permute-start.41) | collective-permute-done | bytes 73760 | tf_op jit(solution)/shard_map/ppermute | solution.py:36
  186.3 1.4 shard_map.182
  (99 shorter events, 22.1 us)
Async XLA Ops:
  2.5 16.5 %all-to-all-start = ((bf16[32,8,384]{2,1,0:T(8,128)(2,1)}), bf16[32,8,384]{2,1,0:T(8,128)(2,1)S(1)}, u32[]{:S(2)}, u32[]{:S(2)}) async-start(bf16[32,8,384]{2,1,0:T(8,128)(2,1)} %fusion.3), calls=%async_computation | async-start | bytes 393216 | tf_op jit(solution)/shard_map/all_to_all | solution.py:345
  20.0 6.3 %copy-start.1 = (bf16[4,192,1536]{2,1,0:T(8,128)(2,1)S(1)}, bf16[4,192,1536]{2,1,0:T(8,128)(2,1)}, u32[]{:S(2)}) copy-start(bf16[4,192,1536]{2,1,0:T(8,128)(2,1)} %param.18) | copy-start | bytes 7077892
  20.0 7.8 %collective-permute-start = (bf16[256,384]{1,0:T(8,128)(2,1)S(1)}, bf16[256,384]{1,0:T(8,128)(2,1)S(1)}, u32[]{:S(2)}, u32[]{:S(2)}) collective-permute-start(bf16[256,384]{1,0:T(8,128)(2,1)S(1)} %convolution_convert_fusion.own), channel_id=1, source_target_pairs={{0,1},{1,0},{2,3},{3,2},{4,5},{5,4},{6,7},{7,6},{8,9},{9,8},{10,11... | collective-permute-start | bytes 589832 | tf_op jit(solution)/shard_map/ppermute | solution.py:36
  21.6 10.8 %collective-permute-start.1 = (bf16[256,384]{1,0:T(8,128)(2,1)S(1)}, bf16[256,384]{1,0:T(8,128)(2,1)S(1)}, u32[]{:S(2)}, u32[]{:S(2)}) collective-permute-start(bf16[256,384]{1,0:T(8,128)(2,1)S(1)} %convolution_convert_fusion.own), channel_id=1, source_target_pairs={{0,3},{1,2},{2,1},{3,0},{4,7},{5,6},{6,5},{7,4},{8,11},{9,10},{10,... | collective-permute-start | bytes 589832 | tf_op jit(solution)/shard_map/ppermute | solution.py:36
  23.8 10.1 %collective-permute-start.2 = (bf16[256,384]{1,0:T(8,128)(2,1)S(1)}, bf16[256,384]{1,0:T(8,128)(2,1)S(1)}, u32[]{:S(2)}, u32[]{:S(2)}) collective-permute-start(bf16[256,384]{1,0:T(8,128)(2,1)S(1)} %convolution_convert_fusion.own), channel_id=1, source_target_pairs={{0,2},{1,3},{2,0},{3,1},{4,6},{5,7},{6,4},{7,5},{8,10},{9,11},{10,... | collective-permute-start | bytes 589832 | tf_op jit(solution)/shard_map/ppermute | solution.py:36
  24.5 20.8 %copy-start = (bf16[4,3,192,1536]{3,2,1,0:T(8,128)(2,1)S(1)}, bf16[4,3,192,1536]{3,2,1,0:T(8,128)(2,1)}, u32[]{:S(2)}) copy-start(bf16[4,3,192,1536]{3,2,1,0:T(8,128)(2,1)} %param.17) | copy-start | bytes 21233668
  35.1 6.4 %collective-permute-start.3 = (bf16[128,768]{1,0:T(8,128)(2,1)S(1)}, bf16[128,768]{1,0:T(8,128)(2,1)S(1)}, u32[]{:S(2)}, u32[]{:S(2)}) collective-permute-start(bf16[128,768]{1,0:T(8,128)(2,1)S(1)} %get-tuple-element.130), channel_id=1, source_target_pairs={{0,1},{1,0},{2,3},{3,2},{4,5},{5,4},{6,7},{7,6},{8,9},{9,8},{10,11... | collective-permute-start | bytes 589832 | tf_op jit(solution)/shard_map/ppermute | solution.py:36
  35.2 7.5 %collective-permute-start.4 = (bf16[128,768]{1,0:T(8,128)(2,1)S(1)}, bf16[128,768]{1,0:T(8,128)(2,1)S(1)}, u32[]{:S(2)}, u32[]{:S(2)}) collective-permute-start(bf16[128,768]{1,0:T(8,128)(2,1)S(1)} %get-tuple-element.131), channel_id=1, source_target_pairs={{0,3},{1,2},{2,1},{3,0},{4,7},{5,6},{6,5},{7,4},{8,11},{9,10},{10,... | collective-permute-start | bytes 589832 | tf_op jit(solution)/shard_map/ppermute | solution.py:36
  42.8 5.7 %collective-permute-start.6 = (bf16[128,768]{1,0:T(8,128)(2,1)S(1)}, bf16[128,768]{1,0:T(8,128)(2,1)S(1)}, u32[]{:S(2)}, u32[]{:S(2)}) collective-permute-start(bf16[128,768]{1,0:T(8,128)(2,1)S(1)} %add_convert_fusion.16.b), channel_id=1, source_target_pairs={{0,1},{1,0},{2,3},{3,2},{4,5},{5,4},{6,7},{7,6},{8,9},{9,8},{10,11... | collective-permute-start | bytes 589832 | tf_op jit(solution)/shard_map/ppermute | solution.py:36
  43.4 7.0 %collective-permute-start.5 = (bf16[128,768]{1,0:T(8,128)(2,1)S(1)}, bf16[128,768]{1,0:T(8,128)(2,1)S(1)}, u32[]{:S(2)}, u32[]{:S(2)}) collective-permute-start(bf16[128,768]{1,0:T(8,128)(2,1)S(1)} %add_convert_fusion.17.a), channel_id=1, source_target_pairs={{0,3},{1,2},{2,1},{3,0},{4,7},{5,6},{6,5},{7,4},{8,11},{9,10},{10,... | collective-permute-start | bytes 589832 | tf_op jit(solution)/shard_map/ppermute | solution.py:36
  51.5 5.7 %collective-permute-start.7 = (bf16[128,768]{1,0:T(8,128)(2,1)S(1)}, bf16[128,768]{1,0:T(8,128)(2,1)S(1)}, u32[]{:S(2)}, u32[]{:S(2)}) collective-permute-start(bf16[128,768]{1,0:T(8,128)(2,1)S(1)} %get-tuple-element.140), channel_id=1, source_target_pairs={{0,1},{1,0},{2,3},{3,2},{4,5},{5,4},{6,7},{7,6},{8,9},{9,8},{10,11... | collective-permute-start | bytes 589832 | tf_op jit(solution)/shard_map/ppermute | solution.py:36
  52.0 6.9 %collective-permute-start.8 = (bf16[128,768]{1,0:T(8,128)(2,1)S(1)}, bf16[128,768]{1,0:T(8,128)(2,1)S(1)}, u32[]{:S(2)}, u32[]{:S(2)}) collective-permute-start(bf16[128,768]{1,0:T(8,128)(2,1)S(1)} %get-tuple-element.141), channel_id=1, source_target_pairs={{0,3},{1,2},{2,1},{3,0},{4,7},{5,6},{6,5},{7,4},{8,11},{9,10},{10,... | collective-permute-start | bytes 589832 | tf_op jit(solution)/shard_map/ppermute | solution.py:36
  58.9 5.7 %collective-permute-start.10 = (bf16[128,768]{1,0:T(8,128)(2,1)S(1)}, bf16[128,768]{1,0:T(8,128)(2,1)S(1)}, u32[]{:S(2)}, u32[]{:S(2)}) collective-permute-start(bf16[128,768]{1,0:T(8,128)(2,1)S(1)} %add_convert_fusion.14.b), channel_id=1, source_target_pairs={{0,1},{1,0},{2,3},{3,2},{4,5},{5,4},{6,7},{7,6},{8,9},{9,8},{10,11... | collective-permute-start | bytes 589832 | tf_op jit(solution)/shard_map/ppermute | solution.py:36
  59.5 7.1 %collective-permute-start.9 = (bf16[128,768]{1,0:T(8,128)(2,1)S(1)}, bf16[128,768]{1,0:T(8,128)(2,1)S(1)}, u32[]{:S(2)}, u32[]{:S(2)}) collective-permute-start(bf16[128,768]{1,0:T(8,128)(2,1)S(1)} %add_convert_fusion.15.a), channel_id=1, source_target_pairs={{0,3},{1,2},{2,1},{3,0},{4,7},{5,6},{6,5},{7,4},{8,11},{9,10},{10,... | collective-permute-start | bytes 589832 | tf_op jit(solution)/shard_map/ppermute | solution.py:36
  67.9 7.5 %collective-permute-start.11 = (bf16[128,768]{1,0:T(8,128)(2,1)S(1)}, bf16[128,768]{1,0:T(8,128)(2,1)S(1)}, u32[]{:S(2)}, u32[]{:S(2)}) collective-permute-start(bf16[128,768]{1,0:T(8,128)(2,1)S(1)} %get-tuple-element.150), channel_id=1, source_target_pairs={{0,1},{1,0},{2,3},{3,2},{4,5},{5,4},{6,7},{7,6},{8,9},{9,8},{10,11... | collective-permute-start | bytes 589832 | tf_op jit(solution)/shard_map/ppermute | solution.py:36
  68.4 8.4 %collective-permute-start.12 = (bf16[128,768]{1,0:T(8,128)(2,1)S(1)}, bf16[128,768]{1,0:T(8,128)(2,1)S(1)}, u32[]{:S(2)}, u32[]{:S(2)}) collective-permute-start(bf16[128,768]{1,0:T(8,128)(2,1)S(1)} %get-tuple-element.151), channel_id=1, source_target_pairs={{0,3},{1,2},{2,1},{3,0},{4,7},{5,6},{6,5},{7,4},{8,11},{9,10},{10,... | collective-permute-start | bytes 589832 | tf_op jit(solution)/shard_map/ppermute | solution.py:36
  76.8 7.8 %collective-permute-start.14 = (bf16[128,768]{1,0:T(8,128)(2,1)S(1)}, bf16[128,768]{1,0:T(8,128)(2,1)S(1)}, u32[]{:S(2)}, u32[]{:S(2)}) collective-permute-start(bf16[128,768]{1,0:T(8,128)(2,1)S(1)} %add_convert_fusion.12.b), channel_id=1, source_target_pairs={{0,1},{1,0},{2,3},{3,2},{4,5},{5,4},{6,7},{7,6},{8,9},{9,8},{10,11... | collective-permute-start | bytes 589832 | tf_op jit(solution)/shard_map/ppermute | solution.py:36
  77.4 8.9 %collective-permute-start.13 = (bf16[128,768]{1,0:T(8,128)(2,1)S(1)}, bf16[128,768]{1,0:T(8,128)(2,1)S(1)}, u32[]{:S(2)}, u32[]{:S(2)}) collective-permute-start(bf16[128,768]{1,0:T(8,128)(2,1)S(1)} %add_convert_fusion.13.a), channel_id=1, source_target_pairs={{0,3},{1,2},{2,1},{3,0},{4,7},{5,6},{6,5},{7,4},{8,11},{9,10},{10,... | collective-permute-start | bytes 589832 | tf_op jit(solution)/shard_map/ppermute | solution.py:36
  87.8 5.7 %collective-permute-start.15 = (bf16[128,768]{1,0:T(8,128)(2,1)S(1)}, bf16[128,768]{1,0:T(8,128)(2,1)S(1)}, u32[]{:S(2)}, u32[]{:S(2)}) collective-permute-start(bf16[128,768]{1,0:T(8,128)(2,1)S(1)} %get-tuple-element.159), channel_id=1, source_target_pairs={{0,1},{1,0},{2,3},{3,2},{4,5},{5,4},{6,7},{7,6},{8,9},{9,8},{10,11... | collective-permute-start | bytes 589832 | tf_op jit(solution)/shard_map/ppermute | solution.py:36
  88.2 6.9 %collective-permute-start.16 = (bf16[128,768]{1,0:T(8,128)(2,1)S(1)}, bf16[128,768]{1,0:T(8,128)(2,1)S(1)}, u32[]{:S(2)}, u32[]{:S(2)}) collective-permute-start(bf16[128,768]{1,0:T(8,128)(2,1)S(1)} %get-tuple-element.160), channel_id=1, source_target_pairs={{0,3},{1,2},{2,1},{3,0},{4,7},{5,6},{6,5},{7,4},{8,11},{9,10},{10,... | collective-permute-start | bytes 589832 | tf_op jit(solution)/shard_map/ppermute | solution.py:36
  91.4 12.2 %collective-permute-start.19 = (bf16[384,1536]{1,0:T(8,128)(2,1)S(1)}, bf16[384,1536]{1,0:T(8,128)(2,1)S(1)}, u32[]{:S(2)}, u32[]{:S(2)}) collective-permute-start(bf16[384,1536]{1,0:T(8,128)(2,1)S(1)} %get-tuple-element.167), channel_id=1, source_target_pairs={{0,4},{4,0},{8,12},{12,8},{16,20},{20,16},{24,28},{28,24},{32,36},... | collective-permute-start | bytes 3538952 | tf_op jit(solution)/shard_map/ppermute | solution.py:36
  95.1 8.5 %collective-permute-start.17 = (bf16[128,768]{1,0:T(8,128)(2,1)S(1)}, bf16[128,768]{1,0:T(8,128)(2,1)S(1)}, u32[]{:S(2)}, u32[]{:S(2)}) collective-permute-start(bf16[128,768]{1,0:T(8,128)(2,1)S(1)} %add_convert_fusion.11.a), channel_id=1, source_target_pairs={{0,3},{1,2},{2,1},{3,0},{4,7},{5,6},{6,5},{7,4},{8,11},{9,10},{10,... | collective-permute-start | bytes 589832 | tf_op jit(solution)/shard_map/ppermute | solution.py:36
  97.1 6.6 %collective-permute-start.18 = (bf16[128,768]{1,0:T(8,128)(2,1)S(1)}, bf16[128,768]{1,0:T(8,128)(2,1)S(1)}, u32[]{:S(2)}, u32[]{:S(2)}) collective-permute-start(bf16[128,768]{1,0:T(8,128)(2,1)S(1)} %add_convert_fusion.10.b), channel_id=1, source_target_pairs={{0,1},{1,0},{2,3},{3,2},{4,5},{5,4},{6,7},{7,6},{8,9},{9,8},{10,11... | collective-permute-start | bytes 589832 | tf_op jit(solution)/shard_map/ppermute | solution.py:36
  105.0 5.7 %collective-permute-start.20 = (bf16[128,768]{1,0:T(8,128)(2,1)S(1)}, bf16[128,768]{1,0:T(8,128)(2,1)S(1)}, u32[]{:S(2)}, u32[]{:S(2)}) collective-permute-start(bf16[128,768]{1,0:T(8,128)(2,1)S(1)} %get-tuple-element.176), channel_id=1, source_target_pairs={{0,1},{1,0},{2,3},{3,2},{4,5},{5,4},{6,7},{7,6},{8,9},{9,8},{10,11... | collective-permute-start | bytes 589832 | tf_op jit(solution)/shard_map/ppermute | solution.py:36
  105.1 7.0 %collective-permute-start.21 = (bf16[128,768]{1,0:T(8,128)(2,1)S(1)}, bf16[128,768]{1,0:T(8,128)(2,1)S(1)}, u32[]{:S(2)}, u32[]{:S(2)}) collective-permute-start(bf16[128,768]{1,0:T(8,128)(2,1)S(1)} %get-tuple-element.177), channel_id=1, source_target_pairs={{0,3},{1,2},{2,1},{3,0},{4,7},{5,6},{6,5},{7,4},{8,11},{9,10},{10,... | collective-permute-start | bytes 589832 | tf_op jit(solution)/shard_map/ppermute | solution.py:36
  106.4 12.7 %collective-permute-start.25 = (bf16[192,1536]{1,0:T(8,128)(2,1)S(1)}, bf16[192,1536]{1,0:T(8,128)(2,1)S(1)}, u32[]{:S(2)}, u32[]{:S(2)}) collective-permute-start(bf16[192,1536]{1,0:T(8,128)(2,1)S(1)} %get-tuple-element.186), channel_id=1, source_target_pairs={{0,32},{4,36},{8,40},{12,44},{16,48},{20,52},{24,56},{28,60},{32,0... | collective-permute-start | bytes 1769480 | tf_op jit(solution)/shard_map/ppermute | solution.py:36
  108.9 10.1 %collective-permute-start.24 = (bf16[384,1536]{1,0:T(8,128)(2,1)S(1)}, bf16[384,1536]{1,0:T(8,128)(2,1)S(1)}, u32[]{:S(2)}, u32[]{:S(2)}) collective-permute-start(bf16[384,1536]{1,0:T(8,128)(2,1)S(1)} %get-tuple-element.183), channel_id=1, source_target_pairs={{0,4},{4,0},{8,12},{12,8},{16,20},{20,16},{24,28},{28,24},{32,36},... | collective-permute-start | bytes 3538952 | tf_op jit(solution)/shard_map/ppermute | solution.py:36
  112.1 7.0 %collective-permute-start.22 = (bf16[128,768]{1,0:T(8,128)(2,1)S(1)}, bf16[128,768]{1,0:T(8,128)(2,1)S(1)}, u32[]{:S(2)}, u32[]{:S(2)}) collective-permute-start(bf16[128,768]{1,0:T(8,128)(2,1)S(1)} %add_convert_fusion.9.a), channel_id=1, source_target_pairs={{0,3},{1,2},{2,1},{3,0},{4,7},{5,6},{6,5},{7,4},{8,11},{9,10},{10,... | collective-permute-start | bytes 589832 | tf_op jit(solution)/shard_map/ppermute | solution.py:36
  113.3 5.7 %collective-permute-start.23 = (bf16[128,768]{1,0:T(8,128)(2,1)S(1)}, bf16[128,768]{1,0:T(8,128)(2,1)S(1)}, u32[]{:S(2)}, u32[]{:S(2)}) collective-permute-start(bf16[128,768]{1,0:T(8,128)(2,1)S(1)} %add_convert_fusion.8.b), channel_id=1, source_target_pairs={{0,1},{1,0},{2,3},{3,2},{4,5},{5,4},{6,7},{7,6},{8,9},{9,8},{10,11... | collective-permute-start | bytes 589832 | tf_op jit(solution)/shard_map/ppermute | solution.py:36
  119.4 17.6 %collective-permute-start.32 = (bf16[192,1536]{1,0:T(8,128)(2,1)S(1)}, bf16[192,1536]{1,0:T(8,128)(2,1)S(1)}, u32[]{:S(2)}, u32[]{:S(2)}) collective-permute-start(bf16[192,1536]{1,0:T(8,128)(2,1)S(1)} %get-tuple-element.209), channel_id=1, source_target_pairs={{0,32},{4,36},{8,40},{12,44},{16,48},{20,52},{24,56},{28,60},{32,0... | collective-permute-start | bytes 1769480 | tf_op jit(solution)/shard_map/ppermute | solution.py:36
  121.9 5.7 %collective-permute-start.26 = (bf16[128,768]{1,0:T(8,128)(2,1)S(1)}, bf16[128,768]{1,0:T(8,128)(2,1)S(1)}, u32[]{:S(2)}, u32[]{:S(2)}) collective-permute-start(bf16[128,768]{1,0:T(8,128)(2,1)S(1)} %get-tuple-element.195), channel_id=1, source_target_pairs={{0,1},{1,0},{2,3},{3,2},{4,5},{5,4},{6,7},{7,6},{8,9},{9,8},{10,11... | collective-permute-start | bytes 589832 | tf_op jit(solution)/shard_map/ppermute | solution.py:36
  122.1 6.9 %collective-permute-start.27 = (bf16[128,768]{1,0:T(8,128)(2,1)S(1)}, bf16[128,768]{1,0:T(8,128)(2,1)S(1)}, u32[]{:S(2)}, u32[]{:S(2)}) collective-permute-start(bf16[128,768]{1,0:T(8,128)(2,1)S(1)} %get-tuple-element.196), channel_id=1, source_target_pairs={{0,3},{1,2},{2,1},{3,0},{4,7},{5,6},{6,5},{7,4},{8,11},{9,10},{10,... | collective-permute-start | bytes 589832 | tf_op jit(solution)/shard_map/ppermute | solution.py:36
  123.9 8.0 %collective-permute-start.31 = (bf16[96,1536]{1,0:T(8,128)(2,1)S(1)}, bf16[96,1536]{1,0:T(8,128)(2,1)S(1)}, u32[]{:S(2)}, u32[]{:S(2)}) collective-permute-start(bf16[96,1536]{1,0:T(8,128)(2,1)S(1)} %get-tuple-element.242), channel_id=1, source_target_pairs={{0,96},{4,100},{8,104},{12,108},{16,112},{20,116},{24,120},{28,124... | collective-permute-start | bytes 884744 | tf_op jit(solution)/shard_map/ppermute | solution.py:36
  126.7 4.7 %collective-permute-start.30 = (bf16[384,1536]{1,0:T(8,128)(2,1)S(1)}, bf16[384,1536]{1,0:T(8,128)(2,1)S(1)}, u32[]{:S(2)}, u32[]{:S(2)}) collective-permute-start(bf16[384,1536]{1,0:T(8,128)(2,1)S(1)} %get-tuple-element.202), channel_id=1, source_target_pairs={{0,4},{4,0},{8,12},{12,8},{16,20},{20,16},{24,28},{28,24},{32,36},... | collective-permute-start | bytes 3538952 | tf_op jit(solution)/shard_map/ppermute | solution.py:36
  129.0 7.9 %collective-permute-start.28 = (bf16[128,768]{1,0:T(8,128)(2,1)S(1)}, bf16[128,768]{1,0:T(8,128)(2,1)S(1)}, u32[]{:S(2)}, u32[]{:S(2)}) collective-permute-start(bf16[128,768]{1,0:T(8,128)(2,1)S(1)} %add_convert_fusion.7.a), channel_id=1, source_target_pairs={{0,3},{1,2},{2,1},{3,0},{4,7},{5,6},{6,5},{7,4},{8,11},{9,10},{10,... | collective-permute-start | bytes 589832 | tf_op jit(solution)/shard_map/ppermute | solution.py:36
  131.2 5.7 %collective-permute-start.29 = (bf16[128,768]{1,0:T(8,128)(2,1)S(1)}, bf16[128,768]{1,0:T(8,128)(2,1)S(1)}, u32[]{:S(2)}, u32[]{:S(2)}) collective-permute-start(bf16[128,768]{1,0:T(8,128)(2,1)S(1)} %add_convert_fusion.6.b), channel_id=1, source_target_pairs={{0,1},{1,0},{2,3},{3,2},{4,5},{5,4},{6,7},{7,6},{8,9},{9,8},{10,11... | collective-permute-start | bytes 589832 | tf_op jit(solution)/shard_map/ppermute | solution.py:36
  137.1 12.1 %collective-permute-start.42 = (bf16[96,1536]{1,0:T(8,128)(2,1)S(1)}, bf16[96,1536]{1,0:T(8,128)(2,1)S(1)}, u32[]{:S(2)}, u32[]{:S(2)}) collective-permute-start(bf16[96,1536]{1,0:T(8,128)(2,1)S(1)} %get-tuple-element.240), channel_id=1, source_target_pairs={{0,96},{4,100},{8,104},{12,108},{16,112},{20,116},{24,120},{28,124... | collective-permute-start | bytes 884744 | tf_op jit(solution)/shard_map/ppermute | solution.py:36
  138.5 12.5 %collective-permute-start.38 = (bf16[192,1536]{1,0:T(8,128)(2,1)S(1)}, bf16[192,1536]{1,0:T(8,128)(2,1)S(1)}, u32[]{:S(2)}, u32[]{:S(2)}) collective-permute-start(bf16[192,1536]{1,0:T(8,128)(2,1)S(1)} %get-tuple-element.231), channel_id=1, source_target_pairs={{0,8},{4,12},{8,0},{12,4},{16,24},{20,28},{24,16},{28,20},{32,40},... | collective-permute-start | bytes 1769480 | tf_op jit(solution)/shard_map/ppermute | solution.py:36
  140.6 5.6 %collective-permute-start.34 = (bf16[128,384]{1,0:T(8,128)(2,1)S(1)}, bf16[128,384]{1,0:T(8,128)(2,1)S(1)}, u32[]{:S(2)}, u32[]{:S(2)}) collective-permute-start(bf16[128,384]{1,0:T(8,128)(2,1)S(1)} %get-tuple-element.222), channel_id=1, source_target_pairs={{0,1},{1,0},{2,3},{3,2},{4,5},{5,4},{6,7},{7,6},{8,9},{9,8},{10,11... | collective-permute-start | bytes 294920 | tf_op jit(solution)/shard_map/ppermute | solution.py:36
  141.0 5.8 %collective-permute-start.35 = (bf16[128,384]{1,0:T(8,128)(2,1)S(1)}, bf16[128,384]{1,0:T(8,128)(2,1)S(1)}, u32[]{:S(2)}, u32[]{:S(2)}) collective-permute-start(bf16[128,384]{1,0:T(8,128)(2,1)S(1)} %get-tuple-element.223), channel_id=1, source_target_pairs={{0,3},{1,2},{2,1},{3,0},{4,7},{5,6},{6,5},{7,4},{8,11},{9,10},{10,... | collective-permute-start | bytes 294920 | tf_op jit(solution)/shard_map/ppermute | solution.py:36
  142.8 6.1 %collective-permute-start.36 = (bf16[128,384]{1,0:T(8,128)(2,1)S(1)}, bf16[128,384]{1,0:T(8,128)(2,1)S(1)}, u32[]{:S(2)}, u32[]{:S(2)}) collective-permute-start(bf16[128,384]{1,0:T(8,128)(2,1)S(1)} %get-tuple-element.224), channel_id=1, source_target_pairs={{0,2},{1,3},{2,0},{3,1},{4,6},{5,7},{6,4},{7,5},{8,10},{9,11},{10,... | collective-permute-start | bytes 294920 | tf_op jit(solution)/shard_map/ppermute | solution.py:36
  146.2 6.4 %collective-permute-start.33 = (bf16[384,1536]{1,0:T(8,128)(2,1)S(1)}, bf16[384,1536]{1,0:T(8,128)(2,1)S(1)}, u32[]{:S(2)}, u32[]{:S(2)}) collective-permute-start(bf16[384,1536]{1,0:T(8,128)(2,1)S(1)} %get-tuple-element.220), channel_id=1, source_target_pairs={{0,4},{4,0},{8,12},{12,8},{16,20},{20,16},{24,28},{28,24},{32,36},... | collective-permute-start | bytes 3538952 | tf_op jit(solution)/shard_map/ppermute | solution.py:36
  149.1 3.6 %collective-permute-start.37 = (bf16[16,1536]{1,0:T(8,128)(2,1)S(1)}, bf16[16,1536]{1,0:T(8,128)(2,1)S(1)}, u32[]{:S(2)}, u32[]{:S(2)}) collective-permute-start(bf16[16,1536]{1,0:T(8,128)(2,1)S(1)} %get-tuple-element.229), channel_id=1, source_target_pairs={{0,4},{4,0},{8,12},{12,8},{16,20},{20,16},{24,28},{28,24},{32,36},... | collective-permute-start | bytes 147464 | tf_op jit(solution)/shard_map/ppermute | solution.py:36
  149.3 9.5 %collective-permute-start.43 = (bf16[96,1536]{1,0:T(8,128)(2,1)S(1)}, bf16[96,1536]{1,0:T(8,128)(2,1)S(1)}, u32[]{:S(2)}, u32[]{:S(2)}) collective-permute-start(bf16[96,1536]{1,0:T(8,128)(2,1)S(1)} %pad_maximum_fusion), channel_id=1, source_target_pairs={{0,8},{4,12},{8,0},{12,4},{16,24},{20,28},{24,16},{28,20},{32,40},... | collective-permute-start | bytes 884744 | tf_op jit(solution)/shard_map/ppermute | solution.py:36
  151.2 10.1 %collective-permute-start.39 = (bf16[96,1536]{1,0:T(8,128)(2,1)S(1)}, bf16[96,1536]{1,0:T(8,128)(2,1)S(1)}, u32[]{:S(2)}, u32[]{:S(2)}) collective-permute-start(bf16[96,1536]{1,0:T(8,128)(2,1)S(1)} %get-tuple-element.244), channel_id=1, source_target_pairs={{0,24},{4,28},{8,16},{12,20},{16,8},{20,12},{24,0},{28,4},{32,56},... | collective-permute-start | bytes 884744 | tf_op jit(solution)/shard_map/ppermute | solution.py:36
  154.2 32.0 %all-to-all-start.1 = ((bf16[16,32,1536]{2,1,0:T(8,128)(2,1)}), bf16[16,32,1536]{2,1,0:T(8,128)(2,1)S(1)}, u32[]{:S(2)}, u32[]{:S(2)}) async-start(bf16[16,32,1536]{2,1,0:T(8,128)(2,1)} %shard_map.181), calls=%async_computation.1 | async-start | bytes 3145728 | tf_op jit(solution)/shard_map/all_to_all | solution.py:318
  161.4 19.2 %collective-permute-start.40 = (bf16[48,1536]{1,0:T(8,128)(2,1)S(1)}, bf16[48,1536]{1,0:T(8,128)(2,1)S(1)}, u32[]{:S(2)}, u32[]{:S(2)}) collective-permute-start(bf16[48,1536]{1,0:T(8,128)(2,1)S(1)} %get-tuple-element.250), channel_id=1, source_target_pairs={{0,32},{4,36},{8,40},{12,44},{16,48},{20,52},{24,56},{28,60},{32,0... | collective-permute-start | bytes 442376 | tf_op jit(solution)/shard_map/ppermute | solution.py:36
  161.7 20.5 %collective-permute-start.44 = (bf16[48,1536]{1,0:T(8,128)(2,1)S(1)}, bf16[48,1536]{1,0:T(8,128)(2,1)S(1)}, u32[]{:S(2)}, u32[]{:S(2)}) collective-permute-start(bf16[48,1536]{1,0:T(8,128)(2,1)S(1)} %pad_maximum_fusion.2), channel_id=1, source_target_pairs={{0,24},{4,28},{8,16},{12,20},{16,8},{20,12},{24,0},{28,4},{32,56},... | collective-permute-start | bytes 442376 | tf_op jit(solution)/shard_map/ppermute | solution.py:36
  180.6 5.6 %collective-permute-start.41 = (bf16[24,1536]{1,0:T(8,128)(2,1)S(1)}, bf16[24,1536]{1,0:T(8,128)(2,1)S(1)}, u32[]{:S(2)}, u32[]{:S(2)}) collective-permute-start(bf16[24,1536]{1,0:T(8,128)(2,1)S(1)} %get-tuple-element.257), channel_id=1, source_target_pairs={{0,96},{4,100},{8,104},{12,108},{16,112},{20,116},{24,120},{28,124... | collective-permute-start | bytes 221192 | tf_op jit(solution)/shard_map/ppermute | solution.py:36

commit v6 on v5

--- a/solution.py
+++ b/solution.py
@@ -110,16 +110,21 @@
 
 
 def start_kernel(me, own, one, three, two, k_mem, p_mem, *rest):
-    x, g, inner, ta, tb, active = rest
+    x, inner, ta, tb, active = rest
     for mask, block in ((0, own), (1, one), (3, three), (2, two)):
         at = pl.ds(pl.multiple_of((me[0] ^ mask) * SHARD, 128), SHARD)
-        x[:, at] = block[:ROWS]
-        g[:, at] = block[ROWS:]
+        x[:, at] = block[...]
     for rows in chunks():
         active[rows] = jax.nn.gelu(x[rows].astype(F32)).astype(BF16)
     values = conv(active[...], k_mem, 1)
     inner[...] = values
     put_halves(dot(jax.nn.gelu(values).astype(BF16), p_mem[...]), ta, tb)
+
+
+def gather_kernel(me, own, one, three, two, out):
+    for mask, block in ((0, own), (1, one), (3, three), (2, two)):
+        at = pl.ds(pl.multiple_of((me[0] ^ mask) * SHARD, 128), SHARD)
+        out[:, at] = block[...]
 
 
 def forward_kernel(layer, x, a, b, a2, b2, k_mem, p_mem, *rest):
@@ -344,14 +349,15 @@
     sent = dot(go, jnp.concatenate([inputs, cotangent], axis=0)).astype(BF16)
     got = lax.all_to_all(sent.reshape(PEERS, 8, SHARD), "seq", 0, 0)
     own = dot(come, got.reshape(256, SHARD)).astype(BF16)
+    own, cotangent = own[:ROWS], own[ROWS:]
     loaded = weights(0)(own)
     one, three, two, *loaded = together(*[swap(own, "mp", mask) for mask in (1, 3, 2)], *loaded)
     full, narrow, hid = struct((ROWS, C), BF16), struct((ROWS, H), F32), struct((ROWS, H), BF16)
     half = struct((ROWS, HALF), BF16)
     scratch = [pltpu.VMEM((ROWS, C), BF16)]
-    x, g, inner, ta, tb = call(
+    x, inner, ta, tb = call(
         start_kernel,
-        [full, full, narrow, half, half],
+        [full, narrow, half, half],
         scratch,
         (me, own, one, three, two, *loaded),
         {0: pltpu.SMEM},
@@ -361,7 +367,14 @@
     tables[3] = tables[2]
     block_go, block_come = residue_to_block()
     for layer in (1, 2):
-        terms, loaded, _, _ = sum_mp(ta, tb, weights(layer))
+        second = []
+        if layer == 1:
+            cotangent, ta = together(cotangent, ta)
+            second = [swap(cotangent, "mp", mask) for mask in (1, 3, 2)]
+        terms, loaded, _, second = sum_mp(ta, tb, weights(layer), (), second)
+        if layer == 1:
+            parts = (me, cotangent, *second)
+            (g,) = call(gather_kernel, [full], [], parts, {0: pltpu.SMEM}, flops=1e6)
         x, inner, ta, tb = call(
             functools.partial(forward_kernel, layer),
             [full, narrow, half, half],

time: 188 us -> 186 us (0.989)
  waiting for transfers between devices: 99.4 us -> 90.3 us
  starting transfers between devices: 58.8 us -> 65.9 us
    ppermute x45 -> x48, waiting for transfers between devices: 92.7 us -> 83.7 us  [swap(): return lax.ppermute(values, axis, [(i, i ^ mask) for i in range(peers)])]
    ppermute x45 -> x48, starting transfers between devices: 46.6 us -> 53.9 us  [swap(): return lax.ppermute(values, axis, [(i, i ^ mask) for i in range(peers)])]
    pallas_call x17 -> x18, Pallas kernels: 18.6 us -> 18.6 us  [call(): pl.pallas_call(body, out_shape=outs, in_specs=[pl.BlockSpec(memory_space=...]
  transfers between devices with their start and end apart: 47 -> 50, of which waited for: 34 -> 36; matrix products, arithmetic and copies ran while one was open for 4% -> 4% of each run, Pallas kernels for 6% -> 6%
where the time goes in v6:
time: 186 us
  waiting for transfers between devices  90.3 us (49%)
  starting transfers between devices  65.9 us (35%)
  Pallas kernels  18.6 us (10%)
  other arithmetic  4.17 us (2%)
  matrix products  2.87 us (2%)
  local copies, waits for them, and re-layouts  2.82 us (2%)
    ppermute x48, waiting for transfers between devices, swap(): return lax.ppermute(values, axis, [(i, i ^ mask) for i in range(peers)])  83.7 us
    ppermute x48, starting transfers between devices, swap(): return lax.ppermute(values, axis, [(i, i ^ mask) for i in range(peers)])  53.9 us
    pallas_call x18, Pallas kernels, call(): pl.pallas_call(body, out_shape=outs, in_specs=[pl.BlockSpec(memory_space=...  18.6 us
    all_to_all x1, starting transfers between devices, shards(): got = lax.all_to_all(sent.reshape(PEERS, 8, SHARD), 'seq', 0, 0)  8.25 us
    all_to_all x1, waiting for transfers between devices, shards(): got = lax.all_to_all(sent.reshape(PEERS, 8, SHARD), 'seq', 0, 0)  6.65 us
    all_to_all x1, starting transfers between devices, over_chips(): return lax.all_to_all(values, 'seq', 0, 0, axis_index_groups=groups)  3.73 us
  transfers between devices with their start and end apart: 50, of which 36 were waited for; matrix products, arithmetic and copies ran while one was open for 4% of the time, Pallas kernels for 6%

profile of v6, /device:TPU:0, one launch (start us, length us, event | category | flops | bytes accessed | tf_op | source)
XLA Modules:
  0.0 185.8 jit_solution(6969344070317103431)
XLA Ops:
  0.6 1.9 %fusion.3 = bf16[32,8,384]{2,1,0:T(8,128)(2,1)} fusion(bf16[128,384]{1,0:T(8,128)(2,1)} %param.16, bf16[128,384]{1,0:T(8,128)(2,1)} %param.15, s32[256]{0:T(256)} %constant.46.clone), kind=kOutput, calls=%fused_computation.15 | convolution fusion | flops 50888704 | bytes 394240 | tf_op jit(solution)/shard_map/dot_general | solution.py:31
  2.5 8.2 %all-to-all-start = ((bf16[32,8,384]{2,1,0:T(8,128)(2,1)}), bf16[32,8,384]{2,1,0:T(8,128)(2,1)S(1)}, u32[]{:S(2)}, u32[]{:S(2)}) async-start(bf16[32,8,384]{2,1,0:T(8,128)(2,1)} %fusion.3), calls=%async_computation | async-start | bytes 393216 | tf_op jit(solution)/shard_map/all_to_all | solution.py:350
  12.3 6.7 %all-to-all-done = bf16[32,8,384]{2,1,0:T(8,128)(2,1)S(1)} async-done(((bf16[32,8,384]{2,1,0:T(8,128)(2,1)}), bf16[32,8,384]{2,1,0:T(8,128)(2,1)S(1)}, u32[]{:S(2)}, u32[]{:S(2)}) %all-to-all-start) | async-done | bytes 196640 | tf_op jit(solution)/shard_map/all_to_all | solution.py:350
  20.0 1.7 collective-permute-start
  21.7 2.2 %collective-permute-start.1 = (bf16[128,384]{1,0:T(8,128)(2,1)S(1)}, bf16[128,384]{1,0:T(8,128)(2,1)S(1)}, u32[]{:S(2)}, u32[]{:S(2)}) collective-permute-start(bf16[128,384]{1,0:T(8,128)(2,1)S(1)} %get-tuple-element.267.own), channel_id=1, source_target_pairs={{0,3},{1,2},{2,1},{3,0},{4,7},{5,6},{6,5},{7,4},{8,11},{9,10},{10,... | collective-permute-start | bytes 294920 | tf_op jit(solution)/shard_map/ppermute | solution.py:36
  24.6 1.7 slice_bitcast_fusion.6.k_mem
  26.4 1.9 %collective-permute-done.1.three = bf16[128,384]{1,0:T(8,128)(2,1)S(1)} collective-permute-done((bf16[128,384]{1,0:T(8,128)(2,1)S(1)}, bf16[128,384]{1,0:T(8,128)(2,1)S(1)}, u32[]{:S(2)}, u32[]{:S(2)}) %collective-permute-start.1) | collective-permute-done | bytes 98336 | tf_op jit(solution)/shard_map/ppermute | solution.py:36
  28.2 1.7 collective-permute-done.2.two
  31.8 1.4 collective-permute-start.5
  33.6 1.4 collective-permute-start.7
  35.0 1.3 collective-permute-start.8
  36.3 1.5 collective-permute-start.9
  38.5 2.1 %collective-permute-done.5 = bf16[128,768]{1,0:T(8,128)(2,1)S(1)} collective-permute-done((bf16[128,768]{1,0:T(8,128)(2,1)S(1)}, bf16[128,768]{1,0:T(8,128)(2,1)S(1)}, u32[]{:S(2)}, u32[]{:S(2)}) %collective-permute-start.5) | collective-permute-done | bytes 196640 | tf_op jit(solution)/shard_map/ppermute | solution.py:36
  40.8 2.1 %collective-permute-start.4 = (bf16[128,768]{1,0:T(8,128)(2,1)S(1)}, bf16[128,768]{1,0:T(8,128)(2,1)S(1)}, u32[]{:S(2)}, u32[]{:S(2)}) collective-permute-start(bf16[128,768]{1,0:T(8,128)(2,1)S(1)} %add_convert_fusion.17.a), channel_id=1, source_target_pairs={{0,3},{1,2},{2,1},{3,0},{4,7},{5,6},{6,5},{7,4},{8,11},{9,10},{10,... | collective-permute-start | bytes 589832 | tf_op jit(solution)/shard_map/ppermute | solution.py:36
  43.9 2.5 %collective-permute-done.6.b2 = bf16[128,768]{1,0:T(8,128)(2,1)S(1)} collective-permute-done((bf16[128,768]{1,0:T(8,128)(2,1)S(1)}, bf16[128,768]{1,0:T(8,128)(2,1)S(1)}, u32[]{:S(2)}, u32[]{:S(2)}) %collective-permute-start.6) | collective-permute-done | bytes 196640 | tf_op jit(solution)/shard_map/ppermute | solution.py:36
  46.4 1.4 collective-permute-done.4.a2
  49.8 2.0 %collective-permute-start.11 = (bf16[128,768]{1,0:T(8,128)(2,1)S(1)}, bf16[128,768]{1,0:T(8,128)(2,1)S(1)}, u32[]{:S(2)}, u32[]{:S(2)}) collective-permute-start(bf16[128,768]{1,0:T(8,128)(2,1)S(1)} %get-tuple-element.149), channel_id=1, source_target_pairs={{0,3},{1,2},{2,1},{3,0},{4,7},{5,6},{6,5},{7,4},{8,11},{9,10},{10,... | collective-permute-start | bytes 589832 | tf_op jit(solution)/shard_map/ppermute | solution.py:36
  52.2 2.8 %collective-permute-done.10 = bf16[128,768]{1,0:T(8,128)(2,1)S(1)} collective-permute-done((bf16[128,768]{1,0:T(8,128)(2,1)S(1)}, bf16[128,768]{1,0:T(8,128)(2,1)S(1)}, u32[]{:S(2)}, u32[]{:S(2)}) %collective-permute-start.10) | collective-permute-done | bytes 196640 | tf_op jit(solution)/shard_map/ppermute | solution.py:36
  55.0 2.6 %collective-permute-done.11 = bf16[128,768]{1,0:T(8,128)(2,1)S(1)} collective-permute-done((bf16[128,768]{1,0:T(8,128)(2,1)S(1)}, bf16[128,768]{1,0:T(8,128)(2,1)S(1)}, u32[]{:S(2)}, u32[]{:S(2)}) %collective-permute-start.11) | collective-permute-done | bytes 196640 | tf_op jit(solution)/shard_map/ppermute | solution.py:36
  57.8 2.4 %collective-permute-start.12 = (bf16[128,768]{1,0:T(8,128)(2,1)S(1)}, bf16[128,768]{1,0:T(8,128)(2,1)S(1)}, u32[]{:S(2)}, u32[]{:S(2)}) collective-permute-start(bf16[128,768]{1,0:T(8,128)(2,1)S(1)} %add_convert_fusion.15.a), channel_id=1, source_target_pairs={{0,3},{1,2},{2,1},{3,0},{4,7},{5,6},{6,5},{7,4},{8,11},{9,10},{10,... | collective-permute-start | bytes 589832 | tf_op jit(solution)/shard_map/ppermute | solution.py:36
  60.3 3.9 %collective-permute-done.13.b2 = bf16[128,768]{1,0:T(8,128)(2,1)S(1)} collective-permute-done((bf16[128,768]{1,0:T(8,128)(2,1)S(1)}, bf16[128,768]{1,0:T(8,128)(2,1)S(1)}, u32[]{:S(2)}, u32[]{:S(2)}) %collective-permute-start.13) | collective-permute-done | bytes 196640 | tf_op jit(solution)/shard_map/ppermute | solution.py:36
  64.2 1.4 collective-permute-done.12.a2
  65.7 1.2 shard_map.169
  66.9 1.3 collective-permute-start.14
  68.2 2.6 %collective-permute-start.15 = (bf16[128,768]{1,0:T(8,128)(2,1)S(1)}, bf16[128,768]{1,0:T(8,128)(2,1)S(1)}, u32[]{:S(2)}, u32[]{:S(2)}) collective-permute-start(bf16[128,768]{1,0:T(8,128)(2,1)S(1)} %get-tuple-element.159), channel_id=1, source_target_pairs={{0,3},{1,2},{2,1},{3,0},{4,7},{5,6},{6,5},{7,4},{8,11},{9,10},{10,... | collective-permute-start | bytes 589832 | tf_op jit(solution)/shard_map/ppermute | solution.py:36
  71.2 2.4 %collective-permute-done.14 = bf16[128,768]{1,0:T(8,128)(2,1)S(1)} collective-permute-done((bf16[128,768]{1,0:T(8,128)(2,1)S(1)}, bf16[128,768]{1,0:T(8,128)(2,1)S(1)}, u32[]{:S(2)}, u32[]{:S(2)}) %collective-permute-start.14) | collective-permute-done | bytes 196640 | tf_op jit(solution)/shard_map/ppermute | solution.py:36
  73.6 2.0 %collective-permute-done.15 = bf16[128,768]{1,0:T(8,128)(2,1)S(1)} collective-permute-done((bf16[128,768]{1,0:T(8,128)(2,1)S(1)}, bf16[128,768]{1,0:T(8,128)(2,1)S(1)}, u32[]{:S(2)}, u32[]{:S(2)}) %collective-permute-start.15) | collective-permute-done | bytes 196640 | tf_op jit(solution)/shard_map/ppermute | solution.py:36
  75.9 2.5 %collective-permute-start.16 = (bf16[128,768]{1,0:T(8,128)(2,1)S(1)}, bf16[128,768]{1,0:T(8,128)(2,1)S(1)}, u32[]{:S(2)}, u32[]{:S(2)}) collective-permute-start(bf16[128,768]{1,0:T(8,128)(2,1)S(1)} %add_convert_fusion.13.a), channel_id=1, source_target_pairs={{0,3},{1,2},{2,1},{3,0},{4,7},{5,6},{6,5},{7,4},{8,11},{9,10},{10,... | collective-permute-start | bytes 589832 | tf_op jit(solution)/shard_map/ppermute | solution.py:36
  78.6 4.1 %collective-permute-done.17.b2 = bf16[128,768]{1,0:T(8,128)(2,1)S(1)} collective-permute-done((bf16[128,768]{1,0:T(8,128)(2,1)S(1)}, bf16[128,768]{1,0:T(8,128)(2,1)S(1)}, u32[]{:S(2)}, u32[]{:S(2)}) %collective-permute-start.17) | collective-permute-done | bytes 196640 | tf_op jit(solution)/shard_map/ppermute | solution.py:36
  82.7 1.4 collective-permute-done.16.a2
  84.1 1.6 shard_map.170
  86.1 2.0 %collective-permute-start.19 = (bf16[128,768]{1,0:T(8,128)(2,1)S(1)}, bf16[128,768]{1,0:T(8,128)(2,1)S(1)}, u32[]{:S(2)}, u32[]{:S(2)}) collective-permute-start(bf16[128,768]{1,0:T(8,128)(2,1)S(1)} %get-tuple-element.168), channel_id=1, source_target_pairs={{0,3},{1,2},{2,1},{3,0},{4,7},{5,6},{6,5},{7,4},{8,11},{9,10},{10,... | collective-permute-start | bytes 589832 | tf_op jit(solution)/shard_map/ppermute | solution.py:36
  88.1 1.3 shard_map.171
  89.5 1.9 collective-permute-done.18
  91.4 1.6 collective-permute-done.19
  93.0 2.0 %collective-permute-start.20 = (bf16[128,768]{1,0:T(8,128)(2,1)S(1)}, bf16[128,768]{1,0:T(8,128)(2,1)S(1)}, u32[]{:S(2)}, u32[]{:S(2)}) collective-permute-start(bf16[128,768]{1,0:T(8,128)(2,1)S(1)} %add_convert_fusion.11.a), channel_id=1, source_target_pairs={{0,3},{1,2},{2,1},{3,0},{4,7},{5,6},{6,5},{7,4},{8,11},{9,10},{10,... | collective-permute-start | bytes 589832 | tf_op jit(solution)/shard_map/ppermute | solution.py:36
  95.4 6.4 %collective-permute-done.21.b2 = bf16[128,768]{1,0:T(8,128)(2,1)S(1)} collective-permute-done((bf16[128,768]{1,0:T(8,128)(2,1)S(1)}, bf16[128,768]{1,0:T(8,128)(2,1)S(1)}, u32[]{:S(2)}, u32[]{:S(2)}) %collective-permute-start.21) | collective-permute-done | bytes 196640 | tf_op jit(solution)/shard_map/ppermute | solution.py:36
  101.8 1.3 shard_map.172
  104.7 1.3 shard_map.173
  106.2 2.7 %collective-permute-done.23 = bf16[128,768]{1,0:T(8,128)(2,1)S(1)} collective-permute-done((bf16[128,768]{1,0:T(8,128)(2,1)S(1)}, bf16[128,768]{1,0:T(8,128)(2,1)S(1)}, u32[]{:S(2)}, u32[]{:S(2)}) %collective-permute-start.23) | collective-permute-done | bytes 196640 | tf_op jit(solution)/shard_map/ppermute | solution.py:36
  108.8 1.3 collective-permute-done.24
  111.3 5.5 %collective-permute-done.26.b2 = bf16[128,768]{1,0:T(8,128)(2,1)S(1)} collective-permute-done((bf16[128,768]{1,0:T(8,128)(2,1)S(1)}, bf16[128,768]{1,0:T(8,128)(2,1)S(1)}, u32[]{:S(2)}, u32[]{:S(2)}) %collective-permute-start.26) | collective-permute-done | bytes 196640 | tf_op jit(solution)/shard_map/ppermute | solution.py:36
  118.4 1.3 shard_map.175
  120.2 2.0 %collective-permute-start.30 = (bf16[128,768]{1,0:T(8,128)(2,1)S(1)}, bf16[128,768]{1,0:T(8,128)(2,1)S(1)}, u32[]{:S(2)}, u32[]{:S(2)}) collective-permute-start(bf16[128,768]{1,0:T(8,128)(2,1)S(1)} %get-tuple-element.204), channel_id=1, source_target_pairs={{0,3},{1,2},{2,1},{3,0},{4,7},{5,6},{6,5},{7,4},{8,11},{9,10},{10,... | collective-permute-start | bytes 589832 | tf_op jit(solution)/shard_map/ppermute | solution.py:36
  122.4 1.6 collective-permute-start.34
  124.0 1.3 shard_map.176
  125.5 1.6 collective-permute-done.30
  127.1 2.1 %collective-permute-start.31 = (bf16[128,768]{1,0:T(8,128)(2,1)S(1)}, bf16[128,768]{1,0:T(8,128)(2,1)S(1)}, u32[]{:S(2)}, u32[]{:S(2)}) collective-permute-start(bf16[128,768]{1,0:T(8,128)(2,1)S(1)} %add_convert_fusion.7.a), channel_id=1, source_target_pairs={{0,3},{1,2},{2,1},{3,0},{4,7},{5,6},{6,5},{7,4},{8,11},{9,10},{10,... | collective-permute-start | bytes 589832 | tf_op jit(solution)/shard_map/ppermute | solution.py:36
  130.6 4.6 %collective-permute-done.32.b2 = bf16[128,768]{1,0:T(8,128)(2,1)S(1)} collective-permute-done((bf16[128,768]{1,0:T(8,128)(2,1)S(1)}, bf16[128,768]{1,0:T(8,128)(2,1)S(1)}, u32[]{:S(2)}, u32[]{:S(2)}) %collective-permute-start.32) | collective-permute-done | bytes 196640 | tf_op jit(solution)/shard_map/ppermute | solution.py:36
  135.3 1.4 collective-permute-start.45
  137.3 1.5 shard_map.179
  139.1 2.1 %collective-permute-start.38 = (bf16[128,384]{1,0:T(8,128)(2,1)S(1)}, bf16[128,384]{1,0:T(8,128)(2,1)S(1)}, u32[]{:S(2)}, u32[]{:S(2)}) collective-permute-start(bf16[128,384]{1,0:T(8,128)(2,1)S(1)} %get-tuple-element.231), channel_id=1, source_target_pairs={{0,3},{1,2},{2,1},{3,0},{4,7},{5,6},{6,5},{7,4},{8,11},{9,10},{10,... | collective-permute-start | bytes 294920 | tf_op jit(solution)/shard_map/ppermute | solution.py:36
  141.2 1.7 collective-permute-start.39
  143.1 1.3 shard_map.180
  145.4 2.0 %collective-permute-done.39.two = bf16[128,384]{1,0:T(8,128)(2,1)S(1)} collective-permute-done((bf16[128,384]{1,0:T(8,128)(2,1)S(1)}, bf16[128,384]{1,0:T(8,128)(2,1)S(1)}, u32[]{:S(2)}, u32[]{:S(2)}) %collective-permute-start.39) | collective-permute-done | bytes 98336 | tf_op jit(solution)/shard_map/ppermute | solution.py:36
  147.8 1.4 collective-permute-start.46
  149.7 1.5 collective-permute-start.42
  151.2 1.5 shard_map.182
  152.7 3.7 %all-to-all-start.1 = ((bf16[16,32,1536]{2,1,0:T(8,128)(2,1)}), bf16[16,32,1536]{2,1,0:T(8,128)(2,1)S(1)}, u32[]{:S(2)}, u32[]{:S(2)}) async-start(bf16[16,32,1536]{2,1,0:T(8,128)(2,1)} %shard_map.182), calls=%async_computation.1 | async-start | bytes 3145728 | tf_op jit(solution)/shard_map/all_to_all | solution.py:323
  157.3 5.5 %collective-permute-done.42 = bf16[96,1536]{1,0:T(8,128)(2,1)S(1)} collective-permute-done((bf16[96,1536]{1,0:T(8,128)(2,1)S(1)}, bf16[96,1536]{1,0:T(8,128)(2,1)S(1)}, u32[]{:S(2)}, u32[]{:S(2)}) %collective-permute-start.42) | collective-permute-done | bytes 294944 | tf_op jit(solution)/shard_map/ppermute | solution.py:36
  163.1 4.3 %collective-permute-start.47 = (bf16[48,1536]{1,0:T(8,128)(2,1)S(1)}, bf16[48,1536]{1,0:T(8,128)(2,1)S(1)}, u32[]{:S(2)}, u32[]{:S(2)}) collective-permute-start(bf16[48,1536]{1,0:T(8,128)(2,1)S(1)} %pad_maximum_fusion.2), channel_id=1, source_target_pairs={{0,24},{4,28},{8,16},{12,20},{16,8},{20,12},{24,0},{28,4},{32,56},... | collective-permute-start | bytes 442376 | tf_op jit(solution)/shard_map/ppermute | solution.py:36
  167.3 11.3 %collective-permute-done.43 = bf16[48,1536]{1,0:T(8,128)(2,1)S(1)} collective-permute-done((bf16[48,1536]{1,0:T(8,128)(2,1)S(1)}, bf16[48,1536]{1,0:T(8,128)(2,1)S(1)}, u32[]{:S(2)}, u32[]{:S(2)}) %collective-permute-start.43) | collective-permute-done | bytes 147488 | tf_op jit(solution)/shard_map/ppermute | solution.py:36
  180.2 4.2 %collective-permute-done.44.come = bf16[24,1536]{1,0:T(8,128)(2,1)S(1)} collective-permute-done((bf16[24,1536]{1,0:T(8,128)(2,1)S(1)}, bf16[24,1536]{1,0:T(8,128)(2,1)S(1)}, u32[]{:S(2)}, u32[]{:S(2)}) %collective-permute-start.44) | collective-permute-done | bytes 73760 | tf_op jit(solution)/shard_map/ppermute | solution.py:36
  184.4 1.4 shard_map.183
  (107 shorter events, 24.1 us)
Async XLA Ops:
  2.5 16.5 %all-to-all-start = ((bf16[32,8,384]{2,1,0:T(8,128)(2,1)}), bf16[32,8,384]{2,1,0:T(8,128)(2,1)S(1)}, u32[]{:S(2)}, u32[]{:S(2)}) async-start(bf16[32,8,384]{2,1,0:T(8,128)(2,1)} %fusion.3), calls=%async_computation | async-start | bytes 393216 | tf_op jit(solution)/shard_map/all_to_all | solution.py:350
  20.0 6.3 %copy-start.1 = (bf16[4,192,1536]{2,1,0:T(8,128)(2,1)S(1)}, bf16[4,192,1536]{2,1,0:T(8,128)(2,1)}, u32[]{:S(2)}) copy-start(bf16[4,192,1536]{2,1,0:T(8,128)(2,1)} %param.18) | copy-start | bytes 7077892
  20.0 6.4 %collective-permute-start = (bf16[128,384]{1,0:T(8,128)(2,1)S(1)}, bf16[128,384]{1,0:T(8,128)(2,1)S(1)}, u32[]{:S(2)}, u32[]{:S(2)}) collective-permute-start(bf16[128,384]{1,0:T(8,128)(2,1)S(1)} %get-tuple-element.267.own), channel_id=1, source_target_pairs={{0,1},{1,0},{2,3},{3,2},{4,5},{5,4},{6,7},{7,6},{8,9},{9,8},{10,11... | collective-permute-start | bytes 294920 | tf_op jit(solution)/shard_map/ppermute | solution.py:36
  21.7 6.6 %collective-permute-start.1 = (bf16[128,384]{1,0:T(8,128)(2,1)S(1)}, bf16[128,384]{1,0:T(8,128)(2,1)S(1)}, u32[]{:S(2)}, u32[]{:S(2)}) collective-permute-start(bf16[128,384]{1,0:T(8,128)(2,1)S(1)} %get-tuple-element.267.own), channel_id=1, source_target_pairs={{0,3},{1,2},{2,1},{3,0},{4,7},{5,6},{6,5},{7,4},{8,11},{9,10},{10,... | collective-permute-start | bytes 294920 | tf_op jit(solution)/shard_map/ppermute | solution.py:36
  23.8 6.1 %collective-permute-start.2 = (bf16[128,384]{1,0:T(8,128)(2,1)S(1)}, bf16[128,384]{1,0:T(8,128)(2,1)S(1)}, u32[]{:S(2)}, u32[]{:S(2)}) collective-permute-start(bf16[128,384]{1,0:T(8,128)(2,1)S(1)} %get-tuple-element.267.own), channel_id=1, source_target_pairs={{0,2},{1,3},{2,0},{3,1},{4,6},{5,7},{6,4},{7,5},{8,10},{9,11},{10,... | collective-permute-start | bytes 294920 | tf_op jit(solution)/shard_map/ppermute | solution.py:36
  24.6 18.3 %copy-start = (bf16[4,3,192,1536]{3,2,1,0:T(8,128)(2,1)S(1)}, bf16[4,3,192,1536]{3,2,1,0:T(8,128)(2,1)}, u32[]{:S(2)}) copy-start(bf16[4,3,192,1536]{3,2,1,0:T(8,128)(2,1)} %param.17) | copy-start | bytes 21233668
  31.1 7.4 %collective-permute-start.3 = (bf16[128,768]{1,0:T(8,128)(2,1)S(1)}, bf16[128,768]{1,0:T(8,128)(2,1)S(1)}, u32[]{:S(2)}, u32[]{:S(2)}) collective-permute-start(bf16[128,768]{1,0:T(8,128)(2,1)S(1)} %get-tuple-element.134), channel_id=1, source_target_pairs={{0,1},{1,0},{2,3},{3,2},{4,5},{5,4},{6,7},{7,6},{8,9},{9,8},{10,11... | collective-permute-start | bytes 589832 | tf_op jit(solution)/shard_map/ppermute | solution.py:36
  31.8 8.7 %collective-permute-start.5 = (bf16[128,768]{1,0:T(8,128)(2,1)S(1)}, bf16[128,768]{1,0:T(8,128)(2,1)S(1)}, u32[]{:S(2)}, u32[]{:S(2)}) collective-permute-start(bf16[128,768]{1,0:T(8,128)(2,1)S(1)} %get-tuple-element.135), channel_id=1, source_target_pairs={{0,3},{1,2},{2,1},{3,0},{4,7},{5,6},{6,5},{7,4},{8,11},{9,10},{10,... | collective-permute-start | bytes 589832 | tf_op jit(solution)/shard_map/ppermute | solution.py:36
  33.6 9.4 %collective-permute-start.7 = (bf16[128,384]{1,0:T(8,128)(2,1)S(1)}, bf16[128,384]{1,0:T(8,128)(2,1)S(1)}, u32[]{:S(2)}, u32[]{:S(2)}) collective-permute-start(bf16[128,384]{1,0:T(8,128)(2,1)S(1)} %get-tuple-element.133.own), channel_id=1, source_target_pairs={{0,1},{1,0},{2,3},{3,2},{4,5},{5,4},{6,7},{7,6},{8,9},{9,8},{10,11... | collective-permute-start | bytes 294920 | tf_op jit(solution)/shard_map/ppermute | solution.py:36
  35.0 8.5 %collective-permute-start.8 = (bf16[128,384]{1,0:T(8,128)(2,1)S(1)}, bf16[128,384]{1,0:T(8,128)(2,1)S(1)}, u32[]{:S(2)}, u32[]{:S(2)}) collective-permute-start(bf16[128,384]{1,0:T(8,128)(2,1)S(1)} %get-tuple-element.133.own), channel_id=1, source_target_pairs={{0,3},{1,2},{2,1},{3,0},{4,7},{5,6},{6,5},{7,4},{8,11},{9,10},{10,... | collective-permute-start | bytes 294920 | tf_op jit(solution)/shard_map/ppermute | solution.py:36
  36.3 7.6 %collective-permute-start.9 = (bf16[128,384]{1,0:T(8,128)(2,1)S(1)}, bf16[128,384]{1,0:T(8,128)(2,1)S(1)}, u32[]{:S(2)}, u32[]{:S(2)}) collective-permute-start(bf16[128,384]{1,0:T(8,128)(2,1)S(1)} %get-tuple-element.133.own), channel_id=1, source_target_pairs={{0,2},{1,3},{2,0},{3,1},{4,6},{5,7},{6,4},{7,5},{8,10},{9,11},{10,... | collective-permute-start | bytes 294920 | tf_op jit(solution)/shard_map/ppermute | solution.py:36
  40.6 5.7 %collective-permute-start.6 = (bf16[128,768]{1,0:T(8,128)(2,1)S(1)}, bf16[128,768]{1,0:T(8,128)(2,1)S(1)}, u32[]{:S(2)}, u32[]{:S(2)}) collective-permute-start(bf16[128,768]{1,0:T(8,128)(2,1)S(1)} %add_convert_fusion.16.b), channel_id=1, source_target_pairs={{0,1},{1,0},{2,3},{3,2},{4,5},{5,4},{6,7},{7,6},{8,9},{9,8},{10,11... | collective-permute-start | bytes 589832 | tf_op jit(solution)/shard_map/ppermute | solution.py:36
  40.8 7.0 %collective-permute-start.4 = (bf16[128,768]{1,0:T(8,128)(2,1)S(1)}, bf16[128,768]{1,0:T(8,128)(2,1)S(1)}, u32[]{:S(2)}, u32[]{:S(2)}) collective-permute-start(bf16[128,768]{1,0:T(8,128)(2,1)S(1)} %add_convert_fusion.17.a), channel_id=1, source_target_pairs={{0,3},{1,2},{2,1},{3,0},{4,7},{5,6},{6,5},{7,4},{8,11},{9,10},{10,... | collective-permute-start | bytes 589832 | tf_op jit(solution)/shard_map/ppermute | solution.py:36
  48.9 6.1 %collective-permute-start.10 = (bf16[128,768]{1,0:T(8,128)(2,1)S(1)}, bf16[128,768]{1,0:T(8,128)(2,1)S(1)}, u32[]{:S(2)}, u32[]{:S(2)}) collective-permute-start(bf16[128,768]{1,0:T(8,128)(2,1)S(1)} %get-tuple-element.148), channel_id=1, source_target_pairs={{0,1},{1,0},{2,3},{3,2},{4,5},{5,4},{6,7},{7,6},{8,9},{9,8},{10,11... | collective-permute-start | bytes 589832 | tf_op jit(solution)/shard_map/ppermute | solution.py:36
  49.8 7.8 %collective-permute-start.11 = (bf16[128,768]{1,0:T(8,128)(2,1)S(1)}, bf16[128,768]{1,0:T(8,128)(2,1)S(1)}, u32[]{:S(2)}, u32[]{:S(2)}) collective-permute-start(bf16[128,768]{1,0:T(8,128)(2,1)S(1)} %get-tuple-element.149), channel_id=1, source_target_pairs={{0,3},{1,2},{2,1},{3,0},{4,7},{5,6},{6,5},{7,4},{8,11},{9,10},{10,... | collective-permute-start | bytes 589832 | tf_op jit(solution)/shard_map/ppermute | solution.py:36
  57.6 6.6 %collective-permute-start.13 = (bf16[128,768]{1,0:T(8,128)(2,1)S(1)}, bf16[128,768]{1,0:T(8,128)(2,1)S(1)}, u32[]{:S(2)}, u32[]{:S(2)}) collective-permute-start(bf16[128,768]{1,0:T(8,128)(2,1)S(1)} %add_convert_fusion.14.b), channel_id=1, source_target_pairs={{0,1},{1,0},{2,3},{3,2},{4,5},{5,4},{6,7},{7,6},{8,9},{9,8},{10,11... | collective-permute-start | bytes 589832 | tf_op jit(solution)/shard_map/ppermute | solution.py:36
  57.8 7.9 %collective-permute-start.12 = (bf16[128,768]{1,0:T(8,128)(2,1)S(1)}, bf16[128,768]{1,0:T(8,128)(2,1)S(1)}, u32[]{:S(2)}, u32[]{:S(2)}) collective-permute-start(bf16[128,768]{1,0:T(8,128)(2,1)S(1)} %add_convert_fusion.15.a), channel_id=1, source_target_pairs={{0,3},{1,2},{2,1},{3,0},{4,7},{5,6},{6,5},{7,4},{8,11},{9,10},{10,... | collective-permute-start | bytes 589832 | tf_op jit(solution)/shard_map/ppermute | solution.py:36
  66.9 6.7 %collective-permute-start.14 = (bf16[128,768]{1,0:T(8,128)(2,1)S(1)}, bf16[128,768]{1,0:T(8,128)(2,1)S(1)}, u32[]{:S(2)}, u32[]{:S(2)}) collective-permute-start(bf16[128,768]{1,0:T(8,128)(2,1)S(1)} %get-tuple-element.158), channel_id=1, source_target_pairs={{0,1},{1,0},{2,3},{3,2},{4,5},{5,4},{6,7},{7,6},{8,9},{9,8},{10,11... | collective-permute-start | bytes 589832 | tf_op jit(solution)/shard_map/ppermute | solution.py:36
  68.2 7.5 %collective-permute-start.15 = (bf16[128,768]{1,0:T(8,128)(2,1)S(1)}, bf16[128,768]{1,0:T(8,128)(2,1)S(1)}, u32[]{:S(2)}, u32[]{:S(2)}) collective-permute-start(bf16[128,768]{1,0:T(8,128)(2,1)S(1)} %get-tuple-element.159), channel_id=1, source_target_pairs={{0,3},{1,2},{2,1},{3,0},{4,7},{5,6},{6,5},{7,4},{8,11},{9,10},{10,... | collective-permute-start | bytes 589832 | tf_op jit(solution)/shard_map/ppermute | solution.py:36
  75.7 7.0 %collective-permute-start.17 = (bf16[128,768]{1,0:T(8,128)(2,1)S(1)}, bf16[128,768]{1,0:T(8,128)(2,1)S(1)}, u32[]{:S(2)}, u32[]{:S(2)}) collective-permute-start(bf16[128,768]{1,0:T(8,128)(2,1)S(1)} %add_convert_fusion.12.b), channel_id=1, source_target_pairs={{0,1},{1,0},{2,3},{3,2},{4,5},{5,4},{6,7},{7,6},{8,9},{9,8},{10,11... | collective-permute-start | bytes 589832 | tf_op jit(solution)/shard_map/ppermute | solution.py:36
  75.9 8.2 %collective-permute-start.16 = (bf16[128,768]{1,0:T(8,128)(2,1)S(1)}, bf16[128,768]{1,0:T(8,128)(2,1)S(1)}, u32[]{:S(2)}, u32[]{:S(2)}) collective-permute-start(bf16[128,768]{1,0:T(8,128)(2,1)S(1)} %add_convert_fusion.13.a), channel_id=1, source_target_pairs={{0,3},{1,2},{2,1},{3,0},{4,7},{5,6},{6,5},{7,4},{8,11},{9,10},{10,... | collective-permute-start | bytes 589832 | tf_op jit(solution)/shard_map/ppermute | solution.py:36
  85.7 5.7 %collective-permute-start.18 = (bf16[128,768]{1,0:T(8,128)(2,1)S(1)}, bf16[128,768]{1,0:T(8,128)(2,1)S(1)}, u32[]{:S(2)}, u32[]{:S(2)}) collective-permute-start(bf16[128,768]{1,0:T(8,128)(2,1)S(1)} %get-tuple-element.167), channel_id=1, source_target_pairs={{0,1},{1,0},{2,3},{3,2},{4,5},{5,4},{6,7},{7,6},{8,9},{9,8},{10,11... | collective-permute-start | bytes 589832 | tf_op jit(solution)/shard_map/ppermute | solution.py:36
  86.1 6.9 %collective-permute-start.19 = (bf16[128,768]{1,0:T(8,128)(2,1)S(1)}, bf16[128,768]{1,0:T(8,128)(2,1)S(1)}, u32[]{:S(2)}, u32[]{:S(2)}) collective-permute-start(bf16[128,768]{1,0:T(8,128)(2,1)S(1)} %get-tuple-element.168), channel_id=1, source_target_pairs={{0,3},{1,2},{2,1},{3,0},{4,7},{5,6},{6,5},{7,4},{8,11},{9,10},{10,... | collective-permute-start | bytes 589832 | tf_op jit(solution)/shard_map/ppermute | solution.py:36
  89.5 12.3 %collective-permute-start.22 = (bf16[384,1536]{1,0:T(8,128)(2,1)S(1)}, bf16[384,1536]{1,0:T(8,128)(2,1)S(1)}, u32[]{:S(2)}, u32[]{:S(2)}) collective-permute-start(bf16[384,1536]{1,0:T(8,128)(2,1)S(1)} %get-tuple-element.175), channel_id=1, source_target_pairs={{0,4},{4,0},{8,12},{12,8},{16,20},{20,16},{24,28},{28,24},{32,36},... | collective-permute-start | bytes 3538952 | tf_op jit(solution)/shard_map/ppermute | solution.py:36
  93.0 8.7 %collective-permute-start.20 = (bf16[128,768]{1,0:T(8,128)(2,1)S(1)}, bf16[128,768]{1,0:T(8,128)(2,1)S(1)}, u32[]{:S(2)}, u32[]{:S(2)}) collective-permute-start(bf16[128,768]{1,0:T(8,128)(2,1)S(1)} %add_convert_fusion.11.a), channel_id=1, source_target_pairs={{0,3},{1,2},{2,1},{3,0},{4,7},{5,6},{6,5},{7,4},{8,11},{9,10},{10,... | collective-permute-start | bytes 589832 | tf_op jit(solution)/shard_map/ppermute | solution.py:36
  95.1 6.7 %collective-permute-start.21 = (bf16[128,768]{1,0:T(8,128)(2,1)S(1)}, bf16[128,768]{1,0:T(8,128)(2,1)S(1)}, u32[]{:S(2)}, u32[]{:S(2)}) collective-permute-start(bf16[128,768]{1,0:T(8,128)(2,1)S(1)} %add_convert_fusion.10.b), channel_id=1, source_target_pairs={{0,1},{1,0},{2,3},{3,2},{4,5},{5,4},{6,7},{7,6},{8,9},{9,8},{10,11... | collective-permute-start | bytes 589832 | tf_op jit(solution)/shard_map/ppermute | solution.py:36
  103.1 5.7 %collective-permute-start.23 = (bf16[128,768]{1,0:T(8,128)(2,1)S(1)}, bf16[128,768]{1,0:T(8,128)(2,1)S(1)}, u32[]{:S(2)}, u32[]{:S(2)}) collective-permute-start(bf16[128,768]{1,0:T(8,128)(2,1)S(1)} %get-tuple-element.184), channel_id=1, source_target_pairs={{0,1},{1,0},{2,3},{3,2},{4,5},{5,4},{6,7},{7,6},{8,9},{9,8},{10,11... | collective-permute-start | bytes 589832 | tf_op jit(solution)/shard_map/ppermute | solution.py:36
  103.2 7.0 %collective-permute-start.24 = (bf16[128,768]{1,0:T(8,128)(2,1)S(1)}, bf16[128,768]{1,0:T(8,128)(2,1)S(1)}, u32[]{:S(2)}, u32[]{:S(2)}) collective-permute-start(bf16[128,768]{1,0:T(8,128)(2,1)S(1)} %get-tuple-element.185), channel_id=1, source_target_pairs={{0,3},{1,2},{2,1},{3,0},{4,7},{5,6},{6,5},{7,4},{8,11},{9,10},{10,... | collective-permute-start | bytes 589832 | tf_op jit(solution)/shard_map/ppermute | solution.py:36
  104.2 13.0 %collective-permute-start.28 = (bf16[192,1536]{1,0:T(8,128)(2,1)S(1)}, bf16[192,1536]{1,0:T(8,128)(2,1)S(1)}, u32[]{:S(2)}, u32[]{:S(2)}) collective-permute-start(bf16[192,1536]{1,0:T(8,128)(2,1)S(1)} %get-tuple-element.194), channel_id=1, source_target_pairs={{0,32},{4,36},{8,40},{12,44},{16,48},{20,52},{24,56},{28,60},{32,0... | collective-permute-start | bytes 1769480 | tf_op jit(solution)/shard_map/ppermute | solution.py:36
  106.1 11.1 %collective-permute-start.27 = (bf16[384,1536]{1,0:T(8,128)(2,1)S(1)}, bf16[384,1536]{1,0:T(8,128)(2,1)S(1)}, u32[]{:S(2)}, u32[]{:S(2)}) collective-permute-start(bf16[384,1536]{1,0:T(8,128)(2,1)S(1)} %get-tuple-element.191), channel_id=1, source_target_pairs={{0,4},{4,0},{8,12},{12,8},{16,20},{20,16},{24,28},{28,24},{32,36},... | collective-permute-start | bytes 3538952 | tf_op jit(solution)/shard_map/ppermute | solution.py:36
  110.2 7.0 %collective-permute-start.25 = (bf16[128,768]{1,0:T(8,128)(2,1)S(1)}, bf16[128,768]{1,0:T(8,128)(2,1)S(1)}, u32[]{:S(2)}, u32[]{:S(2)}) collective-permute-start(bf16[128,768]{1,0:T(8,128)(2,1)S(1)} %add_convert_fusion.9.a), channel_id=1, source_target_pairs={{0,3},{1,2},{2,1},{3,0},{4,7},{5,6},{6,5},{7,4},{8,11},{9,10},{10,... | collective-permute-start | bytes 589832 | tf_op jit(solution)/shard_map/ppermute | solution.py:36
  111.1 5.7 %collective-permute-start.26 = (bf16[128,768]{1,0:T(8,128)(2,1)S(1)}, bf16[128,768]{1,0:T(8,128)(2,1)S(1)}, u32[]{:S(2)}, u32[]{:S(2)}) collective-permute-start(bf16[128,768]{1,0:T(8,128)(2,1)S(1)} %add_convert_fusion.8.b), channel_id=1, source_target_pairs={{0,1},{1,0},{2,3},{3,2},{4,5},{5,4},{6,7},{7,6},{8,9},{9,8},{10,11... | collective-permute-start | bytes 589832 | tf_op jit(solution)/shard_map/ppermute | solution.py:36
  117.4 17.8 %collective-permute-start.35 = (bf16[192,1536]{1,0:T(8,128)(2,1)S(1)}, bf16[192,1536]{1,0:T(8,128)(2,1)S(1)}, u32[]{:S(2)}, u32[]{:S(2)}) collective-permute-start(bf16[192,1536]{1,0:T(8,128)(2,1)S(1)} %get-tuple-element.217), channel_id=1, source_target_pairs={{0,32},{4,36},{8,40},{12,44},{16,48},{20,52},{24,56},{28,60},{32,0... | collective-permute-start | bytes 1769480 | tf_op jit(solution)/shard_map/ppermute | solution.py:36
  119.8 5.7 %collective-permute-start.29 = (bf16[128,768]{1,0:T(8,128)(2,1)S(1)}, bf16[128,768]{1,0:T(8,128)(2,1)S(1)}, u32[]{:S(2)}, u32[]{:S(2)}) collective-permute-start(bf16[128,768]{1,0:T(8,128)(2,1)S(1)} %get-tuple-element.203), channel_id=1, source_target_pairs={{0,1},{1,0},{2,3},{3,2},{4,5},{5,4},{6,7},{7,6},{8,9},{9,8},{10,11... | collective-permute-start | bytes 589832 | tf_op jit(solution)/shard_map/ppermute | solution.py:36
  120.2 6.9 %collective-permute-start.30 = (bf16[128,768]{1,0:T(8,128)(2,1)S(1)}, bf16[128,768]{1,0:T(8,128)(2,1)S(1)}, u32[]{:S(2)}, u32[]{:S(2)}) collective-permute-start(bf16[128,768]{1,0:T(8,128)(2,1)S(1)} %get-tuple-element.204), channel_id=1, source_target_pairs={{0,3},{1,2},{2,1},{3,0},{4,7},{5,6},{6,5},{7,4},{8,11},{9,10},{10,... | collective-permute-start | bytes 589832 | tf_op jit(solution)/shard_map/ppermute | solution.py:36
  122.4 8.2 %collective-permute-start.34 = (bf16[96,1536]{1,0:T(8,128)(2,1)S(1)}, bf16[96,1536]{1,0:T(8,128)(2,1)S(1)}, u32[]{:S(2)}, u32[]{:S(2)}) collective-permute-start(bf16[96,1536]{1,0:T(8,128)(2,1)S(1)} %get-tuple-element.250), channel_id=1, source_target_pairs={{0,96},{4,100},{8,104},{12,108},{16,112},{20,116},{24,120},{28,124... | collective-permute-start | bytes 884744 | tf_op jit(solution)/shard_map/ppermute | solution.py:36
  125.3 4.3 %collective-permute-start.33 = (bf16[384,1536]{1,0:T(8,128)(2,1)S(1)}, bf16[384,1536]{1,0:T(8,128)(2,1)S(1)}, u32[]{:S(2)}, u32[]{:S(2)}) collective-permute-start(bf16[384,1536]{1,0:T(8,128)(2,1)S(1)} %get-tuple-element.210), channel_id=1, source_target_pairs={{0,4},{4,0},{8,12},{12,8},{16,20},{20,16},{24,28},{28,24},{32,36},... | collective-permute-start | bytes 3538952 | tf_op jit(solution)/shard_map/ppermute | solution.py:36
  127.1 8.0 %collective-permute-start.31 = (bf16[128,768]{1,0:T(8,128)(2,1)S(1)}, bf16[128,768]{1,0:T(8,128)(2,1)S(1)}, u32[]{:S(2)}, u32[]{:S(2)}) collective-permute-start(bf16[128,768]{1,0:T(8,128)(2,1)S(1)} %add_convert_fusion.7.a), channel_id=1, source_target_pairs={{0,3},{1,2},{2,1},{3,0},{4,7},{5,6},{6,5},{7,4},{8,11},{9,10},{10,... | collective-permute-start | bytes 589832 | tf_op jit(solution)/shard_map/ppermute | solution.py:36
  129.4 5.7 %collective-permute-start.32 = (bf16[128,768]{1,0:T(8,128)(2,1)S(1)}, bf16[128,768]{1,0:T(8,128)(2,1)S(1)}, u32[]{:S(2)}, u32[]{:S(2)}) collective-permute-start(bf16[128,768]{1,0:T(8,128)(2,1)S(1)} %add_convert_fusion.6.b), channel_id=1, source_target_pairs={{0,1},{1,0},{2,3},{3,2},{4,5},{5,4},{6,7},{7,6},{8,9},{9,8},{10,11... | collective-permute-start | bytes 589832 | tf_op jit(solution)/shard_map/ppermute | solution.py:36
  135.3 12.3 %collective-permute-start.45 = (bf16[96,1536]{1,0:T(8,128)(2,1)S(1)}, bf16[96,1536]{1,0:T(8,128)(2,1)S(1)}, u32[]{:S(2)}, u32[]{:S(2)}) collective-permute-start(bf16[96,1536]{1,0:T(8,128)(2,1)S(1)} %get-tuple-element.248), channel_id=1, source_target_pairs={{0,96},{4,100},{8,104},{12,108},{16,112},{20,116},{24,120},{28,124... | collective-permute-start | bytes 884744 | tf_op jit(solution)/shard_map/ppermute | solution.py:36
  136.7 12.8 %collective-permute-start.41 = (bf16[192,1536]{1,0:T(8,128)(2,1)S(1)}, bf16[192,1536]{1,0:T(8,128)(2,1)S(1)}, u32[]{:S(2)}, u32[]{:S(2)}) collective-permute-start(bf16[192,1536]{1,0:T(8,128)(2,1)S(1)} %get-tuple-element.239), channel_id=1, source_target_pairs={{0,8},{4,12},{8,0},{12,4},{16,24},{20,28},{24,16},{28,20},{32,40},... | collective-permute-start | bytes 1769480 | tf_op jit(solution)/shard_map/ppermute | solution.py:36
  138.8 5.6 %collective-permute-start.37 = (bf16[128,384]{1,0:T(8,128)(2,1)S(1)}, bf16[128,384]{1,0:T(8,128)(2,1)S(1)}, u32[]{:S(2)}, u32[]{:S(2)}) collective-permute-start(bf16[128,384]{1,0:T(8,128)(2,1)S(1)} %get-tuple-element.230), channel_id=1, source_target_pairs={{0,1},{1,0},{2,3},{3,2},{4,5},{5,4},{6,7},{7,6},{8,9},{9,8},{10,11... | collective-permute-start | bytes 294920 | tf_op jit(solution)/shard_map/ppermute | solution.py:36
  139.1 6.3 %collective-permute-start.38 = (bf16[128,384]{1,0:T(8,128)(2,1)S(1)}, bf16[128,384]{1,0:T(8,128)(2,1)S(1)}, u32[]{:S(2)}, u32[]{:S(2)}) collective-permute-start(bf16[128,384]{1,0:T(8,128)(2,1)S(1)} %get-tuple-element.231), channel_id=1, source_target_pairs={{0,3},{1,2},{2,1},{3,0},{4,7},{5,6},{6,5},{7,4},{8,11},{9,10},{10,... | collective-permute-start | bytes 294920 | tf_op jit(solution)/shard_map/ppermute | solution.py:36
  141.2 6.1 %collective-permute-start.39 = (bf16[128,384]{1,0:T(8,128)(2,1)S(1)}, bf16[128,384]{1,0:T(8,128)(2,1)S(1)}, u32[]{:S(2)}, u32[]{:S(2)}) collective-permute-start(bf16[128,384]{1,0:T(8,128)(2,1)S(1)} %get-tuple-element.232), channel_id=1, source_target_pairs={{0,2},{1,3},{2,0},{3,1},{4,6},{5,7},{6,4},{7,5},{8,10},{9,11},{10,... | collective-permute-start | bytes 294920 | tf_op jit(solution)/shard_map/ppermute | solution.py:36
  144.4 6.8 %collective-permute-start.36 = (bf16[384,1536]{1,0:T(8,128)(2,1)S(1)}, bf16[384,1536]{1,0:T(8,128)(2,1)S(1)}, u32[]{:S(2)}, u32[]{:S(2)}) collective-permute-start(bf16[384,1536]{1,0:T(8,128)(2,1)S(1)} %get-tuple-element.228), channel_id=1, source_target_pairs={{0,4},{4,0},{8,12},{12,8},{16,20},{20,16},{24,28},{28,24},{32,36},... | collective-permute-start | bytes 3538952 | tf_op jit(solution)/shard_map/ppermute | solution.py:36
  147.6 3.6 %collective-permute-start.40 = (bf16[16,1536]{1,0:T(8,128)(2,1)S(1)}, bf16[16,1536]{1,0:T(8,128)(2,1)S(1)}, u32[]{:S(2)}, u32[]{:S(2)}) collective-permute-start(bf16[16,1536]{1,0:T(8,128)(2,1)S(1)} %get-tuple-element.237), channel_id=1, source_target_pairs={{0,4},{4,0},{8,12},{12,8},{16,20},{20,16},{24,28},{28,24},{32,36},... | collective-permute-start | bytes 147464 | tf_op jit(solution)/shard_map/ppermute | solution.py:36
  147.8 9.5 %collective-permute-start.46 = (bf16[96,1536]{1,0:T(8,128)(2,1)S(1)}, bf16[96,1536]{1,0:T(8,128)(2,1)S(1)}, u32[]{:S(2)}, u32[]{:S(2)}) collective-permute-start(bf16[96,1536]{1,0:T(8,128)(2,1)S(1)} %pad_maximum_fusion), channel_id=1, source_target_pairs={{0,8},{4,12},{8,0},{12,4},{16,24},{20,28},{24,16},{28,20},{32,40},... | collective-permute-start | bytes 884744 | tf_op jit(solution)/shard_map/ppermute | solution.py:36
  149.7 13.2 %collective-permute-start.42 = (bf16[96,1536]{1,0:T(8,128)(2,1)S(1)}, bf16[96,1536]{1,0:T(8,128)(2,1)S(1)}, u32[]{:S(2)}, u32[]{:S(2)}) collective-permute-start(bf16[96,1536]{1,0:T(8,128)(2,1)S(1)} %get-tuple-element.252), channel_id=1, source_target_pairs={{0,24},{4,28},{8,16},{12,20},{16,8},{20,12},{24,0},{28,4},{32,56},... | collective-permute-start | bytes 884744 | tf_op jit(solution)/shard_map/ppermute | solution.py:36
  152.7 31.6 %all-to-all-start.1 = ((bf16[16,32,1536]{2,1,0:T(8,128)(2,1)}), bf16[16,32,1536]{2,1,0:T(8,128)(2,1)S(1)}, u32[]{:S(2)}, u32[]{:S(2)}) async-start(bf16[16,32,1536]{2,1,0:T(8,128)(2,1)} %shard_map.182), calls=%async_computation.1 | async-start | bytes 3145728 | tf_op jit(solution)/shard_map/all_to_all | solution.py:323
  163.0 15.7 %collective-permute-start.43 = (bf16[48,1536]{1,0:T(8,128)(2,1)S(1)}, bf16[48,1536]{1,0:T(8,128)(2,1)S(1)}, u32[]{:S(2)}, u32[]{:S(2)}) collective-permute-start(bf16[48,1536]{1,0:T(8,128)(2,1)S(1)} %get-tuple-element.258), channel_id=1, source_target_pairs={{0,32},{4,36},{8,40},{12,44},{16,48},{20,52},{24,56},{28,60},{32,0... | collective-permute-start | bytes 442376 | tf_op jit(solution)/shard_map/ppermute | solution.py:36
  163.1 17.1 %collective-permute-start.47 = (bf16[48,1536]{1,0:T(8,128)(2,1)S(1)}, bf16[48,1536]{1,0:T(8,128)(2,1)S(1)}, u32[]{:S(2)}, u32[]{:S(2)}) collective-permute-start(bf16[48,1536]{1,0:T(8,128)(2,1)S(1)} %pad_maximum_fusion.2), channel_id=1, source_target_pairs={{0,24},{4,28},{8,16},{12,20},{16,8},{20,12},{24,0},{28,4},{32,56},... | collective-permute-start | bytes 442376 | tf_op jit(solution)/shard_map/ppermute | solution.py:36
  178.7 5.6 %collective-permute-start.44 = (bf16[24,1536]{1,0:T(8,128)(2,1)S(1)}, bf16[24,1536]{1,0:T(8,128)(2,1)S(1)}, u32[]{:S(2)}, u32[]{:S(2)}) collective-permute-start(bf16[24,1536]{1,0:T(8,128)(2,1)S(1)} %get-tuple-element.265), channel_id=1, source_target_pairs={{0,96},{4,100},{8,104},{12,108},{16,112},{20,116},{24,120},{28,124... | collective-permute-start | bytes 221192 | tf_op jit(solution)/shard_map/ppermute | solution.py:36

commit v7 on v6

--- a/solution.py
+++ b/solution.py
@@ -368,11 +368,11 @@
     block_go, block_come = residue_to_block()
     for layer in (1, 2):
         second = []
-        if layer == 1:
+        if layer == 2:
             cotangent, ta = together(cotangent, ta)
             second = [swap(cotangent, "mp", mask) for mask in (1, 3, 2)]
         terms, loaded, _, second = sum_mp(ta, tb, weights(layer), (), second)
-        if layer == 1:
+        if layer == 2:
             parts = (me, cotangent, *second)
             (g,) = call(gather_kernel, [full], [], parts, {0: pltpu.SMEM}, flops=1e6)
         x, inner, ta, tb = call(

time: 186 us -> 187 us (level)
  transfers between devices with their start and end apart: 50 -> 50, of which waited for: 36 -> 33; matrix products, arithmetic and copies ran while one was open for 4% -> 4% of each run, Pallas kernels for 6% -> 6%
where the time goes in v7:
time: 187 us; the launch traced here: 186 us
  waiting for transfers between devices  90.7 us (49%)
  starting transfers between devices  65.9 us (35%)
  Pallas kernels  18.6 us (10%)
  other arithmetic  4.16 us (2%)
  matrix products  2.87 us (2%)
  local copies, waits for them, and re-layouts  2.82 us (2%)
    ppermute x48, waiting for transfers between devices, swap(): return lax.ppermute(values, axis, [(i, i ^ mask) for i in range(peers)])  84 us
    ppermute x48, starting transfers between devices, swap(): return lax.ppermute(values, axis, [(i, i ^ mask) for i in range(peers)])  53.9 us
    pallas_call x18, Pallas kernels, call(): pl.pallas_call(body, out_shape=outs, in_specs=[pl.BlockSpec(memory_space=...  18.6 us
    all_to_all x1, starting transfers between devices, shards(): got = lax.all_to_all(sent.reshape(PEERS, 8, SHARD), 'seq', 0, 0)  8.25 us
    all_to_all x1, waiting for transfers between devices, shards(): got = lax.all_to_all(sent.reshape(PEERS, 8, SHARD), 'seq', 0, 0)  6.65 us
  transfers between devices with their start and end apart: 50, of which 33 were waited for; matrix products, arithmetic and copies ran while one was open for 4% of the time, Pallas kernels for 6%

profile of v7, /device:TPU:0, one launch (start us, length us, event | category | flops | bytes accessed | tf_op | source)
XLA Modules:
  0.0 186.2 jit_solution(173596277864543469)
XLA Ops:
  0.6 1.9 %fusion.3 = bf16[32,8,384]{2,1,0:T(8,128)(2,1)} fusion(bf16[128,384]{1,0:T(8,128)(2,1)} %param.16, bf16[128,384]{1,0:T(8,128)(2,1)} %param.15, s32[256]{0:T(256)} %constant.46.clone), kind=kOutput, calls=%fused_computation.15 | convolution fusion | flops 50888704 | bytes 394240 | tf_op jit(solution)/shard_map/dot_general | solution.py:31
  2.5 8.2 %all-to-all-start = ((bf16[32,8,384]{2,1,0:T(8,128)(2,1)}), bf16[32,8,384]{2,1,0:T(8,128)(2,1)S(1)}, u32[]{:S(2)}, u32[]{:S(2)}) async-start(bf16[32,8,384]{2,1,0:T(8,128)(2,1)} %fusion.3), calls=%async_computation | async-start | bytes 393216 | tf_op jit(solution)/shard_map/all_to_all | solution.py:350
  12.3 6.7 %all-to-all-done = bf16[32,8,384]{2,1,0:T(8,128)(2,1)S(1)} async-done(((bf16[32,8,384]{2,1,0:T(8,128)(2,1)}), bf16[32,8,384]{2,1,0:T(8,128)(2,1)S(1)}, u32[]{:S(2)}, u32[]{:S(2)}) %all-to-all-start) | async-done | bytes 196640 | tf_op jit(solution)/shard_map/all_to_all | solution.py:350
  20.0 1.7 collective-permute-start
  21.7 2.2 %collective-permute-start.1 = (bf16[128,384]{1,0:T(8,128)(2,1)S(1)}, bf16[128,384]{1,0:T(8,128)(2,1)S(1)}, u32[]{:S(2)}, u32[]{:S(2)}) collective-permute-start(bf16[128,384]{1,0:T(8,128)(2,1)S(1)} %get-tuple-element.267.own), channel_id=1, source_target_pairs={{0,3},{1,2},{2,1},{3,0},{4,7},{5,6},{6,5},{7,4},{8,11},{9,10},{10,... | collective-permute-start | bytes 294920 | tf_op jit(solution)/shard_map/ppermute | solution.py:36
  24.6 1.7 slice_bitcast_fusion.6.k_mem
  26.4 1.9 %collective-permute-done.1.three = bf16[128,384]{1,0:T(8,128)(2,1)S(1)} collective-permute-done((bf16[128,384]{1,0:T(8,128)(2,1)S(1)}, bf16[128,384]{1,0:T(8,128)(2,1)S(1)}, u32[]{:S(2)}, u32[]{:S(2)}) %collective-permute-start.1) | collective-permute-done | bytes 98336 | tf_op jit(solution)/shard_map/ppermute | solution.py:36
  28.2 1.7 collective-permute-done.2.two
  30.0 1.1 shard_map.166
  31.8 1.4 collective-permute-start.4
  33.6 3.2 %collective-permute-done.3 = bf16[128,768]{1,0:T(8,128)(2,1)S(1)} collective-permute-done((bf16[128,768]{1,0:T(8,128)(2,1)S(1)}, bf16[128,768]{1,0:T(8,128)(2,1)S(1)}, u32[]{:S(2)}, u32[]{:S(2)}) %collective-permute-start.3) | collective-permute-done | bytes 196640 | tf_op jit(solution)/shard_map/ppermute | solution.py:36
  36.8 1.9 %collective-permute-done.4 = bf16[128,768]{1,0:T(8,128)(2,1)S(1)} collective-permute-done((bf16[128,768]{1,0:T(8,128)(2,1)S(1)}, bf16[128,768]{1,0:T(8,128)(2,1)S(1)}, u32[]{:S(2)}, u32[]{:S(2)}) %collective-permute-start.4) | collective-permute-done | bytes 196640 | tf_op jit(solution)/shard_map/ppermute | solution.py:36
  39.0 2.0 %collective-permute-start.5 = (bf16[128,768]{1,0:T(8,128)(2,1)S(1)}, bf16[128,768]{1,0:T(8,128)(2,1)S(1)}, u32[]{:S(2)}, u32[]{:S(2)}) collective-permute-start(bf16[128,768]{1,0:T(8,128)(2,1)S(1)} %add_convert_fusion.17.a), channel_id=1, source_target_pairs={{0,3},{1,2},{2,1},{3,0},{4,7},{5,6},{6,5},{7,4},{8,11},{9,10},{10,... | collective-permute-start | bytes 589832 | tf_op jit(solution)/shard_map/ppermute | solution.py:36
  41.3 3.3 %collective-permute-done.6.b2 = bf16[128,768]{1,0:T(8,128)(2,1)S(1)} collective-permute-done((bf16[128,768]{1,0:T(8,128)(2,1)S(1)}, bf16[128,768]{1,0:T(8,128)(2,1)S(1)}, u32[]{:S(2)}, u32[]{:S(2)}) %collective-permute-start.6) | collective-permute-done | bytes 196640 | tf_op jit(solution)/shard_map/ppermute | solution.py:36
  44.5 1.5 collective-permute-done.5.a2
  46.0 1.2 shard_map.167
  48.0 1.4 collective-permute-start.9
  49.8 1.4 collective-permute-start.11
  51.2 1.3 collective-permute-start.12
  52.5 1.5 collective-permute-start.13
  54.7 1.6 collective-permute-done.9
  57.3 2.0 %collective-permute-start.8 = (bf16[128,768]{1,0:T(8,128)(2,1)S(1)}, bf16[128,768]{1,0:T(8,128)(2,1)S(1)}, u32[]{:S(2)}, u32[]{:S(2)}) collective-permute-start(bf16[128,768]{1,0:T(8,128)(2,1)S(1)} %add_convert_fusion.15.a), channel_id=1, source_target_pairs={{0,3},{1,2},{2,1},{3,0},{4,7},{5,6},{6,5},{7,4},{8,11},{9,10},{10,... | collective-permute-start | bytes 589832 | tf_op jit(solution)/shard_map/ppermute | solution.py:36
  59.5 2.9 %collective-permute-done.10.b2 = bf16[128,768]{1,0:T(8,128)(2,1)S(1)} collective-permute-done((bf16[128,768]{1,0:T(8,128)(2,1)S(1)}, bf16[128,768]{1,0:T(8,128)(2,1)S(1)}, u32[]{:S(2)}, u32[]{:S(2)}) %collective-permute-start.10) | collective-permute-done | bytes 196640 | tf_op jit(solution)/shard_map/ppermute | solution.py:36
  62.3 1.9 %collective-permute-done.8.a2 = bf16[128,768]{1,0:T(8,128)(2,1)S(1)} collective-permute-done((bf16[128,768]{1,0:T(8,128)(2,1)S(1)}, bf16[128,768]{1,0:T(8,128)(2,1)S(1)}, u32[]{:S(2)}, u32[]{:S(2)}) %collective-permute-start.8) | collective-permute-done | bytes 196640 | tf_op jit(solution)/shard_map/ppermute | solution.py:36
  64.3 1.2 shard_map.169
  66.2 2.9 %collective-permute-start.15 = (bf16[128,768]{1,0:T(8,128)(2,1)S(1)}, bf16[128,768]{1,0:T(8,128)(2,1)S(1)}, u32[]{:S(2)}, u32[]{:S(2)}) collective-permute-start(bf16[128,768]{1,0:T(8,128)(2,1)S(1)} %get-tuple-element.159), channel_id=1, source_target_pairs={{0,3},{1,2},{2,1},{3,0},{4,7},{5,6},{6,5},{7,4},{8,11},{9,10},{10,... | collective-permute-start | bytes 589832 | tf_op jit(solution)/shard_map/ppermute | solution.py:36
  69.5 3.7 %collective-permute-done.14 = bf16[128,768]{1,0:T(8,128)(2,1)S(1)} collective-permute-done((bf16[128,768]{1,0:T(8,128)(2,1)S(1)}, bf16[128,768]{1,0:T(8,128)(2,1)S(1)}, u32[]{:S(2)}, u32[]{:S(2)}) %collective-permute-start.14) | collective-permute-done | bytes 196640 | tf_op jit(solution)/shard_map/ppermute | solution.py:36
  73.3 1.5 collective-permute-done.15
  75.5 2.0 %collective-permute-start.16 = (bf16[128,768]{1,0:T(8,128)(2,1)S(1)}, bf16[128,768]{1,0:T(8,128)(2,1)S(1)}, u32[]{:S(2)}, u32[]{:S(2)}) collective-permute-start(bf16[128,768]{1,0:T(8,128)(2,1)S(1)} %add_convert_fusion.13.a), channel_id=1, source_target_pairs={{0,3},{1,2},{2,1},{3,0},{4,7},{5,6},{6,5},{7,4},{8,11},{9,10},{10,... | collective-permute-start | bytes 589832 | tf_op jit(solution)/shard_map/ppermute | solution.py:36
  77.7 4.7 %collective-permute-done.17.b2 = bf16[128,768]{1,0:T(8,128)(2,1)S(1)} collective-permute-done((bf16[128,768]{1,0:T(8,128)(2,1)S(1)}, bf16[128,768]{1,0:T(8,128)(2,1)S(1)}, u32[]{:S(2)}, u32[]{:S(2)}) %collective-permute-start.17) | collective-permute-done | bytes 196640 | tf_op jit(solution)/shard_map/ppermute | solution.py:36
  82.4 1.9 %collective-permute-done.16.a2 = bf16[128,768]{1,0:T(8,128)(2,1)S(1)} collective-permute-done((bf16[128,768]{1,0:T(8,128)(2,1)S(1)}, bf16[128,768]{1,0:T(8,128)(2,1)S(1)}, u32[]{:S(2)}, u32[]{:S(2)}) %collective-permute-start.16) | collective-permute-done | bytes 196640 | tf_op jit(solution)/shard_map/ppermute | solution.py:36
  84.4 1.6 shard_map.170
  87.5 1.3 shard_map.171
  88.9 2.8 %collective-permute-done.18 = bf16[128,768]{1,0:T(8,128)(2,1)S(1)} collective-permute-done((bf16[128,768]{1,0:T(8,128)(2,1)S(1)}, bf16[128,768]{1,0:T(8,128)(2,1)S(1)}, u32[]{:S(2)}, u32[]{:S(2)}) %collective-permute-start.18) | collective-permute-done | bytes 196640 | tf_op jit(solution)/shard_map/ppermute | solution.py:36
  91.7 1.6 collective-permute-done.19
  94.7 5.4 %collective-permute-done.21.b2 = bf16[128,768]{1,0:T(8,128)(2,1)S(1)} collective-permute-done((bf16[128,768]{1,0:T(8,128)(2,1)S(1)}, bf16[128,768]{1,0:T(8,128)(2,1)S(1)}, u32[]{:S(2)}, u32[]{:S(2)}) %collective-permute-start.21) | collective-permute-done | bytes 196640 | tf_op jit(solution)/shard_map/ppermute | solution.py:36
  100.4 1.3 shard_map.172
  101.8 3.4 %collective-permute-start.24 = (bf16[128,768]{1,0:T(8,128)(2,1)S(1)}, bf16[128,768]{1,0:T(8,128)(2,1)S(1)}, u32[]{:S(2)}, u32[]{:S(2)}) collective-permute-start(bf16[128,768]{1,0:T(8,128)(2,1)S(1)} %get-tuple-element.185), channel_id=1, source_target_pairs={{0,3},{1,2},{2,1},{3,0},{4,7},{5,6},{6,5},{7,4},{8,11},{9,10},{10,... | collective-permute-start | bytes 589832 | tf_op jit(solution)/shard_map/ppermute | solution.py:36
  105.6 1.3 shard_map.173
  107.5 1.4 collective-permute-done.24
  108.9 3.3 %collective-permute-start.25 = (bf16[128,768]{1,0:T(8,128)(2,1)S(1)}, bf16[128,768]{1,0:T(8,128)(2,1)S(1)}, u32[]{:S(2)}, u32[]{:S(2)}) collective-permute-start(bf16[128,768]{1,0:T(8,128)(2,1)S(1)} %add_convert_fusion.9.a), channel_id=1, source_target_pairs={{0,3},{1,2},{2,1},{3,0},{4,7},{5,6},{6,5},{7,4},{8,11},{9,10},{10,... | collective-permute-start | bytes 589832 | tf_op jit(solution)/shard_map/ppermute | solution.py:36
  112.6 5.6 %collective-permute-done.26.b2 = bf16[128,768]{1,0:T(8,128)(2,1)S(1)} collective-permute-done((bf16[128,768]{1,0:T(8,128)(2,1)S(1)}, bf16[128,768]{1,0:T(8,128)(2,1)S(1)}, u32[]{:S(2)}, u32[]{:S(2)}) %collective-permute-start.26) | collective-permute-done | bytes 196640 | tf_op jit(solution)/shard_map/ppermute | solution.py:36
  118.6 1.3 shard_map.175
  120.0 2.1 %collective-permute-start.30 = (bf16[128,768]{1,0:T(8,128)(2,1)S(1)}, bf16[128,768]{1,0:T(8,128)(2,1)S(1)}, u32[]{:S(2)}, u32[]{:S(2)}) collective-permute-start(bf16[128,768]{1,0:T(8,128)(2,1)S(1)} %get-tuple-element.204), channel_id=1, source_target_pairs={{0,3},{1,2},{2,1},{3,0},{4,7},{5,6},{6,5},{7,4},{8,11},{9,10},{10,... | collective-permute-start | bytes 589832 | tf_op jit(solution)/shard_map/ppermute | solution.py:36
  122.2 1.8 collective-permute-start.34
  124.0 1.3 shard_map.176
  125.6 1.3 collective-permute-done.30
  127.0 2.1 %collective-permute-start.31 = (bf16[128,768]{1,0:T(8,128)(2,1)S(1)}, bf16[128,768]{1,0:T(8,128)(2,1)S(1)}, u32[]{:S(2)}, u32[]{:S(2)}) collective-permute-start(bf16[128,768]{1,0:T(8,128)(2,1)S(1)} %add_convert_fusion.7.a), channel_id=1, source_target_pairs={{0,3},{1,2},{2,1},{3,0},{4,7},{5,6},{6,5},{7,4},{8,11},{9,10},{10,... | collective-permute-start | bytes 589832 | tf_op jit(solution)/shard_map/ppermute | solution.py:36
  130.4 4.6 %collective-permute-done.32.b2 = bf16[128,768]{1,0:T(8,128)(2,1)S(1)} collective-permute-done((bf16[128,768]{1,0:T(8,128)(2,1)S(1)}, bf16[128,768]{1,0:T(8,128)(2,1)S(1)}, u32[]{:S(2)}, u32[]{:S(2)}) %collective-permute-start.32) | collective-permute-done | bytes 196640 | tf_op jit(solution)/shard_map/ppermute | solution.py:36
  135.2 1.6 collective-permute-start.45
  137.0 1.5 shard_map.179
  138.9 2.2 %collective-permute-start.38 = (bf16[128,384]{1,0:T(8,128)(2,1)S(1)}, bf16[128,384]{1,0:T(8,128)(2,1)S(1)}, u32[]{:S(2)}, u32[]{:S(2)}) collective-permute-start(bf16[128,384]{1,0:T(8,128)(2,1)S(1)} %get-tuple-element.231), channel_id=1, source_target_pairs={{0,3},{1,2},{2,1},{3,0},{4,7},{5,6},{6,5},{7,4},{8,11},{9,10},{10,... | collective-permute-start | bytes 294920 | tf_op jit(solution)/shard_map/ppermute | solution.py:36
  141.1 1.6 collective-permute-start.39
  142.8 1.3 shard_map.180
  144.7 2.5 %collective-permute-done.39.two = bf16[128,384]{1,0:T(8,128)(2,1)S(1)} collective-permute-done((bf16[128,384]{1,0:T(8,128)(2,1)S(1)}, bf16[128,384]{1,0:T(8,128)(2,1)S(1)}, u32[]{:S(2)}, u32[]{:S(2)}) %collective-permute-start.39) | collective-permute-done | bytes 98336 | tf_op jit(solution)/shard_map/ppermute | solution.py:36
  147.6 1.4 collective-permute-start.46
  149.5 2.4 %collective-permute-start.42 = (bf16[96,1536]{1,0:T(8,128)(2,1)S(1)}, bf16[96,1536]{1,0:T(8,128)(2,1)S(1)}, u32[]{:S(2)}, u32[]{:S(2)}) collective-permute-start(bf16[96,1536]{1,0:T(8,128)(2,1)S(1)} %get-tuple-element.252), channel_id=1, source_target_pairs={{0,24},{4,28},{8,16},{12,20},{16,8},{20,12},{24,0},{28,4},{32,56},... | collective-permute-start | bytes 884744 | tf_op jit(solution)/shard_map/ppermute | solution.py:36
  151.9 1.5 shard_map.182
  153.4 3.7 %all-to-all-start.1 = ((bf16[16,32,1536]{2,1,0:T(8,128)(2,1)}), bf16[16,32,1536]{2,1,0:T(8,128)(2,1)S(1)}, u32[]{:S(2)}, u32[]{:S(2)}) async-start(bf16[16,32,1536]{2,1,0:T(8,128)(2,1)} %shard_map.182), calls=%async_computation.1 | async-start | bytes 3145728 | tf_op jit(solution)/shard_map/all_to_all | solution.py:323
  157.2 2.3 %collective-permute-done.42 = bf16[96,1536]{1,0:T(8,128)(2,1)S(1)} collective-permute-done((bf16[96,1536]{1,0:T(8,128)(2,1)S(1)}, bf16[96,1536]{1,0:T(8,128)(2,1)S(1)}, u32[]{:S(2)}, u32[]{:S(2)}) %collective-permute-start.42) | collective-permute-done | bytes 294944 | tf_op jit(solution)/shard_map/ppermute | solution.py:36
  159.8 2.2 %collective-permute-start.47 = (bf16[48,1536]{1,0:T(8,128)(2,1)S(1)}, bf16[48,1536]{1,0:T(8,128)(2,1)S(1)}, u32[]{:S(2)}, u32[]{:S(2)}) collective-permute-start(bf16[48,1536]{1,0:T(8,128)(2,1)S(1)} %pad_maximum_fusion.2), channel_id=1, source_target_pairs={{0,24},{4,28},{8,16},{12,20},{16,8},{20,12},{24,0},{28,4},{32,56},... | collective-permute-start | bytes 442376 | tf_op jit(solution)/shard_map/ppermute | solution.py:36
  162.0 17.1 %collective-permute-done.43 = bf16[48,1536]{1,0:T(8,128)(2,1)S(1)} collective-permute-done((bf16[48,1536]{1,0:T(8,128)(2,1)S(1)}, bf16[48,1536]{1,0:T(8,128)(2,1)S(1)}, u32[]{:S(2)}, u32[]{:S(2)}) %collective-permute-start.43) | collective-permute-done | bytes 147488 | tf_op jit(solution)/shard_map/ppermute | solution.py:36
  180.4 4.4 %collective-permute-done.44.come = bf16[24,1536]{1,0:T(8,128)(2,1)S(1)} collective-permute-done((bf16[24,1536]{1,0:T(8,128)(2,1)S(1)}, bf16[24,1536]{1,0:T(8,128)(2,1)S(1)}, u32[]{:S(2)}, u32[]{:S(2)}) %collective-permute-start.44) | collective-permute-done | bytes 73760 | tf_op jit(solution)/shard_map/ppermute | solution.py:36
  184.8 1.4 shard_map.183
  (107 shorter events, 20.4 us)
Async XLA Ops:
  2.5 16.5 %all-to-all-start = ((bf16[32,8,384]{2,1,0:T(8,128)(2,1)}), bf16[32,8,384]{2,1,0:T(8,128)(2,1)S(1)}, u32[]{:S(2)}, u32[]{:S(2)}) async-start(bf16[32,8,384]{2,1,0:T(8,128)(2,1)} %fusion.3), calls=%async_computation | async-start | bytes 393216 | tf_op jit(solution)/shard_map/all_to_all | solution.py:350
  20.0 6.3 %copy-start.1 = (bf16[4,192,1536]{2,1,0:T(8,128)(2,1)S(1)}, bf16[4,192,1536]{2,1,0:T(8,128)(2,1)}, u32[]{:S(2)}) copy-start(bf16[4,192,1536]{2,1,0:T(8,128)(2,1)} %param.18) | copy-start | bytes 7077892
  20.0 6.4 %collective-permute-start = (bf16[128,384]{1,0:T(8,128)(2,1)S(1)}, bf16[128,384]{1,0:T(8,128)(2,1)S(1)}, u32[]{:S(2)}, u32[]{:S(2)}) collective-permute-start(bf16[128,384]{1,0:T(8,128)(2,1)S(1)} %get-tuple-element.267.own), channel_id=1, source_target_pairs={{0,1},{1,0},{2,3},{3,2},{4,5},{5,4},{6,7},{7,6},{8,9},{9,8},{10,11... | collective-permute-start | bytes 294920 | tf_op jit(solution)/shard_map/ppermute | solution.py:36
  21.7 6.6 %collective-permute-start.1 = (bf16[128,384]{1,0:T(8,128)(2,1)S(1)}, bf16[128,384]{1,0:T(8,128)(2,1)S(1)}, u32[]{:S(2)}, u32[]{:S(2)}) collective-permute-start(bf16[128,384]{1,0:T(8,128)(2,1)S(1)} %get-tuple-element.267.own), channel_id=1, source_target_pairs={{0,3},{1,2},{2,1},{3,0},{4,7},{5,6},{6,5},{7,4},{8,11},{9,10},{10,... | collective-permute-start | bytes 294920 | tf_op jit(solution)/shard_map/ppermute | solution.py:36
  23.8 6.1 %collective-permute-start.2 = (bf16[128,384]{1,0:T(8,128)(2,1)S(1)}, bf16[128,384]{1,0:T(8,128)(2,1)S(1)}, u32[]{:S(2)}, u32[]{:S(2)}) collective-permute-start(bf16[128,384]{1,0:T(8,128)(2,1)S(1)} %get-tuple-element.267.own), channel_id=1, source_target_pairs={{0,2},{1,3},{2,0},{3,1},{4,6},{5,7},{6,4},{7,5},{8,10},{9,11},{10,... | collective-permute-start | bytes 294920 | tf_op jit(solution)/shard_map/ppermute | solution.py:36
  24.6 16.5 %copy-start = (bf16[4,3,192,1536]{3,2,1,0:T(8,128)(2,1)S(1)}, bf16[4,3,192,1536]{3,2,1,0:T(8,128)(2,1)}, u32[]{:S(2)}) copy-start(bf16[4,3,192,1536]{3,2,1,0:T(8,128)(2,1)} %param.17) | copy-start | bytes 21233668
  31.1 5.7 %collective-permute-start.3 = (bf16[128,768]{1,0:T(8,128)(2,1)S(1)}, bf16[128,768]{1,0:T(8,128)(2,1)S(1)}, u32[]{:S(2)}, u32[]{:S(2)}) collective-permute-start(bf16[128,768]{1,0:T(8,128)(2,1)S(1)} %get-tuple-element.133), channel_id=1, source_target_pairs={{0,1},{1,0},{2,3},{3,2},{4,5},{5,4},{6,7},{7,6},{8,9},{9,8},{10,11... | collective-permute-start | bytes 589832 | tf_op jit(solution)/shard_map/ppermute | solution.py:36
  31.8 6.9 %collective-permute-start.4 = (bf16[128,768]{1,0:T(8,128)(2,1)S(1)}, bf16[128,768]{1,0:T(8,128)(2,1)S(1)}, u32[]{:S(2)}, u32[]{:S(2)}) collective-permute-start(bf16[128,768]{1,0:T(8,128)(2,1)S(1)} %get-tuple-element.134), channel_id=1, source_target_pairs={{0,3},{1,2},{2,1},{3,0},{4,7},{5,6},{6,5},{7,4},{8,11},{9,10},{10,... | collective-permute-start | bytes 589832 | tf_op jit(solution)/shard_map/ppermute | solution.py:36
  38.8 5.7 %collective-permute-start.6 = (bf16[128,768]{1,0:T(8,128)(2,1)S(1)}, bf16[128,768]{1,0:T(8,128)(2,1)S(1)}, u32[]{:S(2)}, u32[]{:S(2)}) collective-permute-start(bf16[128,768]{1,0:T(8,128)(2,1)S(1)} %add_convert_fusion.16.b), channel_id=1, source_target_pairs={{0,1},{1,0},{2,3},{3,2},{4,5},{5,4},{6,7},{7,6},{8,9},{9,8},{10,11... | collective-permute-start | bytes 589832 | tf_op jit(solution)/shard_map/ppermute | solution.py:36
  39.0 7.0 %collective-permute-start.5 = (bf16[128,768]{1,0:T(8,128)(2,1)S(1)}, bf16[128,768]{1,0:T(8,128)(2,1)S(1)}, u32[]{:S(2)}, u32[]{:S(2)}) collective-permute-start(bf16[128,768]{1,0:T(8,128)(2,1)S(1)} %add_convert_fusion.17.a), channel_id=1, source_target_pairs={{0,3},{1,2},{2,1},{3,0},{4,7},{5,6},{6,5},{7,4},{8,11},{9,10},{10,... | collective-permute-start | bytes 589832 | tf_op jit(solution)/shard_map/ppermute | solution.py:36
  47.2 7.5 %collective-permute-start.7 = (bf16[128,768]{1,0:T(8,128)(2,1)S(1)}, bf16[128,768]{1,0:T(8,128)(2,1)S(1)}, u32[]{:S(2)}, u32[]{:S(2)}) collective-permute-start(bf16[128,768]{1,0:T(8,128)(2,1)S(1)} %get-tuple-element.144), channel_id=1, source_target_pairs={{0,1},{1,0},{2,3},{3,2},{4,5},{5,4},{6,7},{7,6},{8,9},{9,8},{10,11... | collective-permute-start | bytes 589832 | tf_op jit(solution)/shard_map/ppermute | solution.py:36
  48.0 8.3 %collective-permute-start.9 = (bf16[128,768]{1,0:T(8,128)(2,1)S(1)}, bf16[128,768]{1,0:T(8,128)(2,1)S(1)}, u32[]{:S(2)}, u32[]{:S(2)}) collective-permute-start(bf16[128,768]{1,0:T(8,128)(2,1)S(1)} %get-tuple-element.145), channel_id=1, source_target_pairs={{0,3},{1,2},{2,1},{3,0},{4,7},{5,6},{6,5},{7,4},{8,11},{9,10},{10,... | collective-permute-start | bytes 589832 | tf_op jit(solution)/shard_map/ppermute | solution.py:36
  49.8 9.7 %collective-permute-start.11 = (bf16[128,384]{1,0:T(8,128)(2,1)S(1)}, bf16[128,384]{1,0:T(8,128)(2,1)S(1)}, u32[]{:S(2)}, u32[]{:S(2)}) collective-permute-start(bf16[128,384]{1,0:T(8,128)(2,1)S(1)} %get-tuple-element.143.own), channel_id=1, source_target_pairs={{0,1},{1,0},{2,3},{3,2},{4,5},{5,4},{6,7},{7,6},{8,9},{9,8},{10,11... | collective-permute-start | bytes 294920 | tf_op jit(solution)/shard_map/ppermute | solution.py:36
  51.2 8.3 %collective-permute-start.12 = (bf16[128,384]{1,0:T(8,128)(2,1)S(1)}, bf16[128,384]{1,0:T(8,128)(2,1)S(1)}, u32[]{:S(2)}, u32[]{:S(2)}) collective-permute-start(bf16[128,384]{1,0:T(8,128)(2,1)S(1)} %get-tuple-element.143.own), channel_id=1, source_target_pairs={{0,3},{1,2},{2,1},{3,0},{4,7},{5,6},{6,5},{7,4},{8,11},{9,10},{10,... | collective-permute-start | bytes 294920 | tf_op jit(solution)/shard_map/ppermute | solution.py:36
  52.5 7.0 %collective-permute-start.13 = (bf16[128,384]{1,0:T(8,128)(2,1)S(1)}, bf16[128,384]{1,0:T(8,128)(2,1)S(1)}, u32[]{:S(2)}, u32[]{:S(2)}) collective-permute-start(bf16[128,384]{1,0:T(8,128)(2,1)S(1)} %get-tuple-element.143.own), channel_id=1, source_target_pairs={{0,2},{1,3},{2,0},{3,1},{4,6},{5,7},{6,4},{7,5},{8,10},{9,11},{10,... | collective-permute-start | bytes 294920 | tf_op jit(solution)/shard_map/ppermute | solution.py:36
  56.3 6.0 %collective-permute-start.10 = (bf16[128,768]{1,0:T(8,128)(2,1)S(1)}, bf16[128,768]{1,0:T(8,128)(2,1)S(1)}, u32[]{:S(2)}, u32[]{:S(2)}) collective-permute-start(bf16[128,768]{1,0:T(8,128)(2,1)S(1)} %add_convert_fusion.14.b), channel_id=1, source_target_pairs={{0,1},{1,0},{2,3},{3,2},{4,5},{5,4},{6,7},{7,6},{8,9},{9,8},{10,11... | collective-permute-start | bytes 589832 | tf_op jit(solution)/shard_map/ppermute | solution.py:36
  57.3 7.0 %collective-permute-start.8 = (bf16[128,768]{1,0:T(8,128)(2,1)S(1)}, bf16[128,768]{1,0:T(8,128)(2,1)S(1)}, u32[]{:S(2)}, u32[]{:S(2)}) collective-permute-start(bf16[128,768]{1,0:T(8,128)(2,1)S(1)} %add_convert_fusion.15.a), channel_id=1, source_target_pairs={{0,3},{1,2},{2,1},{3,0},{4,7},{5,6},{6,5},{7,4},{8,11},{9,10},{10,... | collective-permute-start | bytes 589832 | tf_op jit(solution)/shard_map/ppermute | solution.py:36
  65.5 7.8 %collective-permute-start.14 = (bf16[128,768]{1,0:T(8,128)(2,1)S(1)}, bf16[128,768]{1,0:T(8,128)(2,1)S(1)}, u32[]{:S(2)}, u32[]{:S(2)}) collective-permute-start(bf16[128,768]{1,0:T(8,128)(2,1)S(1)} %get-tuple-element.158), channel_id=1, source_target_pairs={{0,1},{1,0},{2,3},{3,2},{4,5},{5,4},{6,7},{7,6},{8,9},{9,8},{10,11... | collective-permute-start | bytes 589832 | tf_op jit(solution)/shard_map/ppermute | solution.py:36
  66.2 8.6 %collective-permute-start.15 = (bf16[128,768]{1,0:T(8,128)(2,1)S(1)}, bf16[128,768]{1,0:T(8,128)(2,1)S(1)}, u32[]{:S(2)}, u32[]{:S(2)}) collective-permute-start(bf16[128,768]{1,0:T(8,128)(2,1)S(1)} %get-tuple-element.159), channel_id=1, source_target_pairs={{0,3},{1,2},{2,1},{3,0},{4,7},{5,6},{6,5},{7,4},{8,11},{9,10},{10,... | collective-permute-start | bytes 589832 | tf_op jit(solution)/shard_map/ppermute | solution.py:36
  74.9 7.6 %collective-permute-start.17 = (bf16[128,768]{1,0:T(8,128)(2,1)S(1)}, bf16[128,768]{1,0:T(8,128)(2,1)S(1)}, u32[]{:S(2)}, u32[]{:S(2)}) collective-permute-start(bf16[128,768]{1,0:T(8,128)(2,1)S(1)} %add_convert_fusion.12.b), channel_id=1, source_target_pairs={{0,1},{1,0},{2,3},{3,2},{4,5},{5,4},{6,7},{7,6},{8,9},{9,8},{10,11... | collective-permute-start | bytes 589832 | tf_op jit(solution)/shard_map/ppermute | solution.py:36
  75.5 8.9 %collective-permute-start.16 = (bf16[128,768]{1,0:T(8,128)(2,1)S(1)}, bf16[128,768]{1,0:T(8,128)(2,1)S(1)}, u32[]{:S(2)}, u32[]{:S(2)}) collective-permute-start(bf16[128,768]{1,0:T(8,128)(2,1)S(1)} %add_convert_fusion.13.a), channel_id=1, source_target_pairs={{0,3},{1,2},{2,1},{3,0},{4,7},{5,6},{6,5},{7,4},{8,11},{9,10},{10,... | collective-permute-start | bytes 589832 | tf_op jit(solution)/shard_map/ppermute | solution.py:36
  86.0 5.7 %collective-permute-start.18 = (bf16[128,768]{1,0:T(8,128)(2,1)S(1)}, bf16[128,768]{1,0:T(8,128)(2,1)S(1)}, u32[]{:S(2)}, u32[]{:S(2)}) collective-permute-start(bf16[128,768]{1,0:T(8,128)(2,1)S(1)} %get-tuple-element.167), channel_id=1, source_target_pairs={{0,1},{1,0},{2,3},{3,2},{4,5},{5,4},{6,7},{7,6},{8,9},{9,8},{10,11... | collective-permute-start | bytes 589832 | tf_op jit(solution)/shard_map/ppermute | solution.py:36
  86.5 6.9 %collective-permute-start.19 = (bf16[128,768]{1,0:T(8,128)(2,1)S(1)}, bf16[128,768]{1,0:T(8,128)(2,1)S(1)}, u32[]{:S(2)}, u32[]{:S(2)}) collective-permute-start(bf16[128,768]{1,0:T(8,128)(2,1)S(1)} %get-tuple-element.168), channel_id=1, source_target_pairs={{0,3},{1,2},{2,1},{3,0},{4,7},{5,6},{6,5},{7,4},{8,11},{9,10},{10,... | collective-permute-start | bytes 589832 | tf_op jit(solution)/shard_map/ppermute | solution.py:36
  88.8 11.6 %collective-permute-start.22 = (bf16[384,1536]{1,0:T(8,128)(2,1)S(1)}, bf16[384,1536]{1,0:T(8,128)(2,1)S(1)}, u32[]{:S(2)}, u32[]{:S(2)}) collective-permute-start(bf16[384,1536]{1,0:T(8,128)(2,1)S(1)} %get-tuple-element.175), channel_id=1, source_target_pairs={{0,4},{4,0},{8,12},{12,8},{16,20},{20,16},{24,28},{28,24},{32,36},... | collective-permute-start | bytes 3538952 | tf_op jit(solution)/shard_map/ppermute | solution.py:36
  93.4 7.0 %collective-permute-start.20 = (bf16[128,768]{1,0:T(8,128)(2,1)S(1)}, bf16[128,768]{1,0:T(8,128)(2,1)S(1)}, u32[]{:S(2)}, u32[]{:S(2)}) collective-permute-start(bf16[128,768]{1,0:T(8,128)(2,1)S(1)} %add_convert_fusion.11.a), channel_id=1, source_target_pairs={{0,3},{1,2},{2,1},{3,0},{4,7},{5,6},{6,5},{7,4},{8,11},{9,10},{10,... | collective-permute-start | bytes 589832 | tf_op jit(solution)/shard_map/ppermute | solution.py:36
  94.4 5.7 %collective-permute-start.21 = (bf16[128,768]{1,0:T(8,128)(2,1)S(1)}, bf16[128,768]{1,0:T(8,128)(2,1)S(1)}, u32[]{:S(2)}, u32[]{:S(2)}) collective-permute-start(bf16[128,768]{1,0:T(8,128)(2,1)S(1)} %add_convert_fusion.10.b), channel_id=1, source_target_pairs={{0,1},{1,0},{2,3},{3,2},{4,5},{5,4},{6,7},{7,6},{8,9},{9,8},{10,11... | collective-permute-start | bytes 589832 | tf_op jit(solution)/shard_map/ppermute | solution.py:36
  101.7 5.7 %collective-permute-start.23 = (bf16[128,768]{1,0:T(8,128)(2,1)S(1)}, bf16[128,768]{1,0:T(8,128)(2,1)S(1)}, u32[]{:S(2)}, u32[]{:S(2)}) collective-permute-start(bf16[128,768]{1,0:T(8,128)(2,1)S(1)} %get-tuple-element.184), channel_id=1, source_target_pairs={{0,1},{1,0},{2,3},{3,2},{4,5},{5,4},{6,7},{7,6},{8,9},{9,8},{10,11... | collective-permute-start | bytes 589832 | tf_op jit(solution)/shard_map/ppermute | solution.py:36
  101.8 7.1 %collective-permute-start.24 = (bf16[128,768]{1,0:T(8,128)(2,1)S(1)}, bf16[128,768]{1,0:T(8,128)(2,1)S(1)}, u32[]{:S(2)}, u32[]{:S(2)}) collective-permute-start(bf16[128,768]{1,0:T(8,128)(2,1)S(1)} %get-tuple-element.185), channel_id=1, source_target_pairs={{0,3},{1,2},{2,1},{3,0},{4,7},{5,6},{6,5},{7,4},{8,11},{9,10},{10,... | collective-permute-start | bytes 589832 | tf_op jit(solution)/shard_map/ppermute | solution.py:36
  105.5 12.7 %collective-permute-start.28 = (bf16[192,1536]{1,0:T(8,128)(2,1)S(1)}, bf16[192,1536]{1,0:T(8,128)(2,1)S(1)}, u32[]{:S(2)}, u32[]{:S(2)}) collective-permute-start(bf16[192,1536]{1,0:T(8,128)(2,1)S(1)} %get-tuple-element.194), channel_id=1, source_target_pairs={{0,32},{4,36},{8,40},{12,44},{16,48},{20,52},{24,56},{28,60},{32,0... | collective-permute-start | bytes 1769480 | tf_op jit(solution)/shard_map/ppermute | solution.py:36
  106.9 11.2 %collective-permute-start.27 = (bf16[384,1536]{1,0:T(8,128)(2,1)S(1)}, bf16[384,1536]{1,0:T(8,128)(2,1)S(1)}, u32[]{:S(2)}, u32[]{:S(2)}) collective-permute-start(bf16[384,1536]{1,0:T(8,128)(2,1)S(1)} %get-tuple-element.191), channel_id=1, source_target_pairs={{0,4},{4,0},{8,12},{12,8},{16,20},{20,16},{24,28},{28,24},{32,36},... | collective-permute-start | bytes 3538952 | tf_op jit(solution)/shard_map/ppermute | solution.py:36
  108.9 9.2 %collective-permute-start.25 = (bf16[128,768]{1,0:T(8,128)(2,1)S(1)}, bf16[128,768]{1,0:T(8,128)(2,1)S(1)}, u32[]{:S(2)}, u32[]{:S(2)}) collective-permute-start(bf16[128,768]{1,0:T(8,128)(2,1)S(1)} %add_convert_fusion.9.a), channel_id=1, source_target_pairs={{0,3},{1,2},{2,1},{3,0},{4,7},{5,6},{6,5},{7,4},{8,11},{9,10},{10,... | collective-permute-start | bytes 589832 | tf_op jit(solution)/shard_map/ppermute | solution.py:36
  112.4 5.7 %collective-permute-start.26 = (bf16[128,768]{1,0:T(8,128)(2,1)S(1)}, bf16[128,768]{1,0:T(8,128)(2,1)S(1)}, u32[]{:S(2)}, u32[]{:S(2)}) collective-permute-start(bf16[128,768]{1,0:T(8,128)(2,1)S(1)} %add_convert_fusion.8.b), channel_id=1, source_target_pairs={{0,1},{1,0},{2,3},{3,2},{4,5},{5,4},{6,7},{7,6},{8,9},{9,8},{10,11... | collective-permute-start | bytes 589832 | tf_op jit(solution)/shard_map/ppermute | solution.py:36
  118.5 16.5 %collective-permute-start.35 = (bf16[192,1536]{1,0:T(8,128)(2,1)S(1)}, bf16[192,1536]{1,0:T(8,128)(2,1)S(1)}, u32[]{:S(2)}, u32[]{:S(2)}) collective-permute-start(bf16[192,1536]{1,0:T(8,128)(2,1)S(1)} %get-tuple-element.217), channel_id=1, source_target_pairs={{0,32},{4,36},{8,40},{12,44},{16,48},{20,52},{24,56},{28,60},{32,0... | collective-permute-start | bytes 1769480 | tf_op jit(solution)/shard_map/ppermute | solution.py:36
  119.9 5.7 %collective-permute-start.29 = (bf16[128,768]{1,0:T(8,128)(2,1)S(1)}, bf16[128,768]{1,0:T(8,128)(2,1)S(1)}, u32[]{:S(2)}, u32[]{:S(2)}) collective-permute-start(bf16[128,768]{1,0:T(8,128)(2,1)S(1)} %get-tuple-element.203), channel_id=1, source_target_pairs={{0,1},{1,0},{2,3},{3,2},{4,5},{5,4},{6,7},{7,6},{8,9},{9,8},{10,11... | collective-permute-start | bytes 589832 | tf_op jit(solution)/shard_map/ppermute | solution.py:36
  120.0 7.0 %collective-permute-start.30 = (bf16[128,768]{1,0:T(8,128)(2,1)S(1)}, bf16[128,768]{1,0:T(8,128)(2,1)S(1)}, u32[]{:S(2)}, u32[]{:S(2)}) collective-permute-start(bf16[128,768]{1,0:T(8,128)(2,1)S(1)} %get-tuple-element.204), channel_id=1, source_target_pairs={{0,3},{1,2},{2,1},{3,0},{4,7},{5,6},{6,5},{7,4},{8,11},{9,10},{10,... | collective-permute-start | bytes 589832 | tf_op jit(solution)/shard_map/ppermute | solution.py:36
  122.2 8.2 %collective-permute-start.34 = (bf16[96,1536]{1,0:T(8,128)(2,1)S(1)}, bf16[96,1536]{1,0:T(8,128)(2,1)S(1)}, u32[]{:S(2)}, u32[]{:S(2)}) collective-permute-start(bf16[96,1536]{1,0:T(8,128)(2,1)S(1)} %get-tuple-element.250), channel_id=1, source_target_pairs={{0,96},{4,100},{8,104},{12,108},{16,112},{20,116},{24,120},{28,124... | collective-permute-start | bytes 884744 | tf_op jit(solution)/shard_map/ppermute | solution.py:36
  125.4 4.1 %collective-permute-start.33 = (bf16[384,1536]{1,0:T(8,128)(2,1)S(1)}, bf16[384,1536]{1,0:T(8,128)(2,1)S(1)}, u32[]{:S(2)}, u32[]{:S(2)}) collective-permute-start(bf16[384,1536]{1,0:T(8,128)(2,1)S(1)} %get-tuple-element.210), channel_id=1, source_target_pairs={{0,4},{4,0},{8,12},{12,8},{16,20},{20,16},{24,28},{28,24},{32,36},... | collective-permute-start | bytes 3538952 | tf_op jit(solution)/shard_map/ppermute | solution.py:36
  127.0 8.0 %collective-permute-start.31 = (bf16[128,768]{1,0:T(8,128)(2,1)S(1)}, bf16[128,768]{1,0:T(8,128)(2,1)S(1)}, u32[]{:S(2)}, u32[]{:S(2)}) collective-permute-start(bf16[128,768]{1,0:T(8,128)(2,1)S(1)} %add_convert_fusion.7.a), channel_id=1, source_target_pairs={{0,3},{1,2},{2,1},{3,0},{4,7},{5,6},{6,5},{7,4},{8,11},{9,10},{10,... | collective-permute-start | bytes 589832 | tf_op jit(solution)/shard_map/ppermute | solution.py:36
  129.3 5.7 %collective-permute-start.32 = (bf16[128,768]{1,0:T(8,128)(2,1)S(1)}, bf16[128,768]{1,0:T(8,128)(2,1)S(1)}, u32[]{:S(2)}, u32[]{:S(2)}) collective-permute-start(bf16[128,768]{1,0:T(8,128)(2,1)S(1)} %add_convert_fusion.6.b), channel_id=1, source_target_pairs={{0,1},{1,0},{2,3},{3,2},{4,5},{5,4},{6,7},{7,6},{8,9},{9,8},{10,11... | collective-permute-start | bytes 589832 | tf_op jit(solution)/shard_map/ppermute | solution.py:36
  135.2 12.4 %collective-permute-start.45 = (bf16[96,1536]{1,0:T(8,128)(2,1)S(1)}, bf16[96,1536]{1,0:T(8,128)(2,1)S(1)}, u32[]{:S(2)}, u32[]{:S(2)}) collective-permute-start(bf16[96,1536]{1,0:T(8,128)(2,1)S(1)} %get-tuple-element.248), channel_id=1, source_target_pairs={{0,96},{4,100},{8,104},{12,108},{16,112},{20,116},{24,120},{28,124... | collective-permute-start | bytes 884744 | tf_op jit(solution)/shard_map/ppermute | solution.py:36
  136.8 12.6 %collective-permute-start.41 = (bf16[192,1536]{1,0:T(8,128)(2,1)S(1)}, bf16[192,1536]{1,0:T(8,128)(2,1)S(1)}, u32[]{:S(2)}, u32[]{:S(2)}) collective-permute-start(bf16[192,1536]{1,0:T(8,128)(2,1)S(1)} %get-tuple-element.239), channel_id=1, source_target_pairs={{0,8},{4,12},{8,0},{12,4},{16,24},{20,28},{24,16},{28,20},{32,40},... | collective-permute-start | bytes 1769480 | tf_op jit(solution)/shard_map/ppermute | solution.py:36
  138.6 5.6 %collective-permute-start.37 = (bf16[128,384]{1,0:T(8,128)(2,1)S(1)}, bf16[128,384]{1,0:T(8,128)(2,1)S(1)}, u32[]{:S(2)}, u32[]{:S(2)}) collective-permute-start(bf16[128,384]{1,0:T(8,128)(2,1)S(1)} %get-tuple-element.230), channel_id=1, source_target_pairs={{0,1},{1,0},{2,3},{3,2},{4,5},{5,4},{6,7},{7,6},{8,9},{9,8},{10,11... | collective-permute-start | bytes 294920 | tf_op jit(solution)/shard_map/ppermute | solution.py:36
  138.9 5.8 %collective-permute-start.38 = (bf16[128,384]{1,0:T(8,128)(2,1)S(1)}, bf16[128,384]{1,0:T(8,128)(2,1)S(1)}, u32[]{:S(2)}, u32[]{:S(2)}) collective-permute-start(bf16[128,384]{1,0:T(8,128)(2,1)S(1)} %get-tuple-element.231), channel_id=1, source_target_pairs={{0,3},{1,2},{2,1},{3,0},{4,7},{5,6},{6,5},{7,4},{8,11},{9,10},{10,... | collective-permute-start | bytes 294920 | tf_op jit(solution)/shard_map/ppermute | solution.py:36
  141.1 6.1 %collective-permute-start.39 = (bf16[128,384]{1,0:T(8,128)(2,1)S(1)}, bf16[128,384]{1,0:T(8,128)(2,1)S(1)}, u32[]{:S(2)}, u32[]{:S(2)}) collective-permute-start(bf16[128,384]{1,0:T(8,128)(2,1)S(1)} %get-tuple-element.232), channel_id=1, source_target_pairs={{0,2},{1,3},{2,0},{3,1},{4,6},{5,7},{6,4},{7,5},{8,10},{9,11},{10,... | collective-permute-start | bytes 294920 | tf_op jit(solution)/shard_map/ppermute | solution.py:36
  144.2 7.7 %collective-permute-start.36 = (bf16[384,1536]{1,0:T(8,128)(2,1)S(1)}, bf16[384,1536]{1,0:T(8,128)(2,1)S(1)}, u32[]{:S(2)}, u32[]{:S(2)}) collective-permute-start(bf16[384,1536]{1,0:T(8,128)(2,1)S(1)} %get-tuple-element.228), channel_id=1, source_target_pairs={{0,4},{4,0},{8,12},{12,8},{16,20},{20,16},{24,28},{28,24},{32,36},... | collective-permute-start | bytes 3538952 | tf_op jit(solution)/shard_map/ppermute | solution.py:36
  147.4 4.4 %collective-permute-start.40 = (bf16[16,1536]{1,0:T(8,128)(2,1)S(1)}, bf16[16,1536]{1,0:T(8,128)(2,1)S(1)}, u32[]{:S(2)}, u32[]{:S(2)}) collective-permute-start(bf16[16,1536]{1,0:T(8,128)(2,1)S(1)} %get-tuple-element.237), channel_id=1, source_target_pairs={{0,4},{4,0},{8,12},{12,8},{16,20},{20,16},{24,28},{28,24},{32,36},... | collective-permute-start | bytes 147464 | tf_op jit(solution)/shard_map/ppermute | solution.py:36
  147.6 9.5 %collective-permute-start.46 = (bf16[96,1536]{1,0:T(8,128)(2,1)S(1)}, bf16[96,1536]{1,0:T(8,128)(2,1)S(1)}, u32[]{:S(2)}, u32[]{:S(2)}) collective-permute-start(bf16[96,1536]{1,0:T(8,128)(2,1)S(1)} %pad_maximum_fusion), channel_id=1, source_target_pairs={{0,8},{4,12},{8,0},{12,4},{16,24},{20,28},{24,16},{28,20},{32,40},... | collective-permute-start | bytes 884744 | tf_op jit(solution)/shard_map/ppermute | solution.py:36
  149.5 10.1 %collective-permute-start.42 = (bf16[96,1536]{1,0:T(8,128)(2,1)S(1)}, bf16[96,1536]{1,0:T(8,128)(2,1)S(1)}, u32[]{:S(2)}, u32[]{:S(2)}) collective-permute-start(bf16[96,1536]{1,0:T(8,128)(2,1)S(1)} %get-tuple-element.252), channel_id=1, source_target_pairs={{0,24},{4,28},{8,16},{12,20},{16,8},{20,12},{24,0},{28,4},{32,56},... | collective-permute-start | bytes 884744 | tf_op jit(solution)/shard_map/ppermute | solution.py:36
  153.4 31.4 %all-to-all-start.1 = ((bf16[16,32,1536]{2,1,0:T(8,128)(2,1)}), bf16[16,32,1536]{2,1,0:T(8,128)(2,1)S(1)}, u32[]{:S(2)}, u32[]{:S(2)}) async-start(bf16[16,32,1536]{2,1,0:T(8,128)(2,1)} %shard_map.182), calls=%async_computation.1 | async-start | bytes 3145728 | tf_op jit(solution)/shard_map/all_to_all | solution.py:323
  159.7 19.4 %collective-permute-start.43 = (bf16[48,1536]{1,0:T(8,128)(2,1)S(1)}, bf16[48,1536]{1,0:T(8,128)(2,1)S(1)}, u32[]{:S(2)}, u32[]{:S(2)}) collective-permute-start(bf16[48,1536]{1,0:T(8,128)(2,1)S(1)} %get-tuple-element.258), channel_id=1, source_target_pairs={{0,32},{4,36},{8,40},{12,44},{16,48},{20,52},{24,56},{28,60},{32,0... | collective-permute-start | bytes 442376 | tf_op jit(solution)/shard_map/ppermute | solution.py:36
  159.8 20.6 %collective-permute-start.47 = (bf16[48,1536]{1,0:T(8,128)(2,1)S(1)}, bf16[48,1536]{1,0:T(8,128)(2,1)S(1)}, u32[]{:S(2)}, u32[]{:S(2)}) collective-permute-start(bf16[48,1536]{1,0:T(8,128)(2,1)S(1)} %pad_maximum_fusion.2), channel_id=1, source_target_pairs={{0,24},{4,28},{8,16},{12,20},{16,8},{20,12},{24,0},{28,4},{32,56},... | collective-permute-start | bytes 442376 | tf_op jit(solution)/shard_map/ppermute | solution.py:36
  179.1 5.6 %collective-permute-start.44 = (bf16[24,1536]{1,0:T(8,128)(2,1)S(1)}, bf16[24,1536]{1,0:T(8,128)(2,1)S(1)}, u32[]{:S(2)}, u32[]{:S(2)}) collective-permute-start(bf16[24,1536]{1,0:T(8,128)(2,1)S(1)} %get-tuple-element.265), channel_id=1, source_target_pairs={{0,96},{4,100},{8,104},{12,108},{16,112},{20,116},{24,120},{28,124... | collective-permute-start | bytes 221192 | tf_op jit(solution)/shard_map/ppermute | solution.py:36
